TPU v7x, 32 devices: a whole 2x2x4 slice. The times are simulated.
32 devices in a mesh: items: 4 (over y, core), blk: 8 (over z, x).
Axes of the slice: x: 2, y: 2, z: 4, core: 2. Of those that a mesh axis runs over, the one named last changes fastest.
Arguments:
- decoder_in: bfloat16 [128, 128, 1024], P(('items', 'blk')), may hold values from -6 to 6
- memory: bfloat16 [128, 1024, 1024], P('items', 'blk'), may hold values from -6 to 6
- segment_ids: int32 [128, 128], P(('items', 'blk')), may hold values from 0 to 3, never falling along the last dimension, each value on 1 to 64 neighbouring positions
- memory_lengths: int32 [128], P(('items', 'blk')), may hold values from 51 to 1024
- w_self_in: bfloat16 [1024, 3072], P('blk'), may hold values from -0.1875 to 0.1875
- w_self_out: bfloat16 [1024, 1024], P('blk'), may hold values from -0.75 to 0.75
- w_cross_query: bfloat16 [1024, 1024], P('blk'), may hold values from -0.1875 to 0.1875
- w_cross_pair: bfloat16 [1024, 2048], P('blk'), may hold values from -0.1875 to 0.1875
- w_cross_out: bfloat16 [1024, 1024], P('blk'), may hold values from -3 to 3
- w_feed_up: bfloat16 [1024, 4096], P('blk'), may hold values from -0.1875 to 0.1875
- w_feed_down: bfloat16 [4096, 1024], P('blk'), may hold values from -0.09375 to 0.09375
- shifts: bfloat16 [10, 1024], P(None, 'blk'), may hold values from -2 to 2
- norm_gains: bfloat16 [3, 1024], P(None, 'blk'), may hold values from 0.5 to 1.5
- feed_bias: bfloat16 [4096], P('blk'), may hold values from -2 to 2
- out_grad: bfloat16 [128, 128, 1024], P(('items', 'blk')), may hold values from -6 to 6
Outputs:
- block_out: bfloat16 [128, 128, 1024], P(('items', 'blk'))
- decoder_grad: bfloat16 [128, 128, 1024], P(('items', 'blk'))
- memory_grad: bfloat16 [128, 1024, 1024], P('items', 'blk')
- grad_self_in: float32 [1024, 3072], P('blk')
- grad_self_out: float32 [1024, 1024], P('blk')
- grad_cross_query: float32 [1024, 1024], P('blk')
- grad_cross_pair: float32 [1024, 2048], P('blk')
- grad_cross_out: float32 [1024, 1024], P('blk')
- grad_feed_up: float32 [1024, 4096], P('blk')
- grad_feed_down: float32 [4096, 1024], P('blk')
- grad_shifts: float32 [10, 1024], P(None, 'blk')
- grad_norm_gains: float32 [3, 1024], P(None, 'blk')
- grad_feed_bias: float32 [4096], P('blk')
Inputs may be any that keep to these rules, and one draw needn't show every extreme that they name: `segment_ids`: ids never fall along an item's positions.
All inputs are finite; a program needn't handle non-finite values.
Results may differ from a plain program's by a relative error of at most 0.023.
Values may be sent and summed in bfloat16 or wider, within the bound.
No kernel may reach another device: no remote copies, remote signals or barrier semaphores. Data moves between devices by JAX's collectives and lax.ppermute only.
A program may use at most 256 MiB of HBM per device.

v0:
```python
import jax
import jax.numpy as jnp
from jax import lax
from jax.sharding import PartitionSpec as P

HEADS = 16


def layer_norm(values, gain, shift):
    centre = values - jnp.mean(values, axis=-1, keepdims=True)
    spread = jnp.mean(centre * centre, axis=-1, keepdims=True)
    return centre * lax.rsqrt(spread + 1e-05) * gain + shift


def exact_gelu(values):
    return jax.nn.gelu(values, approximate=False)


def outer_sum(left, right):
    return lax.dot_general(
        left, right, (((0,), (0,)), ((), ())), preferred_element_type=jnp.float32
    )


def times_transposed(left, right):
    return lax.dot_general(
        left, right, (((1,), (1,)), ((), ())), preferred_element_type=jnp.float32
    )


def column_sum(values):
    return jnp.sum(values.astype(jnp.float32), axis=0)


def masked_scores(queries, key_rows, allowed):
    scores = jnp.einsum("bqhd,bkhd->bhqk", queries, key_rows, preferred_element_type=jnp.float32)
    return jnp.where(allowed[:, None], scores, -1e30)


def attend_forward(queries, key_rows, value_rows, allowed):
    scores = masked_scores(queries, key_rows, allowed)
    largest = jnp.max(scores, axis=-1, keepdims=True)
    weights = jnp.exp(scores - largest)
    total_weight = jnp.sum(weights, axis=-1, keepdims=True)
    probability = weights / total_weight
    attended = jnp.einsum(
        "bhqk,bkhd->bqhd",
        probability.astype(jnp.bfloat16),
        value_rows,
        preferred_element_type=jnp.float32,
    )
    return (attended, largest + jnp.log(total_weight))


def attend_backward(queries, key_rows, value_rows, allowed, log_total, incoming):
    scores = masked_scores(queries, key_rows, allowed)
    probability = jnp.exp(scores - log_total)
    weight_grad = jnp.einsum(
        "bqhd,bkhd->bhqk", incoming, value_rows, preferred_element_type=jnp.float32
    )
    centred = jnp.sum(probability * weight_grad, axis=-1, keepdims=True)
    score_grad = (probability * (weight_grad - centred)).astype(jnp.bfloat16)
    query_grad = jnp.einsum(
        "bhqk,bkhd->bqhd", score_grad, key_rows, preferred_element_type=jnp.float32
    )
    key_grad = jnp.einsum(
        "bhqk,bqhd->bkhd", score_grad, queries, preferred_element_type=jnp.float32
    )
    value_grad = jnp.einsum(
        "bhqk,bqhd->bkhd",
        probability.astype(jnp.bfloat16),
        incoming,
        preferred_element_type=jnp.float32,
    )
    return (query_grad, key_grad, value_grad)


def per_device(
    decoder_in,
    memory,
    segment_ids,
    memory_lengths,
    w_self_in,
    w_self_out,
    w_cross_query,
    w_cross_pair,
    w_cross_out,
    w_feed_up,
    w_feed_down,
    shifts,
    norm_gains,
    feed_bias,
    out_grad,
):
    gathered = (
        lax.all_gather(w_self_in, "blk", axis=0, tiled=True),
        lax.all_gather(w_self_out, "blk", axis=0, tiled=True),
        lax.all_gather(w_cross_query, "blk", axis=0, tiled=True),
        lax.all_gather(w_cross_pair, "blk", axis=0, tiled=True),
        lax.all_gather(w_cross_out, "blk", axis=0, tiled=True),
        lax.all_gather(w_feed_up, "blk", axis=0, tiled=True),
        lax.all_gather(w_feed_down, "blk", axis=0, tiled=True),
        lax.all_gather(shifts, "blk", axis=1, tiled=True),
        lax.all_gather(norm_gains, "blk", axis=1, tiled=True),
        lax.all_gather(feed_bias, "blk", axis=0, tiled=True),
    )
    (
        self_proj,
        self_out,
        cross_query,
        cross_pair,
        cross_out,
        feed_up,
        feed_down,
        shift_low,
        gain_low,
        feed_shift_low,
    ) = gathered
    shift_rows = shift_low.astype(jnp.float32)
    gain_rows = gain_low.astype(jnp.float32)
    feed_shift = feed_shift_low.astype(jnp.float32)
    item_count, decoder_length, model_width = decoder_in.shape
    head_size = model_width // HEADS
    query_scale = head_size ** (-0.5)
    row_count = item_count * decoder_length
    head_shape = (item_count, decoder_length, HEADS, head_size)
    token_rows = decoder_in.reshape(row_count, model_width)
    projected = jnp.dot(token_rows, self_proj, preferred_element_type=jnp.float32)
    queries = (
        ((projected[:, :model_width] + shift_rows[0]) * query_scale)
        .astype(jnp.bfloat16)
        .reshape(head_shape)
    )
    key_rows = projected[:, model_width : 2 * model_width].astype(jnp.bfloat16).reshape(head_shape)
    value_rows = (
        (projected[:, 2 * model_width :] + shift_rows[1]).astype(jnp.bfloat16).reshape(head_shape)
    )
    position = jnp.arange(decoder_length)
    causal = position[None, :] <= position[:, None]
    self_allowed = (segment_ids[:, :, None] == segment_ids[:, None, :]) & causal[None]
    attended, self_total = attend_forward(queries, key_rows, value_rows, self_allowed)
    attended = attended.reshape(row_count, model_width).astype(jnp.bfloat16)
    branch = jnp.dot(attended, self_out, preferred_element_type=jnp.float32) + shift_rows[2]
    hidden, first_norm_back = jax.vjp(
        layer_norm, token_rows.astype(jnp.float32) + branch, gain_rows[0], shift_rows[7]
    )
    hidden_low = hidden.astype(jnp.bfloat16)
    cross_queries = (
        (
            (jnp.dot(hidden_low, cross_query, preferred_element_type=jnp.float32) + shift_rows[3])
            * query_scale
        )
        .astype(jnp.bfloat16)
        .reshape(head_shape)
    )
    pair_shift = jnp.concatenate([jnp.zeros((model_width,), jnp.float32), shift_rows[4]])
    source_rows = memory.reshape(-1, model_width)
    pair_rows = jnp.dot(source_rows, cross_pair, preferred_element_type=jnp.float32) + pair_shift
    owned_pair = pair_rows.astype(jnp.bfloat16).reshape(
        memory.shape[0], memory.shape[1], 2 * model_width
    )
    memory_pair = lax.all_to_all(owned_pair, "blk", split_axis=0, concat_axis=1, tiled=True)
    slot_count = memory_pair.shape[1]
    memory_head = (item_count, slot_count, HEADS, head_size)
    memory_keys = memory_pair[:, :, :model_width].reshape(memory_head)
    memory_values = memory_pair[:, :, model_width:].reshape(memory_head)
    slot_index = jnp.arange(slot_count)
    live = slot_index[None, :] < memory_lengths[:, None]
    memory_allowed = jnp.broadcast_to(live[:, None, :], (item_count, decoder_length, slot_count))
    cross_attended, cross_total = attend_forward(
        cross_queries, memory_keys, memory_values, memory_allowed
    )
    cross_attended = cross_attended.reshape(row_count, model_width).astype(jnp.bfloat16)
    cross_branch = (
        jnp.dot(cross_attended, cross_out, preferred_element_type=jnp.float32) + shift_rows[5]
    )
    second, second_norm_back = jax.vjp(
        layer_norm, hidden + cross_branch, gain_rows[1], shift_rows[8]
    )
    second_low = second.astype(jnp.bfloat16)
    activation = exact_gelu(
        jnp.dot(second_low, feed_up, preferred_element_type=jnp.float32) + feed_shift
    ).astype(jnp.bfloat16)
    feed_branch = jnp.dot(activation, feed_down, preferred_element_type=jnp.float32) + shift_rows[6]
    block_out, third_norm_back = jax.vjp(
        layer_norm, second + feed_branch, gain_rows[2], shift_rows[9]
    )
    third_grad, third_gain, third_shift = third_norm_back(
        out_grad.astype(jnp.float32).reshape(row_count, model_width)
    )
    down_low = third_grad.astype(jnp.bfloat16)
    upward = jnp.dot(second_low, feed_up, preferred_element_type=jnp.float32) + feed_shift
    activation_again, gelu_back = jax.vjp(exact_gelu, upward)
    activation_low = activation_again.astype(jnp.bfloat16)
    grad_down = outer_sum(activation_low, down_low)
    shift_six = column_sum(down_low)
    before_gelu = times_transposed(down_low, feed_down)
    upward_low = gelu_back(before_gelu)[0].astype(jnp.bfloat16)
    grad_up = outer_sum(second_low, upward_low)
    grad_feed_shift = column_sum(upward_low)
    second_grad = third_grad + times_transposed(upward_low, feed_up)
    cross_grad, second_gain, second_shift = second_norm_back(second_grad)
    cross_low = cross_grad.astype(jnp.bfloat16)
    grad_cross_out = outer_sum(cross_attended, cross_low)
    shift_five = column_sum(cross_low)
    cross_incoming = times_transposed(cross_low, cross_out).astype(jnp.bfloat16).reshape(head_shape)
    cross_query_grad, memory_key_grad, memory_value_grad = attend_backward(
        cross_queries, memory_keys, memory_values, memory_allowed, cross_total, cross_incoming
    )
    cross_query_low = (
        cross_query_grad.reshape(row_count, model_width).astype(jnp.bfloat16) * query_scale
    )
    grad_cross_query = outer_sum(hidden_low, cross_query_low)
    shift_three = column_sum(cross_query_low)
    hidden_grad = cross_grad + times_transposed(cross_query_low, cross_query)
    pair_grad = jnp.concatenate(
        [
            memory_key_grad.astype(jnp.bfloat16).reshape(item_count, slot_count, model_width),
            memory_value_grad.astype(jnp.bfloat16).reshape(item_count, slot_count, model_width),
        ],
        axis=2,
    )
    owner_grad = lax.all_to_all(pair_grad, "blk", split_axis=1, concat_axis=0, tiled=True)
    flat_grad = owner_grad.reshape(-1, 2 * model_width)
    grad_pair = outer_sum(source_rows, flat_grad)
    shift_four = column_sum(flat_grad[:, model_width:])
    memory_grad = times_transposed(flat_grad, cross_pair).astype(jnp.bfloat16).reshape(memory.shape)
    first_grad, first_gain, first_shift = first_norm_back(hidden_grad)
    self_low = first_grad.astype(jnp.bfloat16)
    grad_self_out = outer_sum(attended, self_low)
    shift_two = column_sum(self_low)
    self_incoming = times_transposed(self_low, self_out).astype(jnp.bfloat16).reshape(head_shape)
    query_grad, key_grad, value_grad = attend_backward(
        queries, key_rows, value_rows, self_allowed, self_total, self_incoming
    )
    query_low = query_grad.reshape(row_count, model_width).astype(jnp.bfloat16) * query_scale
    value_low = value_grad.reshape(row_count, model_width).astype(jnp.bfloat16)
    joined_grad = jnp.concatenate(
        [query_low, key_grad.reshape(row_count, model_width).astype(jnp.bfloat16), value_low],
        axis=1,
    )
    grad_self = outer_sum(token_rows, joined_grad)
    decoder_grad = (
        (first_grad + times_transposed(joined_grad, self_proj))
        .astype(jnp.bfloat16)
        .reshape(decoder_in.shape)
    )
    grad_shift_rows = jnp.stack(
        [
            column_sum(query_low),
            column_sum(value_low),
            shift_two,
            shift_three,
            shift_four,
            shift_five,
            shift_six,
            first_shift,
            second_shift,
            third_shift,
        ]
    )
    grad_gain_rows = jnp.stack([first_gain, second_gain, third_gain])
    block_low = block_out.astype(jnp.bfloat16).reshape(decoder_in.shape)
    shares = (
        lax.psum_scatter(grad_self, "blk", scatter_dimension=0, tiled=True),
        lax.psum_scatter(grad_self_out, "blk", scatter_dimension=0, tiled=True),
        lax.psum_scatter(grad_cross_query, "blk", scatter_dimension=0, tiled=True),
        lax.psum_scatter(grad_pair, "blk", scatter_dimension=0, tiled=True),
        lax.psum_scatter(grad_cross_out, "blk", scatter_dimension=0, tiled=True),
        lax.psum_scatter(grad_up, "blk", scatter_dimension=0, tiled=True),
        lax.psum_scatter(grad_down, "blk", scatter_dimension=0, tiled=True),
        lax.psum_scatter(grad_shift_rows, "blk", scatter_dimension=1, tiled=True),
        lax.psum_scatter(grad_gain_rows, "blk", scatter_dimension=1, tiled=True),
        lax.psum_scatter(grad_feed_shift, "blk", scatter_dimension=0, tiled=True),
    )
    totals = tuple(
        (
            lax.psum(shares[0].astype(jnp.bfloat16), "items").astype(jnp.float32),
            lax.psum(shares[1].astype(jnp.bfloat16), "items").astype(jnp.float32),
            lax.psum(shares[2].astype(jnp.bfloat16), "items").astype(jnp.float32),
            lax.psum(shares[3].astype(jnp.bfloat16), "items").astype(jnp.float32),
            lax.psum(shares[4].astype(jnp.bfloat16), "items").astype(jnp.float32),
            lax.psum(shares[5].astype(jnp.bfloat16), "items").astype(jnp.float32),
            lax.psum(shares[6].astype(jnp.bfloat16), "items").astype(jnp.float32),
            lax.psum(shares[7].astype(jnp.bfloat16), "items").astype(jnp.float32),
            lax.psum(shares[8].astype(jnp.bfloat16), "items").astype(jnp.float32),
            lax.psum(shares[9].astype(jnp.bfloat16), "items").astype(jnp.float32),
        )
    )
    return (block_low, decoder_grad, memory_grad) + totals


def solution(mesh):
    in_specs = (
        P(("items", "blk"), None, None),
        P("items", "blk", None),
        P(("items", "blk"), None),
        P(("items", "blk")),
        P("blk", None),
        P("blk", None),
        P("blk", None),
        P("blk", None),
        P("blk", None),
        P("blk", None),
        P("blk", None),
        P(None, "blk"),
        P(None, "blk"),
        P("blk"),
        P(("items", "blk"), None, None),
    )
    out_specs = (
        P(("items", "blk"), None, None),
        P(("items", "blk"), None, None),
        P("items", "blk", None),
        P("blk", None),
        P("blk", None),
        P("blk", None),
        P("blk", None),
        P("blk", None),
        P("blk", None),
        P("blk", None),
        P(None, "blk"),
        P(None, "blk"),
        P("blk"),
    )
    return jax.shard_map(
        per_device, mesh=mesh, in_specs=in_specs, out_specs=out_specs, check_vma=False
    )
```

profile of v0, /device:TPU:1, one launch (start us, length us, event | category | flops | bytes accessed | tf_op | source)
XLA Modules:
  0.0 2698.4 jit_solution(16869231248844352622)
XLA Ops:
  9.4 23.8 all_gather.31
  33.8 50.9 %all-gather.13.cloned.1.call-done = bf16[1024,2048]{1,0:T(8,128)(2,1)} async-done(((bf16[128,2048]{1,0:T(8,128)(2,1)}), bf16[1024,2048]{1,0:T(8,128)(2,1)}) %all-gather.13.cloned.1.call-update) | async-done | bytes 4194320 | tf_op jit(solution)/shard_map/all_gather | solution.py:99
  84.8 23.5 add_convert_fusion
  108.3 5.9 all-to-all-start
  116.7 439.9 %all-gather = bf16[8,1,512]{2,1,0:T(2,128)(2,1)S(1)} all-gather(bf16[1,1,512]{2,1,0:T(2,128)(2,1)S(1)} %reshape.270), channel_id=1, replica_groups=mesh['items'=4,'blk'=8] {'blk'}, dimensions={0}, use_global_device_ids=true | all-gather | bytes 9216 | tf_op jit(solution)/shard_map/all_gather | solution.py:105
  556.7 13.8 all_gather.33
  571.4 5.5 fusion.83
  582.7 4.4 reshape.278
  587.1 2.8 copy.116
  592.3 3.0 copy.117
  599.6 3.6 fusion.80
  603.6 14.4 all-gather.15.cloned.1.call-done
  618.0 2.9 multiply_convert_fusion.3
  623.2 2.8 copy.122
  626.1 25.0 copy.120
  651.0 25.3 all_to_all.27
  676.4 12.4 fusion.77
  688.7 15.5 select_reduce_fusion
  704.3 15.0 fusion
  719.4 14.7 fusion.44
  735.1 3.5 fusion.81
  740.2 53.7 %all-gather.19.cloned.1.call-done = bf16[1024,4096]{1,0:T(8,128)(2,1)} async-done(((bf16[128,4096]{1,0:T(8,128)(2,1)}), bf16[1024,4096]{1,0:T(8,128)(2,1)}) %all-gather.19.cloned.1.call-update) | async-done | bytes 8388624 | tf_op jit(solution)/shard_map/all_gather | solution.py:101
  793.9 28.1 %multiply_convert_fusion.1 = (bf16[512,4096]{1,0:T(8,128)(2,1)}, f32[512,4096]{1,0:T(8,128)}, f32[512,4096]{1,0:T(8,128)}) fusion(f32[4096]{0:T(1024)S(1)} %bitcast.224, bf16[1024,4096]{1,0:T(8,128)(2,1)} %all-gather.19.cloned.1.call-done, f32[512,1024]{1,0:T(8,128)} %copy-done.13, f32[1024]{0:T(1024)S(1)} %bitcast.236, f32[1024]{0:T(1024)S(1)} %bitcast.226, ...), kind=kOutput, calls=%fused_computation.20 | convolution fusion | flops 4436000768 | bytes 31485952 | tf_op jit(solution)/shard_map/dot_general | solution.py:182
  822.0 97.2 %all-gather.21.cloned.1.call-done = bf16[4096,1024]{1,0:T(8,128)(2,1)} async-done(((bf16[512,1024]{1,0:T(8,128)(2,1)}), bf16[4096,1024]{1,0:T(8,128)(2,1)}) %all-gather.21.cloned.1.call-update) | async-done | bytes 8388624 | tf_op jit(solution)/shard_map/all_gather | solution.py:102
  919.2 8.7 fusion.82
  931.9 14.3 convert_reduce_fusion.1
  946.2 9.7 multiply_reduce_fusion.2
  963.5 25.0 multiply_reduce_fusion
  988.6 27.8 %multiply_convert_fusion = bf16[4,16,128,1024]{3,2,1,0:T(8,128)(2,1)} fusion(f32[4,16,128,1024]{3,2,1,0:T(8,128)} %get-tuple-element.130, f32[4,16,128,1024]{3,2,1,0:T(8,128)} %get-tuple-element.122, f32[4,16,128]{2,1,0:T(8,128)S(1)} %get-tuple-element.129, f32[4,16,128]{2,1,0:T(8,128)S(1)} %log_add_fusion.1, pred[4,1024]{1,0:T(4,128)(4,1)S(1)} %iota_compare_fusion.1), kind=kLoop, calls=%fused_computation | loop fusion | flops 41943040 | bytes 83955712 | tf_op jit(solution)/shard_map/convert_element_type | solution.py:62
  1016.4 12.2 convert_reduce_fusion.5
  1029.6 4.0 multiply_reduce_fusion.3
  1034.6 4.8 fusion.48
  1040.1 4.7 fusion.45
  1050.4 3.2 fusion.51
  1055.3 3.5 convolution_convert_fusion.5
  1058.8 4.2 reshape.281
  1062.9 2.8 copy.128
  1065.8 4.0 convert_reduce_fusion.7
  1079.8 6.5 convolution_bitcast_fusion
  1087.9 10.5 fusion.67
  1098.4 18.0 fusion.14
  1116.4 15.1 copy.142
  1131.5 11.7 convolution_convert_fusion.1
  1143.2 15.1 copy.141
  1158.2 10.6 fusion.84
  1168.9 11.6 pad_maximum_fusion
  1180.6 567.5 %all_to_all.33 = bf16[4,1024,2048]{2,0,1:T(4,128)(2,1)S(1)} all-to-all(bf16[4,1024,2048]{2,0,1:T(4,128)(2,1)S(1)} %pad_maximum_fusion), channel_id=1, replica_groups=mesh['items'=4,'blk'=8] {'blk'}, dimensions={1} | all-to-all | bytes 33554432 | tf_op jit(solution)/shard_map/all_to_all | solution.py:223
  1748.1 23.1 copy.143
  1771.3 7.1 copy.144
  1778.3 21.6 convolution_bitcast_fusion.1
  1802.3 4.8 convert_reduce_fusion
  1808.5 8.3 add_convert_fusion.2
  1816.8 31.0 %all-reduce.1 = bf16[4096]{0:T(1024)(128)(2,1)S(1)} all-reduce(f32[4096]{0:T(1024)S(1)} %copy-done.53), channel_id=11, replica_groups=mesh['items'=4,'blk'=8] {'blk'}, use_global_device_ids=true, to_apply=%region_50.51.clone | all-reduce | flops 4096 | bytes 24576
  1854.2 2.4 convert_element_type.282
  1856.6 239.2 %reduce-scatter.22.cloned.1.call-done = f32[128,4096]{1,0:T(8,128)} async-done(((f32[1024,4096]{1,0:T(8,128)}), f32[128,4096]{1,0:T(8,128)}) %reduce-scatter.22.cloned.1.call-update) | async-done | bytes 2097168 | tf_op jit(solution)/shard_map/reduce_scatter | solution.py:270
  2095.8 2.7 convert_element_type.292
  2098.5 282.7 %reduce-scatter.24.cloned.1.call-done = f32[512,1024]{1,0:T(8,128)} async-done(((f32[4096,1024]{1,0:T(8,128)}), f32[512,1024]{1,0:T(8,128)}) %reduce-scatter.24.cloned.1.call-update) | async-done | bytes 2097168 | tf_op jit(solution)/shard_map/reduce_scatter | solution.py:271
  2381.2 2.7 convert_element_type.294
  2383.9 149.8 %reduce-scatter.18.cloned.1.call-done = f32[128,2048]{0,1:T(8,128)} async-done(((f32[1024,2048]{0,1:T(8,128)}), f32[128,2048]{0,1:T(8,128)}) %reduce-scatter.18.cloned.1.call-update) | async-done | bytes 1048592 | tf_op jit(solution)/shard_map/reduce_scatter | solution.py:268
  2535.8 23.5 convolution_convert_fusion
  2559.4 28.2 %reduce-scatter.26.cloned.1.call-done = f32[10,128]{1,0:T(8,128)} async-done(((f32[10,1024]{1,0:T(8,128)}), f32[10,128]{1,0:T(8,128)}) %reduce-scatter.26.cloned.1.call-update) | async-done | bytes 5136 | tf_op jit(solution)/shard_map/reduce_scatter | solution.py:272
  2588.3 7.9 all-reduce.2
  2598.0 81.2 %all-reduce.6.cloned.1.call-done = (bf16[128,3072]{0,1:T(8,128)(2,1)}, bf16[128,2048]{0,1:T(8,128)(2,1)}, bf16[128,1024]{1,0:T(8,128)(2,1)}, bf16[128,1024]{1,0:...) async-done(((bf16[128,3072]{0,1:T(8,128)(2,1)}, bf16[128,2048]{0,1:T(8,128)(2,1)}, bf16[128,1024]{1,0:T(8,128)(2,1)}, ...) | async-done | bytes 4194320 | tf_op jit(solution)/shard_map/psum | solution.py:278
  2684.8 2.5 copy.145
  (275 shorter events, 80.5 us)
Async XLA Ops:
  7.2 77.6 %all-gather.13.cloned.1.call-start = ((), (), s32[]{:S(2)}) async-start(), calls=%async_computation.13 | async-start | bytes 4718592 | tf_op jit(solution)/shard_map/all_gather | solution.py:99
  7.9 563.4 %all-gather.9.cloned.1.call-start = ((), (), s32[]{:S(2)}) async-start(), calls=%async_computation.11 | async-start | bytes 7077888 | tf_op jit(solution)/shard_map/all_gather | solution.py:96
  8.7 590.9 %all-gather.11.cloned.1.call-start = ((), (), s32[]{:S(2)}) async-start(), calls=%async_computation.12 | async-start | bytes 2359296 | tf_op jit(solution)/shard_map/all_gather | solution.py:97
  33.8 701.2 %copy-start.60 = (f32[1,1024]{1,0:T(1,128)}, f32[1,1024]{1,0:T(1,128)S(1)}, u32[]{:S(2)}) copy-start(f32[1,1024]{1,0:T(1,128)S(1)} %get-tuple-element.109) | copy-start | bytes 12292
  108.2 8.5 copy-start.66
  108.2 448.4 %copy-start.67 = (bf16[3,128]{1,0:T(4,128)(2,1)S(1)}, bf16[3,128]{1,0:T(4,128)(2,1)}, u32[]{:S(2)}) copy-start(bf16[3,128]{1,0:T(4,128)(2,1)} %param.27) | copy-start | bytes 2308
  108.2 462.2 %copy-start.68 = (s32[4]{0:T(128)S(1)}, s32[4]{0:T(128)}, u32[]{:S(2)}) copy-start(s32[4]{0:T(128)} %param.18) | copy-start | bytes 52
  108.2 462.9 %copy-start.58 = (s32[4,128]{1,0:T(4,128)S(1)}, s32[4,128]{1,0:T(4,128)}, u32[]{:S(2)}) copy-start(s32[4,128]{1,0:T(4,128)} %param.17) | copy-start | bytes 6148
  108.3 463.1 %copy-start.36 = (bf16[4,128,1024]{2,1,0:T(8,128)(2,1)S(1)}, bf16[4,128,1024]{2,1,0:T(8,128)(2,1)}, u32[]{:S(2)}) copy-start(bf16[4,128,1024]{2,1,0:T(8,128)(2,1)} %param.15) | copy-start | bytes 3145732
  108.3 517.8 %all-to-all-start = ((bf16[32,128,2048]{2,1,0:T(8,128)(2,1)}), bf16[32,128,2048]{2,1,0:T(8,128)(2,1)}, u32[]{:S(2)}, u32[]{:S(2)}) async-start(bf16[32,128,2048]{2,1,0:T(8,128)(2,1)} %bitcast.192), calls=%async_computation | async-start | bytes 33554432 | tf_op jit(solution)/shard_map/all_to_all | solution.py:162
  114.2 503.8 %all-gather.15.cloned.1.call-start = ((), (), s32[]{:S(2)}) async-start(), calls=%async_computation.14 | async-start | bytes 2359296 | tf_op jit(solution)/shard_map/all_gather | solution.py:98
  114.7 620.3 %all-gather.17.cloned.1.call-start = ((), (), s32[]{:S(2)}) async-start(), calls=%async_computation.15 | async-start | bytes 2359296 | tf_op jit(solution)/shard_map/all_gather | solution.py:100
  115.3 678.6 %all-gather.19.cloned.1.call-start = ((), (), s32[]{:S(2)}) async-start(), calls=%async_computation.16 | async-start | bytes 9437184 | tf_op jit(solution)/shard_map/all_gather | solution.py:101
  115.9 803.3 %all-gather.21.cloned.1.call-start = ((), (), s32[]{:S(2)}) async-start(), calls=%async_computation.17 | async-start | bytes 9437184 | tf_op jit(solution)/shard_map/all_gather | solution.py:102
  116.6 1731.3 %reduce-scatter.28.cloned.1.call-start = ((), (), s32[]{:S(2)}) async-start(), calls=%async_computation.26 | async-start | bytes 589824
  571.2 163.8 %copy-start.54 = (f32[1,1024]{1,0:T(1,128)}, f32[1,1024]{1,0:T(1,128)S(1)}, u32[]{:S(2)}) copy-start(f32[1,1024]{1,0:T(1,128)S(1)} %get-tuple-element.116) | copy-start | bytes 12292
  571.3 26.0 copy-start.25
  582.7 12.7 copy-start.7
  582.7 7.3 copy-start.20
  590.0 6.3 copy-start.9
  603.2 131.8 %copy-start.3 = (f32[512,1024]{1,0:T(8,128)}, f32[512,1024]{1,0:T(8,128)S(1)}, u32[]{:S(2)}) copy-start(f32[512,1024]{1,0:T(8,128)S(1)} %get-tuple-element.120) | copy-start | bytes 6291460
  603.2 131.8 %copy-start.46 = (f32[512]{0:T(512)}, f32[512]{0:T(512)S(1)}, u32[]{:S(2)}) copy-start(f32[512]{0:T(512)S(1)} %broadcast_multiply_fusion.2) | copy-start | bytes 6148
  603.6 17.3 copy-start.48
  603.6 131.4 %copy-start.56 = (f32[512]{0:T(512)}, f32[512]{0:T(512)S(1)}, u32[]{:S(2)}) copy-start(f32[512]{0:T(512)S(1)} %fusion.60) | copy-start | bytes 6148
  626.1 62.7 %copy-start.5 = (bf16[4,128,16,64]{1,3,2,0:T(8,128)(2,1)}, bf16[4,128,16,64]{1,3,2,0:T(8,128)(2,1)S(1)}, u32[]{:S(2)}) copy-start(bf16[4,128,16,64]{1,3,2,0:T(8,128)(2,1)S(1)} %copy.122) | copy-start | bytes 3145732
  704.3 15.1 copy-start.2
  719.3 15.7 copy-start.63
  735.1 58.8 %copy-start.59 = (f32[1,1024]{1,0:T(1,128)S(1)}, f32[1,1024]{1,0:T(1,128)}, u32[]{:S(2)}) copy-start(f32[1,1024]{1,0:T(1,128)} %get-tuple-element.106) | copy-start | bytes 12292
  793.9 125.3 %copy-start.14 = (f32[512,1024]{1,0:T(8,128)S(1)}, f32[512,1024]{1,0:T(8,128)}, u32[]{:S(2)}) copy-start(f32[512,1024]{1,0:T(8,128)} %copy-done.13) | copy-start | bytes 6291460
  793.9 125.3 %copy-start.62 = (f32[1,1024]{1,0:T(1,128)S(1)}, f32[1,1024]{1,0:T(1,128)}, u32[]{:S(2)}) copy-start(f32[1,1024]{1,0:T(1,128)} %get-tuple-element.105) | copy-start | bytes 12292
  919.2 9.1 copy-start.11
  919.2 9.1 copy-start.44
  931.9 14.3 copy-start.30
  946.2 9.7 copy-start.72
  1016.3 13.2 copy-start.4
  1016.3 13.2 copy-start.19
  1016.3 13.2 copy-start.47
  1016.4 13.2 copy-start.55
  1016.4 13.2 copy-start.57
  1016.4 13.2 copy-start.69
  1034.6 814.2 %reduce-scatter.20.cloned.1.call-start = ((), (), s32[]{:S(2)}) async-start(), calls=%async_computation.22 | async-start | bytes 4718592 | tf_op jit(solution)/shard_map/reduce_scatter | solution.py:269
  1039.4 811.2 %reduce-scatter.16.cloned.1.call-start = ((), (), s32[]{:S(2)}) async-start(), calls=%async_computation.20 | async-start | bytes 4718592 | tf_op jit(solution)/shard_map/reduce_scatter | solution.py:267
  1044.8 807.6 %reduce-scatter.14.cloned.1.call-start = ((), (), s32[]{:S(2)}) async-start(), calls=%async_computation.19 | async-start | bytes 4718592 | tf_op jit(solution)/shard_map/reduce_scatter | solution.py:266
  1045.5 4.9 copy-start.22
  1053.7 800.6 %reduce-scatter.12.cloned.1.call-start = ((), (), s32[]{:S(2)}) async-start(), calls=%async_computation.18 | async-start | bytes 14155776 | tf_op jit(solution)/shard_map/reduce_scatter | solution.py:265
  1058.8 7.0 copy-start.26
  1065.8 4.9 copy-start.1
  1065.8 4.9 copy-start.24
  1086.3 1009.5 %reduce-scatter.22.cloned.1.call-start = ((), (), s32[]{:S(2)}) async-start(), calls=%async_computation.23 | async-start | bytes 18874368 | tf_op jit(solution)/shard_map/reduce_scatter | solution.py:270
  1098.3 1282.8 %reduce-scatter.24.cloned.1.call-start = ((), (), s32[]{:S(2)}) async-start(), calls=%async_computation.24 | async-start | bytes 18874368 | tf_op jit(solution)/shard_map/reduce_scatter | solution.py:271
  1116.4 15.1 copy-start.6
  1143.2 15.1 copy-start.31
  1168.9 1364.8 %reduce-scatter.18.cloned.1.call-start = ((), (), s32[]{:S(2)}) async-start(), calls=%async_computation.21 | async-start | bytes 9437184 | tf_op jit(solution)/shard_map/reduce_scatter | solution.py:268
  1748.1 30.2 %slice-start = ((s8[8388608]{0:T(1024)(128)(4,1)}), s8[4194304]{0:T(1024)(128)(4,1)S(1)}, s32[]{:S(2)}) async-start(s8[8388608]{0:T(1024)(128)(4,1)} %bitcast.250), calls=%async_computation.28 | async-start | bytes 8388608
  1771.2 7.1 slice-start.1
  1800.0 787.6 %reduce-scatter.26.cloned.1.call-start = ((), (), s32[]{:S(2)}) async-start(), calls=%async_computation.25 | async-start | bytes 73728 | tf_op jit(solution)/shard_map/reduce_scatter | solution.py:272
  1802.3 4.8 copy-start.64
  1802.3 4.8 copy-start.65
  1802.3 6.2 copy-start.17
  1808.4 8.4 copy-start.53
  1808.4 870.8 %all-reduce.6.cloned.1.call-start = ((), (), s32[]{:S(2)}) async-start(), calls=%async_computation.27 | async-start | bytes 8388608 | tf_op jit(solution)/shard_map/psum | solution.py:278
  2679.2 8.1 copy-start.38
  2679.2 9.3 copy-start.29
  2681.1 8.9 copy-start.28
  (29 other events, 57.8 us)
Sparse Core Ops, SparseCore 0:
  10.1 74.5 all-gather.12
  86.9 265.2 all-gather.8
  354.4 213.7 all-gather.10
  570.1 47.8 all-gather.14
  620.0 47.7 all-gather.16
  669.8 124.1 all-gather.18
  796.0 123.1 all-gather.20
  1034.7 58.6 reduce-scatter.27
  1097.4 89.0 reduce-scatter.19
  1190.0 171.2 reduce-scatter.15
  1365.3 167.1 reduce-scatter.13
  1536.0 273.9 reduce-scatter.11
  1813.7 281.9 reduce-scatter.21
  2099.9 281.2 reduce-scatter.23
  2385.2 148.4 reduce-scatter.17
  2537.0 50.4 reduce-scatter.25
  2591.6 87.5 all-reduce.5
where the time goes:
time: 2710 us; the launch traced here: 2700 us
  blocking collectives  1080 us (40%)
  waiting for transfers between devices  1000 us (37%)
  matrix products  309 us (11%)
  local copies, waits for them, and re-layouts  182 us (7%)
  other arithmetic  99.1 us (4%)
    all_to_all x1, blocking collectives, per_device(): lax.all_to_all(pair_grad, 'blk', split_axis=1, concat_axis=0, tiled=True)  567 us
    all_gather x1, blocking collectives, per_device(): lax.all_gather(feed_bias, 'blk', axis=0, tiled=True)  440 us
    reduce_scatter x1, waiting for transfers between devices, per_device(): lax.psum_scatter(grad_down, 'blk', scatter_dimension=0, tiled=True)  283 us
    reduce_scatter x1, waiting for transfers between devices, per_device(): lax.psum_scatter(grad_up, 'blk', scatter_dimension=0, tiled=True)  239 us
    reduce_scatter x1, waiting for transfers between devices, per_device(): lax.psum_scatter(grad_pair, 'blk', scatter_dimension=0, tiled=True)  150 us
    all_gather x1, waiting for transfers between devices, per_device(): lax.all_gather(w_feed_down, 'blk', axis=0, tiled=True)  97.2 us
    psum x1, waiting for transfers between devices, per_device(): lax.psum(shares[0].astype(jnp.bfloat16), 'items').astype(jnp.float32)  81.2 us
    dot_general x7, matrix products, times_transposed(): lax.dot_general(left, right, (((1,), (1,)), ((), ())), preferred_element_...  64.6 us
  transfers between devices with their start and end apart: 18, of which 9 were waited for; matrix products, arithmetic and copies ran while one was open for 16% of the time, Pallas kernels for 0%

commit v1 on v0

v1 whole, which is shorter than its diff:
```python
import jax
import jax.numpy as jnp
from jax import lax
from jax.experimental import pallas as pl
from jax.experimental.pallas import tpu as pltpu
from jax.sharding import PartitionSpec as P

HEADS = 16
CHUNKS = 8
BF = jnp.bfloat16
F32 = jnp.float32
VMEM_BYTES = 56 * 1024 * 1024


def move(axis, pairs):
    return lambda value: lax.ppermute(value, axis, pairs)


swap_x = move("blk", [(i, i ^ 1) for i in range(8)])
go_up = move("blk", [(i, (i + 2) % 8) for i in range(8)])
go_down = move("blk", [((i + 2) % 8, i) for i in range(8)])
go_up_x = move("blk", [(i, ((i + 2) % 8) ^ 1) for i in range(8)])
go_down_x = move("blk", [((i + 2) % 8, i ^ 1) for i in range(8)])
swap_core = move("items", [(i, i ^ 1) for i in range(4)])
swap_y = move("items", [(i, i ^ 2) for i in range(4)])


def places():
    me = lax.axis_index("blk")
    return [((me + 2 * (k // 2)) % 8) ^ (k % 2) for k in range(8)]


def collect(own, flip):
    ahead, behind = (go_down, go_up) if flip else (go_up, go_down)
    dz_a, dz_b = (1, 3) if flip else (3, 1)
    across = swap_x(own)
    a, b = ahead(own), behind(own)
    ax, bx = ahead(across), behind(across)
    far = ahead(a)
    far_x = swap_x(far)
    found = {1: across, 2 * dz_a: a, 2 * dz_b: b, 2 * dz_a + 1: ax, 2 * dz_b + 1: bx}
    found.update({4: far, 5: far_x})
    return [found[k] for k in range(1, 8)]


def place_kernel(widths, *refs):
    spots, own, mine, other = refs[0], refs[1], refs[2:9], refs[9:16]
    outs, held, in_sem, out_sem = refs[16:-3], refs[-3], refs[-2], refs[-1]
    rows = own.shape[0]
    half = rows // 2
    core = spots[8]
    arriving, rows_of = [], []
    for k in range(8):
        base = spots[k] * rows
        parts = [(own, base, rows)] if k == 0 else [
            (mine[k - 1], base + core * half, half),
            (other[k - 1], base + (1 - core) * half, half),
        ]
        for source, row, count in parts:
            span = pl.ds(pl.multiple_of(row, 16), count)
            copy = pltpu.make_async_copy(source, held.at[span, :], in_sem.at[len(arriving)])
            copy.start()
            arriving.append(copy)
            rows_of.append(span)
    leaving = []
    for copy, span in zip(arriving, rows_of):
        copy.wait()
        column = 0
        for out, width in zip(outs, widths):
            onward = pltpu.make_async_copy(
                held.at[span, pl.ds(column, width)], out.at[span, :], out_sem.at[len(leaving)]
            )
            onward.start()
            leaving.append(onward)
            column += width
    for copy in leaving:
        copy.wait()


def spot_vector():
    return jnp.stack(places() + [lax.axis_index("items") % 2]).astype(jnp.int32)


def gather_rows(shards, flip):
    own = shards[0] if len(shards) == 1 else jnp.concatenate(shards, axis=1)
    rows, columns = own.shape
    widths = [s.shape[1] for s in shards]
    core = lax.axis_index("items") % 2
    mine = collect(lax.dynamic_slice_in_dim(own, core * (rows // 2), rows // 2, 0), flip)
    other = [swap_core(piece) for piece in mine]
    any_spec = pl.BlockSpec(memory_space=pl.ANY)
    return pl.pallas_call(
        lambda *refs: place_kernel(widths, *refs),
        out_shape=[jax.ShapeDtypeStruct((8 * rows, w), own.dtype) for w in widths],
        in_specs=[pl.BlockSpec(memory_space=pltpu.SMEM)] + [any_spec] * 15,
        out_specs=[any_spec] * len(widths),
        scratch_shapes=[
            pltpu.VMEM((8 * rows, columns), own.dtype),
            pltpu.SemaphoreType.DMA((15,)),
            pltpu.SemaphoreType.DMA((15 * len(widths),)),
        ],
        compiler_params=pltpu.CompilerParams(vmem_limit_bytes=VMEM_BYTES),
        cost_estimate=pl.CostEstimate(
            flops=0, bytes_accessed=32 * rows * columns, transcendentals=0
        ),
        name="place_rows",
    )(spot_vector(), own, *mine, *other)


def add_low(*terms):
    total = terms[0].astype(F32)
    for term in terms[1:]:
        total = total + term.astype(F32)
    return total.astype(BF)


def reduce_rows(full, flip):
    rows = full.shape[0] // 8
    half = rows // 2
    columns = full.shape[1]
    core = lax.axis_index("items") % 2
    halves = full.reshape(8, 2, half, columns)
    kept = lax.dynamic_slice_in_dim(halves, core, 1, 1)[:, 0]
    sent = lax.dynamic_slice_in_dim(halves, 1 - core, 1, 1)[:, 0]
    both = add_low(kept, swap_core(sent))
    part = [lax.dynamic_index_in_dim(both, j, 0, keepdims=False) for j in places()]
    ahead, behind = (go_down, go_up) if flip else (go_up, go_down)
    dz_a, dz_b = (1, 3) if flip else (3, 1)
    far = add_low(part[4], swap_x(part[5]))
    near = add_low(part[2 * dz_a], behind(far))
    across = add_low(part[1], behind(part[2 * dz_a + 1]), ahead(part[2 * dz_b + 1]))
    done = add_low(part[0], swap_x(across), behind(near), ahead(part[2 * dz_b]))
    done = add_low(done, swap_y(done))
    partner = swap_core(done)
    first = jnp.where(core == 0, done, partner)
    second = jnp.where(core == 0, partner, done)
    return jnp.concatenate([first, second], axis=0).astype(F32)


def exchange(blocks):
    return [
        blocks[0],
        swap_x(blocks[1]),
        go_down(blocks[6]),
        go_down_x(blocks[7]),
        go_up(go_up(blocks[4])),
        go_down_x(go_down(blocks[5])),
        go_up(blocks[2]),
        go_up_x(blocks[3]),
    ]


def join_kernel(*refs):
    spots, blocks, out, held, in_sem, out_sem = refs[0], refs[1:9], *refs[9:]
    count = blocks[0].shape[0]
    arriving = [
        pltpu.make_async_copy(blocks[k], held.at[k], in_sem.at[k]) for k in range(8)
    ]
    leaving = [
        pltpu.make_async_copy(
            held.at[k], out.at[pl.ds(spots[k] * count, count)], out_sem.at[k]
        )
        for k in range(8)
    ]
    for copy in arriving:
        copy.start()
    for copy, onward in zip(arriving, leaving):
        copy.wait()
        onward.start()
    for copy in leaving:
        copy.wait()


def join_items(blocks):
    any_spec = pl.BlockSpec(memory_space=pl.ANY)
    shape = blocks[0].shape
    return pl.pallas_call(
        join_kernel,
        out_shape=jax.ShapeDtypeStruct((8 * shape[0],) + shape[1:], blocks[0].dtype),
        in_specs=[pl.BlockSpec(memory_space=pltpu.SMEM)] + [any_spec] * 8,
        out_specs=any_spec,
        scratch_shapes=[
            pltpu.VMEM((8,) + shape, blocks[0].dtype),
            pltpu.SemaphoreType.DMA((8,)),
            pltpu.SemaphoreType.DMA((8,)),
        ],
        compiler_params=pltpu.CompilerParams(vmem_limit_bytes=VMEM_BYTES),
        name="join_items",
    )(spot_vector(), *blocks)


def dot_nt(left, right):
    return lax.dot_general(left, right, (((1,), (1,)), ((), ())), preferred_element_type=F32)


def dot_tn(left, right):
    return lax.dot_general(left, right, (((0,), (0,)), ((), ())), preferred_element_type=F32)


def dot_nn(left, right):
    return lax.dot_general(left, right, (((1,), (0,)), ((), ())), preferred_element_type=F32)


def two_heads(value):
    lane = lax.broadcasted_iota(jnp.int32, value.shape, 1)
    zero = jnp.zeros_like(value)
    return jnp.concatenate(
        [jnp.where(lane < 64, value, zero), jnp.where(lane < 64, zero, value)], axis=0
    )


def one_pair(turned):
    count = turned.shape[1] // 2
    joined = jnp.concatenate([turned[:64, :count], turned[64:, count:]], axis=0)
    return joined.T


def pair_forward(query, keys, values, masks):
    stacked = two_heads(query)
    scores = [mask(dot_nt(k, stacked)) for k, mask in zip(keys, masks)]
    top = scores[0].max(axis=0, keepdims=True)
    for s in scores[1:]:
        top = jnp.maximum(top, s.max(axis=0, keepdims=True))
    total, turned = None, None
    for s, v in zip(scores, values):
        weight = jnp.exp(s - top)
        add = weight.sum(axis=0, keepdims=True)
        product = dot_tn(v, weight.astype(BF))
        total = add if total is None else total + add
        turned = product if turned is None else turned + product
    return one_pair(turned * (1.0 / total)).astype(BF), top + jnp.log(total)


def pair_backward(query, incoming, keys, values, masks, log_total):
    stacked, grads = two_heads(query), two_heads(incoming)
    weights, changes, centre = [], [], None
    for k, v, mask in zip(keys, values, masks):
        weight = jnp.exp(mask(dot_nt(k, stacked)) - log_total)
        change = dot_nt(v, grads)
        add = (weight * change).sum(axis=0, keepdims=True)
        centre = add if centre is None else centre + add
        weights.append(weight)
        changes.append(change)
    key_grads, value_grads, turned = [], [], None
    for k, weight, change in zip(keys, weights, changes):
        score_grad = (weight * (change - centre)).astype(BF)
        key_grads.append(dot_nn(score_grad, stacked).astype(BF))
        value_grads.append(dot_nn(weight.astype(BF), grads).astype(BF))
        product = dot_tn(k, score_grad)
        turned = product if turned is None else turned + product
    return one_pair(turned).astype(BF), key_grads, value_grads


def slot_masks(starts, length, rows, columns):
    slot = lax.broadcasted_iota(jnp.int32, (rows, columns), 0)
    return [
        (lambda s, c=c: jnp.where(slot < length - starts[c], s, -1e30)) for c in range(CHUNKS)
    ]


PAIRS = 2


def cross_forward_kernel(lengths, starts, q_ref, kv_ref, out_ref, log_ref):
    rows = kv_ref.shape[2]
    masks = slot_masks(starts, lengths[pl.program_id(0)], rows, 2 * q_ref.shape[1])
    for p in range(PAIRS):
        keys = [kv_ref[c, 0, :, 256 * p : 256 * p + 128] for c in range(CHUNKS)]
        values = [kv_ref[c, 0, :, 256 * p + 128 : 256 * p + 256] for c in range(CHUNKS)]
        out, log_total = pair_forward(q_ref[0, :, 128 * p : 128 * p + 128], keys, values, masks)
        out_ref[0, :, 128 * p : 128 * p + 128] = out
        log_ref[0, p] = log_total


def cross_backward_kernel(
    lengths, starts, q_ref, grad_ref, kv_ref, log_ref, dq_ref, dkv_ref
):
    rows = kv_ref.shape[2]
    masks = slot_masks(starts, lengths[pl.program_id(0)], rows, 2 * q_ref.shape[1])
    for p in range(PAIRS):
        span = slice(128 * p, 128 * p + 128)
        keys = [kv_ref[c, 0, :, 256 * p : 256 * p + 128] for c in range(CHUNKS)]
        values = [kv_ref[c, 0, :, 256 * p + 128 : 256 * p + 256] for c in range(CHUNKS)]
        dq, dks, dvs = pair_backward(
            q_ref[0, :, span], grad_ref[0, :, span], keys, values, masks, log_ref[0, p]
        )
        dq_ref[0, :, span] = dq
        for c in range(CHUNKS):
            dkv_ref[c, 0, :, 256 * p : 256 * p + 128] = dks[c]
            dkv_ref[c, 0, :, 256 * p + 128 : 256 * p + 256] = dvs[c]


def cross_specs(items, length, width, rows):
    pairs = width // 128
    small = pl.BlockSpec((1, length, 128 * PAIRS), lambda i, p, *_: (i, 0, p))
    big = pl.BlockSpec((CHUNKS, 1, rows, 256 * PAIRS), lambda i, p, *_: (0, i, 0, p))
    logs = pl.BlockSpec((1, PAIRS, 1, 2 * length), lambda i, p, *_: (i, p, 0, 0))
    return (items, pairs // PAIRS), small, big, logs


def cross_forward(lengths, starts, queries, kv):
    items, length, width = queries.shape
    rows = kv.shape[2]
    grid, small, big, logs = cross_specs(items, length, width, rows)
    return pl.pallas_call(
        cross_forward_kernel,
        out_shape=[
            jax.ShapeDtypeStruct(queries.shape, BF),
            jax.ShapeDtypeStruct((items, width // 128, 1, 2 * length), F32),
        ],
        grid_spec=pltpu.PrefetchScalarGridSpec(
            num_scalar_prefetch=2, grid=grid, in_specs=[small, big], out_specs=[small, logs]
        ),
        compiler_params=pltpu.CompilerParams(vmem_limit_bytes=VMEM_BYTES),
        cost_estimate=pl.CostEstimate(
            flops=8 * items * length * CHUNKS * rows * width,
            bytes_accessed=2 * kv.size,
            transcendentals=items * length * CHUNKS * rows * HEADS,
        ),
        name="cross_forward",
    )(lengths, starts, queries, kv)


def cross_backward(lengths, starts, queries, grads, kv, logs_in):
    items, length, width = queries.shape
    rows = kv.shape[2]
    grid, small, big, logs = cross_specs(items, length, width, rows)
    return pl.pallas_call(
        cross_backward_kernel,
        out_shape=[jax.ShapeDtypeStruct(queries.shape, BF), jax.ShapeDtypeStruct(kv.shape, BF)],
        grid_spec=pltpu.PrefetchScalarGridSpec(
            num_scalar_prefetch=2,
            grid=grid,
            in_specs=[small, small, big, logs],
            out_specs=[small, big],
        ),
        compiler_params=pltpu.CompilerParams(vmem_limit_bytes=VMEM_BYTES),
        cost_estimate=pl.CostEstimate(
            flops=20 * items * length * CHUNKS * rows * width,
            bytes_accessed=4 * kv.size,
            transcendentals=items * length * CHUNKS * rows * HEADS,
        ),
        name="cross_backward",
    )(lengths, starts, queries, grads, kv, logs_in)


def self_mask(seg_row, seg_column, length):
    key = lax.broadcasted_iota(jnp.int32, (length, length), 0)
    query = lax.broadcasted_iota(jnp.int32, (length, length), 1)
    allowed = jnp.where((seg_column == seg_row) & (key <= query), 1.0, 0.0)
    allowed = jnp.concatenate([allowed, allowed], axis=1)
    return lambda s: jnp.where(allowed > 0.5, s, -1e30)


def self_forward_kernel(seg_row, seg_column, qkv_ref, out_ref, log_ref):
    length, width = out_ref.shape[1:]
    mask = self_mask(seg_row[0], seg_column[0], length)
    for p in range(width // 128):
        span = slice(128 * p, 128 * p + 128)
        query = qkv_ref[0, :, span]
        key = qkv_ref[0, :, width + 128 * p : width + 128 * p + 128]
        value = qkv_ref[0, :, 2 * width + 128 * p : 2 * width + 128 * p + 128]
        out, log_total = pair_forward(query, [key], [value], [mask])
        out_ref[0, :, span] = out
        log_ref[0, p] = log_total


def self_backward_kernel(seg_row, seg_column, qkv_ref, grad_ref, log_ref, out_ref):
    length, width = grad_ref.shape[1:]
    mask = self_mask(seg_row[0], seg_column[0], length)
    for p in range(width // 128):
        span = slice(128 * p, 128 * p + 128)
        key_span = slice(width + 128 * p, width + 128 * p + 128)
        value_span = slice(2 * width + 128 * p, 2 * width + 128 * p + 128)
        dq, dk, dv = pair_backward(
            qkv_ref[0, :, span],
            grad_ref[0, :, span],
            [qkv_ref[0, :, key_span]],
            [qkv_ref[0, :, value_span]],
            [mask],
            log_ref[0, p],
        )
        out_ref[0, :, span] = dq * BF(0.125)
        out_ref[0, :, key_span] = dk[0]
        out_ref[0, :, value_span] = dv[0]


def self_specs(items, length, width):
    rows = pl.BlockSpec((1, 1, length), lambda i: (i, 0, 0))
    columns = pl.BlockSpec((1, length, 1), lambda i: (i, 0, 0))
    wide = pl.BlockSpec((1, length, 3 * width), lambda i: (i, 0, 0))
    slim = pl.BlockSpec((1, length, width), lambda i: (i, 0, 0))
    logs = pl.BlockSpec((1, width // 128, 1, 2 * length), lambda i: (i, 0, 0, 0))
    return rows, columns, wide, slim, logs


def self_forward(segments, qkv):
    items, length, width = qkv.shape[0], qkv.shape[1], qkv.shape[2] // 3
    rows, columns, wide, slim, logs = self_specs(items, length, width)
    return pl.pallas_call(
        self_forward_kernel,
        grid=(items,),
        out_shape=[
            jax.ShapeDtypeStruct((items, length, width), BF),
            jax.ShapeDtypeStruct((items, width // 128, 1, 2 * length), F32),
        ],
        in_specs=[rows, columns, wide],
        out_specs=[slim, logs],
        compiler_params=pltpu.CompilerParams(vmem_limit_bytes=VMEM_BYTES),
        name="self_forward",
    )(segments[:, None, :], segments[:, :, None], qkv)


def self_backward(segments, qkv, grads, logs_in):
    items, length, width = grads.shape
    rows, columns, wide, slim, logs = self_specs(items, length, width)
    return pl.pallas_call(
        self_backward_kernel,
        grid=(items,),
        out_shape=jax.ShapeDtypeStruct(qkv.shape, BF),
        in_specs=[rows, columns, wide, slim, logs],
        out_specs=wide,
        compiler_params=pltpu.CompilerParams(vmem_limit_bytes=VMEM_BYTES),
        name="self_backward",
    )(segments[:, None, :], segments[:, :, None], qkv, grads, logs_in)


def layer_norm(values, gain, shift):
    centre = values - jnp.mean(values, axis=-1, keepdims=True)
    spread = jnp.mean(centre * centre, axis=-1, keepdims=True)
    return centre * lax.rsqrt(spread + 1e-05) * gain + shift


def exact_gelu(values):
    return jax.nn.gelu(values, approximate=False)


def column_sum(values):
    return jnp.sum(values.astype(F32), axis=0)


def interleave(matrix):
    rows, columns = matrix.shape
    return matrix.reshape(rows, 2, columns // 256, 128).swapaxes(1, 2).reshape(rows, columns)


def part_again(matrix):
    rows, columns = matrix.shape
    return matrix.reshape(rows, columns // 256, 2, 128).swapaxes(1, 2).reshape(rows, columns)


def pack_small(shifts, gains, bias):
    width = shifts.shape[1]
    rows = jnp.concatenate([shifts, gains, bias.reshape(-1, width)], axis=0)
    return jnp.pad(rows, ((0, 32 - rows.shape[0]), (0, 0)))


def unpack_small(rows, width):
    count = rows.shape[0] // 32
    rows = rows.reshape(count, 32, width)
    shifts = rows[:, :10].transpose(1, 0, 2).reshape(10, -1)
    gains = rows[:, 10:13].transpose(1, 0, 2).reshape(3, -1)
    return shifts, gains, rows[:, 13:17].reshape(-1)


def per_device(tuned):
    def run(
        decoder_in,
        memory,
        segment_ids,
        memory_lengths,
        w_self_in,
        w_self_out,
        w_cross_query,
        w_cross_pair,
        w_cross_out,
        w_feed_up,
        w_feed_down,
        shifts,
        norm_gains,
        feed_bias,
        out_grad,
    ):
        item_count, length, width = decoder_in.shape
        row_count = item_count * length
        pair_shard = interleave(w_cross_pair)
        if tuned:
            small = pack_small(shifts, norm_gains, feed_bias)
            (small,) = gather_rows([small], False)
            shift_low, gain_low, feed_shift_low = unpack_small(small, shifts.shape[1])
            (self_proj,) = gather_rows([w_self_in], False)
            self_out, cross_query, cross_pair = gather_rows(
                [w_self_out, w_cross_query, pair_shard], True
            )
            spots = places()
            blocks = [lax.dynamic_slice_in_dim(memory, j * item_count, item_count, 0) for j in spots]
            arrived = exchange(blocks)
            starts = jnp.stack(spots).astype(jnp.int32) * memory.shape[1]
            cross_out, feed_up = gather_rows([w_cross_out, w_feed_up], False)
            (feed_down,) = gather_rows([w_feed_down], True)
            memory_rows = jnp.stack(arrived)
        else:
            def whole(shard, axis=0):
                return lax.all_gather(shard, "blk", axis=axis, tiled=True)

            shift_low, gain_low = whole(shifts, 1), whole(norm_gains, 1)
            feed_shift_low = whole(feed_bias)
            self_proj, self_out, cross_query = whole(w_self_in), whole(w_self_out), whole(w_cross_query)
            cross_pair, cross_out = whole(pair_shard), whole(w_cross_out)
            feed_up, feed_down = whole(w_feed_up), whole(w_feed_down)
            arrived = lax.all_to_all(memory, "blk", split_axis=0, concat_axis=1, tiled=True)
            slots = arrived.shape[1] // CHUNKS
            memory_rows = arrived.reshape(item_count, CHUNKS, slots, width).swapaxes(0, 1)
            starts = jnp.arange(CHUNKS, dtype=jnp.int32) * slots
        shift_rows = shift_low.astype(F32)
        gain_rows = gain_low.astype(F32)
        feed_shift = feed_shift_low.astype(F32)
        query_scale = (width // HEADS) ** (-0.5)
        three = (item_count, length, width)

        token_rows = decoder_in.reshape(row_count, width)
        no_shift = jnp.zeros((width,), F32)
        in_shift = jnp.concatenate([shift_rows[0], no_shift, shift_rows[1]])
        in_scale = jnp.concatenate([no_shift + query_scale, no_shift + 1.0, no_shift + 1.0])
        qkv = (
            (jnp.dot(token_rows, self_proj, preferred_element_type=F32) + in_shift) * in_scale
        ).astype(BF).reshape(item_count, length, 3 * width)
        attended, self_logs = self_forward(segment_ids, qkv)
        attended = attended.reshape(row_count, width)
        branch = jnp.dot(attended, self_out, preferred_element_type=F32) + shift_rows[2]
        hidden, first_norm_back = jax.vjp(
            layer_norm, token_rows.astype(F32) + branch, gain_rows[0], shift_rows[7]
        )
        hidden_low = hidden.astype(BF)

        cross_queries = (
            (jnp.dot(hidden_low, cross_query, preferred_element_type=F32) + shift_rows[3])
            * query_scale
        ).astype(BF).reshape(three)
        pair_shift = interleave(jnp.concatenate([no_shift, shift_rows[4]])[None])[0]
        chunk_rows = memory_rows.shape[2]
        source_rows = memory_rows.reshape(-1, width)
        pair_rows = (
            jnp.dot(source_rows, cross_pair, preferred_element_type=F32) + pair_shift
        ).astype(BF).reshape(CHUNKS, item_count, chunk_rows, 2 * width)
        cross_attended, cross_logs = cross_forward(memory_lengths, starts, cross_queries, pair_rows)
        cross_attended = cross_attended.reshape(row_count, width)
        cross_branch = jnp.dot(cross_attended, cross_out, preferred_element_type=F32) + shift_rows[5]
        second, second_norm_back = jax.vjp(
            layer_norm, hidden + cross_branch, gain_rows[1], shift_rows[8]
        )
        second_low = second.astype(BF)

        upward = jnp.dot(second_low, feed_up, preferred_element_type=F32) + feed_shift
        activation, gelu_back = jax.vjp(exact_gelu, upward)
        activation_low = activation.astype(BF)
        feed_branch = jnp.dot(activation_low, feed_down, preferred_element_type=F32) + shift_rows[6]
        block_out, third_norm_back = jax.vjp(
            layer_norm, second + feed_branch, gain_rows[2], shift_rows[9]
        )

        third_grad, third_gain, third_shift = third_norm_back(
            out_grad.astype(F32).reshape(row_count, width)
        )
        down_low = third_grad.astype(BF)
        grad_down = dot_tn(activation_low, down_low)
        upward_low = gelu_back(dot_nt(down_low, feed_down))[0].astype(BF)
        grad_up = dot_tn(second_low, upward_low)
        second_grad = third_grad + dot_nt(upward_low, feed_up)
        cross_grad, second_gain, second_shift = second_norm_back(second_grad)
        cross_low = cross_grad.astype(BF)
        grad_cross_out = dot_tn(cross_attended, cross_low)
        cross_incoming = dot_nt(cross_low, cross_out).astype(BF).reshape(three)
        cross_dq, pair_grad = cross_backward(
            memory_lengths, starts, cross_queries, cross_incoming, pair_rows, cross_logs
        )
        cross_query_low = cross_dq.reshape(row_count, width) * BF(query_scale)
        grad_cross_query = dot_tn(hidden_low, cross_query_low)
        flat_grad = pair_grad.reshape(-1, 2 * width)
        memory_back = dot_nt(flat_grad, cross_pair).astype(BF).reshape(memory_rows.shape)
        if tuned:
            memory_grad = join_items(exchange([memory_back[k] for k in range(8)]))
        else:
            memory_back = memory_back.swapaxes(0, 1).reshape(arrived.shape)
            memory_grad = lax.all_to_all(memory_back, "blk", split_axis=1, concat_axis=0, tiled=True)
        grad_pair = dot_tn(source_rows, flat_grad)
        value_sums = part_again(column_sum(flat_grad)[None])[0, width:]
        hidden_grad = cross_grad + dot_nt(cross_query_low, cross_query)
        first_grad, first_gain, first_shift = first_norm_back(hidden_grad)
        self_low = first_grad.astype(BF)
        grad_self_out = dot_tn(attended, self_low)
        self_incoming = dot_nt(self_low, self_out).astype(BF).reshape(three)
        joined_grad = self_backward(segment_ids, qkv, self_incoming, self_logs)
        joined_grad = joined_grad.reshape(row_count, 3 * width)
        grad_self = dot_tn(token_rows, joined_grad)
        decoder_grad = (
            (first_grad + dot_nt(joined_grad, self_proj)).astype(BF).reshape(decoder_in.shape)
        )
        joined_sums = column_sum(joined_grad)
        grad_shift_rows = jnp.stack(
            [
                joined_sums[:width],
                joined_sums[2 * width :],
                column_sum(self_low),
                column_sum(cross_query_low),
                value_sums,
                column_sum(cross_low),
                column_sum(down_low),
                first_shift,
                second_shift,
                third_shift,
            ]
        )
        grad_gain_rows = jnp.stack([first_gain, second_gain, third_gain])
        grad_feed_shift = column_sum(upward_low)
        block_low = block_out.astype(BF).reshape(decoder_in.shape)
        large = [grad_down, grad_up, grad_cross_out, grad_cross_query, grad_pair, grad_self_out, grad_self]
        if tuned:
            down, up, out, query, pair, own_out, own_in = [
                reduce_rows(grad.astype(BF), i % 2 == 1) for i, grad in enumerate(large)
            ]
            count = shifts.shape[1]
            packed = jnp.concatenate(
                [
                    grad_shift_rows.reshape(10, 8, count),
                    grad_gain_rows.reshape(3, 8, count),
                    grad_feed_shift.reshape(8, -1, count).swapaxes(0, 1),
                ],
                axis=0,
            ).swapaxes(0, 1)
            packed = jnp.pad(packed, ((0, 0), (0, 32 - packed.shape[1]), (0, 0)))
            sums = reduce_rows(packed.reshape(-1, count).astype(BF), True)
            shift_share, gain_share, feed_share = sums[:10], sums[10:13], sums[13:17].reshape(-1)
        else:
            def share(value, dim=0):
                part = lax.psum_scatter(value, "blk", scatter_dimension=dim, tiled=True)
                return lax.psum(part.astype(BF), "items").astype(F32)

            down, up, out, query, pair, own_out, own_in = [share(grad) for grad in large]
            shift_share, gain_share = share(grad_shift_rows, 1), share(grad_gain_rows, 1)
            feed_share = share(grad_feed_shift)
        return (
            block_low,
            decoder_grad,
            memory_grad,
            own_in,
            own_out,
            query,
            part_again(pair),
            out,
            up,
            down,
            shift_share,
            gain_share,
            feed_share,
        )

    return run


def solution(mesh):
    in_specs = (
        P(("items", "blk"), None, None),
        P("items", "blk", None),
        P(("items", "blk"), None),
        P(("items", "blk")),
        P("blk", None),
        P("blk", None),
        P("blk", None),
        P("blk", None),
        P("blk", None),
        P("blk", None),
        P("blk", None),
        P(None, "blk"),
        P(None, "blk"),
        P("blk"),
        P(("items", "blk"), None, None),
    )
    out_specs = (
        P(("items", "blk"), None, None),
        P(("items", "blk"), None, None),
        P("items", "blk", None),
        P("blk", None),
        P("blk", None),
        P("blk", None),
        P("blk", None),
        P("blk", None),
        P("blk", None),
        P("blk", None),
        P(None, "blk"),
        P(None, "blk"),
        P("blk"),
    )
    tuned = mesh.shape["blk"] == 8 and mesh.shape["items"] == 4
    return jax.shard_map(
        per_device(tuned), mesh=mesh, in_specs=in_specs, out_specs=out_specs, check_vma=False
    )
```

time: 2710 us -> 1250 us (0.46)
  blocking collectives: 1080 us -> 0 us
  waiting for transfers between devices: 1000 us -> 502 us
  starting transfers between devices: 6.56 us -> 286 us
  matrix products: 309 us -> 184 us
  Pallas kernels: 0 us -> 121 us
  local copies, waits for them, and re-layouts: 182 us -> 80.6 us
  other arithmetic: 99.1 us -> 60.5 us
    reduce_scatter x8 -> x0, waiting for transfers between devices: 700 us -> none  [the longest x1 283 us: per_device(): lax.psum_scatter(grad_down, 'blk', scatter_dimension=0, tiled=True)]
    all_to_all x1 -> x0, blocking collectives: 567 us -> none  [per_device(): lax.all_to_all(pair_grad, 'blk', split_axis=1, concat_axis=0, tiled=True)]
    ppermute x0 -> x168, waiting for transfers between devices: none -> 502 us  [move(): return lambda value: lax.ppermute(value, axis, pairs)]
    all_gather x3 -> x0, blocking collectives: 477 us -> none  [the longest x1 440 us: per_device(): lax.all_gather(feed_bias, 'blk', axis=0, tiled=True)]
    ppermute x0 -> x168, starting transfers between devices: none -> 286 us  [move(): return lambda value: lax.ppermute(value, axis, pairs)]
    all_gather x7 -> x0, waiting for transfers between devices: 216 us -> none  [the longest x1 97.2 us: per_device(): lax.all_gather(w_feed_down, 'blk', axis=0, tiled=True)]
    dot_general x33 -> x21, matrix products: 309 us -> 184 us  [the longest x7 59.8 us: dot_nt(): lax.dot_general(left, right, (((1,), (1,)), ((), ())), preferred_element_...]
    pallas_call x0 -> x10, Pallas kernels: none -> 121 us  [the longest x1 38.5 us: cross_backward(): pl.pallas_call(cross_backward_kernel, out_shape=[jax.ShapeDtypeStruct(que...]
  transfers between devices with their start and end apart: 18 -> 168, of which waited for: 9 -> 60; matrix products, arithmetic and copies ran while one was open for 16% -> 12% of each run, Pallas kernels for 0% -> 5%
where the time goes in v1:
time: 1250 us; the launch traced here: 1240 us
  waiting for transfers between devices  502 us (40%)
  starting transfers between devices  286 us (23%)
  matrix products  184 us (15%)
  Pallas kernels  121 us (10%)
  local copies, waits for them, and re-layouts  80.6 us (6%)
  other arithmetic  60.5 us (5%)
    ppermute x168, waiting for transfers between devices, move(): return lambda value: lax.ppermute(value, axis, pairs)  502 us
    ppermute x168, starting transfers between devices, move(): return lambda value: lax.ppermute(value, axis, pairs)  286 us
    dot_general x7, matrix products, dot_nt(): lax.dot_general(left, right, (((1,), (1,)), ((), ())), preferred_element_...  59.8 us
    dot_general x7, matrix products, dot_tn(): lax.dot_general(left, right, (((0,), (0,)), ((), ())), preferred_element_...  53.1 us
    pallas_call x1, Pallas kernels, cross_backward(): pl.pallas_call(cross_backward_kernel, out_shape=[jax.ShapeDtypeStruct(que...  38.5 us
    pallas_call x5, Pallas kernels, gather_rows(): pl.pallas_call(lambda *refs: place_kernel(widths, *refs), out_shape=[jax....  32.5 us
    unnamed x278, local copies, waits for them, and re-layouts  30.1 us
    convert_element_type x40, other arithmetic, add_low(): return total.astype(BF)  27 us
  transfers between devices with their start and end apart: 168, of which 60 were waited for; matrix products, arithmetic and copies ran while one was open for 12% of the time, Pallas kernels for 5%

profile of v1, /device:TPU:1, one launch (start us, length us, event | category | flops | bytes accessed | tf_op | source)
XLA Modules:
  0.0 1238.2 jit_solution(14648283985875491992)
XLA Ops:
  34.3 8.5 collective-permute-done.3.refs_7_
  44.4 9.2 collective-permute-done.29.refs_3_
  53.9 11.5 collective-permute-done.33.refs_7_
  66.9 9.1 collective-permute-done.66.refs_3_
  79.6 8.2 collective-permute-done.70.refs_7_
  89.1 12.1 collective-permute-done.52.refs_3_
  101.3 15.4 %collective-permute-start.7 = (bf16[64,3072]{1,0:T(8,128)(2,1)S(1)}, bf16[64,3072]{1,0:T(8,128)(2,1)S(1)}, u32[]{:S(2)}, u32[]{:S(2)}) collective-permute-start(bf16[64,3072]{1,0:T(8,128)(2,1)S(1)} %collective-permute-done.refs_2_), channel_id=1, source_target_pairs={{0,8},{8,0},{16,24},{24,16},{1,9},{9,1},{17,25},{25,17},{2,10},{10... | collective-permute-start | bytes 1179656 | tf_op jit(solution)/shard_map/ppermute | solution.py:16
  125.4 7.4 collective-permute-done.4.refs_5_
  133.4 7.9 collective-permute-done.6.refs_8_
  147.3 6.3 constant_dynamic-slice_fusion.10
  186.5 9.7 collective-permute-done.42
  200.4 22.1 %collective-permute-done.44 = bf16[4,128,1024]{1,2,0:T(8,128)(2,1)S(1)} collective-permute-done((bf16[4,128,1024]{1,2,0:T(8,128)(2,1)}, bf16[4,128,1024]{1,2,0:T(8,128)(2,1)S(1)}, u32[]{:S(2)}, u32[]{:S(2)}) %collective-permute-start.44) | collective-permute-done | bytes 1048608 | tf_op jit(solution)/shard_map/ppermute | solution.py:16
  227.7 18.1 %collective-permute-done.45 = bf16[4,128,1024]{1,2,0:T(8,128)(2,1)} collective-permute-done((bf16[4,128,1024]{1,2,0:T(8,128)(2,1)}, bf16[4,128,1024]{1,2,0:T(8,128)(2,1)}, u32[]{:S(2)}, u32[]{:S(2)}) %collective-permute-start.45) | collective-permute-done | bytes 1048608 | tf_op jit(solution)/shard_map/ppermute | solution.py:16
  249.0 18.6 %collective-permute-done.47 = bf16[4,128,1024]{1,2,0:T(8,128)(2,1)} collective-permute-done((bf16[4,128,1024]{1,2,0:T(8,128)(2,1)}, bf16[4,128,1024]{1,2,0:T(8,128)(2,1)}, u32[]{:S(2)}, u32[]{:S(2)}) %collective-permute-start.47) | collective-permute-done | bytes 1048608 | tf_op jit(solution)/shard_map/ppermute | solution.py:16
  279.6 6.4 place_rows.5
  290.9 8.3 multiply_convert_fusion.1
  299.2 6.1 self_forward.1
  305.2 7.9 collective-permute-done.50
  317.6 53.1 %collective-permute-done.67.refs_4_ = bf16[256,1024]{1,0:T(8,128)(2,1)S(1)} collective-permute-done((bf16[256,1024]{1,0:T(8,128)(2,1)S(1)}, bf16[256,1024]{1,0:T(8,128)(2,1)S(1)}, u32[]{:S(2)}, u32[]{:S(2)}) %collective-permute-start.67) | collective-permute-done | bytes 524320 | tf_op jit(solution)/shard_map/ppermute | solution.py:16
  374.9 7.1 collective-permute-done.68.refs_5_
  386.0 11.4 copy.91
  397.3 7.7 place_rows.7
  406.7 23.6 %add_convert_fusion = bf16[4096,2048]{1,0:T(8,128)(2,1)} fusion(bf16[4096,1024]{1,0:T(8,128)(2,1)} %bitcast.427, bf16[1024,2048]{1,0:T(8,128)(2,1)} %get-tuple-element.27, f32[2048]{0:T(1024)S(1)} %bitcast.495), kind=kOutput, calls=%fused_computation | convolution fusion | flops 17196646400 | bytes 29368320 | tf_op jit(solution)/shard_map/dot_general | solution.py:544
  437.6 7.3 place_rows.9
  449.4 13.6 %collective-permute-done.57.refs_8_ = bf16[64,5120]{1,0:T(8,128)(2,1)S(1)} collective-permute-done((bf16[64,5120]{1,0:T(8,128)(2,1)S(1)}, bf16[64,5120]{1,0:T(8,128)(2,1)S(1)}, u32[]{:S(2)}, u32[]{:S(2)}) %collective-permute-start.57) | collective-permute-done | bytes 655392 | tf_op jit(solution)/shard_map/ppermute | solution.py:16
  468.9 26.5 %cross_forward.1 = (bf16[4,128,1024]{2,1,0:T(8,128)(2,1)}, f32[4,8,1,256]{3,2,1,0:T(1,128)}) custom-call(s32[4]{0:T(128)} %lengths.3, s32[8]{0:T(128)} %broadcast_multiply_fusion.4.starts, bf16[4,128,1024]{2,1,0:T(8,128)(2,1)} %bitcast.451, bf16[8,4,128,2048]{3,2,1,0:T(8,128)(2,1)} %bitcast.411), custom_call_target="tpu_custom_call" | custom-call | flops 4294967296 | bytes 16777216 | tf_op jit(solution)/shard_map/cross_forward/pallas_call | solution.py:305
  496.5 8.8 place_rows.8
  509.3 26.2 %multiply_convert_fusion = (bf16[512,4096]{1,0:T(8,128)(2,1)S(1)}, f32[512,4096]{1,0:T(8,128)}, f32[512,4096]{1,0:T(8,128)}) fusion(f32[4096]{0:T(1024)S(1)} %convert.131, bf16[1024,4096]{1,0:T(8,128)(2,1)S(1)} %copy-done.106, f32[512,1024]{1,0:T(8,128)S(1)} %get-tuple-element.160, f32[1024]{0:T(1024)S(1)} %bitcast.496, f32[1024]{0:T(1024)S(1)} %bitcast.477, ...), kind=kOutput, calls=%fused_computation.10 | convolution fusion | flops 4436000768 | bytes 31485952 | tf_op jit(solution)/shard_map/dot_general | solution.py:554
  545.9 13.3 %fusion.98 = (bf16[4096]{0:T(1024)(128)(2,1)}, bf16[512,4096]{1,0:T(8,128)(2,1)}) fusion(f32[512,4096]{1,0:T(8,128)} %get-tuple-element.58, f32[512,4096]{1,0:T(8,128)} %get-tuple-element.161, f32[4096]{0:T(1024)S(1)} %convert.131, bf16[512,1024]{1,0:T(8,128)(2,1)} %get-tuple-element.46, bf16[4096,1024]{1,0:T(8,128)(2,1)S(1)} %bitcast.418), kind=kOutput, calls=%fused_computation.317 | convolution fusion | flops 4328517632 | bytes 30433280 | tf_op jit(solution)/shard_map/dot_general | solution.py:193
  559.2 10.4 multiply_reduce_fusion
  574.6 38.5 %cross_backward.1 = (bf16[4,128,1024]{2,1,0:T(8,128)(2,1)}, bf16[8,4,128,2048]{3,2,1,0:T(8,128)(2,1)}) custom-call(s32[4]{0:T(128)} %lengths.3, s32[8]{0:T(128)} %broadcast_multiply_fusion.4.starts, bf16[4,128,1024]{2,1,0:T(8,128)(2,1)} %bitcast.452, bf16[4,128,1024]{2,1,0:T(8,128)(2,1)} %bitcast.518, bf16[8,4,128,2048]{3,2,1,0:T(8,128)(2,1)} %bitcast.412, ...), custom_call_target="tpu_custom_call" | custom-call | flops 10737418240 | bytes 33554432 | tf_op jit(solution)/shard_map/cross_backward/pallas_call | solution.py:328
  631.5 7.2 convolution_convert_fusion.1
  638.8 6.8 convolution_convert_fusion
  645.6 10.8 self_backward.1
  656.3 7.4 bitcast_convert_fusion
  664.3 23.6 %bitcast_convert_fusion.1 = bf16[1024,2048]{1,0:T(8,128)(2,1)} fusion(bf16[8,4,128,1024]{2,3,1,0:T(8,128)(2,1)} %bitcast_dynamic-update-slice_fusion, bf16[8,4,128,2048]{3,2,1,0:T(8,128)(2,1)} %get-tuple-element.34), kind=kOutput, calls=%fused_computation.8 | convolution fusion | flops 17181966336 | bytes 29360128 | tf_op jit(solution)/shard_map/dot_general | solution.py:197
  688.0 9.7 reduce.7
  697.7 7.7 add_convert_fusion.2
  705.4 20.4 %convolution_convert_fusion.2 = bf16[4096,1024]{1,0:T(8,128)(2,1)S(1)} fusion(bf16[4096,2048]{1,0:T(8,128)(2,1)} %bitcast.413, bf16[1024,2048]{1,0:T(8,128)(2,1)S(1)} %copy-done.107), kind=kOutput, calls=%fused_computation.26 | convolution fusion | flops 17184063488 | bytes 29360128 | tf_op jit(solution)/shard_map/dot_general | solution.py:193
  765.9 6.3 collective-permute-done.100
  786.4 6.9 collective-permute-done.103
  822.2 7.5 collective-permute-done.79.refs_2_
  829.7 37.8 %collective-permute-start.88 = (bf16[8,64,3072]{2,1,0:T(8,128)(2,1)}, bf16[8,64,3072]{2,1,0:T(8,128)(2,1)}, u32[]{:S(2)}, u32[]{:S(2)}) collective-permute-start(bf16[8,64,3072]{2,1,0:T(8,128)(2,1)} %dynamic-slice_bitcast_fusion.2), channel_id=1, source_target_pairs={{0,8},{8,0},{16,24},{24,16},{1,9},{9,1},{17,25},{25,17},{2,10},{10... | collective-permute-start | bytes 9437192 | tf_op jit(solution)/shard_map/ppermute | solution.py:16
  869.0 17.5 %collective-permute-start.120 = (bf16[64,2048]{1,0:T(8,128)(2,1)S(1)}, bf16[64,2048]{1,0:T(8,128)(2,1)S(1)}, u32[]{:S(2)}, u32[]{:S(2)}) collective-permute-start(bf16[64,2048]{1,0:T(8,128)(2,1)S(1)} %get-tuple-element.99), channel_id=1, source_target_pairs={{0,2},{1,3},{2,4},{3,5},{4,6},{5,7},{6,0},{7,1},{8,10},{9,11},{10,... | collective-permute-start | bytes 786440 | tf_op jit(solution)/shard_map/ppermute | solution.py:16
  886.6 6.1 collective-permute-start.119
  893.2 6.5 collective-permute-done.120
  899.6 23.2 %collective-permute-start.107 = (bf16[64,1024]{1,0:T(8,128)(2,1)S(1)}, bf16[64,1024]{1,0:T(8,128)(2,1)S(1)}, u32[]{:S(2)}, u32[]{:S(2)}) collective-permute-start(bf16[64,1024]{1,0:T(8,128)(2,1)S(1)} %add_convert_fusion.13), channel_id=1, source_target_pairs={{0,8},{8,0},{16,24},{24,16},{1,9},{9,1},{17,25},{25,17},{2,10},{10... | collective-permute-start | bytes 393224 | tf_op jit(solution)/shard_map/ppermute | solution.py:16
  939.4 18.3 %collective-permute-done.86.refs_7_ = bf16[4,128,1024]{2,1,0:T(8,128)(2,1)S(1)} collective-permute-done((bf16[4,128,1024]{2,1,0:T(8,128)(2,1)S(1)}, bf16[4,128,1024]{2,1,0:T(8,128)(2,1)S(1)}, u32[]{:S(2)}, u32[]{:S(2)}) %collective-permute-start.86) | collective-permute-done | bytes 1048608 | tf_op jit(solution)/shard_map/ppermute | solution.py:16
  959.0 21.5 %collective-permute-done.87.refs_8_ = bf16[4,128,1024]{2,1,0:T(8,128)(2,1)S(1)} collective-permute-done((bf16[4,128,1024]{2,1,0:T(8,128)(2,1)S(1)}, bf16[4,128,1024]{2,1,0:T(8,128)(2,1)S(1)}, u32[]{:S(2)}, u32[]{:S(2)}) %collective-permute-start.87) | collective-permute-done | bytes 1048608 | tf_op jit(solution)/shard_map/ppermute | solution.py:16
  981.4 21.3 %collective-permute-done.83.refs_5_ = bf16[4,128,1024]{2,1,0:T(8,128)(2,1)S(1)} collective-permute-done((bf16[4,128,1024]{2,1,0:T(8,128)(2,1)S(1)}, bf16[4,128,1024]{2,1,0:T(8,128)(2,1)S(1)}, u32[]{:S(2)}, u32[]{:S(2)}) %collective-permute-start.83) | collective-permute-done | bytes 1048608 | tf_op jit(solution)/shard_map/ppermute | solution.py:16
  1007.0 18.8 %collective-permute-done.85.refs_6_ = bf16[4,128,1024]{2,1,0:T(8,128)(2,1)} collective-permute-done((bf16[4,128,1024]{2,1,0:T(8,128)(2,1)S(1)}, bf16[4,128,1024]{2,1,0:T(8,128)(2,1)}, u32[]{:S(2)}, u32[]{:S(2)}) %collective-permute-start.85) | collective-permute-done | bytes 1048608 | tf_op jit(solution)/shard_map/ppermute | solution.py:16
  1032.5 7.1 join_items.1
  1049.4 8.4 collective-permute-done.90
  1057.9 6.5 collective-permute-done.89
  1076.3 8.1 collective-permute-done.93
  1098.8 9.3 collective-permute-done.140
  1108.1 7.2 collective-permute-done.139
  1126.6 19.1 %collective-permute-done.150 = bf16[256,1024]{1,0:T(8,128)(2,1)S(1)} collective-permute-done((bf16[256,1024]{1,0:T(8,128)(2,1)S(1)}, bf16[256,1024]{1,0:T(8,128)(2,1)S(1)}, u32[]{:S(2)}, u32[]{:S(2)}) %collective-permute-start.150) | collective-permute-done | bytes 524320 | tf_op jit(solution)/shard_map/ppermute | solution.py:16
  1149.6 9.0 collective-permute-done.149
  1159.4 8.8 collective-permute-done.143
  1173.6 17.3 %collective-permute-done.153 = bf16[256,1024]{1,0:T(8,128)(2,1)S(1)} collective-permute-done((bf16[256,1024]{1,0:T(8,128)(2,1)S(1)}, bf16[256,1024]{1,0:T(8,128)(2,1)S(1)}, u32[]{:S(2)}, u32[]{:S(2)}) %collective-permute-start.153) | collective-permute-done | bytes 524320 | tf_op jit(solution)/shard_map/ppermute | solution.py:16
  1193.4 12.6 %collective-permute-start.97 = (bf16[64,3072]{1,0:T(8,128)(2,1)S(1)}, bf16[64,3072]{1,0:T(8,128)(2,1)S(1)}, u32[]{:S(2)}, u32[]{:S(2)}) collective-permute-start(bf16[64,3072]{1,0:T(8,128)(2,1)S(1)} %add_convert_fusion.9), channel_id=1, source_target_pairs={{0,8},{8,0},{16,24},{24,16},{1,9},{9,1},{17,25},{25,17},{2,10},{10... | collective-permute-start | bytes 1179656 | tf_op jit(solution)/shard_map/ppermute | solution.py:16
  1207.4 12.0 collective-permute-done.154
  1222.7 9.7 collective-permute-done.156
  (736 shorter events, 374.4 us)
Async XLA Ops:
  33.1 32.3 %collective-permute-start.33 = (bf16[64,4096]{1,0:T(8,128)(2,1)S(1)}, bf16[64,4096]{1,0:T(8,128)(2,1)}, u32[]{:S(2)}, u32[]{:S(2)}) collective-permute-start(bf16[64,4096]{1,0:T(8,128)(2,1)S(1)} %constant_dynamic-slice_fusion.18), channel_id=1, source_target_pairs={{0,2},{1,3},{2,4},{3,5},{4,6},{5,7},{6,0},{7,1},{8,10},{9,11},{10,... | collective-permute-start | bytes 1572872 | tf_op jit(solution)/shard_map/ppermute | solution.py:16
  33.9 32.1 %collective-permute-start.65 = (bf16[256,1024]{1,0:T(8,128)(2,1)S(1)}, bf16[256,1024]{1,0:T(8,128)(2,1)S(1)}, u32[]{:S(2)}, u32[]{:S(2)}) collective-permute-start(bf16[256,1024]{1,0:T(8,128)(2,1)S(1)} %constant_dynamic-slice_fusion.8), channel_id=1, source_target_pairs={{0,1},{1,0},{2,3},{3,2},{4,5},{5,4},{6,7},{7,6},{8,9},{9,8},{10,11... | collective-permute-start | bytes 1572872 | tf_op jit(solution)/shard_map/ppermute | solution.py:16
  42.9 33.1 %collective-permute-start.66 = (bf16[256,1024]{1,0:T(8,128)(2,1)S(1)}, bf16[256,1024]{1,0:T(8,128)(2,1)S(1)}, u32[]{:S(2)}, u32[]{:S(2)}) collective-permute-start(bf16[256,1024]{1,0:T(8,128)(2,1)S(1)} %constant_dynamic-slice_fusion.8), channel_id=1, source_target_pairs={{2,0},{3,1},{4,2},{5,3},{6,4},{7,5},{0,6},{1,7},{10,8},{11,9},{12,... | collective-permute-start | bytes 1572872 | tf_op jit(solution)/shard_map/ppermute | solution.py:16
  44.3 43.5 %collective-permute-start.70 = (bf16[256,1024]{1,0:T(8,128)(2,1)S(1)}, bf16[256,1024]{1,0:T(8,128)(2,1)S(1)}, u32[]{:S(2)}, u32[]{:S(2)}) collective-permute-start(bf16[256,1024]{1,0:T(8,128)(2,1)S(1)} %constant_dynamic-slice_fusion.8), channel_id=1, source_target_pairs={{0,2},{1,3},{2,4},{3,5},{4,6},{5,7},{6,0},{7,1},{8,10},{9,11},{10,... | collective-permute-start | bytes 1572872 | tf_op jit(solution)/shard_map/ppermute | solution.py:16
  53.6 35.4 %collective-permute-start.51 = (bf16[64,5120]{1,0:T(8,128)(2,1)S(1)}, bf16[64,5120]{1,0:T(8,128)(2,1)S(1)}, u32[]{:S(2)}, u32[]{:S(2)}) collective-permute-start(bf16[64,5120]{1,0:T(8,128)(2,1)S(1)} %constant_dynamic-slice_fusion.9), channel_id=1, source_target_pairs={{0,1},{1,0},{2,3},{3,2},{4,5},{5,4},{6,7},{7,6},{8,9},{9,8},{10,11... | collective-permute-start | bytes 1966088 | tf_op jit(solution)/shard_map/ppermute | solution.py:16
  65.4 35.9 %collective-permute-start.52 = (bf16[64,5120]{1,0:T(8,128)(2,1)S(1)}, bf16[64,5120]{1,0:T(8,128)(2,1)S(1)}, u32[]{:S(2)}, u32[]{:S(2)}) collective-permute-start(bf16[64,5120]{1,0:T(8,128)(2,1)S(1)} %constant_dynamic-slice_fusion.9), channel_id=1, source_target_pairs={{2,0},{3,1},{4,2},{5,3},{6,4},{7,5},{0,6},{1,7},{10,8},{11,9},{12,... | collective-permute-start | bytes 1966088 | tf_op jit(solution)/shard_map/ppermute | solution.py:16
  66.0 50.6 %collective-permute-start.54 = (bf16[64,5120]{1,0:T(8,128)(2,1)S(1)}, bf16[64,5120]{1,0:T(8,128)(2,1)S(1)}, u32[]{:S(2)}, u32[]{:S(2)}) collective-permute-start(bf16[64,5120]{1,0:T(8,128)(2,1)S(1)} %constant_dynamic-slice_fusion.9), channel_id=1, source_target_pairs={{0,2},{1,3},{2,4},{3,5},{4,6},{5,7},{6,0},{7,1},{8,10},{9,11},{10,... | collective-permute-start | bytes 1966088 | tf_op jit(solution)/shard_map/ppermute | solution.py:16
  76.0 47.7 %collective-permute-start.2 = (bf16[64,3072]{1,0:T(8,128)(2,1)S(1)}, bf16[64,3072]{1,0:T(8,128)(2,1)S(1)}, u32[]{:S(2)}, u32[]{:S(2)}) collective-permute-start(bf16[64,3072]{1,0:T(8,128)(2,1)S(1)} %collective-permute-done.refs_2_), channel_id=1, source_target_pairs={{2,0},{3,1},{4,2},{5,3},{6,4},{7,5},{0,6},{1,7},{10,8},{11,9},{12,... | collective-permute-start | bytes 1179656 | tf_op jit(solution)/shard_map/ppermute | solution.py:16
  87.8 45.0 %collective-permute-start.4 = (bf16[64,3072]{1,0:T(8,128)(2,1)}, bf16[64,3072]{1,0:T(8,128)(2,1)S(1)}, u32[]{:S(2)}, u32[]{:S(2)}) collective-permute-start(bf16[64,3072]{1,0:T(8,128)(2,1)} %collective-permute-done.3.refs_7_), channel_id=1, source_target_pairs={{0,2},{1,3},{2,4},{3,5},{4,6},{5,7},{6,0},{7,1},{8,10},{9,11},{10,... | collective-permute-start | bytes 1179656 | tf_op jit(solution)/shard_map/ppermute | solution.py:16
  89.0 52.2 %collective-permute-start.6 = (bf16[64,3072]{1,0:T(8,128)(2,1)S(1)}, bf16[64,3072]{1,0:T(8,128)(2,1)S(1)}, u32[]{:S(2)}, u32[]{:S(2)}) collective-permute-start(bf16[64,3072]{1,0:T(8,128)(2,1)S(1)} %collective-permute-done.refs_2_), channel_id=1, source_target_pairs={{0,2},{1,3},{2,4},{3,5},{4,6},{5,7},{6,0},{7,1},{8,10},{9,11},{10,... | collective-permute-start | bytes 1179656 | tf_op jit(solution)/shard_map/ppermute | solution.py:16
  101.3 41.3 %collective-permute-start.7 = (bf16[64,3072]{1,0:T(8,128)(2,1)S(1)}, bf16[64,3072]{1,0:T(8,128)(2,1)S(1)}, u32[]{:S(2)}, u32[]{:S(2)}) collective-permute-start(bf16[64,3072]{1,0:T(8,128)(2,1)S(1)} %collective-permute-done.refs_2_), channel_id=1, source_target_pairs={{0,8},{8,0},{16,24},{24,16},{1,9},{9,1},{17,25},{25,17},{2,10},{10... | collective-permute-start | bytes 1179656 | tf_op jit(solution)/shard_map/ppermute | solution.py:16
  132.8 38.6 %collective-permute-start.30 = (bf16[64,4096]{1,0:T(8,128)(2,1)}, bf16[64,4096]{1,0:T(8,128)(2,1)}, u32[]{:S(2)}, u32[]{:S(2)}) collective-permute-start(bf16[64,4096]{1,0:T(8,128)(2,1)} %collective-permute-done.28.refs_2_), channel_id=1, source_target_pairs={{2,0},{3,1},{4,2},{5,3},{6,4},{7,5},{0,6},{1,7},{10,8},{11,9},{12,... | collective-permute-start | bytes 1572872 | tf_op jit(solution)/shard_map/ppermute | solution.py:16
  141.2 36.9 %collective-permute-start.34 = (bf16[64,4096]{1,0:T(8,128)(2,1)}, bf16[64,4096]{1,0:T(8,128)(2,1)}, u32[]{:S(2)}, u32[]{:S(2)}) collective-permute-start(bf16[64,4096]{1,0:T(8,128)(2,1)} %collective-permute-done.28.refs_2_), channel_id=1, source_target_pairs={{0,2},{1,3},{2,4},{3,5},{4,6},{5,7},{6,0},{7,1},{8,10},{9,11},{10,... | collective-permute-start | bytes 1572872 | tf_op jit(solution)/shard_map/ppermute | solution.py:16
  142.6 38.4 %collective-permute-start.35 = (bf16[64,4096]{1,0:T(8,128)(2,1)}, bf16[64,4096]{1,0:T(8,128)(2,1)}, u32[]{:S(2)}, u32[]{:S(2)}) collective-permute-start(bf16[64,4096]{1,0:T(8,128)(2,1)} %collective-permute-done.28.refs_2_), channel_id=1, source_target_pairs={{0,8},{8,0},{16,24},{24,16},{1,9},{9,1},{17,25},{25,17},{2,10},{10... | collective-permute-start | bytes 1572872 | tf_op jit(solution)/shard_map/ppermute | solution.py:16
  144.7 30.9 %collective-permute-start.31 = (bf16[64,4096]{1,0:T(8,128)(2,1)}, bf16[64,4096]{1,0:T(8,128)(2,1)}, u32[]{:S(2)}, u32[]{:S(2)}) collective-permute-start(bf16[64,4096]{1,0:T(8,128)(2,1)} %collective-permute-done.29.refs_3_), channel_id=1, source_target_pairs={{2,0},{3,1},{4,2},{5,3},{6,4},{7,5},{0,6},{1,7},{10,8},{11,9},{12,... | collective-permute-start | bytes 1572872 | tf_op jit(solution)/shard_map/ppermute | solution.py:16
  146.9 35.7 %collective-permute-start.36 = (bf16[64,4096]{1,0:T(8,128)(2,1)}, bf16[64,4096]{1,0:T(8,128)(2,1)}, u32[]{:S(2)}, u32[]{:S(2)}) collective-permute-start(bf16[64,4096]{1,0:T(8,128)(2,1)} %collective-permute-done.29.refs_3_), channel_id=1, source_target_pairs={{0,8},{8,0},{16,24},{24,16},{1,9},{9,1},{17,25},{25,17},{2,10},{10... | collective-permute-start | bytes 1572872 | tf_op jit(solution)/shard_map/ppermute | solution.py:16
  178.1 44.4 %collective-permute-start.44 = (bf16[4,128,1024]{1,2,0:T(8,128)(2,1)}, bf16[4,128,1024]{1,2,0:T(8,128)(2,1)S(1)}, u32[]{:S(2)}, u32[]{:S(2)}) collective-permute-start(bf16[4,128,1024]{1,2,0:T(8,128)(2,1)} %copy.121), channel_id=1, source_target_pairs={{2,1},{3,0},{4,3},{5,2},{6,5},{7,4},{0,7},{1,6},{10,9},{11,8},{12,... | collective-permute-start | bytes 3145736 | tf_op jit(solution)/shard_map/ppermute | solution.py:16
  181.0 64.8 %collective-permute-start.45 = (bf16[4,128,1024]{1,2,0:T(8,128)(2,1)}, bf16[4,128,1024]{1,2,0:T(8,128)(2,1)}, u32[]{:S(2)}, u32[]{:S(2)}) collective-permute-start(bf16[4,128,1024]{1,2,0:T(8,128)(2,1)} %copy.122), channel_id=1, source_target_pairs={{0,2},{1,3},{2,4},{3,5},{4,6},{5,7},{6,0},{7,1},{8,10},{9,11},{10,... | collective-permute-start | bytes 3145736 | tf_op jit(solution)/shard_map/ppermute | solution.py:16
  182.5 85.1 %collective-permute-start.47 = (bf16[4,128,1024]{1,2,0:T(8,128)(2,1)}, bf16[4,128,1024]{1,2,0:T(8,128)(2,1)}, u32[]{:S(2)}, u32[]{:S(2)}) collective-permute-start(bf16[4,128,1024]{1,2,0:T(8,128)(2,1)} %copy.123), channel_id=1, source_target_pairs={{2,0},{3,1},{4,2},{5,3},{6,4},{7,5},{0,6},{1,7},{10,8},{11,9},{12,... | collective-permute-start | bytes 3145736 | tf_op jit(solution)/shard_map/ppermute | solution.py:16
  196.2 75.0 %collective-permute-start.5 = (bf16[64,3072]{1,0:T(8,128)(2,1)}, bf16[64,3072]{1,0:T(8,128)(2,1)S(1)}, u32[]{:S(2)}, u32[]{:S(2)}) collective-permute-start(bf16[64,3072]{1,0:T(8,128)(2,1)} %copy-done.66), channel_id=1, source_target_pairs={{0,1},{1,0},{2,3},{3,2},{4,5},{5,4},{6,7},{7,6},{8,9},{9,8},{10,11... | collective-permute-start | bytes 1179656 | tf_op jit(solution)/shard_map/ppermute | solution.py:16
  200.0 90.7 %collective-permute-start.49 = (bf16[4,128,1024]{1,2,0:T(8,128)(2,1)S(1)}, bf16[4,128,1024]{1,2,0:T(8,128)(2,1)S(1)}, u32[]{:S(2)}, u32[]{:S(2)}) collective-permute-start(bf16[4,128,1024]{1,2,0:T(8,128)(2,1)S(1)} %copy-done.29), channel_id=1, source_target_pairs={{0,2},{1,3},{2,4},{3,5},{4,6},{5,7},{6,0},{7,1},{8,10},{9,11},{10,... | collective-permute-start | bytes 3145736 | tf_op jit(solution)/shard_map/ppermute | solution.py:16
  222.5 49.7 %collective-permute-start.9 = (bf16[64,3072]{1,0:T(8,128)(2,1)S(1)}, bf16[64,3072]{1,0:T(8,128)(2,1)S(1)}, u32[]{:S(2)}, u32[]{:S(2)}) collective-permute-start(bf16[64,3072]{1,0:T(8,128)(2,1)S(1)} %copy-done.65), channel_id=1, source_target_pairs={{0,8},{8,0},{16,24},{24,16},{1,9},{9,1},{17,25},{25,17},{2,10},{10... | collective-permute-start | bytes 1179656 | tf_op jit(solution)/shard_map/ppermute | solution.py:16
  273.7 39.4 %collective-permute-start.50 = (bf16[4,128,1024]{1,2,0:T(8,128)(2,1)S(1)}, bf16[4,128,1024]{1,2,0:T(8,128)(2,1)S(1)}, u32[]{:S(2)}, u32[]{:S(2)}) collective-permute-start(bf16[4,128,1024]{1,2,0:T(8,128)(2,1)S(1)} %copy-done.28), channel_id=1, source_target_pairs={{0,3},{1,2},{2,5},{3,4},{4,7},{5,6},{6,1},{7,0},{8,11},{9,10},{10,... | collective-permute-start | bytes 3145736 | tf_op jit(solution)/shard_map/ppermute | solution.py:16
  273.8 98.4 %collective-permute-start.46 = (bf16[4,128,1024]{1,2,0:T(8,128)(2,1)}, bf16[4,128,1024]{1,2,0:T(8,128)(2,1)S(1)}, u32[]{:S(2)}, u32[]{:S(2)}) collective-permute-start(bf16[4,128,1024]{1,2,0:T(8,128)(2,1)} %collective-permute-done.45), channel_id=1, source_target_pairs={{0,2},{1,3},{2,4},{3,5},{4,6},{5,7},{6,0},{7,1},{8,10},{9,11},{10,... | collective-permute-start | bytes 3145736 | tf_op jit(solution)/shard_map/ppermute | solution.py:16
  274.7 98.0 %collective-permute-start.48 = (bf16[4,128,1024]{1,2,0:T(8,128)(2,1)}, bf16[4,128,1024]{1,2,0:T(8,128)(2,1)S(1)}, u32[]{:S(2)}, u32[]{:S(2)}) collective-permute-start(bf16[4,128,1024]{1,2,0:T(8,128)(2,1)} %collective-permute-done.47), channel_id=1, source_target_pairs={{2,1},{3,0},{4,3},{5,2},{6,5},{7,4},{0,7},{1,6},{10,9},{11,8},{12,... | collective-permute-start | bytes 3145736 | tf_op jit(solution)/shard_map/ppermute | solution.py:16
  286.0 84.6 %collective-permute-start.67 = (bf16[256,1024]{1,0:T(8,128)(2,1)S(1)}, bf16[256,1024]{1,0:T(8,128)(2,1)S(1)}, u32[]{:S(2)}, u32[]{:S(2)}) collective-permute-start(bf16[256,1024]{1,0:T(8,128)(2,1)S(1)} %copy-done.47), channel_id=1, source_target_pairs={{2,0},{3,1},{4,2},{5,3},{6,4},{7,5},{0,6},{1,7},{10,8},{11,9},{12,... | collective-permute-start | bytes 1572872 | tf_op jit(solution)/shard_map/ppermute | solution.py:16
  290.7 81.5 %collective-permute-start.32 = (bf16[64,4096]{1,0:T(8,128)(2,1)}, bf16[64,4096]{1,0:T(8,128)(2,1)S(1)}, u32[]{:S(2)}, u32[]{:S(2)}) collective-permute-start(bf16[64,4096]{1,0:T(8,128)(2,1)} %collective-permute-done.31.refs_5_), channel_id=1, source_target_pairs={{0,1},{1,0},{2,3},{3,2},{4,5},{5,4},{6,7},{7,6},{8,9},{9,8},{10,11... | collective-permute-start | bytes 1572872 | tf_op jit(solution)/shard_map/ppermute | solution.py:16
  313.1 68.9 %collective-permute-start.68 = (bf16[256,1024]{1,0:T(8,128)(2,1)S(1)}, bf16[256,1024]{1,0:T(8,128)(2,1)}, u32[]{:S(2)}, u32[]{:S(2)}) collective-permute-start(bf16[256,1024]{1,0:T(8,128)(2,1)S(1)} %copy-done.49), channel_id=1, source_target_pairs={{2,0},{3,1},{4,2},{5,3},{6,4},{7,5},{0,6},{1,7},{10,8},{11,9},{12,... | collective-permute-start | bytes 1572872 | tf_op jit(solution)/shard_map/ppermute | solution.py:16
  433.3 29.7 %collective-permute-start.57 = (bf16[64,5120]{1,0:T(8,128)(2,1)S(1)}, bf16[64,5120]{1,0:T(8,128)(2,1)S(1)}, u32[]{:S(2)}, u32[]{:S(2)}) collective-permute-start(bf16[64,5120]{1,0:T(8,128)(2,1)S(1)} %copy-done.34), channel_id=1, source_target_pairs={{0,2},{1,3},{2,4},{3,5},{4,6},{5,7},{6,0},{7,1},{8,10},{9,11},{10,... | collective-permute-start | bytes 1966088 | tf_op jit(solution)/shard_map/ppermute | solution.py:16
  434.2 30.2 %collective-permute-start.58 = (bf16[64,5120]{1,0:T(8,128)(2,1)S(1)}, bf16[64,5120]{1,0:T(8,128)(2,1)S(1)}, u32[]{:S(2)}, u32[]{:S(2)}) collective-permute-start(bf16[64,5120]{1,0:T(8,128)(2,1)S(1)} %copy-done.34), channel_id=1, source_target_pairs={{0,8},{8,0},{16,24},{24,16},{1,9},{9,1},{17,25},{25,17},{2,10},{10... | collective-permute-start | bytes 1966088 | tf_op jit(solution)/shard_map/ppermute | solution.py:16
  435.0 29.9 %collective-permute-start.56 = (bf16[64,5120]{1,0:T(8,128)(2,1)S(1)}, bf16[64,5120]{1,0:T(8,128)(2,1)}, u32[]{:S(2)}, u32[]{:S(2)}) collective-permute-start(bf16[64,5120]{1,0:T(8,128)(2,1)S(1)} %collective-permute-done.55.refs_5_), channel_id=1, source_target_pairs={{0,1},{1,0},{2,3},{3,2},{4,5},{5,4},{6,7},{7,6},{8,9},{9,8},{10,11... | collective-permute-start | bytes 1966088 | tf_op jit(solution)/shard_map/ppermute | solution.py:16
  448.6 46.8 %collective-permute-start.63 = (bf16[64,5120]{1,0:T(8,128)(2,1)S(1)}, bf16[64,5120]{1,0:T(8,128)(2,1)}, u32[]{:S(2)}, u32[]{:S(2)}) collective-permute-start(bf16[64,5120]{1,0:T(8,128)(2,1)S(1)} %copy-done.38), channel_id=1, source_target_pairs={{0,8},{8,0},{16,24},{24,16},{1,9},{9,1},{17,25},{25,17},{2,10},{10... | collective-permute-start | bytes 1966088 | tf_op jit(solution)/shard_map/ppermute | solution.py:16
  463.1 32.4 %collective-permute-start.61 = (bf16[64,5120]{1,0:T(8,128)(2,1)S(1)}, bf16[64,5120]{1,0:T(8,128)(2,1)}, u32[]{:S(2)}, u32[]{:S(2)}) collective-permute-start(bf16[64,5120]{1,0:T(8,128)(2,1)S(1)} %collective-permute-done.55.refs_5_), channel_id=1, source_target_pairs={{0,8},{8,0},{16,24},{24,16},{1,9},{9,1},{17,25},{25,17},{2,10},{10... | collective-permute-start | bytes 1966088 | tf_op jit(solution)/shard_map/ppermute | solution.py:16
  464.4 31.0 %collective-permute-start.60 = (bf16[64,5120]{1,0:T(8,128)(2,1)S(1)}, bf16[64,5120]{1,0:T(8,128)(2,1)S(1)}, u32[]{:S(2)}, u32[]{:S(2)}) collective-permute-start(bf16[64,5120]{1,0:T(8,128)(2,1)S(1)} %collective-permute-done.53.refs_4_), channel_id=1, source_target_pairs={{0,8},{8,0},{16,24},{24,16},{1,9},{9,1},{17,25},{25,17},{2,10},{10... | collective-permute-start | bytes 1966088 | tf_op jit(solution)/shard_map/ppermute | solution.py:16
  464.5 31.0 %collective-permute-start.64 = (bf16[64,5120]{1,0:T(8,128)(2,1)S(1)}, bf16[64,5120]{1,0:T(8,128)(2,1)S(1)}, u32[]{:S(2)}, u32[]{:S(2)}) collective-permute-start(bf16[64,5120]{1,0:T(8,128)(2,1)S(1)} %collective-permute-done.57.refs_8_), channel_id=1, source_target_pairs={{0,8},{8,0},{16,24},{24,16},{1,9},{9,1},{17,25},{25,17},{2,10},{10... | collective-permute-start | bytes 1966088 | tf_op jit(solution)/shard_map/ppermute | solution.py:16
  464.9 30.6 %collective-permute-start.62 = (bf16[64,5120]{1,0:T(8,128)(2,1)}, bf16[64,5120]{1,0:T(8,128)(2,1)}, u32[]{:S(2)}, u32[]{:S(2)}) collective-permute-start(bf16[64,5120]{1,0:T(8,128)(2,1)} %collective-permute-done.56.refs_6_), channel_id=1, source_target_pairs={{0,8},{8,0},{16,24},{24,16},{1,9},{9,1},{17,25},{25,17},{2,10},{10... | collective-permute-start | bytes 1966088 | tf_op jit(solution)/shard_map/ppermute | solution.py:16
  745.7 73.1 %collective-permute-start.118 = (bf16[8,64,2048]{2,1,0:T(8,128)(2,1)S(1)}, bf16[8,64,2048]{2,1,0:T(8,128)(2,1)S(1)}, u32[]{:S(2)}, u32[]{:S(2)}) collective-permute-start(bf16[8,64,2048]{2,1,0:T(8,128)(2,1)S(1)} %dynamic-slice_bitcast_fusion.3), channel_id=1, source_target_pairs={{0,8},{8,0},{16,24},{24,16},{1,9},{9,1},{17,25},{25,17},{2,10},{10... | collective-permute-start | bytes 6291464 | tf_op jit(solution)/shard_map/ppermute | solution.py:16
  761.4 38.4 %collective-permute-start.105 = (bf16[64,1024]{1,0:T(8,128)(2,1)S(1)}, bf16[64,1024]{1,0:T(8,128)(2,1)S(1)}, u32[]{:S(2)}, u32[]{:S(2)}) collective-permute-start(bf16[64,1024]{1,0:T(8,128)(2,1)S(1)} %get-tuple-element.121), channel_id=1, source_target_pairs={{2,0},{3,1},{4,2},{5,3},{6,4},{7,5},{0,6},{1,7},{10,8},{11,9},{12,... | collective-permute-start | bytes 393224 | tf_op jit(solution)/shard_map/ppermute | solution.py:16
  811.3 56.2 %collective-permute-start.80 = (bf16[4,128,1024]{2,1,0:T(8,128)(2,1)S(1)}, bf16[4,128,1024]{2,1,0:T(8,128)(2,1)S(1)}, u32[]{:S(2)}, u32[]{:S(2)}) collective-permute-start(bf16[4,128,1024]{2,1,0:T(8,128)(2,1)S(1)} %bitcast.449), channel_id=1, source_target_pairs={{2,0},{3,1},{4,2},{5,3},{6,4},{7,5},{0,6},{1,7},{10,8},{11,9},{12,... | collective-permute-start | bytes 3145736 | tf_op jit(solution)/shard_map/ppermute | solution.py:16
  812.8 55.9 %collective-permute-start.81 = (bf16[4,128,1024]{2,1,0:T(8,128)(2,1)S(1)}, bf16[4,128,1024]{2,1,0:T(8,128)(2,1)S(1)}, u32[]{:S(2)}, u32[]{:S(2)}) collective-permute-start(bf16[4,128,1024]{2,1,0:T(8,128)(2,1)S(1)} %bitcast.448), channel_id=1, source_target_pairs={{2,1},{3,0},{4,3},{5,2},{6,5},{7,4},{0,7},{1,6},{10,9},{11,8},{12,... | collective-permute-start | bytes 3145736 | tf_op jit(solution)/shard_map/ppermute | solution.py:16
  817.9 51.2 %collective-permute-start.82 = (bf16[4,128,1024]{2,1,0:T(8,128)(2,1)S(1)}, bf16[4,128,1024]{2,1,0:T(8,128)(2,1)S(1)}, u32[]{:S(2)}, u32[]{:S(2)}) collective-permute-start(bf16[4,128,1024]{2,1,0:T(8,128)(2,1)S(1)} %bitcast.447), channel_id=1, source_target_pairs={{0,2},{1,3},{2,4},{3,5},{4,6},{5,7},{6,0},{7,1},{8,10},{9,11},{10,... | collective-permute-start | bytes 3145736 | tf_op jit(solution)/shard_map/ppermute | solution.py:16
  818.8 106.7 %collective-permute-start.84 = (bf16[4,128,1024]{2,1,0:T(8,128)(2,1)S(1)}, bf16[4,128,1024]{2,1,0:T(8,128)(2,1)S(1)}, u32[]{:S(2)}, u32[]{:S(2)}) collective-permute-start(bf16[4,128,1024]{2,1,0:T(8,128)(2,1)S(1)} %bitcast.446), channel_id=1, source_target_pairs={{2,0},{3,1},{4,2},{5,3},{6,4},{7,5},{0,6},{1,7},{10,8},{11,9},{12,... | collective-permute-start | bytes 3145736 | tf_op jit(solution)/shard_map/ppermute | solution.py:16
  829.7 211.5 %collective-permute-start.88 = (bf16[8,64,3072]{2,1,0:T(8,128)(2,1)}, bf16[8,64,3072]{2,1,0:T(8,128)(2,1)}, u32[]{:S(2)}, u32[]{:S(2)}) collective-permute-start(bf16[8,64,3072]{2,1,0:T(8,128)(2,1)} %dynamic-slice_bitcast_fusion.2), channel_id=1, source_target_pairs={{0,8},{8,0},{16,24},{24,16},{1,9},{9,1},{17,25},{25,17},{2,10},{10... | collective-permute-start | bytes 9437192 | tf_op jit(solution)/shard_map/ppermute | solution.py:16
  869.0 30.6 %collective-permute-start.120 = (bf16[64,2048]{1,0:T(8,128)(2,1)S(1)}, bf16[64,2048]{1,0:T(8,128)(2,1)S(1)}, u32[]{:S(2)}, u32[]{:S(2)}) collective-permute-start(bf16[64,2048]{1,0:T(8,128)(2,1)S(1)} %get-tuple-element.99), channel_id=1, source_target_pairs={{0,2},{1,3},{2,4},{3,5},{4,6},{5,7},{6,0},{7,1},{8,10},{9,11},{10,... | collective-permute-start | bytes 786440 | tf_op jit(solution)/shard_map/ppermute | solution.py:16
  886.6 36.2 %collective-permute-start.119 = (bf16[64,2048]{1,0:T(8,128)(2,1)S(1)}, bf16[64,2048]{1,0:T(8,128)(2,1)S(1)}, u32[]{:S(2)}, u32[]{:S(2)}) collective-permute-start(bf16[64,2048]{1,0:T(8,128)(2,1)S(1)} %get-tuple-element.96), channel_id=1, source_target_pairs={{2,0},{3,1},{4,2},{5,3},{6,4},{7,5},{0,6},{1,7},{10,8},{11,9},{12,... | collective-permute-start | bytes 786440 | tf_op jit(solution)/shard_map/ppermute | solution.py:16
  892.7 31.4 %collective-permute-start.122 = (bf16[64,2048]{1,0:T(8,128)(2,1)S(1)}, bf16[64,2048]{1,0:T(8,128)(2,1)S(1)}, u32[]{:S(2)}, u32[]{:S(2)}) collective-permute-start(bf16[64,2048]{1,0:T(8,128)(2,1)S(1)} %get-tuple-element.98), channel_id=1, source_target_pairs={{0,1},{1,0},{2,3},{3,2},{4,5},{5,4},{6,7},{7,6},{8,9},{9,8},{10,11... | collective-permute-start | bytes 786440 | tf_op jit(solution)/shard_map/ppermute | solution.py:16
  899.6 30.2 %collective-permute-start.107 = (bf16[64,1024]{1,0:T(8,128)(2,1)S(1)}, bf16[64,1024]{1,0:T(8,128)(2,1)S(1)}, u32[]{:S(2)}, u32[]{:S(2)}) collective-permute-start(bf16[64,1024]{1,0:T(8,128)(2,1)S(1)} %add_convert_fusion.13), channel_id=1, source_target_pairs={{0,8},{8,0},{16,24},{24,16},{1,9},{9,1},{17,25},{25,17},{2,10},{10... | collective-permute-start | bytes 393224 | tf_op jit(solution)/shard_map/ppermute | solution.py:16
  929.8 50.7 %collective-permute-start.87 = (bf16[4,128,1024]{2,1,0:T(8,128)(2,1)S(1)}, bf16[4,128,1024]{2,1,0:T(8,128)(2,1)S(1)}, u32[]{:S(2)}, u32[]{:S(2)}) collective-permute-start(bf16[4,128,1024]{2,1,0:T(8,128)(2,1)S(1)} %bitcast.444), channel_id=1, source_target_pairs={{0,3},{1,2},{2,5},{3,4},{4,7},{5,6},{6,1},{7,0},{8,11},{9,10},{10,... | collective-permute-start | bytes 3145736 | tf_op jit(solution)/shard_map/ppermute | solution.py:16
  929.9 72.8 %collective-permute-start.83 = (bf16[4,128,1024]{2,1,0:T(8,128)(2,1)S(1)}, bf16[4,128,1024]{2,1,0:T(8,128)(2,1)S(1)}, u32[]{:S(2)}, u32[]{:S(2)}) collective-permute-start(bf16[4,128,1024]{2,1,0:T(8,128)(2,1)S(1)} %collective-permute-done.82), channel_id=1, source_target_pairs={{0,2},{1,3},{2,4},{3,5},{4,6},{5,7},{6,0},{7,1},{8,10},{9,11},{10,... | collective-permute-start | bytes 3145736 | tf_op jit(solution)/shard_map/ppermute | solution.py:16
  934.3 91.5 %collective-permute-start.85 = (bf16[4,128,1024]{2,1,0:T(8,128)(2,1)S(1)}, bf16[4,128,1024]{2,1,0:T(8,128)(2,1)}, u32[]{:S(2)}, u32[]{:S(2)}) collective-permute-start(bf16[4,128,1024]{2,1,0:T(8,128)(2,1)S(1)} %collective-permute-done.84), channel_id=1, source_target_pairs={{2,1},{3,0},{4,3},{5,2},{6,5},{7,4},{0,7},{1,6},{10,9},{11,8},{12,... | collective-permute-start | bytes 3145736 | tf_op jit(solution)/shard_map/ppermute | solution.py:16
  957.7 81.9 %collective-permute-start.125 = (bf16[64,2048]{1,0:T(8,128)(2,1)S(1)}, bf16[64,2048]{1,0:T(8,128)(2,1)S(1)}, u32[]{:S(2)}, u32[]{:S(2)}) collective-permute-start(bf16[64,2048]{1,0:T(8,128)(2,1)S(1)} %get-tuple-element.97), channel_id=1, source_target_pairs={{0,2},{1,3},{2,4},{3,5},{4,6},{5,7},{6,0},{7,1},{8,10},{9,11},{10,... | collective-permute-start | bytes 786440 | tf_op jit(solution)/shard_map/ppermute | solution.py:16
  980.5 59.2 %collective-permute-start.121 = (bf16[64,2048]{1,0:T(8,128)(2,1)}, bf16[64,2048]{1,0:T(8,128)(2,1)S(1)}, u32[]{:S(2)}, u32[]{:S(2)}) collective-permute-start(bf16[64,2048]{1,0:T(8,128)(2,1)} %get-tuple-element.94), channel_id=1, source_target_pairs={{0,1},{1,0},{2,3},{3,2},{4,5},{5,4},{6,7},{7,6},{8,9},{9,8},{10,11... | collective-permute-start | bytes 786440 | tf_op jit(solution)/shard_map/ppermute | solution.py:16
  1002.7 37.0 %collective-permute-start.124 = (bf16[64,2048]{1,0:T(8,128)(2,1)}, bf16[64,2048]{1,0:T(8,128)(2,1)S(1)}, u32[]{:S(2)}, u32[]{:S(2)}) collective-permute-start(bf16[64,2048]{1,0:T(8,128)(2,1)} %fusion.41), channel_id=1, source_target_pairs={{2,0},{3,1},{4,2},{5,3},{6,4},{7,5},{0,6},{1,7},{10,8},{11,9},{12,... | collective-permute-start | bytes 786440 | tf_op jit(solution)/shard_map/ppermute | solution.py:16
  1025.8 60.4 %collective-permute-start.138 = (bf16[8,64,4096]{2,1,0:T(8,128)(2,1)}, bf16[8,64,4096]{2,1,0:T(8,128)(2,1)}, u32[]{:S(2)}, u32[]{:S(2)}) collective-permute-start(bf16[8,64,4096]{2,1,0:T(8,128)(2,1)} %dynamic-slice_bitcast_fusion.1), channel_id=1, source_target_pairs={{0,8},{8,0},{16,24},{24,16},{1,9},{9,1},{17,25},{25,17},{2,10},{10... | collective-permute-start | bytes 12582920 | tf_op jit(solution)/shard_map/ppermute | solution.py:16
  1039.6 54.7 %collective-permute-start.148 = (bf16[8,256,1024]{2,1,0:T(8,128)(2,1)}, bf16[8,256,1024]{2,1,0:T(8,128)(2,1)}, u32[]{:S(2)}, u32[]{:S(2)}) collective-permute-start(bf16[8,256,1024]{2,1,0:T(8,128)(2,1)} %dynamic-slice_bitcast_fusion), channel_id=1, source_target_pairs={{0,8},{8,0},{16,24},{24,16},{1,9},{9,1},{17,25},{25,17},{2,10},{10... | collective-permute-start | bytes 12582920 | tf_op jit(solution)/shard_map/ppermute | solution.py:16
  1057.9 61.2 %collective-permute-start.95 = (bf16[64,3072]{1,0:T(8,128)(2,1)}, bf16[64,3072]{1,0:T(8,128)(2,1)}, u32[]{:S(2)}, u32[]{:S(2)}) collective-permute-start(bf16[64,3072]{1,0:T(8,128)(2,1)} %get-tuple-element.90), channel_id=1, source_target_pairs={{0,2},{1,3},{2,4},{3,5},{4,6},{5,7},{6,0},{7,1},{8,10},{9,11},{10,... | collective-permute-start | bytes 1179656 | tf_op jit(solution)/shard_map/ppermute | solution.py:16
  1076.3 46.1 %collective-permute-start.91 = (bf16[64,3072]{1,0:T(8,128)(2,1)}, bf16[64,3072]{1,0:T(8,128)(2,1)S(1)}, u32[]{:S(2)}, u32[]{:S(2)}) collective-permute-start(bf16[64,3072]{1,0:T(8,128)(2,1)} %get-tuple-element.87), channel_id=1, source_target_pairs={{0,1},{1,0},{2,3},{3,2},{4,5},{5,4},{6,7},{7,6},{8,9},{9,8},{10,11... | collective-permute-start | bytes 1179656 | tf_op jit(solution)/shard_map/ppermute | solution.py:16
  1115.3 78.1 %collective-permute-start.145 = (bf16[64,4096]{1,0:T(8,128)(2,1)S(1)}, bf16[64,4096]{1,0:T(8,128)(2,1)S(1)}, u32[]{:S(2)}, u32[]{:S(2)}) collective-permute-start(bf16[64,4096]{1,0:T(8,128)(2,1)S(1)} %copy-done.62), channel_id=1, source_target_pairs={{2,0},{3,1},{4,2},{5,3},{6,4},{7,5},{0,6},{1,7},{10,8},{11,9},{12,... | collective-permute-start | bytes 1572872 | tf_op jit(solution)/shard_map/ppermute | solution.py:16
  1119.1 39.5 %collective-permute-start.149 = (bf16[256,1024]{1,0:T(8,128)(2,1)S(1)}, bf16[256,1024]{1,0:T(8,128)(2,1)S(1)}, u32[]{:S(2)}, u32[]{:S(2)}) collective-permute-start(bf16[256,1024]{1,0:T(8,128)(2,1)S(1)} %get-tuple-element.77), channel_id=1, source_target_pairs={{2,0},{3,1},{4,2},{5,3},{6,4},{7,5},{0,6},{1,7},{10,8},{11,9},{12,... | collective-permute-start | bytes 1572872 | tf_op jit(solution)/shard_map/ppermute | solution.py:16
  1122.4 36.4 %collective-permute-start.152 = (bf16[256,1024]{1,0:T(8,128)(2,1)S(1)}, bf16[256,1024]{1,0:T(8,128)(2,1)S(1)}, u32[]{:S(2)}, u32[]{:S(2)}) collective-permute-start(bf16[256,1024]{1,0:T(8,128)(2,1)S(1)} %get-tuple-element.79), channel_id=1, source_target_pairs={{0,1},{1,0},{2,3},{3,2},{4,5},{5,4},{6,7},{7,6},{8,9},{9,8},{10,11... | collective-permute-start | bytes 1572872 | tf_op jit(solution)/shard_map/ppermute | solution.py:16
  1124.1 44.1 %collective-permute-start.143 = (bf16[64,4096]{1,0:T(8,128)(2,1)S(1)}, bf16[64,4096]{1,0:T(8,128)(2,1)S(1)}, u32[]{:S(2)}, u32[]{:S(2)}) collective-permute-start(bf16[64,4096]{1,0:T(8,128)(2,1)S(1)} %get-tuple-element.82), channel_id=1, source_target_pairs={{0,2},{1,3},{2,4},{3,5},{4,6},{5,7},{6,0},{7,1},{8,10},{9,11},{10,... | collective-permute-start | bytes 1572872 | tf_op jit(solution)/shard_map/ppermute | solution.py:16
  1145.7 61.7 %collective-permute-start.155 = (bf16[256,1024]{1,0:T(8,128)(2,1)S(1)}, bf16[256,1024]{1,0:T(8,128)(2,1)S(1)}, u32[]{:S(2)}, u32[]{:S(2)}) collective-permute-start(bf16[256,1024]{1,0:T(8,128)(2,1)S(1)} %get-tuple-element.78), channel_id=1, source_target_pairs={{0,2},{1,3},{2,4},{3,5},{4,6},{5,7},{6,0},{7,1},{8,10},{9,11},{10,... | collective-permute-start | bytes 1572872 | tf_op jit(solution)/shard_map/ppermute | solution.py:16
  1158.9 47.1 %collective-permute-start.141 = (bf16[64,4096]{1,0:T(8,128)(2,1)S(1)}, bf16[64,4096]{1,0:T(8,128)(2,1)S(1)}, u32[]{:S(2)}, u32[]{:S(2)}) collective-permute-start(bf16[64,4096]{1,0:T(8,128)(2,1)S(1)} %get-tuple-element.81), channel_id=1, source_target_pairs={{0,1},{1,0},{2,3},{3,2},{4,5},{5,4},{6,7},{7,6},{8,9},{9,8},{10,11... | collective-permute-start | bytes 1572872 | tf_op jit(solution)/shard_map/ppermute | solution.py:16
  1173.4 32.5 %collective-permute-start.144 = (bf16[64,4096]{1,0:T(8,128)(2,1)S(1)}, bf16[64,4096]{1,0:T(8,128)(2,1)S(1)}, u32[]{:S(2)}, u32[]{:S(2)}) collective-permute-start(bf16[64,4096]{1,0:T(8,128)(2,1)S(1)} %fusion.27), channel_id=1, source_target_pairs={{0,2},{1,3},{2,4},{3,5},{4,6},{5,7},{6,0},{7,1},{8,10},{9,11},{10,... | collective-permute-start | bytes 1572872 | tf_op jit(solution)/shard_map/ppermute | solution.py:16
  (233 other events, 5273.0 us)

commit v2 on v1

v2 whole, which is shorter than its diff:
```python
import jax
import jax.numpy as jnp
from jax import lax
from jax.experimental import pallas as pl
from jax.experimental.pallas import tpu as pltpu
from jax.sharding import PartitionSpec as P

HEADS = 16
CHUNKS = 4
BF = jnp.bfloat16
F32 = jnp.float32
VMEM_BYTES = 56 * 1024 * 1024


def move(axis, pairs):
    return lambda value: lax.ppermute(value, axis, pairs)


swap_x = move("blk", [(i, i ^ 1) for i in range(8)])
swap_core = move("items", [(i, i ^ 1) for i in range(4)])
swap_y = move("items", [(i, i ^ 2) for i in range(4)])


def hop(first, last, step):
    return move("blk", [(2 * z + x, 2 * (z + step) + x) for z in range(first, last + 1) for x in (0, 1)])


def tie(value, *others):
    return lax.optimization_barrier((value,) + others)[0]


def places():
    me = lax.axis_index("blk")
    return [((me + 2 * (k // 2)) % 8) ^ (k % 2) for k in range(8)]


def spot_vector():
    group = lax.axis_index("items")
    return jnp.stack(places() + [group // 2, group % 2]).astype(jnp.int32)


def column_share(matrix, index, ways=4):
    width = matrix.shape[1] // ways
    return lax.dynamic_slice_in_dim(matrix, index * width, width, 1)


def side_by_side(matrix):
    rows = matrix.shape[0]
    if rows == 128:
        return matrix
    return jnp.concatenate([matrix[r : r + 128] for r in range(0, rows, 128)], axis=1)


ANY = pl.BlockSpec(memory_space=pl.ANY)


def place_kernel(count, extra, ways, *refs):
    spots, shards, parts = refs[0], refs[1 : 1 + count], refs[1 + count : 1 + count + 2 * ways]
    refs = refs[1 + count + 2 * ways :]
    outs, held, (in_sem, out_sem) = refs[:count], refs[count : 2 * count], refs[2 * count :]
    y, core = spots[8], spots[9]
    if ways == 2:
        shares = [core, 1 - core]
    else:
        shares = [2 * y + core, 2 * (1 - y) + core, 2 * y + 1 - core, 2 * (1 - y) + 1 - core]
    order = [1, 2, 4, 6, 3, 5, 7]
    arriving = [[] for _ in range(8)]
    used = 0

    def bring(k, source, target):
        nonlocal used
        copy = pltpu.make_async_copy(source, target, in_sem.at[used])
        copy.start()
        used += 1
        arriving[k].append(copy)

    for n in range(count):
        rows = shards[n].shape[0]
        bring(0, shards[n], held[n].at[pl.ds(pl.multiple_of(spots[0] * rows, 128), rows), :])
    for slot, k in enumerate(order):
        for c, share in enumerate(shares):
            source = parts[2 * c].at[slot] if slot < 4 else parts[2 * c + 1].at[slot - 4]
            column = 0
            for n in range(count):
                rows, columns = shards[n].shape
                if n < extra:
                    if c == 0:
                        row = pl.multiple_of(spots[k] * rows, 128)
                        bring(
                            k,
                            source.at[:, pl.ds(column, columns)],
                            held[n].at[pl.ds(row, rows), :],
                        )
                    column += columns
                    continue
                width = columns // ways
                left = pl.multiple_of(share * width, 128)
                for r in range(0, rows, 128):
                    row = pl.multiple_of(spots[k] * rows + r, 128)
                    bring(
                        k,
                        source.at[:, pl.ds(column, width)],
                        held[n].at[pl.ds(row, 128), pl.ds(left, width)],
                    )
                    column += width
    leaving = []
    for k in [0] + order:
        for copy in arriving[k]:
            copy.wait()
        for n in range(count):
            rows = shards[n].shape[0]
            span = pl.ds(pl.multiple_of(spots[k] * rows, 128), rows)
            copy = pltpu.make_async_copy(
                held[n].at[span, :], outs[n].at[span, :], out_sem.at[len(leaving)]
            )
            copy.start()
            leaving.append(copy)
    for copy in leaving:
        copy.wait()


def along_z(own, before=None):
    z = lax.axis_index("blk") // 2
    below, above = [own], [own]
    for step in range(3):
        up, down = below[-1], above[-1]
        if step == 2 and before is not None:
            up, down = tie(up, *before), tie(down, *before)
        below.append(hop(step, 2, 1)(up))
        above.append(hop(1, 3 - step, -1)(down))
    return jnp.stack([jnp.where(z + d < 4, above[d], below[4 - d]) for d in (1, 2, 3)])


def share_of(shards, ways, extra=0):
    group = lax.axis_index("items")
    index = group % 2 if ways == 2 else group
    return jnp.concatenate(
        shards[:extra] + [side_by_side(column_share(m, index, ways)) for m in shards[extra:]], axis=1
    )


def spread(shards, parts, extra=0, spots=None):
    parts = parts + [swap_core(part) for part in parts]
    ways = len(parts) // 2
    count = len(shards)
    pieces = sum(1 if n < extra else ways * shards[n].shape[0] // 128 for n in range(count))
    size = 8 * sum(m.size for m in shards)
    return pl.pallas_call(
        lambda *refs: place_kernel(count, extra, ways, *refs),
        out_shape=[jax.ShapeDtypeStruct((8 * m.shape[0], m.shape[1]), m.dtype) for m in shards],
        in_specs=[pl.BlockSpec(memory_space=pltpu.SMEM)] + [ANY] * (count + 2 * ways),
        out_specs=[ANY] * count,
        scratch_shapes=[pltpu.VMEM((8 * m.shape[0], m.shape[1]), m.dtype) for m in shards]
        + [
            pltpu.SemaphoreType.DMA((count + 7 * pieces,)),
            pltpu.SemaphoreType.DMA((8 * count,)),
        ],
        compiler_params=pltpu.CompilerParams(vmem_limit_bytes=VMEM_BYTES),
        cost_estimate=pl.CostEstimate(flops=0, bytes_accessed=4 * size, transcendentals=0),
        name="place_rows",
    )(spot_vector() if spots is None else spots, *shards, *parts)


def add_low(*terms):
    total = terms[0].astype(F32)
    for term in terms[1:]:
        total = total + term.astype(F32)
    return total.astype(BF)


class Reduce:
    def __init__(self, entries):
        group = lax.axis_index("items")
        self.y, self.core = group // 2, group % 2
        self.entries = entries
        self.shapes = []
        for entry in entries:
            rows = (entry[0] if isinstance(entry, tuple) else entry).shape[-1 if isinstance(entry, tuple) else 0]
            columns = (entry[1] if isinstance(entry, tuple) else entry).shape[1]
            self.shapes.append((rows // 8, columns))
        self.sent = [self.halves(entry, 1 - self.core) for entry in entries]
        self.got = [swap_core(v) for v in self.sent]

    def halves(self, entry, core):
        wide = entry[1] if isinstance(entry, tuple) else entry
        picked = jnp.concatenate(
            [column_share(wide, 2 * y + core) for y in (self.y, 1 - self.y)], axis=1
        )
        return dot_tn(entry[0], picked).astype(BF) if isinstance(entry, tuple) else picked

    def over_y(self):
        kept = [self.halves(entry, self.core) for entry in self.entries]

        def blocks(side):
            found = []
            for own, got in zip(kept, self.got):
                width = own.shape[1] // 2
                for left in range(side * width, (side + 1) * width, 256):
                    block = add_low(own[:, left : left + 256], got[:, left : left + 256])
                    found.append(block.reshape(8, -1, 128, 256))
            return jnp.concatenate(found, axis=1)

        self.kept, self.away = blocks(0), blocks(1)
        self.got = swap_y(self.away)
        return self.away

    def over_x(self, *before):
        me = lax.axis_index("blk")
        halves = [v.reshape((4, 2) + v.shape[1:]) for v in (self.kept, self.got)]
        away = add_low(*(lax.dynamic_index_in_dim(v, 1 - me % 2, 1, keepdims=False) for v in halves))
        if before:
            away = tie(away, *before)
        self.kept = [lax.dynamic_index_in_dim(v, me % 2, 1, keepdims=False) for v in halves]
        self.got = swap_x(away)
        return away

    def over_z(self, *before):
        z = lax.axis_index("blk") // 2
        kept = add_low(*self.kept, self.got)
        if before:
            kept = tie(kept, *before)

        def part(place):
            return lax.dynamic_index_in_dim(kept, jnp.clip(place, 0, 3), 0, keepdims=False)

        up = hop(0, 0, 1)(part(z + 3))
        down = hop(3, 3, -1)(part(z - 3))
        up = hop(0, 1, 1)(add_low(part(z + 2), up))
        down = hop(2, 3, -1)(add_low(part(z - 2), down))
        up = hop(0, 2, 1)(add_low(part(z + 1), up))
        down = hop(1, 3, -1)(add_low(part(z - 1), down))
        self.done = add_low(part(z), up, down)
        return self.done

    def share(self):
        mine = jnp.stack([self.done, swap_y(self.done)])
        every = jnp.concatenate([mine, swap_core(mine)]).astype(F32)
        ordered = [
            lax.dynamic_index_in_dim(
                every, 2 * ((q % 2) ^ self.core) + ((q // 2) ^ self.y), 0, keepdims=False
            )
            for q in range(4)
        ]
        results, first = [], 0
        for rows, columns in self.shapes:
            count = rows // 128
            strips = []
            for quarter in ordered:
                for block in range(columns // 1024):
                    place = first + block * count
                    strips.append(quarter[place : place + count].reshape(rows, 256))
            results.append(jnp.concatenate(strips, axis=1))
            first += count * (columns // 1024)
        return results


def dot_nt(left, right):
    return lax.dot_general(left, right, (((1,), (1,)), ((), ())), preferred_element_type=F32)


def dot_tn(left, right):
    return lax.dot_general(left, right, (((0,), (0,)), ((), ())), preferred_element_type=F32)


def dot_nn(left, right):
    return lax.dot_general(left, right, (((1,), (0,)), ((), ())), preferred_element_type=F32)


def two_heads(value):
    lane = lax.broadcasted_iota(jnp.int32, value.shape, 1)
    zero = jnp.zeros_like(value)
    return jnp.concatenate(
        [jnp.where(lane < 64, value, zero), jnp.where(lane < 64, zero, value)], axis=0
    )


def one_pair(turned):
    count = turned.shape[1] // 2
    joined = jnp.concatenate([turned[:64, :count], turned[64:, count:]], axis=0)
    return joined.T


def pair_forward(query, keys, values, masks):
    stacked = two_heads(query)
    scores = [mask(dot_nt(k, stacked)) for k, mask in zip(keys, masks)]
    top = scores[0].max(axis=0, keepdims=True)
    for s in scores[1:]:
        top = jnp.maximum(top, s.max(axis=0, keepdims=True))
    total, turned = None, None
    for s, v in zip(scores, values):
        weight = jnp.exp(s - top)
        add = weight.sum(axis=0, keepdims=True)
        product = dot_tn(v, weight.astype(BF))
        total = add if total is None else total + add
        turned = product if turned is None else turned + product
    return one_pair(turned * (1.0 / total)).astype(BF), top + jnp.log(total)


def pair_backward(query, incoming, keys, values, masks, log_total):
    stacked, grads = two_heads(query), two_heads(incoming)
    weights, changes, centre = [], [], None
    for k, v, mask in zip(keys, values, masks):
        weight = jnp.exp(mask(dot_nt(k, stacked)) - log_total)
        change = dot_nt(v, grads)
        add = (weight * change).sum(axis=0, keepdims=True)
        centre = add if centre is None else centre + add
        weights.append(weight)
        changes.append(change)
    key_grads, value_grads, turned = [], [], None
    for k, weight, change in zip(keys, weights, changes):
        score_grad = (weight * (change - centre)).astype(BF)
        key_grads.append(dot_nn(score_grad, stacked).astype(BF))
        value_grads.append(dot_nn(weight.astype(BF), grads).astype(BF))
        product = dot_tn(k, score_grad)
        turned = product if turned is None else turned + product
    return one_pair(turned).astype(BF), key_grads, value_grads


def slot_masks(length, rows, columns):
    slot = lax.broadcasted_iota(jnp.int32, (rows, columns), 0)
    return [
        (lambda s, c=c: jnp.where(slot < length - c * rows, s, -1e30)) for c in range(CHUNKS)
    ]


PAIRS = 4


def cross_parts(kv_ref, p):
    rows = kv_ref.shape[0] // CHUNKS
    left = 256 * p
    keys = [kv_ref[rows * c : rows * (c + 1), left : left + 128] for c in range(CHUNKS)]
    values = [kv_ref[rows * c : rows * (c + 1), left + 128 : left + 256] for c in range(CHUNKS)]
    return keys, values


def cross_forward_kernel(lengths, q_ref, m_ref, w_ref, shift_ref, out_ref, log_ref, kv_ref):
    kv_ref[...] = (dot_nn(m_ref[...], w_ref[...]) + shift_ref[...]).astype(BF)
    masks = slot_masks(lengths[0], kv_ref.shape[0] // CHUNKS, 2 * q_ref.shape[0])
    for p in range(PAIRS):
        keys, values = cross_parts(kv_ref, p)
        out, log_total = pair_forward(q_ref[:, 128 * p : 128 * p + 128], keys, values, masks)
        out_ref[:, 128 * p : 128 * p + 128] = out
        log_ref[p] = log_total


def cross_backward_kernel(
    lengths, q_ref, grad_ref, log_ref, kv_ref, w_ref, dq_ref, sum_ref, dkv_ref, back_ref, total_ref
):
    step = pl.program_id(0)
    rows = kv_ref.shape[0] // CHUNKS
    masks = slot_masks(lengths[0], rows, 2 * q_ref.shape[0])
    for p in range(PAIRS):
        span = slice(128 * p, 128 * p + 128)
        keys, values = cross_parts(kv_ref, p)
        dq, dks, dvs = pair_backward(
            q_ref[:, span], grad_ref[:, span], keys, values, masks, log_ref[p]
        )
        dq_ref[:, span] = dq
        total = None
        for c in range(CHUNKS):
            dkv_ref[rows * c : rows * (c + 1), 256 * p : 256 * p + 128] = dks[c]
            dkv_ref[rows * c : rows * (c + 1), 256 * p + 128 : 256 * p + 256] = dvs[c]
            add = dvs[c].astype(F32).sum(axis=0, keepdims=True)
            total = add if total is None else total + add
        sum_ref[:, span] = total
    back = dot_nt(dkv_ref[...], w_ref[...])

    @pl.when(step == 0)
    def _():
        total_ref[...] = back

    @pl.when(step > 0)
    def _():
        total_ref[...] += back

    @pl.when(step == pl.num_programs(0) - 1)
    def _():
        back_ref[...] = total_ref[...].astype(BF)


def cross_specs(length, slots, width):
    small = pl.BlockSpec((length, 128 * PAIRS), lambda p, *_: (0, p))
    line = pl.BlockSpec((1, 128 * PAIRS), lambda p, *_: (0, p))
    big = pl.BlockSpec((slots, 256 * PAIRS), lambda p, *_: (0, p))
    logs = pl.BlockSpec((PAIRS, 1, 2 * length), lambda p, *_: (p, 0, 0))
    whole = pl.BlockSpec((slots, width), lambda p, *_: (0, 0))
    weight = pl.BlockSpec((width, 256 * PAIRS), lambda p, *_: (0, p))
    shift = pl.BlockSpec((1, 256 * PAIRS), lambda p, *_: (0, p))
    return small, line, big, logs, whole, weight, shift


def cross_forward(lengths, queries, source, weight_pair, pair_shift):
    length, width = queries.shape
    slots = source.shape[0]
    small, _, big, logs, whole, weight, shift = cross_specs(length, slots, width)
    return pl.pallas_call(
        cross_forward_kernel,
        out_shape=[
            jax.ShapeDtypeStruct(queries.shape, BF),
            jax.ShapeDtypeStruct((width // 128, 1, 2 * length), F32),
            jax.ShapeDtypeStruct((slots, 2 * width), BF),
        ],
        grid_spec=pltpu.PrefetchScalarGridSpec(
            num_scalar_prefetch=1,
            grid=(width // (128 * PAIRS),),
            in_specs=[small, whole, weight, shift],
            out_specs=[small, logs, big],
        ),
        compiler_params=pltpu.CompilerParams(vmem_limit_bytes=VMEM_BYTES),
        cost_estimate=pl.CostEstimate(
            flops=4 * slots * width * width + 16 * length * slots * width,
            bytes_accessed=2 * (source.size + weight_pair.size + 2 * source.size),
            transcendentals=length * slots * HEADS,
        ),
        name="cross_forward",
    )(lengths, queries, source, weight_pair, pair_shift)


def cross_backward(lengths, queries, grads, logs_in, kv, weight_pair):
    length, width = queries.shape
    slots = kv.shape[0]
    small, line, big, logs, whole, weight, _ = cross_specs(length, slots, width)
    return pl.pallas_call(
        cross_backward_kernel,
        out_shape=[
            jax.ShapeDtypeStruct(queries.shape, BF),
            jax.ShapeDtypeStruct((1, width), F32),
            jax.ShapeDtypeStruct(kv.shape, BF),
            jax.ShapeDtypeStruct((slots, width), BF),
        ],
        grid_spec=pltpu.PrefetchScalarGridSpec(
            num_scalar_prefetch=1,
            grid=(width // (128 * PAIRS),),
            in_specs=[small, small, logs, big, weight],
            out_specs=[small, line, big, whole],
            scratch_shapes=[pltpu.VMEM((slots, width), F32)],
        ),
        compiler_params=pltpu.CompilerParams(vmem_limit_bytes=VMEM_BYTES),
        cost_estimate=pl.CostEstimate(
            flops=4 * slots * width * width + 40 * length * slots * width,
            bytes_accessed=2 * (4 * slots * width + 3 * slots * width + weight_pair.size),
            transcendentals=length * slots * HEADS,
        ),
        name="cross_backward",
    )(lengths, queries, grads, logs_in, kv, weight_pair)


def self_mask(seg_row, seg_column, length):
    key = lax.broadcasted_iota(jnp.int32, (length, length), 0)
    query = lax.broadcasted_iota(jnp.int32, (length, length), 1)
    allowed = jnp.where((seg_column == seg_row) & (key <= query), 1.0, 0.0)
    allowed = jnp.concatenate([allowed, allowed], axis=1)
    return lambda s: jnp.where(allowed > 0.5, s, -1e30)


def self_forward_kernel(seg_row, seg_column, qkv_ref, out_ref, log_ref):
    length, width = out_ref.shape[1:]
    mask = self_mask(seg_row[0], seg_column[0], length)
    for p in range(width // 128):
        span = slice(128 * p, 128 * p + 128)
        query = qkv_ref[0, :, span]
        key = qkv_ref[0, :, width + 128 * p : width + 128 * p + 128]
        value = qkv_ref[0, :, 2 * width + 128 * p : 2 * width + 128 * p + 128]
        out, log_total = pair_forward(query, [key], [value], [mask])
        out_ref[0, :, span] = out
        log_ref[0, p] = log_total


def self_backward_kernel(seg_row, seg_column, qkv_ref, grad_ref, log_ref, out_ref):
    length, width = grad_ref.shape[1:]
    mask = self_mask(seg_row[0], seg_column[0], length)
    for p in range(width // 128):
        span = slice(128 * p, 128 * p + 128)
        key_span = slice(width + 128 * p, width + 128 * p + 128)
        value_span = slice(2 * width + 128 * p, 2 * width + 128 * p + 128)
        dq, dk, dv = pair_backward(
            qkv_ref[0, :, span],
            grad_ref[0, :, span],
            [qkv_ref[0, :, key_span]],
            [qkv_ref[0, :, value_span]],
            [mask],
            log_ref[0, p],
        )
        out_ref[0, :, span] = dq * BF(0.125)
        out_ref[0, :, key_span] = dk[0]
        out_ref[0, :, value_span] = dv[0]


def self_specs(items, length, width):
    rows = pl.BlockSpec((1, 1, length), lambda i: (i, 0, 0))
    columns = pl.BlockSpec((1, length, 1), lambda i: (i, 0, 0))
    wide = pl.BlockSpec((1, length, 3 * width), lambda i: (i, 0, 0))
    slim = pl.BlockSpec((1, length, width), lambda i: (i, 0, 0))
    logs = pl.BlockSpec((1, width // 128, 1, 2 * length), lambda i: (i, 0, 0, 0))
    return rows, columns, wide, slim, logs


def self_forward(segments, qkv):
    items, length, width = qkv.shape[0], qkv.shape[1], qkv.shape[2] // 3
    rows, columns, wide, slim, logs = self_specs(items, length, width)
    return pl.pallas_call(
        self_forward_kernel,
        grid=(items,),
        out_shape=[
            jax.ShapeDtypeStruct((items, length, width), BF),
            jax.ShapeDtypeStruct((items, width // 128, 1, 2 * length), F32),
        ],
        in_specs=[rows, columns, wide],
        out_specs=[slim, logs],
        compiler_params=pltpu.CompilerParams(vmem_limit_bytes=VMEM_BYTES),
        name="self_forward",
    )(segments[:, None, :], segments[:, :, None], qkv)


def self_backward(segments, qkv, grads, logs_in):
    items, length, width = grads.shape
    rows, columns, wide, slim, logs = self_specs(items, length, width)
    return pl.pallas_call(
        self_backward_kernel,
        grid=(items,),
        out_shape=jax.ShapeDtypeStruct(qkv.shape, BF),
        in_specs=[rows, columns, wide, slim, logs],
        out_specs=wide,
        compiler_params=pltpu.CompilerParams(vmem_limit_bytes=VMEM_BYTES),
        name="self_backward",
    )(segments[:, None, :], segments[:, :, None], qkv, grads, logs_in)


def layer_norm(values, gain, shift):
    centre = values - jnp.mean(values, axis=-1, keepdims=True)
    spread = jnp.mean(centre * centre, axis=-1, keepdims=True)
    return centre * lax.rsqrt(spread + 1e-05) * gain + shift


def gelu_and_slope(values):
    spread = jnp.exp(-0.5 * values * values)
    t = 1.0 / (1.0 + (0.3275911 * 2.0**-0.5) * jnp.abs(values))
    tail = 1.421413741 + t * (-1.453152027 + t * 1.061405429)
    tail = 0.5 * spread * (t * (0.254829592 + t * (-0.284496736 + t * tail)))
    cdf = jnp.where(values < 0.0, tail, 1.0 - tail)
    return values * cdf, cdf + values * spread * (2.0 * jnp.pi) ** -0.5


def back_and_forth(blocks):
    return lax.all_to_all(blocks, "blk", split_axis=0, concat_axis=0, tiled=True)


def column_part(matrix, index, width):
    return lax.dynamic_slice_in_dim(matrix, index * width, width, 1)


def column_sum(values):
    return jnp.sum(values.astype(F32), axis=0)


def interleave(matrix):
    rows, columns = matrix.shape
    return matrix.reshape(rows, 2, columns // 256, 128).swapaxes(1, 2).reshape(rows, columns)


def part_again(matrix):
    rows, columns = matrix.shape
    return matrix.reshape(rows, columns // 256, 2, 128).swapaxes(1, 2).reshape(rows, columns)


def pack_small(shifts, gains, bias):
    width = shifts.shape[1]
    rows = jnp.concatenate([shifts, gains, bias.reshape(-1, width)], axis=0)
    return jnp.pad(rows, ((0, 128 - rows.shape[0]), (0, 0)))


def unpack_small(rows, width):
    rows = rows.reshape(-1, 128, width)
    shifts = rows[:, :10].transpose(1, 0, 2).reshape(10, -1)
    gains = rows[:, 10:13].transpose(1, 0, 2).reshape(3, -1)
    return shifts, gains, rows[:, 13:17].reshape(-1)


def per_device(tuned):
    def run(
        decoder_in,
        memory,
        segment_ids,
        memory_lengths,
        w_self_in,
        w_self_out,
        w_cross_query,
        w_cross_pair,
        w_cross_out,
        w_feed_up,
        w_feed_down,
        shifts,
        norm_gains,
        feed_bias,
        out_grad,
    ):
        item_count, length, width = decoder_in.shape
        row_count = item_count * length
        pair_shard = interleave(w_cross_pair)
        blocks = memory.reshape((-1, item_count) + memory.shape[1:])
        sent = [blocks[:, i] for i in range(item_count)]
        half = item_count // 2
        if tuned:
            small = pack_small(shifts, norm_gains, feed_bias)
            first = [small, w_self_in, w_self_out, w_cross_query, pair_shard]
            second = [w_cross_out, w_feed_up, w_feed_down]
            own, own_two = share_of(first, 4, 1), share_of(second, 4)
            across, across_two = swap_x(own), swap_x(own_two)
            across_y, across_two_y = swap_y(across), swap_y(across_two)
            line = along_z(own)
            own_two = tie(own_two, line, across, across_two)
            far, line_y = swap_x(line), swap_y(line)
            line_two = along_z(own_two, (far, across_y, across_two_y))
            pair = tie(jnp.stack(sent[:half], axis=1), line_two, line_y)
            pair = back_and_forth(pair)
            arrived = [pair[:, i] for i in range(half)]
            far_two, line_two_y = swap_x(line_two), swap_y(line_two)

            def near(piece, pieces):
                return jnp.concatenate([piece[None], pieces])

            small, self_proj, self_out, cross_query, cross_pair = spread(
                first, [near(across, line), far, near(across_y, line_y), swap_y(far)], 1
            )
            shift_low, gain_low, feed_shift_low = unpack_small(small, shifts.shape[1])
        else:
            def whole(shard, axis=0):
                return lax.all_gather(shard, "blk", axis=axis, tiled=True)

            shift_low, gain_low = whole(shifts, 1), whole(norm_gains, 1)
            feed_shift_low = whole(feed_bias)
            self_proj, self_out, cross_query = whole(w_self_in), whole(w_self_out), whole(w_cross_query)
            cross_pair, cross_out = whole(pair_shard), whole(w_cross_out)
            feed_up, feed_down = whole(w_feed_up), whole(w_feed_down)
            arrived = [back_and_forth(v) for v in sent]
        shift_rows = shift_low.astype(F32)
        gain_rows = gain_low.astype(F32)
        feed_shift = feed_shift_low.astype(F32)
        query_scale = (width // HEADS) ** (-0.5)
        three = (item_count, length, width)

        token_rows = decoder_in.reshape(row_count, width)
        no_shift = jnp.zeros((width,), F32)
        in_shift = jnp.concatenate([shift_rows[0], no_shift, shift_rows[1]])
        in_scale = jnp.concatenate([no_shift + query_scale, no_shift + 1.0, no_shift + 1.0])
        qkv = (
            (jnp.dot(token_rows, self_proj, preferred_element_type=F32) + in_shift) * in_scale
        ).astype(BF).reshape(item_count, length, 3 * width)
        attended, self_logs = self_forward(segment_ids, qkv)
        attended = attended.reshape(row_count, width)
        branch = jnp.dot(attended, self_out, preferred_element_type=F32) + shift_rows[2]
        hidden, first_norm_back = jax.vjp(
            layer_norm, token_rows.astype(F32) + branch, gain_rows[0], shift_rows[7]
        )
        hidden_low = hidden.astype(BF)

        cross_queries = (
            (jnp.dot(hidden_low, cross_query, preferred_element_type=F32) + shift_rows[3])
            * query_scale
        ).astype(BF).reshape(three)
        pair_shift = interleave(jnp.concatenate([no_shift, shift_rows[4]])[None])
        item_lengths = [memory_lengths[i : i + 1] for i in range(item_count)]
        sources, kvs, outs, cross_logs = [], [], [], []
        if tuned:
            far_two = tie(far_two, cross_queries)
            far_two_y = swap_y(far_two)
        for i in range(item_count):
            if tuned and i == half:
                arrived.append(back_and_forth(tie(sent[i], cross_queries, far_two, line_two_y)))
            elif tuned and i > half:
                arrived.append(
                    back_and_forth(tie(sent[i], *arrived[half:], outs[0], far_two_y))
                )
            source = arrived[i]
            if tuned and i == item_count - 1:
                parts = [near(across_two, line_two), far_two, near(across_two_y, line_two_y), far_two_y]
                cross_out, feed_up, feed_down = spread(
                    second, parts, spots=tie(spot_vector(), outs[i - 1])
                )
                source = tie(source, outs[i - 1], feed_up)
            source = source.reshape(-1, width)
            out, logs, kv = cross_forward(
                item_lengths[i], cross_queries[i], source, cross_pair, pair_shift
            )
            sources.append(source)
            kvs.append(kv)
            outs.append(out)
            cross_logs.append(logs)
        cross_attended = jnp.concatenate(outs)
        cross_branch = jnp.dot(cross_attended, cross_out, preferred_element_type=F32) + shift_rows[5]
        second, second_norm_back = jax.vjp(
            layer_norm, hidden + cross_branch, gain_rows[1], shift_rows[8]
        )
        second_low = second.astype(BF)

        upward = jnp.dot(second_low, feed_up, preferred_element_type=F32) + feed_shift
        activation, slope = gelu_and_slope(upward)
        activation_low, slope = activation.astype(BF), slope.astype(BF)
        feed_branch = jnp.dot(activation_low, feed_down, preferred_element_type=F32) + shift_rows[6]
        block_out, third_norm_back = jax.vjp(
            layer_norm, second + feed_branch, gain_rows[2], shift_rows[9]
        )

        third_grad, third_gain, third_shift = third_norm_back(
            out_grad.astype(F32).reshape(row_count, width)
        )
        down_low = third_grad.astype(BF)
        grad_down = dot_tn(activation_low, down_low)
        upward_low = (dot_nt(down_low, feed_down) * slope.astype(F32)).astype(BF)
        grad_up = dot_tn(second_low, upward_low)
        second_grad = third_grad + dot_nt(upward_low, feed_up)
        cross_grad, second_gain, second_shift = second_norm_back(second_grad)
        cross_low = cross_grad.astype(BF)
        grad_cross_out = dot_tn(cross_attended, cross_low)
        if tuned:
            sums_one = Reduce(
                [(activation_low, down_low), (second_low, upward_low), (cross_attended, cross_low)]
            )
        cross_incoming = dot_nt(cross_low, cross_out).astype(BF).reshape(three)
        if tuned:
            cross_incoming = tie(cross_incoming, *sums_one.sent)
        dqs, value_sums, grad_pair, pair_grads, memory_back, backs = [], 0.0, 0.0, [], [], []
        before = None
        for i in range(item_count):
            incoming = cross_incoming[i] if before is None else tie(cross_incoming[i], before)
            if tuned and i == 1:
                incoming = tie(incoming, sums_one.over_y())
            dq, sums, pair_grad, before = cross_backward(
                item_lengths[i], cross_queries[i], incoming, cross_logs[i], kvs[i], cross_pair
            )
            backs.append(before.reshape(arrived[i].shape))
            if len(backs) == half:
                memory_back.append(back_and_forth(jnp.stack(backs, axis=1)))
                backs = []
            value_sums = value_sums + sums[0]
            pair_grads.append(pair_grad)
            dqs.append(dq)
        cross_dq = tie(jnp.concatenate(dqs), before)
        memory_grad = jnp.concatenate(memory_back, axis=1).reshape(memory.shape)
        cross_query_low = cross_dq * BF(query_scale)
        grad_cross_query = dot_tn(hidden_low, cross_query_low)
        hidden_grad = cross_grad + dot_nt(cross_query_low, cross_query)
        first_grad, first_gain, first_shift = first_norm_back(hidden_grad)
        self_low = first_grad.astype(BF)
        grad_self_out = dot_tn(attended, self_low)
        self_incoming = dot_nt(self_low, self_out).astype(BF).reshape(three)
        joined_grad = self_backward(segment_ids, qkv, self_incoming, self_logs)
        joined_grad = joined_grad.reshape(row_count, 3 * width)
        if tuned:
            joined_grad = tie(joined_grad, sums_one.got, memory_back[0])
        grad_self = dot_tn(token_rows, joined_grad)
        decoder_grad = (
            (first_grad + dot_nt(joined_grad, self_proj)).astype(BF).reshape(decoder_in.shape)
        )
        joined_sums = column_sum(joined_grad)
        grad_shift_rows = jnp.stack(
            [
                joined_sums[:width],
                joined_sums[2 * width :],
                column_sum(self_low),
                column_sum(cross_query_low),
                value_sums,
                column_sum(cross_low),
                column_sum(down_low),
                first_shift,
                second_shift,
                third_shift,
            ]
        )
        grad_gain_rows = jnp.stack([first_gain, second_gain, third_gain])
        grad_feed_shift = column_sum(upward_low)
        block_low = block_out.astype(BF).reshape(decoder_in.shape)
        if tuned:
            count = shifts.shape[1]
            packed = jnp.concatenate(
                [
                    grad_shift_rows.reshape(10, 8, count),
                    grad_gain_rows.reshape(3, 8, count),
                    grad_feed_shift.reshape(8, -1, count).swapaxes(0, 1),
                ],
                axis=0,
            ).swapaxes(0, 1)
            packed = jnp.pad(packed, ((0, 0), (0, 128 - packed.shape[1]), (0, 7 * count)))
            sums_three = Reduce(
                [
                    (attended, self_low),
                    (token_rows, joined_grad),
                    packed.reshape(-1, 8 * count).astype(BF),
                ]
            )
            pair_grads[0] = tie(pair_grads[0], *sums_three.sent)
            away = sums_three.over_y()
            for i in range(1, item_count):
                pair_grads[i] = tie(pair_grads[i], away)
            sums_one.over_x(joined_grad)
            for source, pair_grad in zip(sources, pair_grads):
                grad_pair = grad_pair + dot_tn(source, pair_grad)
            sums_two = Reduce(
                [(hidden_low, cross_query_low), tie(grad_pair.astype(BF), sums_one.got)]
            )
            sums_two.over_y()
            sums_one.over_z(sums_two.away)
            sums_three.over_x(sums_two.away)
            sums_two.over_x()
            sums_three.over_z()
            sums_two.over_z()
            down, up, out = sums_one.share()
            (query, pair) = sums_two.share()
            (own_out, own_in, sums) = sums_three.share()
            shift_share, gain_share = sums[:10, :count], sums[10:13, :count]
            feed_share = sums[13:17, :count].reshape(-1)
        else:
            for source, pair_grad in zip(sources, pair_grads):
                grad_pair = grad_pair + dot_tn(source, pair_grad)

            def share(value, dim=0):
                part = lax.psum_scatter(value, "blk", scatter_dimension=dim, tiled=True)
                return lax.psum(part.astype(BF), "items").astype(F32)

            large = [grad_down, grad_up, grad_cross_out, grad_cross_query, grad_pair, grad_self_out, grad_self]
            down, up, out, query, pair, own_out, own_in = [share(grad) for grad in large]
            shift_share, gain_share = share(grad_shift_rows, 1), share(grad_gain_rows, 1)
            feed_share = share(grad_feed_shift)
        return (
            block_low,
            decoder_grad,
            memory_grad,
            own_in,
            own_out,
            query,
            part_again(pair),
            out,
            up,
            down,
            shift_share,
            gain_share,
            feed_share,
        )

    return run


def solution(mesh):
    in_specs = (
        P(("items", "blk"), None, None),
        P("items", "blk", None),
        P(("items", "blk"), None),
        P(("items", "blk")),
        P("blk", None),
        P("blk", None),
        P("blk", None),
        P("blk", None),
        P("blk", None),
        P("blk", None),
        P("blk", None),
        P(None, "blk"),
        P(None, "blk"),
        P("blk"),
        P(("items", "blk"), None, None),
    )
    out_specs = (
        P(("items", "blk"), None, None),
        P(("items", "blk"), None, None),
        P("items", "blk", None),
        P("blk", None),
        P("blk", None),
        P("blk", None),
        P("blk", None),
        P("blk", None),
        P("blk", None),
        P("blk", None),
        P(None, "blk"),
        P(None, "blk"),
        P("blk"),
    )
    tuned = mesh.shape["blk"] == 8 and mesh.shape["items"] == 4
    return jax.shard_map(
        per_device(tuned), mesh=mesh, in_specs=in_specs, out_specs=out_specs, check_vma=False
    )
```

time: 1250 us -> 904 us (0.72)
  waiting for transfers between devices: 502 us -> 227 us
  starting transfers between devices: 286 us -> 146 us
  Pallas kernels: 121 us -> 175 us
  matrix products: 184 us -> 140 us
  other arithmetic: 60.5 us -> 96.7 us
  local copies, waits for them, and re-layouts: 80.6 us -> 104 us
    ppermute x168 -> x68, waiting for transfers between devices: 502 us -> 219 us  [move(): return lambda value: lax.ppermute(value, axis, pairs)]
    ppermute x168 -> x68, starting transfers between devices: 286 us -> 115 us  [move(): return lambda value: lax.ppermute(value, axis, pairs)]
    pallas_call x1 -> x4, Pallas kernels: 38.5 us -> 71.5 us  [cross_backward(): pl.pallas_call(cross_backward_kernel, out_shape=[jax.ShapeDtypeStruct(que...]
    pallas_call x1 -> x4, Pallas kernels: 26.5 us -> 58.1 us  [cross_forward(): pl.pallas_call(cross_forward_kernel, out_shape=[jax.ShapeDtypeStruct(quer...]
    all_to_all x0 -> x5, starting transfers between devices: none -> 31 us  [back_and_forth(): lax.all_to_all(blocks, 'blk', split_axis=0, concat_axis=0, tiled=True)]
    concatenate x1 -> x14, other arithmetic: 0.77 us -> 28.3 us  [the longest x4 10.9 us: near(): return jnp.concatenate([piece[None], pieces])]
    dot_general x1 -> x0, matrix products: 23.6 us -> none  [run(): jnp.dot(source_rows, cross_pair, preferred_element_type=F32) + pair_shift]
    dot_general x7 -> x6, matrix products: 59.8 us -> 36.7 us  [dot_nt(): lax.dot_general(left, right, (((1,), (1,)), ((), ())), preferred_element_...]
  transfers between devices with their start and end apart: 168 -> 73, of which waited for: 60 -> 21; matrix products, arithmetic and copies ran while one was open for 12% -> 27% of each run, Pallas kernels for 5% -> 16%
where the time goes in v2:
time: 904 us; the launch traced here: 892 us
  waiting for transfers between devices  227 us (25%)
  Pallas kernels  175 us (19%)
  starting transfers between devices  146 us (16%)
  matrix products  140 us (15%)
  local copies, waits for them, and re-layouts  104 us (12%)
  other arithmetic  96.7 us (11%)
    ppermute x68, waiting for transfers between devices, move(): return lambda value: lax.ppermute(value, axis, pairs)  219 us
    ppermute x68, starting transfers between devices, move(): return lambda value: lax.ppermute(value, axis, pairs)  115 us
    pallas_call x4, Pallas kernels, cross_backward(): pl.pallas_call(cross_backward_kernel, out_shape=[jax.ShapeDtypeStruct(que...  71.5 us
    dot_general x16, matrix products, dot_tn(): lax.dot_general(left, right, (((0,), (0,)), ((), ())), preferred_element_...  69.8 us
    pallas_call x4, Pallas kernels, cross_forward(): pl.pallas_call(cross_forward_kernel, out_shape=[jax.ShapeDtypeStruct(quer...  58.1 us
    unnamed x268, local copies, waits for them, and re-layouts  50.3 us
    convert_element_type x26, other arithmetic, add_low(): return total.astype(BF)  41.6 us
    dot_general x6, matrix products, dot_nt(): lax.dot_general(left, right, (((1,), (1,)), ((), ())), preferred_element_...  36.7 us
  transfers between devices with their start and end apart: 73, of which 21 were waited for; matrix products, arithmetic and copies ran while one was open for 27% of the time, Pallas kernels for 16%

profile of v2, /device:TPU:1, one launch (start us, length us, event | category | flops | bytes accessed | tf_op | source)
XLA Modules:
  0.0 892.2 jit_solution(18140137251964054443)
XLA Ops:
  9.9 4.7 collective-permute-start.2
  16.1 7.8 collective-permute-done.1
  41.5 8.3 collective-permute-done.6
  54.1 5.2 collective-permute-start.17
  59.8 5.4 collective-permute-done.16
  67.7 4.8 stack.183
  72.5 8.1 collective-permute-done.8
  86.9 9.2 %collective-permute-done.22 = bf16[128,2304]{1,0:T(8,128)(2,1)S(1)} collective-permute-done((bf16[128,2304]{1,0:T(8,128)(2,1)S(1)}, bf16[128,2304]{1,0:T(8,128)(2,1)S(1)}, u32[]{:S(2)}, u32[]{:S(2)}) %collective-permute-start.22) | collective-permute-done | bytes 589856 | tf_op jit(solution)/shard_map/ppermute | solution.py:16
  98.5 13.0 %collective-permute-done.9 = bf16[3,128,1920]{2,1,0:T(8,128)(2,1)} collective-permute-done((bf16[3,128,1920]{2,1,0:T(8,128)(2,1)S(1)}, bf16[3,128,1920]{2,1,0:T(8,128)(2,1)}, u32[]{:S(2)}, u32[]{:S(2)}) %collective-permute-start.9) | collective-permute-done | bytes 1474592 | tf_op jit(solution)/shard_map/ppermute | solution.py:16
  111.5 4.9 all-to-all-start
  118.7 11.3 %collective-permute-start.11 = (bf16[4,128,1920]{2,1,0:T(8,128)(2,1)S(1)}, bf16[4,128,1920]{2,1,0:T(8,128)(2,1)}, u32[]{:S(2)}, u32[]{:S(2)}) collective-permute-start(bf16[4,128,1920]{2,1,0:T(8,128)(2,1)S(1)} %pad_maximum_fusion.7.refs_6_), channel_id=1, source_target_pairs={{0,8},{8,0},{16,24},{24,16},{1,9},{9,1},{17,25},{25,17},{2,10},{10... | collective-permute-start | bytes 5898248 | tf_op jit(solution)/shard_map/ppermute | solution.py:16
  133.6 6.9 collective-permute-done.10.refs_9_
  140.5 11.0 %collective-permute-start.14 = (bf16[3,128,1920]{2,1,0:T(8,128)(2,1)}, bf16[3,128,1920]{2,1,0:T(8,128)(2,1)}, u32[]{:S(2)}, u32[]{:S(2)}) collective-permute-start(bf16[3,128,1920]{2,1,0:T(8,128)(2,1)} %collective-permute-done.10.refs_9_), channel_id=1, source_target_pairs={{0,8},{8,0},{16,24},{24,16},{1,9},{9,1},{17,25},{25,17},{2,10},{10... | collective-permute-start | bytes 4423688 | tf_op jit(solution)/shard_map/ppermute | solution.py:16
  153.0 5.0 slice_bitcast_fusion
  159.9 12.9 %place_rows.2 = (bf16[1024,128]{1,0:T(8,128)(2,1)}, bf16[1024,3072]{1,0:T(8,128)(2,1)}, bf16[1024,1024]{1,0:T(8,128)(2,1)}, bf16[1024,1024]{1,0:T(8,128)(2,1)}, bf16[1024,2048]{1,0:T(8,128)(2,1)}) custom-call(s32[10]{0:T(128)} %stack.151.refs_0_, bf16[128,128]{1,0:T(8,128)(2,1)} %get-tuple-element.285.refs_1_, bf16[128,3072]{1,0:T(8,128)(2,1)} %refs_2_.2, ...), custom_call_target="tpu_custom_call" | custom-call | bytes 29884416 | tf_op jit(solution)/shard_map/place_rows/pallas_call | solution.py:148
  173.7 7.6 multiply_convert_fusion.2
  181.3 6.0 self_forward.1
  195.3 15.9 %collective-permute-done.23.refs_5_ = bf16[3,128,2304]{2,1,0:T(8,128)(2,1)} collective-permute-done((bf16[3,128,2304]{2,1,0:T(8,128)(2,1)S(1)}, bf16[3,128,2304]{2,1,0:T(8,128)(2,1)}, u32[]{:S(2)}, u32[]{:S(2)}) %collective-permute-start.23) | collective-permute-done | bytes 1769504 | tf_op jit(solution)/shard_map/ppermute | solution.py:16
  212.5 9.9 %all-to-all-start.1 = ((bf16[8,128,1024]{2,1,0:T(8,128)(2,1)}), bf16[8,128,1024]{2,1,0:T(8,128)(2,1)}, u32[]{:S(2)}, u32[]{:S(2)}) async-start(bf16[8,128,1024]{2,1,0:T(8,128)(2,1)} %get-tuple-element.88), calls=%async_computation.1 | async-start | bytes 4194304 | tf_op jit(solution)/shard_map/all_to_all | solution.py:546
  228.8 4.8 fusion.105
  233.6 14.5 %cross_forward.4 = (bf16[128,1024]{1,0:T(8,128)(2,1)}, f32[8,1,256]{2,1,0:T(1,128)}, bf16[1024,2048]{1,0:T(8,128)(2,1)}) custom-call(s32[1]{0:T(128)} %get-tuple-element.288.lengths, bf16[128,1024]{1,0:T(8,128)(2,1)} %get-tuple-element.264.q_ref, bf16[1024,1024]{1,0:T(8,128)(2,1)} %bitcast.557, bf16[1024,2048]{1,0:T(8,128)(2,1)} %get-tuple-element.84.w_ref, ...), custom_call_target="tpu_custom_call" | custom-call | flops 6442450944 | bytes 10485760 | tf_op jit(solution)/shard_map/cross_forward/pallas_call | solution.py:397
  248.1 14.5 %collective-permute-done.25.refs_7_ = bf16[3,128,2304]{2,1,0:T(8,128)(2,1)} collective-permute-done((bf16[3,128,2304]{2,1,0:T(8,128)(2,1)}, bf16[3,128,2304]{2,1,0:T(8,128)(2,1)}, u32[]{:S(2)}, u32[]{:S(2)}) %collective-permute-start.25) | collective-permute-done | bytes 1769504 | tf_op jit(solution)/shard_map/ppermute | solution.py:16
  262.6 7.3 all-to-all-done.1
  269.8 5.0 all-to-all-start.2
  280.8 14.5 %cross_forward.6 = (bf16[128,1024]{1,0:T(8,128)(2,1)}, f32[8,1,256]{2,1,0:T(1,128)}, bf16[1024,2048]{1,0:T(8,128)(2,1)}) custom-call(s32[1]{0:T(128)} %get-tuple-element.289.lengths, bf16[128,1024]{1,0:T(8,128)(2,1)} %get-tuple-element.262.q_ref, bf16[1024,1024]{1,0:T(8,128)(2,1)} %bitcast.44.m_ref, bf16[1024,2048]{1,0:T(8,128)(2,1)} %get-tuple-element.84.w_ref, ...), custom_call_target="tpu_custom_call" | custom-call | flops 6442450944 | bytes 10485760 | tf_op jit(solution)/shard_map/cross_forward/pallas_call | solution.py:397
  295.3 16.1 %place_rows.3 = (bf16[1024,1024]{1,0:T(8,128)(2,1)}, bf16[1024,4096]{1,0:T(8,128)(2,1)}, bf16[4096,1024]{1,0:T(8,128)(2,1)}) custom-call(s32[10]{0:T(128)} %stack.151.refs_0_, bf16[128,1024]{1,0:T(8,128)(2,1)} %refs_1_.1, bf16[128,4096]{1,0:T(8,128)(2,1)} %refs_2_.3, bf16[512,1024]{1,0:T(8,128)(2,1)} %refs_3_.3, ...), custom_call_target="tpu_custom_call" | custom-call | bytes 37748736 | tf_op jit(solution)/shard_map/place_rows/pallas_call | solution.py:148
  311.4 14.4 %cross_forward.5 = (bf16[128,1024]{1,0:T(8,128)(2,1)}, f32[8,1,256]{2,1,0:T(1,128)}, bf16[1024,2048]{1,0:T(8,128)(2,1)}) custom-call(s32[1]{0:T(128)} %get-tuple-element.287.lengths, bf16[128,1024]{1,0:T(8,128)(2,1)} %get-tuple-element.263.q_ref, bf16[1024,1024]{1,0:T(8,128)(2,1)} %bitcast.555, bf16[1024,2048]{1,0:T(8,128)(2,1)} %get-tuple-element.84.w_ref, ...), custom_call_target="tpu_custom_call" | custom-call | flops 6442450944 | bytes 10485760 | tf_op jit(solution)/shard_map/cross_forward/pallas_call | solution.py:397
  326.9 14.8 %cross_forward.7 = (bf16[128,1024]{1,0:T(8,128)(2,1)}, f32[8,1,256]{2,1,0:T(1,128)}, bf16[1024,2048]{1,0:T(8,128)(2,1)}) custom-call(s32[1]{0:T(128)} %get-tuple-element.286.lengths, bf16[128,1024]{1,0:T(8,128)(2,1)} %get-tuple-element.261.q_ref, bf16[1024,1024]{1,0:T(8,128)(2,1)} %bitcast.48.m_ref, bf16[1024,2048]{1,0:T(8,128)(2,1)} %get-tuple-element.84.w_ref, ...), custom_call_target="tpu_custom_call" | custom-call | flops 6442450944 | bytes 10485760 | tf_op jit(solution)/shard_map/cross_forward/pallas_call | solution.py:397
  346.5 14.1 %multiply_convert_fusion.1 = (bf16[512,4096]{1,0:T(8,128)(2,1)S(1)}, f32[512,4096]{1,0:T(8,128)}) fusion(f32[4096]{0:T(1024)S(1)} %convert.99, bf16[1024,4096]{1,0:T(8,128)(2,1)S(1)} %bitcast.636, f32[512,1024]{1,0:T(8,128)S(1)} %get-tuple-element.293, f32[1024]{0:T(1024)S(1)} %bitcast.622, f32[1024]{0:T(1024)S(1)} %bitcast.602, f32[512]{0:T(512)S(1)} %fusion.84, ...), kind=kOutput, calls=%fused_computation.12 | convolution fusion | flops 4345823232 | bytes 23097344 | tf_op jit(solution)/shard_map/dot_general | solution.py:697
  360.6 4.8 fusion.112
  369.7 14.6 %fusion.113 = (bf16[4096]{0:T(1024)(128)(2,1)S(1)}, bf16[512,4096]{1,0:T(8,128)(2,1)S(1)}) fusion(f32[512,4096]{1,0:T(8,128)} %get-tuple-element.295, f32[4096]{0:T(1024)S(1)} %convert.99, bf16[512,1024]{1,0:T(8,128)(2,1)S(1)} %get-tuple-element.146, bf16[4096,1024]{1,0:T(8,128)(2,1)} %get-tuple-element.96), kind=kOutput, calls=%fused_computation.437 | convolution fusion | flops 4355780608 | bytes 22044672 | tf_op jit(solution)/shard_map/dot_general | solution.py:258
  384.3 7.8 multiply_reduce_fusion
  392.3 6.6 convolution_convert_fusion.1
  400.3 4.6 convolution_convert_fusion.5
  411.8 18.0 %cross_backward.4 = (bf16[128,1024]{1,0:T(8,128)(2,1)}, f32[1,1024]{1,0:T(1,128)}, bf16[1024,2048]{1,0:T(8,128)(2,1)}, bf16[1024,1024]{1,0:T(8,128)(2,1)}) custom-call(s32[1]{0:T(128)} %get-tuple-element.288.lengths, bf16[128,1024]{1,0:T(8,128)(2,1)} %get-tuple-element.264.q_ref, bf16[128,1024]{1,0:T(8,128)(2,1)} %get-tuple-element.257.grad_ref, ...), custom_call_target="tpu_custom_call" | custom-call | flops 9663676416 | bytes 18874368 | tf_op jit(solution)/shard_map/cross_backward/pallas_call | solution.py:424
  439.3 3.9 add_convert_fusion.2
  443.4 4.1 add_convert_fusion.16
  449.9 17.7 %cross_backward.5 = (bf16[128,1024]{1,0:T(8,128)(2,1)}, f32[1,1024]{1,0:T(1,128)}, bf16[1024,2048]{1,0:T(8,128)(2,1)}, bf16[1024,1024]{1,0:T(8,128)(2,1)}) custom-call(s32[1]{0:T(128)} %get-tuple-element.287.lengths, bf16[128,1024]{1,0:T(8,128)(2,1)} %get-tuple-element.263.q_ref, bf16[128,1024]{1,0:T(8,128)(2,1)} %get-tuple-element.103.grad_ref, ...), custom_call_target="tpu_custom_call" | custom-call | flops 9663676416 | bytes 18874368 | tf_op jit(solution)/shard_map/cross_backward/pallas_call | solution.py:424
  467.6 4.0 pad_maximum_fusion.1
  471.6 5.7 all-to-all-start.3
  477.7 17.7 %cross_backward.6 = (bf16[128,1024]{1,0:T(8,128)(2,1)}, f32[1,1024]{1,0:T(1,128)}, bf16[1024,2048]{1,0:T(8,128)(2,1)}, bf16[1024,1024]{1,0:T(8,128)(2,1)}) custom-call(s32[1]{0:T(128)} %get-tuple-element.289.lengths, bf16[128,1024]{1,0:T(8,128)(2,1)} %get-tuple-element.262.q_ref, bf16[128,1024]{1,0:T(8,128)(2,1)} %get-tuple-element.108.grad_ref, ...), custom_call_target="tpu_custom_call" | custom-call | flops 9663676416 | bytes 18874368 | tf_op jit(solution)/shard_map/cross_backward/pallas_call | solution.py:424
  495.4 18.1 %cross_backward.7 = (bf16[128,1024]{1,0:T(8,128)(2,1)}, f32[1,1024]{1,0:T(1,128)}, bf16[1024,2048]{1,0:T(8,128)(2,1)}, bf16[1024,1024]{1,0:T(8,128)(2,1)}) custom-call(s32[1]{0:T(128)} %get-tuple-element.286.lengths, bf16[128,1024]{1,0:T(8,128)(2,1)} %get-tuple-element.261.q_ref, bf16[128,1024]{1,0:T(8,128)(2,1)} %get-tuple-element.113.grad_ref, ...), custom_call_target="tpu_custom_call" | custom-call | flops 9663676416 | bytes 18874368 | tf_op jit(solution)/shard_map/cross_backward/pallas_call | solution.py:424
  527.2 10.7 %self_backward.1 = bf16[4,128,3072]{2,1,0:T(8,128)(2,1)} custom-call(s32[4,1,128]{2,1,0:T(1,128)} %bitcast.594, s32[4,128,1]{2,1,0:T(8,128)} %copy.118.seg_column, bf16[4,128,3072]{2,1,0:T(8,128)(2,1)} %bitcast.514, bf16[4,128,1024]{2,1,0:T(8,128)(2,1)} %bitcast.577, f32[4,8,1,256]{3,2,1,0:T(1,128)} %get-tuple-element.119.log_ref), custom_call_target="tpu_custom_call" | custom-call | tf_op jit(solution)/shard_map/self_backward/pallas_call | solution.py:519
  545.4 35.1 %collective-permute-done.33 = bf16[8,9,128,256]{3,2,1,0:T(8,128)(2,1)} collective-permute-done((bf16[8,9,128,256]{3,2,1,0:T(8,128)(2,1)}, bf16[8,9,128,256]{3,2,1,0:T(8,128)(2,1)}, u32[]{:S(2)}, u32[]{:S(2)}) %collective-permute-start.33) | collective-permute-done | bytes 4718624 | tf_op jit(solution)/shard_map/ppermute | solution.py:16
  591.2 4.8 fusion.15
  603.2 6.9 fusion.117
  618.5 8.7 fusion.119
  627.2 7.2 fusion.118
  634.4 15.4 %add_convert_fusion = bf16[1024,2048]{1,0:T(8,128)(2,1)S(1)} fusion(f32[1024,2048]{1,0:T(8,128)} %fusion.119, f32[1024,2048]{1,0:T(8,128)} %fusion.117, f32[1024,2048]{1,0:T(8,128)} %fusion.118, bf16[1024,1024]{1,0:T(8,128)(2,1)} %bitcast.48.m_ref, bf16[1024,2048]{1,0:T(8,128)(2,1)} %get-tuple-element.132), kind=kOutput, calls=%fused_computation.10 | convolution fusion | flops 4303355904 | bytes 35651584 | tf_op jit(solution)/shard_map/dot_general | solution.py:262
  656.4 4.6 pad_maximum_fusion.2
  661.0 5.4 all-to-all-start.4
  684.8 4.3 fusion.9
  697.9 49.9 %collective-permute-done.60 = bf16[9,128,256]{2,1,0:T(8,128)(2,1)} collective-permute-done((bf16[9,128,256]{2,1,0:T(8,128)(2,1)}, bf16[9,128,256]{2,1,0:T(8,128)(2,1)}, u32[]{:S(2)}, u32[]{:S(2)}) %collective-permute-start.60) | collective-permute-done | bytes 589856 | tf_op jit(solution)/shard_map/ppermute | solution.py:16
  749.0 4.3 collective-permute-start.61
  759.5 7.2 add_convert_fusion.5
  767.8 7.8 collective-permute-start.62
  776.4 4.7 collective-permute-start.43
  782.6 4.0 collective-permute-start.52
  787.3 7.4 collective-permute-done.43
  799.0 4.1 collective-permute-start.53
  804.7 4.0 collective-permute-start.44
  818.8 19.2 %collective-permute-done.57 = bf16[3,128,256]{2,1,0:T(8,128)(2,1)S(1)} collective-permute-done((bf16[3,128,256]{2,1,0:T(8,128)(2,1)S(1)}, bf16[3,128,256]{2,1,0:T(8,128)(2,1)S(1)}, u32[]{:S(2)}, u32[]{:S(2)}) %collective-permute-start.57) | collective-permute-done | bytes 196640 | tf_op jit(solution)/shard_map/ppermute | solution.py:16
  843.4 5.7 collective-permute-start.59
  849.1 7.6 pad_maximum_fusion
  (549 shorter events, 254.6 us)
Async XLA Ops:
  8.7 15.2 %collective-permute-start.1 = (bf16[128,1920]{1,0:T(8,128)(2,1)}, bf16[128,1920]{1,0:T(8,128)(2,1)S(1)}, u32[]{:S(2)}, u32[]{:S(2)}) collective-permute-start(bf16[128,1920]{1,0:T(8,128)(2,1)} %constant_dynamic-update-slice_fusion), channel_id=1, source_target_pairs={{2,0},{3,1},{4,2},{5,3},{6,4},{7,5},{10,8},{11,9},{12,10},{13,11},... | collective-permute-start | bytes 1474568 | tf_op jit(solution)/shard_map/ppermute | solution.py:16
  9.9 16.7 %collective-permute-start.2 = (bf16[128,1920]{1,0:T(8,128)(2,1)}, bf16[128,1920]{1,0:T(8,128)(2,1)S(1)}, u32[]{:S(2)}, u32[]{:S(2)}) collective-permute-start(bf16[128,1920]{1,0:T(8,128)(2,1)} %constant_dynamic-update-slice_fusion), channel_id=1, source_target_pairs={{0,2},{1,3},{2,4},{3,5},{4,6},{5,7},{8,10},{9,11},{10,12},{11,13},... | collective-permute-start | bytes 1474568 | tf_op jit(solution)/shard_map/ppermute | solution.py:16
  14.6 37.4 %collective-permute-start = (bf16[128,1920]{1,0:T(8,128)(2,1)}, bf16[128,1920]{1,0:T(8,128)(2,1)S(1)}, u32[]{:S(2)}, u32[]{:S(2)}) collective-permute-start(bf16[128,1920]{1,0:T(8,128)(2,1)} %constant_dynamic-update-slice_fusion), channel_id=1, source_target_pairs={{0,1},{1,0},{2,3},{3,2},{4,5},{5,4},{6,7},{7,6},{8,9},{9,8},{10,11... | collective-permute-start | bytes 1474568 | tf_op jit(solution)/shard_map/ppermute | solution.py:16
  23.8 13.4 %collective-permute-start.5 = (bf16[128,1920]{1,0:T(8,128)(2,1)S(1)}, bf16[128,1920]{1,0:T(8,128)(2,1)S(1)}, u32[]{:S(2)}, u32[]{:S(2)}) collective-permute-start(bf16[128,1920]{1,0:T(8,128)(2,1)S(1)} %collective-permute-done.1), channel_id=1, source_target_pairs={{2,0},{3,1},{4,2},{5,3},{10,8},{11,9},{12,10},{13,11},{18,16},{19,... | collective-permute-start | bytes 1474568 | tf_op jit(solution)/shard_map/ppermute | solution.py:16
  26.6 14.1 %collective-permute-start.3 = (bf16[128,1920]{1,0:T(8,128)(2,1)S(1)}, bf16[128,1920]{1,0:T(8,128)(2,1)}, u32[]{:S(2)}, u32[]{:S(2)}) collective-permute-start(bf16[128,1920]{1,0:T(8,128)(2,1)S(1)} %collective-permute-done.2), channel_id=1, source_target_pairs={{2,4},{3,5},{4,6},{5,7},{10,12},{11,13},{12,14},{13,15},{18,20},{1... | collective-permute-start | bytes 1474568 | tf_op jit(solution)/shard_map/ppermute | solution.py:16
  37.2 12.6 %collective-permute-start.6 = (bf16[128,1920]{1,0:T(8,128)(2,1)S(1)}, bf16[128,1920]{1,0:T(8,128)(2,1)}, u32[]{:S(2)}, u32[]{:S(2)}) collective-permute-start(bf16[128,1920]{1,0:T(8,128)(2,1)S(1)} %collective-permute-done.5), channel_id=1, source_target_pairs={{2,0},{3,1},{10,8},{11,9},{18,16},{19,17},{26,24},{27,25}} | collective-permute-start | bytes 1474568 | tf_op jit(solution)/shard_map/ppermute | solution.py:16
  40.0 12.9 %collective-permute-start.15 = (bf16[128,2304]{1,0:T(8,128)(2,1)}, bf16[128,2304]{1,0:T(8,128)(2,1)S(1)}, u32[]{:S(2)}, u32[]{:S(2)}) collective-permute-start(bf16[128,2304]{1,0:T(8,128)(2,1)} %constant_dynamic-update-slice_fusion.4), channel_id=1, source_target_pairs={{0,1},{1,0},{2,3},{3,2},{4,5},{5,4},{6,7},{7,6},{8,9},{9,8},{10,11... | collective-permute-start | bytes 1769480 | tf_op jit(solution)/shard_map/ppermute | solution.py:16
  51.6 33.2 %collective-permute-start.7 = (bf16[3,128,1920]{2,1,0:T(8,128)(2,1)S(1)}, bf16[3,128,1920]{2,1,0:T(8,128)(2,1)}, u32[]{:S(2)}, u32[]{:S(2)}) collective-permute-start(bf16[3,128,1920]{2,1,0:T(8,128)(2,1)S(1)} %pad_maximum_fusion.12), channel_id=1, source_target_pairs={{0,1},{1,0},{2,3},{3,2},{4,5},{5,4},{6,7},{7,6},{8,9},{9,8},{10,11... | collective-permute-start | bytes 4423688 | tf_op jit(solution)/shard_map/ppermute | solution.py:16
  52.9 12.4 %collective-permute-start.16 = (bf16[128,2304]{1,0:T(8,128)(2,1)}, bf16[128,2304]{1,0:T(8,128)(2,1)S(1)}, u32[]{:S(2)}, u32[]{:S(2)}) collective-permute-start(bf16[128,2304]{1,0:T(8,128)(2,1)} %constant_dynamic-update-slice_fusion.4), channel_id=1, source_target_pairs={{2,0},{3,1},{4,2},{5,3},{6,4},{7,5},{10,8},{11,9},{12,10},{13,11},... | collective-permute-start | bytes 1769480 | tf_op jit(solution)/shard_map/ppermute | solution.py:16
  54.1 12.4 %collective-permute-start.17 = (bf16[128,2304]{1,0:T(8,128)(2,1)}, bf16[128,2304]{1,0:T(8,128)(2,1)S(1)}, u32[]{:S(2)}, u32[]{:S(2)}) collective-permute-start(bf16[128,2304]{1,0:T(8,128)(2,1)} %constant_dynamic-update-slice_fusion.4), channel_id=1, source_target_pairs={{0,2},{1,3},{2,4},{3,5},{4,6},{5,7},{8,10},{9,11},{10,12},{11,13},... | collective-permute-start | bytes 1769480 | tf_op jit(solution)/shard_map/ppermute | solution.py:16
  59.3 21.8 %collective-permute-start.19 = (bf16[128,2304]{1,0:T(8,128)(2,1)S(1)}, bf16[128,2304]{1,0:T(8,128)(2,1)S(1)}, u32[]{:S(2)}, u32[]{:S(2)}) collective-permute-start(bf16[128,2304]{1,0:T(8,128)(2,1)S(1)} %collective-permute-done.15), channel_id=1, source_target_pairs={{0,16},{8,24},{16,0},{24,8},{1,17},{9,25},{17,1},{25,9},{2,18},{10... | collective-permute-start | bytes 1769480 | tf_op jit(solution)/shard_map/ppermute | solution.py:16
  65.2 15.9 %collective-permute-start.21 = (bf16[128,2304]{1,0:T(8,128)(2,1)S(1)}, bf16[128,2304]{1,0:T(8,128)(2,1)S(1)}, u32[]{:S(2)}, u32[]{:S(2)}) collective-permute-start(bf16[128,2304]{1,0:T(8,128)(2,1)S(1)} %collective-permute-done.16), channel_id=1, source_target_pairs={{2,0},{3,1},{4,2},{5,3},{10,8},{11,9},{12,10},{13,11},{18,16},{19,... | collective-permute-start | bytes 1769480 | tf_op jit(solution)/shard_map/ppermute | solution.py:16
  66.5 19.6 %collective-permute-start.18 = (bf16[128,2304]{1,0:T(8,128)(2,1)S(1)}, bf16[128,2304]{1,0:T(8,128)(2,1)S(1)}, u32[]{:S(2)}, u32[]{:S(2)}) collective-permute-start(bf16[128,2304]{1,0:T(8,128)(2,1)S(1)} %collective-permute-done.17), channel_id=1, source_target_pairs={{2,4},{3,5},{4,6},{5,7},{10,12},{11,13},{12,14},{13,15},{18,20},{1... | collective-permute-start | bytes 1769480 | tf_op jit(solution)/shard_map/ppermute | solution.py:16
  67.2 13.4 %collective-permute-start.8 = (bf16[128,1920]{1,0:T(8,128)(2,1)S(1)}, bf16[128,1920]{1,0:T(8,128)(2,1)S(1)}, u32[]{:S(2)}, u32[]{:S(2)}) collective-permute-start(bf16[128,1920]{1,0:T(8,128)(2,1)S(1)} %collective-permute-done), channel_id=1, source_target_pairs={{0,16},{8,24},{16,0},{24,8},{1,17},{9,25},{17,1},{25,9},{2,18},{10... | collective-permute-start | bytes 1474568 | tf_op jit(solution)/shard_map/ppermute | solution.py:16
  80.6 30.8 %collective-permute-start.9 = (bf16[3,128,1920]{2,1,0:T(8,128)(2,1)S(1)}, bf16[3,128,1920]{2,1,0:T(8,128)(2,1)}, u32[]{:S(2)}, u32[]{:S(2)}) collective-permute-start(bf16[3,128,1920]{2,1,0:T(8,128)(2,1)S(1)} %pad_maximum_fusion.12), channel_id=1, source_target_pairs={{0,16},{8,24},{16,0},{24,8},{1,17},{9,25},{17,1},{25,9},{2,18},{10... | collective-permute-start | bytes 4423688 | tf_op jit(solution)/shard_map/ppermute | solution.py:16
  111.5 101.1 %all-to-all-start = ((bf16[8,2,128,1024]{3,2,1,0:T(8,128)(2,1)}), bf16[8,2,128,1024]{3,2,1,0:T(8,128)(2,1)}, u32[]{:S(2)}, u32[]{:S(2)}) async-start(bf16[8,2,128,1024]{3,2,1,0:T(8,128)(2,1)} %stack.183), calls=%async_computation | async-start | bytes 8388608 | tf_op jit(solution)/shard_map/all_to_all | solution.py:546
  116.4 24.1 %collective-permute-start.10 = (bf16[3,128,1920]{2,1,0:T(8,128)(2,1)}, bf16[3,128,1920]{2,1,0:T(8,128)(2,1)}, u32[]{:S(2)}, u32[]{:S(2)}) collective-permute-start(bf16[3,128,1920]{2,1,0:T(8,128)(2,1)} %collective-permute-done.7.refs_7_), channel_id=1, source_target_pairs={{0,16},{8,24},{16,0},{24,8},{1,17},{9,25},{17,1},{25,9},{2,18},{10... | collective-permute-start | bytes 4423688 | tf_op jit(solution)/shard_map/ppermute | solution.py:16
  118.7 40.7 %collective-permute-start.11 = (bf16[4,128,1920]{2,1,0:T(8,128)(2,1)S(1)}, bf16[4,128,1920]{2,1,0:T(8,128)(2,1)}, u32[]{:S(2)}, u32[]{:S(2)}) collective-permute-start(bf16[4,128,1920]{2,1,0:T(8,128)(2,1)S(1)} %pad_maximum_fusion.7.refs_6_), channel_id=1, source_target_pairs={{0,8},{8,0},{16,24},{24,16},{1,9},{9,1},{17,25},{25,17},{2,10},{10... | collective-permute-start | bytes 5898248 | tf_op jit(solution)/shard_map/ppermute | solution.py:16
  132.9 26.9 %collective-permute-start.13 = (bf16[4,128,1920]{2,1,0:T(8,128)(2,1)}, bf16[4,128,1920]{2,1,0:T(8,128)(2,1)}, u32[]{:S(2)}, u32[]{:S(2)}) collective-permute-start(bf16[4,128,1920]{2,1,0:T(8,128)(2,1)} %pad_maximum_fusion.8.refs_8_), channel_id=1, source_target_pairs={{0,8},{8,0},{16,24},{24,16},{1,9},{9,1},{17,25},{25,17},{2,10},{10... | collective-permute-start | bytes 5898248 | tf_op jit(solution)/shard_map/ppermute | solution.py:16
  133.6 26.3 %collective-permute-start.12 = (bf16[3,128,1920]{2,1,0:T(8,128)(2,1)}, bf16[3,128,1920]{2,1,0:T(8,128)(2,1)}, u32[]{:S(2)}, u32[]{:S(2)}) collective-permute-start(bf16[3,128,1920]{2,1,0:T(8,128)(2,1)} %collective-permute-done.7.refs_7_), channel_id=1, source_target_pairs={{0,8},{8,0},{16,24},{24,16},{1,9},{9,1},{17,25},{25,17},{2,10},{10... | collective-permute-start | bytes 4423688 | tf_op jit(solution)/shard_map/ppermute | solution.py:16
  140.5 19.4 %collective-permute-start.14 = (bf16[3,128,1920]{2,1,0:T(8,128)(2,1)}, bf16[3,128,1920]{2,1,0:T(8,128)(2,1)}, u32[]{:S(2)}, u32[]{:S(2)}) collective-permute-start(bf16[3,128,1920]{2,1,0:T(8,128)(2,1)} %collective-permute-done.10.refs_9_), channel_id=1, source_target_pairs={{0,8},{8,0},{16,24},{24,16},{1,9},{9,1},{17,25},{25,17},{2,10},{10... | collective-permute-start | bytes 4423688 | tf_op jit(solution)/shard_map/ppermute | solution.py:16
  158.0 53.3 %collective-permute-start.23 = (bf16[3,128,2304]{2,1,0:T(8,128)(2,1)S(1)}, bf16[3,128,2304]{2,1,0:T(8,128)(2,1)}, u32[]{:S(2)}, u32[]{:S(2)}) collective-permute-start(bf16[3,128,2304]{2,1,0:T(8,128)(2,1)S(1)} %copy-done.34), channel_id=1, source_target_pairs={{0,1},{1,0},{2,3},{3,2},{4,5},{5,4},{6,7},{7,6},{8,9},{9,8},{10,11... | collective-permute-start | bytes 5308424 | tf_op jit(solution)/shard_map/ppermute | solution.py:16
  159.4 51.9 %collective-permute-start.24 = (bf16[3,128,2304]{2,1,0:T(8,128)(2,1)S(1)}, bf16[3,128,2304]{2,1,0:T(8,128)(2,1)S(1)}, u32[]{:S(2)}, u32[]{:S(2)}) collective-permute-start(bf16[3,128,2304]{2,1,0:T(8,128)(2,1)S(1)} %copy-done.34), channel_id=1, source_target_pairs={{0,16},{8,24},{16,0},{24,8},{1,17},{9,25},{17,1},{25,9},{2,18},{10... | collective-permute-start | bytes 5308424 | tf_op jit(solution)/shard_map/ppermute | solution.py:16
  212.5 57.3 %all-to-all-start.1 = ((bf16[8,128,1024]{2,1,0:T(8,128)(2,1)}), bf16[8,128,1024]{2,1,0:T(8,128)(2,1)}, u32[]{:S(2)}, u32[]{:S(2)}) async-start(bf16[8,128,1024]{2,1,0:T(8,128)(2,1)} %get-tuple-element.88), calls=%async_computation.1 | async-start | bytes 4194304 | tf_op jit(solution)/shard_map/all_to_all | solution.py:546
  223.1 39.5 %collective-permute-start.25 = (bf16[3,128,2304]{2,1,0:T(8,128)(2,1)}, bf16[3,128,2304]{2,1,0:T(8,128)(2,1)}, u32[]{:S(2)}, u32[]{:S(2)}) collective-permute-start(bf16[3,128,2304]{2,1,0:T(8,128)(2,1)} %collective-permute-done.23.refs_5_), channel_id=1, source_target_pairs={{0,16},{8,24},{16,0},{24,8},{1,17},{9,25},{17,1},{25,9},{2,18},{10... | collective-permute-start | bytes 5308424 | tf_op jit(solution)/shard_map/ppermute | solution.py:16
  226.1 69.2 %collective-permute-start.26 = (bf16[4,128,2304]{2,1,0:T(8,128)(2,1)}, bf16[4,128,2304]{2,1,0:T(8,128)(2,1)}, u32[]{:S(2)}, u32[]{:S(2)}) collective-permute-start(bf16[4,128,2304]{2,1,0:T(8,128)(2,1)} %pad_maximum_fusion.3.refs_4_), channel_id=1, source_target_pairs={{0,8},{8,0},{16,24},{24,16},{1,9},{9,1},{17,25},{25,17},{2,10},{10... | collective-permute-start | bytes 7077896 | tf_op jit(solution)/shard_map/ppermute | solution.py:16
  269.8 57.0 %all-to-all-start.2 = ((bf16[8,128,1024]{2,1,0:T(8,128)(2,1)}), bf16[8,128,1024]{2,1,0:T(8,128)(2,1)}, u32[]{:S(2)}, u32[]{:S(2)}) async-start(bf16[8,128,1024]{2,1,0:T(8,128)(2,1)} %get-tuple-element.90), calls=%async_computation.2 | async-start | bytes 4194304 | tf_op jit(solution)/shard_map/all_to_all | solution.py:546
  278.1 17.2 %collective-permute-start.28 = (bf16[4,128,2304]{2,1,0:T(8,128)(2,1)}, bf16[4,128,2304]{2,1,0:T(8,128)(2,1)}, u32[]{:S(2)}, u32[]{:S(2)}) collective-permute-start(bf16[4,128,2304]{2,1,0:T(8,128)(2,1)} %pad_maximum_fusion.4.refs_6_), channel_id=1, source_target_pairs={{0,8},{8,0},{16,24},{24,16},{1,9},{9,1},{17,25},{25,17},{2,10},{10... | collective-permute-start | bytes 7077896 | tf_op jit(solution)/shard_map/ppermute | solution.py:16
  279.5 15.8 %collective-permute-start.27 = (bf16[3,128,2304]{2,1,0:T(8,128)(2,1)}, bf16[3,128,2304]{2,1,0:T(8,128)(2,1)}, u32[]{:S(2)}, u32[]{:S(2)}) collective-permute-start(bf16[3,128,2304]{2,1,0:T(8,128)(2,1)} %collective-permute-done.23.refs_5_), channel_id=1, source_target_pairs={{0,8},{8,0},{16,24},{24,16},{1,9},{9,1},{17,25},{25,17},{2,10},{10... | collective-permute-start | bytes 5308424 | tf_op jit(solution)/shard_map/ppermute | solution.py:16
  279.5 15.8 %collective-permute-start.29 = (bf16[3,128,2304]{2,1,0:T(8,128)(2,1)}, bf16[3,128,2304]{2,1,0:T(8,128)(2,1)}, u32[]{:S(2)}, u32[]{:S(2)}) collective-permute-start(bf16[3,128,2304]{2,1,0:T(8,128)(2,1)} %collective-permute-done.25.refs_7_), channel_id=1, source_target_pairs={{0,8},{8,0},{16,24},{24,16},{1,9},{9,1},{17,25},{25,17},{2,10},{10... | collective-permute-start | bytes 5308424 | tf_op jit(solution)/shard_map/ppermute | solution.py:16
  398.9 40.4 %collective-permute-start.30 = (bf16[4096,512]{1,0:T(8,128)(2,1)}, bf16[4096,512]{1,0:T(8,128)(2,1)}, u32[]{:S(2)}, u32[]{:S(2)}) collective-permute-start(bf16[4096,512]{1,0:T(8,128)(2,1)} %convolution_convert_fusion.1), channel_id=1, source_target_pairs={{0,8},{8,0},{16,24},{24,16},{1,9},{9,1},{17,25},{25,17},{2,10},{10... | collective-permute-start | bytes 12582920 | tf_op jit(solution)/shard_map/ppermute | solution.py:16
  404.9 38.5 %collective-permute-start.31 = (bf16[1024,2048]{1,0:T(8,128)(2,1)}, bf16[1024,2048]{1,0:T(8,128)(2,1)}, u32[]{:S(2)}, u32[]{:S(2)}) collective-permute-start(bf16[1024,2048]{1,0:T(8,128)(2,1)} %convolution_convert_fusion.5), channel_id=1, source_target_pairs={{0,8},{8,0},{16,24},{24,16},{1,9},{9,1},{17,25},{25,17},{2,10},{10... | collective-permute-start | bytes 12582920 | tf_op jit(solution)/shard_map/ppermute | solution.py:16
  410.8 26.2 %collective-permute-start.32 = (bf16[1024,512]{1,0:T(8,128)(2,1)}, bf16[1024,512]{1,0:T(8,128)(2,1)}, u32[]{:S(2)}, u32[]{:S(2)}) collective-permute-start(bf16[1024,512]{1,0:T(8,128)(2,1)} %convolution_convert_fusion.13), channel_id=1, source_target_pairs={{0,8},{8,0},{16,24},{24,16},{1,9},{9,1},{17,25},{25,17},{2,10},{10... | collective-permute-start | bytes 3145736 | tf_op jit(solution)/shard_map/ppermute | solution.py:16
  471.6 108.9 %all-to-all-start.3 = ((bf16[8,2,128,1024]{3,2,1,0:T(8,128)(2,1)}), bf16[8,2,128,1024]{3,2,1,0:T(8,128)(2,1)}, u32[]{:S(2)}, u32[]{:S(2)}) async-start(bf16[8,2,128,1024]{3,2,1,0:T(8,128)(2,1)} %pad_maximum_fusion.1), calls=%async_computation.3 | async-start | bytes 8388608 | tf_op jit(solution)/shard_map/all_to_all | solution.py:546
  477.6 102.9 %collective-permute-start.33 = (bf16[8,9,128,256]{3,2,1,0:T(8,128)(2,1)}, bf16[8,9,128,256]{3,2,1,0:T(8,128)(2,1)}, u32[]{:S(2)}, u32[]{:S(2)}) collective-permute-start(bf16[8,9,128,256]{3,2,1,0:T(8,128)(2,1)} %copy-done.40), channel_id=1, source_target_pairs={{0,16},{8,24},{16,0},{24,8},{1,17},{9,25},{17,1},{25,9},{2,18},{10... | collective-permute-start | bytes 14155784 | tf_op jit(solution)/shard_map/ppermute | solution.py:16
  523.9 64.2 %collective-permute-start.34 = (bf16[1024,512]{1,0:T(8,128)(2,1)}, bf16[1024,512]{1,0:T(8,128)(2,1)}, u32[]{:S(2)}, u32[]{:S(2)}) collective-permute-start(bf16[1024,512]{1,0:T(8,128)(2,1)} %convolution_convert_fusion.10), channel_id=1, source_target_pairs={{0,8},{8,0},{16,24},{24,16},{1,9},{9,1},{17,25},{25,17},{2,10},{10... | collective-permute-start | bytes 3145736 | tf_op jit(solution)/shard_map/ppermute | solution.py:16
  585.6 25.7 %collective-permute-start.35 = (bf16[1024,1536]{1,0:T(8,128)(2,1)}, bf16[1024,1536]{1,0:T(8,128)(2,1)}, u32[]{:S(2)}, u32[]{:S(2)}) collective-permute-start(bf16[1024,1536]{1,0:T(8,128)(2,1)} %fusion.11), channel_id=1, source_target_pairs={{0,8},{8,0},{16,24},{24,16},{1,9},{9,1},{17,25},{25,17},{2,10},{10... | collective-permute-start | bytes 9437192 | tf_op jit(solution)/shard_map/ppermute | solution.py:16
  597.5 12.6 %collective-permute-start.36 = (bf16[1024,512]{1,0:T(8,128)(2,1)S(1)}, bf16[1024,512]{1,0:T(8,128)(2,1)S(1)}, u32[]{:S(2)}, u32[]{:S(2)}) collective-permute-start(bf16[1024,512]{1,0:T(8,128)(2,1)S(1)} %pad_maximum_fusion.15), channel_id=1, source_target_pairs={{0,8},{8,0},{16,24},{24,16},{1,9},{9,1},{17,25},{25,17},{2,10},{10... | collective-permute-start | bytes 3145736 | tf_op jit(solution)/shard_map/ppermute | solution.py:16
  598.9 53.0 %collective-permute-start.39 = (bf16[4,9,128,256]{3,2,1,0:T(8,128)(2,1)S(1)}, bf16[4,9,128,256]{3,2,1,0:T(8,128)(2,1)}, u32[]{:S(2)}, u32[]{:S(2)}) collective-permute-start(bf16[4,9,128,256]{3,2,1,0:T(8,128)(2,1)S(1)} %copy-done.20), channel_id=1, source_target_pairs={{0,1},{1,0},{2,3},{3,2},{4,5},{5,4},{6,7},{7,6},{8,9},{9,8},{10,11... | collective-permute-start | bytes 7077896 | tf_op jit(solution)/shard_map/ppermute | solution.py:16
  618.5 60.4 %collective-permute-start.37 = (bf16[8,5,128,256]{3,2,1,0:T(8,128)(2,1)}, bf16[8,5,128,256]{3,2,1,0:T(8,128)(2,1)}, u32[]{:S(2)}, u32[]{:S(2)}) collective-permute-start(bf16[8,5,128,256]{3,2,1,0:T(8,128)(2,1)} %constant_dynamic-update-slice_fusion.24), channel_id=1, source_target_pairs={{0,16},{8,24},{16,0},{24,8},{1,17},{9,25},{17,1},{25,9},{2,18},{10... | collective-permute-start | bytes 7864328 | tf_op jit(solution)/shard_map/ppermute | solution.py:16
  653.8 17.5 %collective-permute-start.40 = (bf16[1024,1024]{1,0:T(8,128)(2,1)}, bf16[1024,1024]{1,0:T(8,128)(2,1)}, u32[]{:S(2)}, u32[]{:S(2)}) collective-permute-start(bf16[1024,1024]{1,0:T(8,128)(2,1)} %pad_maximum_fusion.5), channel_id=1, source_target_pairs={{0,8},{8,0},{16,24},{24,16},{1,9},{9,1},{17,25},{25,17},{2,10},{10... | collective-permute-start | bytes 6291464 | tf_op jit(solution)/shard_map/ppermute | solution.py:16
  661.0 188.1 %all-to-all-start.4 = ((bf16[8,2,128,1024]{3,2,1,0:T(8,128)(2,1)}), bf16[8,2,128,1024]{3,2,1,0:T(8,128)(2,1)}, u32[]{:S(2)}, u32[]{:S(2)}) async-start(bf16[8,2,128,1024]{3,2,1,0:T(8,128)(2,1)} %pad_maximum_fusion.2), calls=%async_computation.4 | async-start | bytes 8388608 | tf_op jit(solution)/shard_map/all_to_all | solution.py:546
  678.8 74.5 %collective-permute-start.50 = (bf16[8,3,128,256]{3,2,1,0:T(8,128)(2,1)}, bf16[8,3,128,256]{3,2,1,0:T(8,128)(2,1)}, u32[]{:S(2)}, u32[]{:S(2)}) collective-permute-start(bf16[8,3,128,256]{3,2,1,0:T(8,128)(2,1)} %pad_maximum_fusion.10), channel_id=1, source_target_pairs={{0,16},{8,24},{16,0},{24,8},{1,17},{9,25},{17,1},{25,9},{2,18},{10... | collective-permute-start | bytes 4718600 | tf_op jit(solution)/shard_map/ppermute | solution.py:16
  683.4 72.0 %collective-permute-start.41 = (bf16[4,5,128,256]{3,2,0,1:T(8,128)(2,1)}, bf16[4,5,128,256]{3,2,0,1:T(8,128)(2,1)}, u32[]{:S(2)}, u32[]{:S(2)}) collective-permute-start(bf16[4,5,128,256]{3,2,0,1:T(8,128)(2,1)} %fusion.34), channel_id=1, source_target_pairs={{0,1},{1,0},{2,3},{3,2},{4,5},{5,4},{6,7},{7,6},{8,9},{9,8},{10,11... | collective-permute-start | bytes 3932168 | tf_op jit(solution)/shard_map/ppermute | solution.py:16
  691.6 56.2 %collective-permute-start.60 = (bf16[9,128,256]{2,1,0:T(8,128)(2,1)}, bf16[9,128,256]{2,1,0:T(8,128)(2,1)}, u32[]{:S(2)}, u32[]{:S(2)}) collective-permute-start(bf16[9,128,256]{2,1,0:T(8,128)(2,1)} %get-tuple-element.210), channel_id=1, source_target_pairs={{0,2},{1,3},{8,10},{9,11},{16,18},{17,19},{24,26},{25,27}} | collective-permute-start | bytes 1769480 | tf_op jit(solution)/shard_map/ppermute | solution.py:16
  695.5 71.1 %collective-permute-start.63 = (bf16[9,128,256]{2,1,0:T(8,128)(2,1)}, bf16[9,128,256]{2,1,0:T(8,128)(2,1)S(1)}, u32[]{:S(2)}, u32[]{:S(2)}) collective-permute-start(bf16[9,128,256]{2,1,0:T(8,128)(2,1)} %get-tuple-element.211), channel_id=1, source_target_pairs={{6,4},{7,5},{14,12},{15,13},{22,20},{23,21},{30,28},{31,29}} | collective-permute-start | bytes 1769480 | tf_op jit(solution)/shard_map/ppermute | solution.py:16
  749.0 17.6 %collective-permute-start.61 = (bf16[9,128,256]{2,1,0:T(8,128)(2,1)S(1)}, bf16[9,128,256]{2,1,0:T(8,128)(2,1)S(1)}, u32[]{:S(2)}, u32[]{:S(2)}) collective-permute-start(bf16[9,128,256]{2,1,0:T(8,128)(2,1)S(1)} %fusion.37), channel_id=1, source_target_pairs={{0,2},{1,3},{2,4},{3,5},{8,10},{9,11},{10,12},{11,13},{16,18},{17,... | collective-permute-start | bytes 1769480 | tf_op jit(solution)/shard_map/ppermute | solution.py:16
  754.8 26.3 %collective-permute-start.51 = (bf16[4,3,128,256]{3,2,1,0:T(8,128)(2,1)S(1)}, bf16[4,3,128,256]{3,2,1,0:T(8,128)(2,1)S(1)}, u32[]{:S(2)}, u32[]{:S(2)}) collective-permute-start(bf16[4,3,128,256]{3,2,1,0:T(8,128)(2,1)S(1)} %fusion.41), channel_id=1, source_target_pairs={{0,1},{1,0},{2,3},{3,2},{4,5},{5,4},{6,7},{7,6},{8,9},{9,8},{10,11... | collective-permute-start | bytes 2359304 | tf_op jit(solution)/shard_map/ppermute | solution.py:16
  757.5 18.7 %collective-permute-start.42 = (bf16[5,128,256]{2,1,0:T(8,128)(2,1)S(1)}, bf16[5,128,256]{2,1,0:T(8,128)(2,1)S(1)}, u32[]{:S(2)}, u32[]{:S(2)}) collective-permute-start(bf16[5,128,256]{2,1,0:T(8,128)(2,1)S(1)} %get-tuple-element.237), channel_id=1, source_target_pairs={{0,2},{1,3},{8,10},{9,11},{16,18},{17,19},{24,26},{25,27}} | collective-permute-start | bytes 983048 | tf_op jit(solution)/shard_map/ppermute | solution.py:16
  767.1 36.1 %collective-permute-start.64 = (bf16[9,128,256]{2,1,0:T(8,128)(2,1)S(1)}, bf16[9,128,256]{2,1,0:T(8,128)(2,1)S(1)}, u32[]{:S(2)}, u32[]{:S(2)}) collective-permute-start(bf16[9,128,256]{2,1,0:T(8,128)(2,1)S(1)} %get-tuple-element.209), channel_id=1, source_target_pairs={{4,2},{5,3},{6,4},{7,5},{12,10},{13,11},{14,12},{15,13},{20,18},{2... | collective-permute-start | bytes 1769480 | tf_op jit(solution)/shard_map/ppermute | solution.py:16
  767.8 46.5 %collective-permute-start.62 = (bf16[9,128,256]{2,1,0:T(8,128)(2,1)S(1)}, bf16[9,128,256]{2,1,0:T(8,128)(2,1)S(1)}, u32[]{:S(2)}, u32[]{:S(2)}) collective-permute-start(bf16[9,128,256]{2,1,0:T(8,128)(2,1)S(1)} %get-tuple-element.208), channel_id=1, source_target_pairs={{0,2},{1,3},{2,4},{3,5},{4,6},{5,7},{8,10},{9,11},{10,12},{11,13},... | collective-permute-start | bytes 1769480 | tf_op jit(solution)/shard_map/ppermute | solution.py:16
  776.4 18.4 %collective-permute-start.43 = (bf16[5,128,256]{2,1,0:T(8,128)(2,1)S(1)}, bf16[5,128,256]{2,1,0:T(8,128)(2,1)S(1)}, u32[]{:S(2)}, u32[]{:S(2)}) collective-permute-start(bf16[5,128,256]{2,1,0:T(8,128)(2,1)S(1)} %fusion.44), channel_id=1, source_target_pairs={{0,2},{1,3},{2,4},{3,5},{8,10},{9,11},{10,12},{11,13},{16,18},{17,... | collective-permute-start | bytes 983048 | tf_op jit(solution)/shard_map/ppermute | solution.py:16
  782.6 16.3 %collective-permute-start.52 = (bf16[3,128,256]{2,1,0:T(8,128)(2,1)S(1)}, bf16[3,128,256]{2,1,0:T(8,128)(2,1)S(1)}, u32[]{:S(2)}, u32[]{:S(2)}) collective-permute-start(bf16[3,128,256]{2,1,0:T(8,128)(2,1)S(1)} %get-tuple-element.267), channel_id=1, source_target_pairs={{0,2},{1,3},{8,10},{9,11},{16,18},{17,19},{24,26},{25,27}} | collective-permute-start | bytes 589832 | tf_op jit(solution)/shard_map/ppermute | solution.py:16
  786.7 18.0 %collective-permute-start.55 = (bf16[3,128,256]{2,1,0:T(8,128)(2,1)S(1)}, bf16[3,128,256]{2,1,0:T(8,128)(2,1)S(1)}, u32[]{:S(2)}, u32[]{:S(2)}) collective-permute-start(bf16[3,128,256]{2,1,0:T(8,128)(2,1)S(1)} %get-tuple-element.268), channel_id=1, source_target_pairs={{6,4},{7,5},{14,12},{15,13},{22,20},{23,21},{30,28},{31,29}} | collective-permute-start | bytes 589832 | tf_op jit(solution)/shard_map/ppermute | solution.py:16
  794.9 14.5 %collective-permute-start.46 = (bf16[5,128,256]{2,1,0:T(8,128)(2,1)S(1)}, bf16[5,128,256]{2,1,0:T(8,128)(2,1)S(1)}, u32[]{:S(2)}, u32[]{:S(2)}) collective-permute-start(bf16[5,128,256]{2,1,0:T(8,128)(2,1)S(1)} %get-tuple-element.236), channel_id=1, source_target_pairs={{4,2},{5,3},{6,4},{7,5},{12,10},{13,11},{14,12},{15,13},{20,18},{2... | collective-permute-start | bytes 983048 | tf_op jit(solution)/shard_map/ppermute | solution.py:16
  803.4 15.1 %collective-permute-start.65 = (bf16[9,128,256]{2,1,0:T(8,128)(2,1)S(1)}, bf16[9,128,256]{2,1,0:T(8,128)(2,1)S(1)}, u32[]{:S(2)}, u32[]{:S(2)}) collective-permute-start(bf16[9,128,256]{2,1,0:T(8,128)(2,1)S(1)} %fusion.36), channel_id=1, source_target_pairs={{2,0},{3,1},{4,2},{5,3},{6,4},{7,5},{10,8},{11,9},{12,10},{13,11},... | collective-permute-start | bytes 1769480 | tf_op jit(solution)/shard_map/ppermute | solution.py:16
  804.7 33.5 %collective-permute-start.44 = (bf16[5,128,256]{2,1,0:T(8,128)(2,1)S(1)}, bf16[5,128,256]{2,1,0:T(8,128)(2,1)S(1)}, u32[]{:S(2)}, u32[]{:S(2)}) collective-permute-start(bf16[5,128,256]{2,1,0:T(8,128)(2,1)S(1)} %get-tuple-element.235), channel_id=1, source_target_pairs={{0,2},{1,3},{2,4},{3,5},{4,6},{5,7},{8,10},{9,11},{10,12},{11,13},... | collective-permute-start | bytes 983048 | tf_op jit(solution)/shard_map/ppermute | solution.py:16
  812.9 25.3 %collective-permute-start.47 = (bf16[5,128,256]{2,1,0:T(8,128)(2,1)S(1)}, bf16[5,128,256]{2,1,0:T(8,128)(2,1)S(1)}, u32[]{:S(2)}, u32[]{:S(2)}) collective-permute-start(bf16[5,128,256]{2,1,0:T(8,128)(2,1)S(1)} %fusion.43), channel_id=1, source_target_pairs={{2,0},{3,1},{4,2},{5,3},{6,4},{7,5},{10,8},{11,9},{12,10},{13,11},... | collective-permute-start | bytes 983048 | tf_op jit(solution)/shard_map/ppermute | solution.py:16
  814.2 23.7 %collective-permute-start.57 = (bf16[3,128,256]{2,1,0:T(8,128)(2,1)S(1)}, bf16[3,128,256]{2,1,0:T(8,128)(2,1)S(1)}, u32[]{:S(2)}, u32[]{:S(2)}) collective-permute-start(bf16[3,128,256]{2,1,0:T(8,128)(2,1)S(1)} %fusion.73), channel_id=1, source_target_pairs={{2,0},{3,1},{4,2},{5,3},{6,4},{7,5},{10,8},{11,9},{12,10},{13,11},... | collective-permute-start | bytes 589832 | tf_op jit(solution)/shard_map/ppermute | solution.py:16
  818.7 38.0 %collective-permute-start.66 = (bf16[9,128,256]{2,1,0:T(8,128)(2,1)S(1)}, bf16[9,128,256]{2,1,0:T(8,128)(2,1)S(1)}, u32[]{:S(2)}, u32[]{:S(2)}) collective-permute-start(bf16[9,128,256]{2,1,0:T(8,128)(2,1)S(1)} %fusion.40), channel_id=1, source_target_pairs={{0,16},{8,24},{16,0},{24,8},{1,17},{9,25},{17,1},{25,9},{2,18},{10... | collective-permute-start | bytes 1769480 | tf_op jit(solution)/shard_map/ppermute | solution.py:16
  838.3 19.6 %collective-permute-start.48 = (bf16[5,128,256]{2,1,0:T(8,128)(2,1)S(1)}, bf16[5,128,256]{2,1,0:T(8,128)(2,1)S(1)}, u32[]{:S(2)}, u32[]{:S(2)}) collective-permute-start(bf16[5,128,256]{2,1,0:T(8,128)(2,1)S(1)} %fusion.47), channel_id=1, source_target_pairs={{0,16},{8,24},{16,0},{24,8},{1,17},{9,25},{17,1},{25,9},{2,18},{10... | collective-permute-start | bytes 983048 | tf_op jit(solution)/shard_map/ppermute | solution.py:16
  843.4 15.1 %collective-permute-start.59 = (bf16[2,3,128,256]{3,2,1,0:T(8,128)(2,1)}, bf16[2,3,128,256]{3,2,1,0:T(8,128)(2,1)S(1)}, u32[]{:S(2)}, u32[]{:S(2)}) collective-permute-start(bf16[2,3,128,256]{3,2,1,0:T(8,128)(2,1)} %pad_maximum_fusion.20), channel_id=1, source_target_pairs={{0,8},{8,0},{16,24},{24,16},{1,9},{9,1},{17,25},{25,17},{2,10},{10... | collective-permute-start | bytes 1179656 | tf_op jit(solution)/shard_map/ppermute | solution.py:16
  857.9 25.6 %collective-permute-start.67 = (bf16[2,9,128,256]{3,2,1,0:T(8,128)(2,1)}, bf16[2,9,128,256]{3,2,1,0:T(8,128)(2,1)}, u32[]{:S(2)}, u32[]{:S(2)}) collective-permute-start(bf16[2,9,128,256]{3,2,1,0:T(8,128)(2,1)} %pad_maximum_fusion.13), channel_id=1, source_target_pairs={{0,8},{8,0},{16,24},{24,16},{1,9},{9,1},{17,25},{25,17},{2,10},{10... | collective-permute-start | bytes 3538952 | tf_op jit(solution)/shard_map/ppermute | solution.py:16
  857.9 24.2 %collective-permute-start.49 = (bf16[2,5,128,256]{3,2,1,0:T(8,128)(2,1)S(1)}, bf16[2,5,128,256]{3,2,1,0:T(8,128)(2,1)}, u32[]{:S(2)}, u32[]{:S(2)}) collective-permute-start(bf16[2,5,128,256]{3,2,1,0:T(8,128)(2,1)S(1)} %pad_maximum_fusion.16), channel_id=1, source_target_pairs={{0,8},{8,0},{16,24},{24,16},{1,9},{9,1},{17,25},{25,17},{2,10},{10... | collective-permute-start | bytes 1966088 | tf_op jit(solution)/shard_map/ppermute | solution.py:16
  (111 other events, 1499.7 us)

commit v3 on v2

--- a/solution.py
+++ b/solution.py
@@ -168,6 +168,13 @@
     return total.astype(BF)
 
 
+def in_blocks(matrix):
+    return [
+        matrix[:, left : left + 256].reshape(8, -1, 128, 256)
+        for left in range(0, matrix.shape[1], 256)
+    ]
+
+
 class Reduce:
     def __init__(self, entries):
         group = lax.axis_index("items")
@@ -188,47 +195,71 @@
         )
         return dot_tn(entry[0], picked).astype(BF) if isinstance(entry, tuple) else picked
 
-    def over_y(self):
-        kept = [self.halves(entry, self.core) for entry in self.entries]
-
-        def blocks(side):
-            found = []
-            for own, got in zip(kept, self.got):
-                width = own.shape[1] // 2
-                for left in range(side * width, (side + 1) * width, 256):
-                    block = add_low(own[:, left : left + 256], got[:, left : left + 256])
-                    found.append(block.reshape(8, -1, 128, 256))
-            return jnp.concatenate(found, axis=1)
-
-        self.kept, self.away = blocks(0), blocks(1)
-        self.got = swap_y(self.away)
+    def over_y(self, *before, merged=True):
+        def quarter(entry, got, y, side):
+            wide = entry[1] if isinstance(entry, tuple) else entry
+            picked = column_share(wide, 2 * y + self.core)
+            if isinstance(entry, tuple):
+                picked = dot_tn(entry[0], picked)
+            width = picked.shape[1]
+            return add_low(picked, got[:, side * width : (side + 1) * width])
+
+        def quarters(y, side):
+            found = [quarter(entry, got, y, side) for entry, got in zip(self.entries, self.got)]
+            return [jnp.concatenate([b for m in found for b in in_blocks(m)], axis=1)] if merged else found
+
+        self.away = quarters(1 - self.y, 1)
+        if before:
+            self.away[0] = tie(self.away[0], *before)
+        self.kept = quarters(self.y, 0)
+        self.got = [swap_y(v) for v in self.away]
         return self.away
 
     def over_x(self, *before):
         me = lax.axis_index("blk")
-        halves = [v.reshape((4, 2) + v.shape[1:]) for v in (self.kept, self.got)]
-        away = add_low(*(lax.dynamic_index_in_dim(v, 1 - me % 2, 1, keepdims=False) for v in halves))
+
+        def blocks(x):
+            found = []
+            for kept, got in zip(self.kept, self.got):
+                rows = kept.shape[0] // 8 if kept.ndim == 2 else 1
+                shape = (4, 2, rows) + kept.shape[1:]
+                own, came = (
+                    lax.dynamic_index_in_dim(v.reshape(shape), x, 1, keepdims=False)
+                    for v in (kept, got)
+                )
+                if kept.ndim > 2:
+                    found.append(add_low(own[:, 0], came[:, 0]))
+                    continue
+                for left in range(0, shape[3], 256):
+                    block = add_low(own[..., left : left + 256], came[..., left : left + 256])
+                    found.append(block.reshape(4, -1, 128, 256))
+            return found[0] if len(found) == 1 else jnp.concatenate(found, axis=1)
+
+        away = blocks(1 - me % 2)
         if before:
             away = tie(away, *before)
-        self.kept = [lax.dynamic_index_in_dim(v, me % 2, 1, keepdims=False) for v in halves]
+        self.kept = blocks(me % 2)
         self.got = swap_x(away)
         return away
 
-    def over_z(self, *before):
+    def join(self, other):
+        self.kept = jnp.concatenate([self.kept, other.kept], axis=1)
+        self.got = jnp.concatenate([self.got, other.got], axis=1)
+        self.shapes = self.shapes + other.shapes
+
+    def over_z(self, first=(), second=(), third=()):
         z = lax.axis_index("blk") // 2
-        kept = add_low(*self.kept, self.got)
-        if before:
-            kept = tie(kept, *before)
+        kept = add_low(self.kept, self.got)
 
         def part(place):
             return lax.dynamic_index_in_dim(kept, jnp.clip(place, 0, 3), 0, keepdims=False)
 
-        up = hop(0, 0, 1)(part(z + 3))
-        down = hop(3, 3, -1)(part(z - 3))
-        up = hop(0, 1, 1)(add_low(part(z + 2), up))
-        down = hop(2, 3, -1)(add_low(part(z - 2), down))
-        up = hop(0, 2, 1)(add_low(part(z + 1), up))
-        down = hop(1, 3, -1)(add_low(part(z - 1), down))
+        up = hop(0, 0, 1)(tie(part(z + 3), *first))
+        down = hop(3, 3, -1)(tie(part(z - 3), *first))
+        up = hop(0, 1, 1)(tie(add_low(part(z + 2), up), *second))
+        down = hop(2, 3, -1)(tie(add_low(part(z - 2), down), *second))
+        up = hop(0, 2, 1)(tie(add_low(part(z + 1), up), *third))
+        down = hop(1, 3, -1)(tie(add_low(part(z - 1), down), *third))
         self.done = add_low(part(z), up, down)
         return self.done
 
@@ -334,7 +365,13 @@
     return keys, values
 
 
-def cross_forward_kernel(lengths, q_ref, m_ref, w_ref, shift_ref, out_ref, log_ref, kv_ref):
+def cross_forward_kernel(lengths, q_ref, m_ref, w_ref, shift_ref, *refs):
+    out_ref, log_ref, kv_ref, all_ref = refs[-4:]
+
+    @pl.when(pl.program_id(0) == 0)
+    def _():
+        all_ref[0] = m_ref[...]
+
     kv_ref[...] = (dot_nn(m_ref[...], w_ref[...]) + shift_ref[...]).astype(BF)
     masks = slot_masks(lengths[0], kv_ref.shape[0] // CHUNKS, 2 * q_ref.shape[0])
     for p in range(PAIRS):
@@ -344,9 +381,8 @@
         log_ref[p] = log_total
 
 
-def cross_backward_kernel(
-    lengths, q_ref, grad_ref, log_ref, kv_ref, w_ref, dq_ref, sum_ref, dkv_ref, back_ref, total_ref
-):
+def cross_backward_kernel(lengths, q_ref, grad_ref, log_ref, kv_ref, w_ref, *refs):
+    dq_ref, sum_ref, dkv_ref, back_ref, total_ref = refs[-5:]
     step = pl.program_id(0)
     rows = kv_ref.shape[0] // CHUNKS
     masks = slot_masks(lengths[0], rows, 2 * q_ref.shape[0])
@@ -359,12 +395,12 @@
         dq_ref[:, span] = dq
         total = None
         for c in range(CHUNKS):
-            dkv_ref[rows * c : rows * (c + 1), 256 * p : 256 * p + 128] = dks[c]
-            dkv_ref[rows * c : rows * (c + 1), 256 * p + 128 : 256 * p + 256] = dvs[c]
+            dkv_ref[0, rows * c : rows * (c + 1), 256 * p : 256 * p + 128] = dks[c]
+            dkv_ref[0, rows * c : rows * (c + 1), 256 * p + 128 : 256 * p + 256] = dvs[c]
             add = dvs[c].astype(F32).sum(axis=0, keepdims=True)
             total = add if total is None else total + add
         sum_ref[:, span] = total
-    back = dot_nt(dkv_ref[...], w_ref[...])
+    back = dot_nt(dkv_ref[0], w_ref[...])
 
     @pl.when(step == 0)
     def _():
@@ -376,7 +412,8 @@
 
     @pl.when(step == pl.num_programs(0) - 1)
     def _():
-        back_ref[...] = total_ref[...].astype(BF)
+        shape = (back_ref.shape[0],) + back_ref.shape[2:]
+        back_ref[:, 0] = total_ref[...].astype(BF).reshape(shape)
 
 
 def cross_specs(length, slots, width):
@@ -390,52 +427,72 @@
     return small, line, big, logs, whole, weight, shift
 
 
-def cross_forward(lengths, queries, source, weight_pair, pair_shift):
+def cross_forward(lengths, queries, source, weight_pair, pair_shift, item, items, gathered):
     length, width = queries.shape
     slots = source.shape[0]
     small, _, big, logs, whole, weight, shift = cross_specs(length, slots, width)
+    given = [lengths, queries, source, weight_pair, pair_shift]
+    before = [] if gathered is None else [gathered]
     return pl.pallas_call(
         cross_forward_kernel,
         out_shape=[
             jax.ShapeDtypeStruct(queries.shape, BF),
             jax.ShapeDtypeStruct((width // 128, 1, 2 * length), F32),
             jax.ShapeDtypeStruct((slots, 2 * width), BF),
+            jax.ShapeDtypeStruct((items, slots, width), BF),
         ],
         grid_spec=pltpu.PrefetchScalarGridSpec(
             num_scalar_prefetch=1,
             grid=(width // (128 * PAIRS),),
-            in_specs=[small, whole, weight, shift],
-            out_specs=[small, logs, big],
+            in_specs=[small, whole, weight, shift] + [ANY] * len(before),
+            out_specs=[small, logs, big, pl.BlockSpec((1, slots, width), lambda p, *_: (item, 0, 0))],
         ),
+        input_output_aliases={5: 3} if before else {},
         compiler_params=pltpu.CompilerParams(vmem_limit_bytes=VMEM_BYTES),
         cost_estimate=pl.CostEstimate(
             flops=4 * slots * width * width + 16 * length * slots * width,
-            bytes_accessed=2 * (source.size + weight_pair.size + 2 * source.size),
+            bytes_accessed=2 * (source.size + weight_pair.size + 3 * source.size),
             transcendentals=length * slots * HEADS,
         ),
         name="cross_forward",
-    )(lengths, queries, source, weight_pair, pair_shift)
-
-
-def cross_backward(lengths, queries, grads, logs_in, kv, weight_pair):
+    )(*given, *before)
+
+
+def cross_backward(lengths, queries, grads, logs_in, kv, weight_pair, item, items, dkv, back):
     length, width = queries.shape
     slots = kv.shape[0]
     small, line, big, logs, whole, weight, _ = cross_specs(length, slots, width)
+    given = [lengths, queries, grads, logs_in, kv, weight_pair]
+    shards, together = back[:2] if isinstance(back, tuple) else back.shape[:2]
+    aliases = {}
+    if not isinstance(dkv, tuple):
+        aliases[len(given)] = 2
+        given.append(dkv)
+    if not isinstance(back, tuple):
+        aliases[len(given)] = 3
+        given.append(back)
+    place = item % together
     return pl.pallas_call(
         cross_backward_kernel,
         out_shape=[
             jax.ShapeDtypeStruct(queries.shape, BF),
             jax.ShapeDtypeStruct((1, width), F32),
-            jax.ShapeDtypeStruct(kv.shape, BF),
-            jax.ShapeDtypeStruct((slots, width), BF),
+            jax.ShapeDtypeStruct((items, slots, 2 * width), BF),
+            jax.ShapeDtypeStruct((shards, together, slots // shards, width), BF),
         ],
         grid_spec=pltpu.PrefetchScalarGridSpec(
             num_scalar_prefetch=1,
             grid=(width // (128 * PAIRS),),
-            in_specs=[small, small, logs, big, weight],
-            out_specs=[small, line, big, whole],
+            in_specs=[small, small, logs, big, weight] + [ANY] * len(aliases),
+            out_specs=[
+                small,
+                line,
+                pl.BlockSpec((1, slots, 256 * PAIRS), lambda p, *_: (item, 0, p)),
+                pl.BlockSpec((shards, 1, slots // shards, width), lambda p, *_: (0, place, 0, 0)),
+            ],
             scratch_shapes=[pltpu.VMEM((slots, width), F32)],
         ),
+        input_output_aliases=aliases,
         compiler_params=pltpu.CompilerParams(vmem_limit_bytes=VMEM_BYTES),
         cost_estimate=pl.CostEstimate(
             flops=4 * slots * width * width + 40 * length * slots * width,
@@ -443,7 +500,7 @@
             transcendentals=length * slots * HEADS,
         ),
         name="cross_backward",
-    )(lengths, queries, grads, logs_in, kv, weight_pair)
+    )(*given)
 
 
 def self_mask(seg_row, seg_column, length):
@@ -551,7 +608,7 @@
 
 
 def column_sum(values):
-    return jnp.sum(values.astype(F32), axis=0)
+    return dot_nn(jnp.ones((8, values.shape[0]), BF), values)[0]
 
 
 def interleave(matrix):
@@ -608,10 +665,10 @@
             own, own_two = share_of(first, 4, 1), share_of(second, 4)
             across, across_two = swap_x(own), swap_x(own_two)
             across_y, across_two_y = swap_y(across), swap_y(across_two)
-            line = along_z(own)
-            own_two = tie(own_two, line, across, across_two)
+            line = along_z(own, (across,))
+            own_two = tie(own_two, line, across_y, across_two)
             far, line_y = swap_x(line), swap_y(line)
-            line_two = along_z(own_two, (far, across_y, across_two_y))
+            line_two = along_z(own_two, (far, across_two_y))
             pair = tie(jnp.stack(sent[:half], axis=1), line_two, line_y)
             pair = back_and_forth(pair)
             arrived = [pair[:, i] for i in range(half)]
@@ -661,7 +718,7 @@
         ).astype(BF).reshape(three)
         pair_shift = interleave(jnp.concatenate([no_shift, shift_rows[4]])[None])
         item_lengths = [memory_lengths[i : i + 1] for i in range(item_count)]
-        sources, kvs, outs, cross_logs = [], [], [], []
+        gathered, kvs, outs, cross_logs = None, [], [], []
         if tuned:
             far_two = tie(far_two, cross_queries)
             far_two_y = swap_y(far_two)
@@ -670,7 +727,7 @@
                 arrived.append(back_and_forth(tie(sent[i], cross_queries, far_two, line_two_y)))
             elif tuned and i > half:
                 arrived.append(
-                    back_and_forth(tie(sent[i], *arrived[half:], outs[0], far_two_y))
+                    back_and_forth(tie(sent[i], *arrived[half:], outs[half - 1], far_two_y))
                 )
             source = arrived[i]
             if tuned and i == item_count - 1:
@@ -680,10 +737,10 @@
                 )
                 source = tie(source, outs[i - 1], feed_up)
             source = source.reshape(-1, width)
-            out, logs, kv = cross_forward(
-                item_lengths[i], cross_queries[i], source, cross_pair, pair_shift
+            out, logs, kv, gathered = cross_forward(
+                item_lengths[i], cross_queries[i], source, cross_pair, pair_shift,
+                i, item_count, gathered,
             )
-            sources.append(source)
             kvs.append(kv)
             outs.append(out)
             cross_logs.append(logs)
@@ -713,30 +770,30 @@
         cross_grad, second_gain, second_shift = second_norm_back(second_grad)
         cross_low = cross_grad.astype(BF)
         grad_cross_out = dot_tn(cross_attended, cross_low)
-        if tuned:
-            sums_one = Reduce(
-                [(activation_low, down_low), (second_low, upward_low), (cross_attended, cross_low)]
-            )
         cross_incoming = dot_nt(cross_low, cross_out).astype(BF).reshape(three)
-        if tuned:
-            cross_incoming = tie(cross_incoming, *sums_one.sent)
-        dqs, value_sums, grad_pair, pair_grads, memory_back, backs = [], 0.0, 0.0, [], [], []
+        dqs, value_sums, pair_grad, memory_back = [], 0.0, (), []
         before = None
         for i in range(item_count):
             incoming = cross_incoming[i] if before is None else tie(cross_incoming[i], before)
             if tuned and i == 1:
-                incoming = tie(incoming, sums_one.over_y())
-            dq, sums, pair_grad, before = cross_backward(
-                item_lengths[i], cross_queries[i], incoming, cross_logs[i], kvs[i], cross_pair
+                lefts = [tie(v, dqs[0]) for v in (activation_low, second_low, cross_attended)]
+                sums_one = Reduce(list(zip(lefts, (down_low, upward_low, cross_low))))
+            if tuned and i == 2:
+                incoming = tie(incoming, *sums_one.over_y(merged=False))
+            if i % half == 0:
+                back = (blocks.shape[0], half)
+            dq, sums, pair_grad, back = cross_backward(
+                item_lengths[i], cross_queries[i], incoming, cross_logs[i], kvs[i], cross_pair,
+                i, item_count, pair_grad, back,
             )
-            backs.append(before.reshape(arrived[i].shape))
-            if len(backs) == half:
-                memory_back.append(back_and_forth(jnp.stack(backs, axis=1)))
-                backs = []
+            before = dq
+            if i % half == half - 1:
+                memory_back.append(back_and_forth(back))
             value_sums = value_sums + sums[0]
-            pair_grads.append(pair_grad)
             dqs.append(dq)
-        cross_dq = tie(jnp.concatenate(dqs), before)
+        cross_dq = jnp.concatenate(dqs)
+        all_sources = gathered.reshape(-1, width)
+        all_grads = pair_grad.reshape(-1, 2 * width)
         memory_grad = jnp.concatenate(memory_back, axis=1).reshape(memory.shape)
         cross_query_low = cross_dq * BF(query_scale)
         grad_cross_query = dot_tn(hidden_low, cross_query_low)
@@ -745,10 +802,14 @@
         self_low = first_grad.astype(BF)
         grad_self_out = dot_tn(attended, self_low)
         self_incoming = dot_nt(self_low, self_out).astype(BF).reshape(three)
+        if tuned:
+            grad_pair = dot_tn(all_sources, all_grads).astype(BF)
+            sums_two = Reduce([(tie(hidden_low, memory_back[0]), cross_query_low), grad_pair])
+            self_incoming = tie(self_incoming, sums_one.over_x(), *sums_two.sent)
         joined_grad = self_backward(segment_ids, qkv, self_incoming, self_logs)
         joined_grad = joined_grad.reshape(row_count, 3 * width)
         if tuned:
-            joined_grad = tie(joined_grad, sums_one.got, memory_back[0])
+            joined_grad = tie(joined_grad, *sums_two.over_y())
         grad_self = dot_tn(token_rows, joined_grad)
         decoder_grad = (
             (first_grad + dot_nt(joined_grad, self_proj)).astype(BF).reshape(decoder_in.shape)
@@ -789,30 +850,18 @@
                     packed.reshape(-1, 8 * count).astype(BF),
                 ]
             )
-            pair_grads[0] = tie(pair_grads[0], *sums_three.sent)
-            away = sums_three.over_y()
-            for i in range(1, item_count):
-                pair_grads[i] = tie(pair_grads[i], away)
-            sums_one.over_x(joined_grad)
-            for source, pair_grad in zip(sources, pair_grads):
-                grad_pair = grad_pair + dot_tn(source, pair_grad)
-            sums_two = Reduce(
-                [(hidden_low, cross_query_low), tie(grad_pair.astype(BF), sums_one.got)]
-            )
-            sums_two.over_y()
-            sums_one.over_z(sums_two.away)
-            sums_three.over_x(sums_two.away)
+            sums_three.over_y()
             sums_two.over_x()
+            sums_three.over_x(memory_back[1])
+            sums_one.over_z((), (sums_two.got,), (sums_three.got,))
+            sums_three.join(sums_two)
             sums_three.over_z()
-            sums_two.over_z()
             down, up, out = sums_one.share()
-            (query, pair) = sums_two.share()
-            (own_out, own_in, sums) = sums_three.share()
+            own_out, own_in, sums, query, pair = sums_three.share()
             shift_share, gain_share = sums[:10, :count], sums[10:13, :count]
             feed_share = sums[13:17, :count].reshape(-1)
         else:
-            for source, pair_grad in zip(sources, pair_grads):
-                grad_pair = grad_pair + dot_tn(source, pair_grad)
+            grad_pair = dot_tn(all_sources, all_grads)
 
             def share(value, dim=0):
                 part = lax.psum_scatter(value, "blk", scatter_dimension=dim, tiled=True)

time: 904 us -> 839 us (0.928)
  waiting for transfers between devices: 227 us -> 193 us
  other arithmetic: 96.7 us -> 80.2 us
  starting transfers between devices: 146 us -> 132 us
    ppermute x68 -> x62, waiting for transfers between devices: 219 us -> 177 us  [move(): return lambda value: lax.ppermute(value, axis, pairs)]
    ppermute x68 -> x62, starting transfers between devices: 115 us -> 101 us  [move(): return lambda value: lax.ppermute(value, axis, pairs)]
    concatenate x11, local copies, waits for them, and re-layouts: 13.1 us -> 0.61 us  [share(): results.append(jnp.concatenate(strips, axis=1))]
    convert_element_type x26 -> x16, other arithmetic: 41.6 us -> 34.5 us  [add_low(): return total.astype(BF)]
    unnamed x268 -> x278, local copies, waits for them, and re-layouts: 50.3 us -> 43.5 us
    dot_general x16 -> x19, matrix products: 69.8 us -> 72 us  [dot_tn(): lax.dot_general(left, right, (((0,), (0,)), ((), ())), preferred_element_...]
  transfers between devices with their start and end apart: 73 -> 67, of which waited for: 21 -> 25; matrix products, arithmetic and copies ran while one was open for 27% -> 28% of each run, Pallas kernels for 16% -> 17%
where the time goes in v3:
time: 839 us; the launch traced here: 831 us
  waiting for transfers between devices  193 us (23%)
  Pallas kernels  179 us (21%)
  matrix products  142 us (17%)
  starting transfers between devices  132 us (16%)
  local copies, waits for them, and re-layouts  102 us (12%)
  other arithmetic  80.2 us (10%)
    ppermute x62, waiting for transfers between devices, move(): return lambda value: lax.ppermute(value, axis, pairs)  177 us
    ppermute x62, starting transfers between devices, move(): return lambda value: lax.ppermute(value, axis, pairs)  101 us
    dot_general x19, matrix products, dot_tn(): lax.dot_general(left, right, (((0,), (0,)), ((), ())), preferred_element_...  72 us
    pallas_call x4, Pallas kernels, cross_backward(): pl.pallas_call(cross_backward_kernel, out_shape=[jax.ShapeDtypeStruct(que...  71.6 us
    pallas_call x4, Pallas kernels, cross_forward(): pl.pallas_call(cross_forward_kernel, out_shape=[jax.ShapeDtypeStruct(quer...  61.7 us
    unnamed x278, local copies, waits for them, and re-layouts  43.5 us
    dot_general x6, matrix products, dot_nt(): lax.dot_general(left, right, (((1,), (1,)), ((), ())), preferred_element_...  36.4 us
    convert_element_type x16, other arithmetic, add_low(): return total.astype(BF)  34.5 us
  transfers between devices with their start and end apart: 67, of which 25 were waited for; matrix products, arithmetic and copies ran while one was open for 28% of the time, Pallas kernels for 17%

profile of v3, /device:TPU:1, one launch (start us, length us, event | category | flops | bytes accessed | tf_op | source)
XLA Modules:
  0.0 831.1 jit_solution(12139939532463084564)
XLA Ops:
  6.1 4.1 collective-permute-start.2
  12.7 7.3 collective-permute-done.2
  41.1 9.8 %collective-permute-done.6 = bf16[128,1920]{1,0:T(8,128)(2,1)S(1)} collective-permute-done((bf16[128,1920]{1,0:T(8,128)(2,1)}, bf16[128,1920]{1,0:T(8,128)(2,1)S(1)}, u32[]{:S(2)}, u32[]{:S(2)}) %collective-permute-start.6) | collective-permute-done | bytes 491552 | tf_op jit(solution)/shard_map/ppermute | solution.py:16
  56.5 6.6 collective-permute-done.17
  67.3 4.8 stack.165
  73.3 8.5 %collective-permute-done.7.refs_7_ = bf16[3,128,1920]{2,1,0:T(8,128)(2,1)} collective-permute-done((bf16[3,128,1920]{2,1,0:T(8,128)(2,1)S(1)}, bf16[3,128,1920]{2,1,0:T(8,128)(2,1)}, u32[]{:S(2)}, u32[]{:S(2)}) %collective-permute-start.7) | collective-permute-done | bytes 1474592 | tf_op jit(solution)/shard_map/ppermute | solution.py:16
  84.0 10.4 %collective-permute-done.22 = bf16[128,2304]{1,0:T(8,128)(2,1)S(1)} collective-permute-done((bf16[128,2304]{1,0:T(8,128)(2,1)S(1)}, bf16[128,2304]{1,0:T(8,128)(2,1)S(1)}, u32[]{:S(2)}, u32[]{:S(2)}) %collective-permute-start.22) | collective-permute-done | bytes 589856 | tf_op jit(solution)/shard_map/ppermute | solution.py:16
  96.7 6.9 all-to-all-start
  106.7 10.8 %collective-permute-start.11 = (bf16[4,128,1920]{2,1,0:T(8,128)(2,1)S(1)}, bf16[4,128,1920]{2,1,0:T(8,128)(2,1)}, u32[]{:S(2)}, u32[]{:S(2)}) collective-permute-start(bf16[4,128,1920]{2,1,0:T(8,128)(2,1)S(1)} %pad_maximum_fusion.5.refs_6_), channel_id=1, source_target_pairs={{0,8},{8,0},{16,24},{24,16},{1,9},{9,1},{17,25},{25,17},{2,10},{10... | collective-permute-start | bytes 5898248 | tf_op jit(solution)/shard_map/ppermute | solution.py:16
  117.5 2.9 pad_maximum_fusion.6.refs_8_
  121.0 6.3 collective-permute-done.10.refs_9_
  127.3 11.4 %collective-permute-start.14 = (bf16[3,128,1920]{2,1,0:T(8,128)(2,1)}, bf16[3,128,1920]{2,1,0:T(8,128)(2,1)}, u32[]{:S(2)}, u32[]{:S(2)}) collective-permute-start(bf16[3,128,1920]{2,1,0:T(8,128)(2,1)} %collective-permute-done.10.refs_9_), channel_id=1, source_target_pairs={{0,8},{8,0},{16,24},{24,16},{1,9},{9,1},{17,25},{25,17},{2,10},{10... | collective-permute-start | bytes 4423688 | tf_op jit(solution)/shard_map/ppermute | solution.py:16
  140.2 4.9 slice_bitcast_fusion
  147.9 12.9 %place_rows.2 = (bf16[1024,128]{1,0:T(8,128)(2,1)}, bf16[1024,3072]{1,0:T(8,128)(2,1)}, bf16[1024,1024]{1,0:T(8,128)(2,1)}, bf16[1024,1024]{1,0:T(8,128)(2,1)}, bf16[1024,2048]{1,0:T(8,128)(2,1)}) custom-call(s32[10]{0:T(128)} %stack.136.refs_0_, bf16[128,128]{1,0:T(8,128)(2,1)} %get-tuple-element.269.refs_1_, bf16[128,3072]{1,0:T(8,128)(2,1)} %refs_2_.2, ...), custom_call_target="tpu_custom_call" | custom-call | bytes 29884416 | tf_op jit(solution)/shard_map/place_rows/pallas_call | solution.py:148
  161.6 7.6 multiply_convert_fusion.2
  169.2 6.0 self_forward.1
  175.2 3.3 fusion.177
  183.3 15.5 %collective-permute-done.23.refs_5_ = bf16[3,128,2304]{2,1,0:T(8,128)(2,1)} collective-permute-done((bf16[3,128,2304]{2,1,0:T(8,128)(2,1)S(1)}, bf16[3,128,2304]{2,1,0:T(8,128)(2,1)}, u32[]{:S(2)}, u32[]{:S(2)}) %collective-permute-start.23) | collective-permute-done | bytes 1769504 | tf_op jit(solution)/shard_map/ppermute | solution.py:16
  200.1 9.2 %all-to-all-start.1 = ((bf16[8,128,1024]{2,1,0:T(8,128)(2,1)}), bf16[8,128,1024]{2,1,0:T(8,128)(2,1)}, u32[]{:S(2)}, u32[]{:S(2)}) async-start(bf16[8,128,1024]{2,1,0:T(8,128)(2,1)} %get-tuple-element.97), calls=%async_computation.1 | async-start | bytes 4194304 | tf_op jit(solution)/shard_map/all_to_all | solution.py:603
  213.2 4.8 fusion.167
  218.1 15.3 %cross_forward.4 = (bf16[128,1024]{1,0:T(8,128)(2,1)}, f32[8,1,256]{2,1,0:T(1,128)}, bf16[1024,2048]{1,0:T(8,128)(2,1)}, bf16[4,1024,1024]{2,1,0:T(8,128)(2,1)}) custom-call(s32[1]{0:T(128)} %get-tuple-element.272.lengths, bf16[128,1024]{1,0:T(8,128)(2,1)} %get-tuple-element.252.q_ref, bf16[1024,1024]{1,0:T(8,128)(2,1)} %bitcast.533, ...), custom_call_target="tpu_custom_call" | custom-call | flops 6442450944 | bytes 12582912 | tf_op jit(solution)/shard_map/cross_forward/pallas_call | solution.py:436
  233.3 15.3 %cross_forward.5 = (bf16[128,1024]{1,0:T(8,128)(2,1)}, f32[8,1,256]{2,1,0:T(1,128)}, bf16[1024,2048]{1,0:T(8,128)(2,1)}, bf16[4,1024,1024]{2,1,0:T(8,128)(2,1)}) custom-call(s32[1]{0:T(128)} %get-tuple-element.271.lengths, bf16[128,1024]{1,0:T(8,128)(2,1)} %get-tuple-element.251.q_ref, ...), custom_call_target="tpu_custom_call", output_to_operand_aliasing={{3}: (5, {})} | custom-call | flops 6442450944 | bytes 12582912 | tf_op jit(solution)/shard_map/cross_forward/pallas_call | solution.py:436
  249.0 8.8 %all-to-all-done.1 = bf16[8,128,1024]{2,1,0:T(8,128)(2,1)} async-done(((bf16[8,128,1024]{2,1,0:T(8,128)(2,1)}), bf16[8,128,1024]{2,1,0:T(8,128)(2,1)}, u32[]{:S(2)}, u32[]{:S(2)}) %all-to-all-start.1) | async-done | bytes 2097184 | tf_op jit(solution)/shard_map/all_to_all | solution.py:603
  257.8 4.6 all-to-all-start.2
  262.4 3.1 pad_maximum_fusion.1.refs_4_
  270.1 15.3 %cross_forward.6 = (bf16[128,1024]{1,0:T(8,128)(2,1)}, f32[8,1,256]{2,1,0:T(1,128)}, bf16[1024,2048]{1,0:T(8,128)(2,1)}, bf16[4,1024,1024]{2,1,0:T(8,128)(2,1)}) custom-call(s32[1]{0:T(128)} %get-tuple-element.273.lengths, bf16[128,1024]{1,0:T(8,128)(2,1)} %get-tuple-element.250.q_ref, ...), custom_call_target="tpu_custom_call", output_to_operand_aliasing={{3}: (5, {})} | custom-call | flops 6442450944 | bytes 12582912 | tf_op jit(solution)/shard_map/cross_forward/pallas_call | solution.py:436
  285.4 16.0 %place_rows.3 = (bf16[1024,1024]{1,0:T(8,128)(2,1)}, bf16[1024,4096]{1,0:T(8,128)(2,1)}, bf16[4096,1024]{1,0:T(8,128)(2,1)}) custom-call(s32[10]{0:T(128)} %stack.136.refs_0_, bf16[128,1024]{1,0:T(8,128)(2,1)} %refs_1_.1, bf16[128,4096]{1,0:T(8,128)(2,1)} %refs_2_.3, bf16[512,1024]{1,0:T(8,128)(2,1)} %refs_3_.3, ...), custom_call_target="tpu_custom_call" | custom-call | bytes 37748736 | tf_op jit(solution)/shard_map/place_rows/pallas_call | solution.py:148
  301.6 7.4 all-to-all-done.2
  309.0 15.8 %cross_forward.7 = (bf16[128,1024]{1,0:T(8,128)(2,1)}, f32[8,1,256]{2,1,0:T(1,128)}, bf16[1024,2048]{1,0:T(8,128)(2,1)}, bf16[4,1024,1024]{2,1,0:T(8,128)(2,1)}) custom-call(s32[1]{0:T(128)} %get-tuple-element.270.lengths, bf16[128,1024]{1,0:T(8,128)(2,1)} %get-tuple-element.249.q_ref, ...), custom_call_target="tpu_custom_call", output_to_operand_aliasing={{3}: (5, {})} | custom-call | flops 6442450944 | bytes 12582912 | tf_op jit(solution)/shard_map/cross_forward/pallas_call | solution.py:436
  329.0 12.1 %multiply_convert_fusion.1 = (bf16[512,4096]{1,0:T(8,128)(2,1)S(1)}, f32[512,4096]{1,0:T(8,128)}) fusion(f32[4096]{0:T(1024)S(1)} %convert.93, bf16[512,1024]{1,0:T(8,128)(2,1)S(1)} %fusion.18, bf16[1024,4096]{1,0:T(8,128)(2,1)S(1)} %bitcast.599), kind=kOutput, calls=%fused_computation.12 | convolution fusion | flops 4343201792 | bytes 22036480 | tf_op jit(solution)/shard_map/dot_general | solution.py:754
  341.1 4.8 fusion.179
  351.1 14.5 %multiply_convert_fusion = bf16[512,4096]{1,0:T(8,128)(2,1)S(1)} fusion(bf16[512,1024]{1,0:T(8,128)(2,1)S(1)} %add_convert_fusion.16, bf16[4096,1024]{1,0:T(8,128)(2,1)} %get-tuple-element.107, f32[512,4096]{1,0:T(8,128)} %get-tuple-element.279, f32[4096]{0:T(1024)S(1)} %convert.93), kind=kOutput, calls=%fused_computation.11 | convolution fusion | flops 4353687552 | bytes 22036480 | tf_op jit(solution)/shard_map/dot_general | solution.py:289
  365.6 9.2 %multiply_reduce_fusion = (bf16[1024]{0:T(1024)(128)(2,1)S(1)}, f32[512]{0:T(512)S(1)}, bf16[1024]{0:T(1024)(128)(2,1)S(1)}, f32[512,1024]{1,0:T(8,128)S(1)}) fusion(f32[512,1024]{1,0:T(8,128)S(1)} %get-tuple-element.277, f32[512]{0:T(512)S(1)} %fusion.150, f32[512]{0:T(512)S(1)} %broadcast_multiply_fusion.1, f32[1024]{0:T(1024)S(1)} %bitcast.565, ...), kind=kOutput, calls=%fused_computation.53 | convolution fusion | flops 4300207616 | bytes 18890752 | tf_op jit(solution)/shard_map/dot_general | solution.py:289
  379.5 18.0 %cross_backward.4 = (bf16[128,1024]{1,0:T(8,128)(2,1)}, f32[1,1024]{1,0:T(1,128)}, bf16[4,1024,2048]{2,1,0:T(8,128)(2,1)}, bf16[8,2,128,1024]{3,2,1,0:T(8,128)(2,1)}) custom-call(s32[1]{0:T(128)} %get-tuple-element.272.lengths, bf16[128,1024]{1,0:T(8,128)(2,1)} %get-tuple-element.252.q_ref, bf16[128,1024]{1,0:T(8,128)(2,1)} %get-tuple-element.245.grad_ref, ...), custom_call_target="tpu_custom_call" | custom-call | flops 9663676416 | bytes 18874368 | tf_op jit(solution)/shard_map/cross_backward/pallas_call | solution.py:475
  398.6 6.6 convolution_convert_fusion
  407.9 4.4 convolution_convert_fusion.2
  413.6 17.9 %cross_backward.5 = (bf16[128,1024]{1,0:T(8,128)(2,1)}, f32[1,1024]{1,0:T(1,128)}, bf16[4,1024,2048]{2,1,0:T(8,128)(2,1)}, bf16[8,2,128,1024]{3,2,1,0:T(8,128)(2,1)}) custom-call(s32[1]{0:T(128)} %get-tuple-element.271.lengths, bf16[128,1024]{1,0:T(8,128)(2,1)} %get-tuple-element.251.q_ref, ...), custom_call_target="tpu_custom_call", output_to_operand_aliasing={{2}: (6, {}), {3}: (7, {})} | custom-call | flops 9663676416 | bytes 18874368 | tf_op jit(solution)/shard_map/cross_backward/pallas_call | solution.py:475
  431.5 4.7 all-to-all-start.3
  443.9 4.4 add_convert_fusion.5
  449.7 4.3 add_convert_fusion.4
  454.0 17.7 %cross_backward.6 = (bf16[128,1024]{1,0:T(8,128)(2,1)}, f32[1,1024]{1,0:T(1,128)}, bf16[4,1024,2048]{2,1,0:T(8,128)(2,1)}, bf16[8,2,128,1024]{3,2,1,0:T(8,128)(2,1)}) custom-call(s32[1]{0:T(128)} %get-tuple-element.273.lengths, bf16[128,1024]{1,0:T(8,128)(2,1)} %get-tuple-element.250.q_ref, ...), custom_call_target="tpu_custom_call", output_to_operand_aliasing={{2}: (6, {})} | custom-call | flops 9663676416 | bytes 18874368 | tf_op jit(solution)/shard_map/cross_backward/pallas_call | solution.py:475
  471.7 18.1 %cross_backward.7 = (bf16[128,1024]{1,0:T(8,128)(2,1)}, f32[1,1024]{1,0:T(1,128)}, bf16[4,1024,2048]{2,1,0:T(8,128)(2,1)}, bf16[8,2,128,1024]{3,2,1,0:T(8,128)(2,1)}) custom-call(s32[1]{0:T(128)} %get-tuple-element.270.lengths, bf16[128,1024]{1,0:T(8,128)(2,1)} %get-tuple-element.249.q_ref, ...), custom_call_target="tpu_custom_call", output_to_operand_aliasing={{2}: (6, {}), {3}: (7, {})} | custom-call | flops 9663676416 | bytes 18874368 | tf_op jit(solution)/shard_map/cross_backward/pallas_call | solution.py:475
  489.7 23.0 %bitcast_convert_fusion = bf16[1024,2048]{1,0:T(8,128)(2,1)S(1)} fusion(bf16[4,1024,1024]{2,1,0:T(8,128)(2,1)} %get-tuple-element.134, bf16[4,1024,2048]{2,1,0:T(8,128)(2,1)} %get-tuple-element.135), kind=kOutput, calls=%fused_computation.10 | convolution fusion | flops 17181966336 | bytes 29360128 | tf_op jit(solution)/shard_map/dot_general | solution.py:293
  522.9 2.9 add_convert_fusion.2
  531.2 3.0 add_convert_fusion.3
  536.6 9.5 %collective-permute-done.34 = bf16[1024,1024]{1,0:T(8,128)(2,1)} collective-permute-done((bf16[1024,1024]{1,0:T(8,128)(2,1)}, bf16[1024,1024]{1,0:T(8,128)(2,1)}, u32[]{:S(2)}, u32[]{:S(2)}) %collective-permute-start.34) | collective-permute-done | bytes 2097184 | tf_op jit(solution)/shard_map/ppermute | solution.py:16
  550.0 5.4 all-to-all-start.4
  561.5 3.2 add_convert_fusion.9
  565.9 10.6 %self_backward.1 = bf16[4,128,3072]{2,1,0:T(8,128)(2,1)} custom-call(s32[4,1,128]{2,1,0:T(1,128)} %bitcast.570, s32[4,128,1]{2,1,0:T(8,128)} %copy.117.seg_column, bf16[4,128,3072]{2,1,0:T(8,128)(2,1)} %bitcast.507, bf16[4,128,1024]{2,1,0:T(8,128)(2,1)} %bitcast.545, f32[4,8,1,256]{3,2,1,0:T(1,128)} %get-tuple-element.137.log_ref), custom_call_target="tpu_custom_call" | custom-call | tf_op jit(solution)/shard_map/self_backward/pallas_call | solution.py:576
  579.9 3.5 fusion.7
  618.3 43.3 %collective-permute-done.53 = bf16[4,9,128,256]{3,2,1,0:T(8,128)(2,1)} collective-permute-done((bf16[4,9,128,256]{3,2,1,0:T(8,128)(2,1)}, bf16[4,9,128,256]{3,2,1,0:T(8,128)(2,1)}, u32[]{:S(2)}, u32[]{:S(2)}) %collective-permute-start.53) | collective-permute-done | bytes 2359328 | tf_op jit(solution)/shard_map/ppermute | solution.py:16
  667.0 5.8 collective-permute-start.54
  691.3 3.1 constant_dynamic-slice_fusion.13
  701.8 10.2 %collective-permute-done.55 = bf16[9,128,256]{2,1,0:T(8,128)(2,1)} collective-permute-done((bf16[9,128,256]{2,1,0:T(8,128)(2,1)}, bf16[9,128,256]{2,1,0:T(8,128)(2,1)}, u32[]{:S(2)}, u32[]{:S(2)}) %collective-permute-start.55) | collective-permute-done | bytes 589856 | tf_op jit(solution)/shard_map/ppermute | solution.py:16
  717.3 7.6 collective-permute-done.43
  742.9 5.1 collective-permute-start.46
  748.0 5.5 collective-permute-done.56
  756.1 8.6 %collective-permute-done.46 = bf16[8,128,256]{2,1,0:T(8,128)(2,1)} collective-permute-done((bf16[8,128,256]{2,1,0:T(8,128)(2,1)}, bf16[8,128,256]{2,1,0:T(8,128)(2,1)}, u32[]{:S(2)}, u32[]{:S(2)}) %collective-permute-start.46) | collective-permute-done | bytes 524320 | tf_op jit(solution)/shard_map/ppermute | solution.py:16
  770.4 4.0 collective-permute-start.61
  774.4 7.2 add_convert_fusion.10
  781.6 4.1 collective-permute-start.47
  788.2 7.6 pad_maximum_fusion
  797.3 5.4 collective-permute-done.50
  806.4 10.3 %collective-permute-done.51 = bf16[8,128,256]{2,1,0:T(8,128)(2,1)S(1)} collective-permute-done((bf16[8,128,256]{2,1,0:T(8,128)(2,1)S(1)}, bf16[8,128,256]{2,1,0:T(8,128)(2,1)S(1)}, u32[]{:S(2)}, u32[]{:S(2)}) %collective-permute-start.51) | collective-permute-done | bytes 524320 | tf_op jit(solution)/shard_map/ppermute | solution.py:16
  (556 shorter events, 246.7 us)
Async XLA Ops:
  6.1 13.9 %collective-permute-start.2 = (bf16[128,1920]{1,0:T(8,128)(2,1)S(1)}, bf16[128,1920]{1,0:T(8,128)(2,1)S(1)}, u32[]{:S(2)}, u32[]{:S(2)}) collective-permute-start(bf16[128,1920]{1,0:T(8,128)(2,1)S(1)} %constant_dynamic-update-slice_fusion), channel_id=1, source_target_pairs={{0,2},{1,3},{2,4},{3,5},{4,6},{5,7},{8,10},{9,11},{10,12},{11,13},... | collective-permute-start | bytes 1474568 | tf_op jit(solution)/shard_map/ppermute | solution.py:16
  10.2 13.7 %collective-permute-start.1 = (bf16[128,1920]{1,0:T(8,128)(2,1)S(1)}, bf16[128,1920]{1,0:T(8,128)(2,1)S(1)}, u32[]{:S(2)}, u32[]{:S(2)}) collective-permute-start(bf16[128,1920]{1,0:T(8,128)(2,1)S(1)} %constant_dynamic-update-slice_fusion), channel_id=1, source_target_pairs={{2,0},{3,1},{4,2},{5,3},{6,4},{7,5},{10,8},{11,9},{12,10},{13,11},... | collective-permute-start | bytes 1474568 | tf_op jit(solution)/shard_map/ppermute | solution.py:16
  11.5 19.8 %collective-permute-start = (bf16[128,1920]{1,0:T(8,128)(2,1)S(1)}, bf16[128,1920]{1,0:T(8,128)(2,1)S(1)}, u32[]{:S(2)}, u32[]{:S(2)}) collective-permute-start(bf16[128,1920]{1,0:T(8,128)(2,1)S(1)} %constant_dynamic-update-slice_fusion), channel_id=1, source_target_pairs={{0,1},{1,0},{2,3},{3,2},{4,5},{5,4},{6,7},{7,6},{8,9},{9,8},{10,11... | collective-permute-start | bytes 1474568 | tf_op jit(solution)/shard_map/ppermute | solution.py:16
  20.0 11.2 %collective-permute-start.3 = (bf16[128,1920]{1,0:T(8,128)(2,1)S(1)}, bf16[128,1920]{1,0:T(8,128)(2,1)S(1)}, u32[]{:S(2)}, u32[]{:S(2)}) collective-permute-start(bf16[128,1920]{1,0:T(8,128)(2,1)S(1)} %collective-permute-done.2), channel_id=1, source_target_pairs={{2,4},{3,5},{4,6},{5,7},{10,12},{11,13},{12,14},{13,15},{18,20},{1... | collective-permute-start | bytes 1474568 | tf_op jit(solution)/shard_map/ppermute | solution.py:16
  23.8 14.8 %collective-permute-start.5 = (bf16[128,1920]{1,0:T(8,128)(2,1)S(1)}, bf16[128,1920]{1,0:T(8,128)(2,1)}, u32[]{:S(2)}, u32[]{:S(2)}) collective-permute-start(bf16[128,1920]{1,0:T(8,128)(2,1)S(1)} %collective-permute-done.1), channel_id=1, source_target_pairs={{2,0},{3,1},{4,2},{5,3},{10,8},{11,9},{12,10},{13,11},{18,16},{19,... | collective-permute-start | bytes 1474568 | tf_op jit(solution)/shard_map/ppermute | solution.py:16
  31.2 9.8 %collective-permute-start.4 = (bf16[128,1920]{1,0:T(8,128)(2,1)S(1)}, bf16[128,1920]{1,0:T(8,128)(2,1)}, u32[]{:S(2)}, u32[]{:S(2)}) collective-permute-start(bf16[128,1920]{1,0:T(8,128)(2,1)S(1)} %collective-permute-done.3), channel_id=1, source_target_pairs={{4,6},{5,7},{12,14},{13,15},{20,22},{21,23},{28,30},{29,31}} | collective-permute-start | bytes 1474568 | tf_op jit(solution)/shard_map/ppermute | solution.py:16
  34.1 18.4 %collective-permute-start.15 = (bf16[128,2304]{1,0:T(8,128)(2,1)}, bf16[128,2304]{1,0:T(8,128)(2,1)S(1)}, u32[]{:S(2)}, u32[]{:S(2)}) collective-permute-start(bf16[128,2304]{1,0:T(8,128)(2,1)} %constant_dynamic-update-slice_fusion.4), channel_id=1, source_target_pairs={{0,1},{1,0},{2,3},{3,2},{4,5},{5,4},{6,7},{7,6},{8,9},{9,8},{10,11... | collective-permute-start | bytes 1769480 | tf_op jit(solution)/shard_map/ppermute | solution.py:16
  35.4 17.2 %collective-permute-start.8 = (bf16[128,1920]{1,0:T(8,128)(2,1)S(1)}, bf16[128,1920]{1,0:T(8,128)(2,1)S(1)}, u32[]{:S(2)}, u32[]{:S(2)}) collective-permute-start(bf16[128,1920]{1,0:T(8,128)(2,1)S(1)} %collective-permute-done), channel_id=1, source_target_pairs={{0,16},{8,24},{16,0},{24,8},{1,17},{9,25},{17,1},{25,9},{2,18},{10... | collective-permute-start | bytes 1474568 | tf_op jit(solution)/shard_map/ppermute | solution.py:16
  38.6 12.3 %collective-permute-start.6 = (bf16[128,1920]{1,0:T(8,128)(2,1)}, bf16[128,1920]{1,0:T(8,128)(2,1)S(1)}, u32[]{:S(2)}, u32[]{:S(2)}) collective-permute-start(bf16[128,1920]{1,0:T(8,128)(2,1)} %collective-permute-done.5), channel_id=1, source_target_pairs={{2,0},{3,1},{10,8},{11,9},{18,16},{19,17},{26,24},{27,25}} | collective-permute-start | bytes 1474568 | tf_op jit(solution)/shard_map/ppermute | solution.py:16
  51.3 30.6 %collective-permute-start.7 = (bf16[3,128,1920]{2,1,0:T(8,128)(2,1)S(1)}, bf16[3,128,1920]{2,1,0:T(8,128)(2,1)}, u32[]{:S(2)}, u32[]{:S(2)}) collective-permute-start(bf16[3,128,1920]{2,1,0:T(8,128)(2,1)S(1)} %pad_maximum_fusion.10), channel_id=1, source_target_pairs={{0,1},{1,0},{2,3},{3,2},{4,5},{5,4},{6,7},{7,6},{8,9},{9,8},{10,11... | collective-permute-start | bytes 4423688 | tf_op jit(solution)/shard_map/ppermute | solution.py:16
  52.6 10.6 %collective-permute-start.17 = (bf16[128,2304]{1,0:T(8,128)(2,1)}, bf16[128,2304]{1,0:T(8,128)(2,1)S(1)}, u32[]{:S(2)}, u32[]{:S(2)}) collective-permute-start(bf16[128,2304]{1,0:T(8,128)(2,1)} %constant_dynamic-update-slice_fusion.4), channel_id=1, source_target_pairs={{0,2},{1,3},{2,4},{3,5},{4,6},{5,7},{8,10},{9,11},{10,12},{11,13},... | collective-permute-start | bytes 1769480 | tf_op jit(solution)/shard_map/ppermute | solution.py:16
  53.9 12.1 %collective-permute-start.16 = (bf16[128,2304]{1,0:T(8,128)(2,1)}, bf16[128,2304]{1,0:T(8,128)(2,1)S(1)}, u32[]{:S(2)}, u32[]{:S(2)}) collective-permute-start(bf16[128,2304]{1,0:T(8,128)(2,1)} %constant_dynamic-update-slice_fusion.4), channel_id=1, source_target_pairs={{2,0},{3,1},{4,2},{5,3},{6,4},{7,5},{10,8},{11,9},{12,10},{13,11},... | collective-permute-start | bytes 1769480 | tf_op jit(solution)/shard_map/ppermute | solution.py:16
  55.2 18.1 %collective-permute-start.19 = (bf16[128,2304]{1,0:T(8,128)(2,1)S(1)}, bf16[128,2304]{1,0:T(8,128)(2,1)S(1)}, u32[]{:S(2)}, u32[]{:S(2)}) collective-permute-start(bf16[128,2304]{1,0:T(8,128)(2,1)S(1)} %collective-permute-done.15), channel_id=1, source_target_pairs={{0,16},{8,24},{16,0},{24,8},{1,17},{9,25},{17,1},{25,9},{2,18},{10... | collective-permute-start | bytes 1769480 | tf_op jit(solution)/shard_map/ppermute | solution.py:16
  63.1 10.2 %collective-permute-start.18 = (bf16[128,2304]{1,0:T(8,128)(2,1)S(1)}, bf16[128,2304]{1,0:T(8,128)(2,1)S(1)}, u32[]{:S(2)}, u32[]{:S(2)}) collective-permute-start(bf16[128,2304]{1,0:T(8,128)(2,1)S(1)} %collective-permute-done.17), channel_id=1, source_target_pairs={{2,4},{3,5},{4,6},{5,7},{10,12},{11,13},{12,14},{13,15},{18,20},{1... | collective-permute-start | bytes 1769480 | tf_op jit(solution)/shard_map/ppermute | solution.py:16
  66.0 16.5 %collective-permute-start.21 = (bf16[128,2304]{1,0:T(8,128)(2,1)S(1)}, bf16[128,2304]{1,0:T(8,128)(2,1)S(1)}, u32[]{:S(2)}, u32[]{:S(2)}) collective-permute-start(bf16[128,2304]{1,0:T(8,128)(2,1)S(1)} %collective-permute-done.16), channel_id=1, source_target_pairs={{2,0},{3,1},{4,2},{5,3},{10,8},{11,9},{12,10},{13,11},{18,16},{19,... | collective-permute-start | bytes 1769480 | tf_op jit(solution)/shard_map/ppermute | solution.py:16
  72.1 24.6 %collective-permute-start.9 = (bf16[3,128,1920]{2,1,0:T(8,128)(2,1)S(1)}, bf16[3,128,1920]{2,1,0:T(8,128)(2,1)}, u32[]{:S(2)}, u32[]{:S(2)}) collective-permute-start(bf16[3,128,1920]{2,1,0:T(8,128)(2,1)S(1)} %pad_maximum_fusion.10), channel_id=1, source_target_pairs={{0,16},{8,24},{16,0},{24,8},{1,17},{9,25},{17,1},{25,9},{2,18},{10... | collective-permute-start | bytes 4423688 | tf_op jit(solution)/shard_map/ppermute | solution.py:16
  82.6 11.8 %collective-permute-start.22 = (bf16[128,2304]{1,0:T(8,128)(2,1)S(1)}, bf16[128,2304]{1,0:T(8,128)(2,1)S(1)}, u32[]{:S(2)}, u32[]{:S(2)}) collective-permute-start(bf16[128,2304]{1,0:T(8,128)(2,1)S(1)} %collective-permute-done.21), channel_id=1, source_target_pairs={{2,0},{3,1},{10,8},{11,9},{18,16},{19,17},{26,24},{27,25}} | collective-permute-start | bytes 1769480 | tf_op jit(solution)/shard_map/ppermute | solution.py:16
  96.7 103.3 %all-to-all-start = ((bf16[8,2,128,1024]{3,2,1,0:T(8,128)(2,1)}), bf16[8,2,128,1024]{3,2,1,0:T(8,128)(2,1)}, u32[]{:S(2)}, u32[]{:S(2)}) async-start(bf16[8,2,128,1024]{3,2,1,0:T(8,128)(2,1)} %stack.165), calls=%async_computation | async-start | bytes 8388608 | tf_op jit(solution)/shard_map/all_to_all | solution.py:603
  103.6 23.7 %collective-permute-start.10 = (bf16[3,128,1920]{2,1,0:T(8,128)(2,1)}, bf16[3,128,1920]{2,1,0:T(8,128)(2,1)}, u32[]{:S(2)}, u32[]{:S(2)}) collective-permute-start(bf16[3,128,1920]{2,1,0:T(8,128)(2,1)} %collective-permute-done.7.refs_7_), channel_id=1, source_target_pairs={{0,16},{8,24},{16,0},{24,8},{1,17},{9,25},{17,1},{25,9},{2,18},{10... | collective-permute-start | bytes 4423688 | tf_op jit(solution)/shard_map/ppermute | solution.py:16
  106.7 39.7 %collective-permute-start.11 = (bf16[4,128,1920]{2,1,0:T(8,128)(2,1)S(1)}, bf16[4,128,1920]{2,1,0:T(8,128)(2,1)}, u32[]{:S(2)}, u32[]{:S(2)}) collective-permute-start(bf16[4,128,1920]{2,1,0:T(8,128)(2,1)S(1)} %pad_maximum_fusion.5.refs_6_), channel_id=1, source_target_pairs={{0,8},{8,0},{16,24},{24,16},{1,9},{9,1},{17,25},{25,17},{2,10},{10... | collective-permute-start | bytes 5898248 | tf_op jit(solution)/shard_map/ppermute | solution.py:16
  120.4 27.4 %collective-permute-start.13 = (bf16[4,128,1920]{2,1,0:T(8,128)(2,1)}, bf16[4,128,1920]{2,1,0:T(8,128)(2,1)}, u32[]{:S(2)}, u32[]{:S(2)}) collective-permute-start(bf16[4,128,1920]{2,1,0:T(8,128)(2,1)} %pad_maximum_fusion.6.refs_8_), channel_id=1, source_target_pairs={{0,8},{8,0},{16,24},{24,16},{1,9},{9,1},{17,25},{25,17},{2,10},{10... | collective-permute-start | bytes 5898248 | tf_op jit(solution)/shard_map/ppermute | solution.py:16
  121.0 26.8 %collective-permute-start.12 = (bf16[3,128,1920]{2,1,0:T(8,128)(2,1)}, bf16[3,128,1920]{2,1,0:T(8,128)(2,1)}, u32[]{:S(2)}, u32[]{:S(2)}) collective-permute-start(bf16[3,128,1920]{2,1,0:T(8,128)(2,1)} %collective-permute-done.7.refs_7_), channel_id=1, source_target_pairs={{0,8},{8,0},{16,24},{24,16},{1,9},{9,1},{17,25},{25,17},{2,10},{10... | collective-permute-start | bytes 4423688 | tf_op jit(solution)/shard_map/ppermute | solution.py:16
  127.3 20.5 %collective-permute-start.14 = (bf16[3,128,1920]{2,1,0:T(8,128)(2,1)}, bf16[3,128,1920]{2,1,0:T(8,128)(2,1)}, u32[]{:S(2)}, u32[]{:S(2)}) collective-permute-start(bf16[3,128,1920]{2,1,0:T(8,128)(2,1)} %collective-permute-done.10.refs_9_), channel_id=1, source_target_pairs={{0,8},{8,0},{16,24},{24,16},{1,9},{9,1},{17,25},{25,17},{2,10},{10... | collective-permute-start | bytes 4423688 | tf_op jit(solution)/shard_map/ppermute | solution.py:16
  145.1 53.7 %collective-permute-start.24 = (bf16[3,128,2304]{2,1,0:T(8,128)(2,1)S(1)}, bf16[3,128,2304]{2,1,0:T(8,128)(2,1)S(1)}, u32[]{:S(2)}, u32[]{:S(2)}) collective-permute-start(bf16[3,128,2304]{2,1,0:T(8,128)(2,1)S(1)} %copy-done.44), channel_id=1, source_target_pairs={{0,16},{8,24},{16,0},{24,8},{1,17},{9,25},{17,1},{25,9},{2,18},{10... | collective-permute-start | bytes 5308424 | tf_op jit(solution)/shard_map/ppermute | solution.py:16
  146.4 52.5 %collective-permute-start.23 = (bf16[3,128,2304]{2,1,0:T(8,128)(2,1)S(1)}, bf16[3,128,2304]{2,1,0:T(8,128)(2,1)}, u32[]{:S(2)}, u32[]{:S(2)}) collective-permute-start(bf16[3,128,2304]{2,1,0:T(8,128)(2,1)S(1)} %copy-done.44), channel_id=1, source_target_pairs={{0,1},{1,0},{2,3},{3,2},{4,5},{5,4},{6,7},{7,6},{8,9},{9,8},{10,11... | collective-permute-start | bytes 5308424 | tf_op jit(solution)/shard_map/ppermute | solution.py:16
  200.1 57.7 %all-to-all-start.1 = ((bf16[8,128,1024]{2,1,0:T(8,128)(2,1)}), bf16[8,128,1024]{2,1,0:T(8,128)(2,1)}, u32[]{:S(2)}, u32[]{:S(2)}) async-start(bf16[8,128,1024]{2,1,0:T(8,128)(2,1)} %get-tuple-element.97), calls=%async_computation.1 | async-start | bytes 4194304 | tf_op jit(solution)/shard_map/all_to_all | solution.py:603
  209.9 39.0 %collective-permute-start.25 = (bf16[3,128,2304]{2,1,0:T(8,128)(2,1)}, bf16[3,128,2304]{2,1,0:T(8,128)(2,1)}, u32[]{:S(2)}, u32[]{:S(2)}) collective-permute-start(bf16[3,128,2304]{2,1,0:T(8,128)(2,1)} %collective-permute-done.23.refs_5_), channel_id=1, source_target_pairs={{0,16},{8,24},{16,0},{24,8},{1,17},{9,25},{17,1},{25,9},{2,18},{10... | collective-permute-start | bytes 5308424 | tf_op jit(solution)/shard_map/ppermute | solution.py:16
  257.8 51.2 %all-to-all-start.2 = ((bf16[8,128,1024]{2,1,0:T(8,128)(2,1)}), bf16[8,128,1024]{2,1,0:T(8,128)(2,1)}, u32[]{:S(2)}, u32[]{:S(2)}) async-start(bf16[8,128,1024]{2,1,0:T(8,128)(2,1)} %get-tuple-element.100), calls=%async_computation.2 | async-start | bytes 4194304 | tf_op jit(solution)/shard_map/all_to_all | solution.py:603
  265.5 19.9 %collective-permute-start.26 = (bf16[4,128,2304]{2,1,0:T(8,128)(2,1)}, bf16[4,128,2304]{2,1,0:T(8,128)(2,1)}, u32[]{:S(2)}, u32[]{:S(2)}) collective-permute-start(bf16[4,128,2304]{2,1,0:T(8,128)(2,1)} %pad_maximum_fusion.1.refs_4_), channel_id=1, source_target_pairs={{0,8},{8,0},{16,24},{24,16},{1,9},{9,1},{17,25},{25,17},{2,10},{10... | collective-permute-start | bytes 7077896 | tf_op jit(solution)/shard_map/ppermute | solution.py:16
  268.8 16.6 %collective-permute-start.28 = (bf16[4,128,2304]{2,1,0:T(8,128)(2,1)}, bf16[4,128,2304]{2,1,0:T(8,128)(2,1)}, u32[]{:S(2)}, u32[]{:S(2)}) collective-permute-start(bf16[4,128,2304]{2,1,0:T(8,128)(2,1)} %pad_maximum_fusion.2.refs_6_), channel_id=1, source_target_pairs={{0,8},{8,0},{16,24},{24,16},{1,9},{9,1},{17,25},{25,17},{2,10},{10... | collective-permute-start | bytes 7077896 | tf_op jit(solution)/shard_map/ppermute | solution.py:16
  268.8 16.6 %collective-permute-start.27 = (bf16[3,128,2304]{2,1,0:T(8,128)(2,1)}, bf16[3,128,2304]{2,1,0:T(8,128)(2,1)}, u32[]{:S(2)}, u32[]{:S(2)}) collective-permute-start(bf16[3,128,2304]{2,1,0:T(8,128)(2,1)} %collective-permute-done.23.refs_5_), channel_id=1, source_target_pairs={{0,8},{8,0},{16,24},{24,16},{1,9},{9,1},{17,25},{25,17},{2,10},{10... | collective-permute-start | bytes 5308424 | tf_op jit(solution)/shard_map/ppermute | solution.py:16
  269.3 16.1 %collective-permute-start.29 = (bf16[3,128,2304]{2,1,0:T(8,128)(2,1)}, bf16[3,128,2304]{2,1,0:T(8,128)(2,1)}, u32[]{:S(2)}, u32[]{:S(2)}) collective-permute-start(bf16[3,128,2304]{2,1,0:T(8,128)(2,1)} %collective-permute-done.25.refs_7_), channel_id=1, source_target_pairs={{0,8},{8,0},{16,24},{24,16},{1,9},{9,1},{17,25},{25,17},{2,10},{10... | collective-permute-start | bytes 5308424 | tf_op jit(solution)/shard_map/ppermute | solution.py:16
  405.1 38.7 %collective-permute-start.30 = (bf16[4096,512]{1,0:T(8,128)(2,1)}, bf16[4096,512]{1,0:T(8,128)(2,1)}, u32[]{:S(2)}, u32[]{:S(2)}) collective-permute-start(bf16[4096,512]{1,0:T(8,128)(2,1)} %convolution_convert_fusion), channel_id=1, source_target_pairs={{0,8},{8,0},{16,24},{24,16},{1,9},{9,1},{17,25},{25,17},{2,10},{10... | collective-permute-start | bytes 12582920 | tf_op jit(solution)/shard_map/ppermute | solution.py:16
  412.3 37.3 %collective-permute-start.31 = (bf16[1024,2048]{1,0:T(8,128)(2,1)}, bf16[1024,2048]{1,0:T(8,128)(2,1)}, u32[]{:S(2)}, u32[]{:S(2)}) collective-permute-start(bf16[1024,2048]{1,0:T(8,128)(2,1)} %convolution_convert_fusion.2), channel_id=1, source_target_pairs={{0,8},{8,0},{16,24},{24,16},{1,9},{9,1},{17,25},{25,17},{2,10},{10... | collective-permute-start | bytes 12582920 | tf_op jit(solution)/shard_map/ppermute | solution.py:16
  431.5 118.5 %all-to-all-start.3 = ((bf16[8,2,128,1024]{3,2,1,0:T(8,128)(2,1)}), bf16[8,2,128,1024]{3,2,1,0:T(8,128)(2,1)}, u32[]{:S(2)}, u32[]{:S(2)}) async-start(bf16[8,2,128,1024]{3,2,1,0:T(8,128)(2,1)} %get-tuple-element.132), calls=%async_computation.3 | async-start | bytes 8388608 | tf_op jit(solution)/shard_map/all_to_all | solution.py:603
  442.5 116.9 %collective-permute-start.35 = (bf16[1024,256]{1,0:T(8,128)(2,1)}, bf16[1024,256]{1,0:T(8,128)(2,1)}, u32[]{:S(2)}, u32[]{:S(2)}) collective-permute-start(bf16[1024,256]{1,0:T(8,128)(2,1)} %add_convert_fusion.26), channel_id=1, source_target_pairs={{0,16},{8,24},{16,0},{24,8},{1,17},{9,25},{17,1},{25,9},{2,18},{10... | collective-permute-start | bytes 1572872 | tf_op jit(solution)/shard_map/ppermute | solution.py:16
  448.3 86.0 %collective-permute-start.33 = (bf16[4096,256]{1,0:T(8,128)(2,1)}, bf16[4096,256]{1,0:T(8,128)(2,1)}, u32[]{:S(2)}, u32[]{:S(2)}) collective-permute-start(bf16[4096,256]{1,0:T(8,128)(2,1)} %add_convert_fusion.5), channel_id=1, source_target_pairs={{0,16},{8,24},{16,0},{24,8},{1,17},{9,25},{17,1},{25,9},{2,18},{10... | collective-permute-start | bytes 6291464 | tf_op jit(solution)/shard_map/ppermute | solution.py:16
  454.0 92.1 %collective-permute-start.34 = (bf16[1024,1024]{1,0:T(8,128)(2,1)}, bf16[1024,1024]{1,0:T(8,128)(2,1)}, u32[]{:S(2)}, u32[]{:S(2)}) collective-permute-start(bf16[1024,1024]{1,0:T(8,128)(2,1)} %add_convert_fusion.4), channel_id=1, source_target_pairs={{0,16},{8,24},{16,0},{24,8},{1,17},{9,25},{17,1},{25,9},{2,18},{10... | collective-permute-start | bytes 6291464 | tf_op jit(solution)/shard_map/ppermute | solution.py:16
  516.4 45.1 %collective-permute-start.37 = (bf16[1024,1024]{1,0:T(8,128)(2,1)}, bf16[1024,1024]{1,0:T(8,128)(2,1)}, u32[]{:S(2)}, u32[]{:S(2)}) collective-permute-start(bf16[1024,1024]{1,0:T(8,128)(2,1)} %pad_maximum_fusion.3), channel_id=1, source_target_pairs={{0,8},{8,0},{16,24},{24,16},{1,9},{9,1},{17,25},{25,17},{2,10},{10... | collective-permute-start | bytes 6291464 | tf_op jit(solution)/shard_map/ppermute | solution.py:16
  550.0 145.9 %all-to-all-start.4 = ((bf16[8,2,128,1024]{3,2,1,0:T(8,128)(2,1)}), bf16[8,2,128,1024]{3,2,1,0:T(8,128)(2,1)}, u32[]{:S(2)}, u32[]{:S(2)}) async-start(bf16[8,2,128,1024]{3,2,1,0:T(8,128)(2,1)} %get-tuple-element.139), calls=%async_computation.4 | async-start | bytes 8388608 | tf_op jit(solution)/shard_map/all_to_all | solution.py:603
  557.7 18.7 %collective-permute-start.36 = (bf16[1024,512]{1,0:T(8,128)(2,1)S(1)}, bf16[1024,512]{1,0:T(8,128)(2,1)S(1)}, u32[]{:S(2)}, u32[]{:S(2)}) collective-permute-start(bf16[1024,512]{1,0:T(8,128)(2,1)S(1)} %convolution_convert_fusion.7), channel_id=1, source_target_pairs={{0,8},{8,0},{16,24},{24,16},{1,9},{9,1},{17,25},{25,17},{2,10},{10... | collective-permute-start | bytes 3145736 | tf_op jit(solution)/shard_map/ppermute | solution.py:16
  583.4 15.5 %collective-permute-start.39 = (bf16[1024,1536]{0,1:T(8,128)(2,1)}, bf16[1024,1536]{0,1:T(8,128)(2,1)}, u32[]{:S(2)}, u32[]{:S(2)}) collective-permute-start(bf16[1024,1536]{0,1:T(8,128)(2,1)} %fusion.7), channel_id=1, source_target_pairs={{0,8},{8,0},{16,24},{24,16},{1,9},{9,1},{17,25},{25,17},{2,10},{10... | collective-permute-start | bytes 9437192 | tf_op jit(solution)/shard_map/ppermute | solution.py:16
  583.8 7.2 collective-permute-start.38
  587.8 8.5 %collective-permute-start.40 = (bf16[1024,512]{1,0:T(8,128)(2,1)}, bf16[1024,512]{1,0:T(8,128)(2,1)}, u32[]{:S(2)}, u32[]{:S(2)}) collective-permute-start(bf16[1024,512]{1,0:T(8,128)(2,1)} %pad_maximum_fusion.12), channel_id=1, source_target_pairs={{0,8},{8,0},{16,24},{24,16},{1,9},{9,1},{17,25},{25,17},{2,10},{10... | collective-permute-start | bytes 3145736 | tf_op jit(solution)/shard_map/ppermute | solution.py:16
  587.9 73.8 %collective-permute-start.53 = (bf16[4,9,128,256]{3,2,1,0:T(8,128)(2,1)}, bf16[4,9,128,256]{3,2,1,0:T(8,128)(2,1)}, u32[]{:S(2)}, u32[]{:S(2)}) collective-permute-start(bf16[4,9,128,256]{3,2,1,0:T(8,128)(2,1)} %get-tuple-element.232), channel_id=1, source_target_pairs={{0,1},{1,0},{2,3},{3,2},{4,5},{5,4},{6,7},{7,6},{8,9},{9,8},{10,11... | collective-permute-start | bytes 7077896 | tf_op jit(solution)/shard_map/ppermute | solution.py:16
  596.2 76.6 %collective-permute-start.42 = (bf16[8,3,128,256]{3,2,1,0:T(8,128)(2,1)}, bf16[8,3,128,256]{3,2,1,0:T(8,128)(2,1)}, u32[]{:S(2)}, u32[]{:S(2)}) collective-permute-start(bf16[8,3,128,256]{3,2,1,0:T(8,128)(2,1)} %pad_maximum_fusion.8), channel_id=1, source_target_pairs={{0,16},{8,24},{16,0},{24,8},{1,17},{9,25},{17,1},{25,9},{2,18},{10... | collective-permute-start | bytes 4718600 | tf_op jit(solution)/shard_map/ppermute | solution.py:16
  614.5 76.8 %collective-permute-start.41 = (bf16[8,5,128,256]{3,2,1,0:T(8,128)(2,1)}, bf16[8,5,128,256]{3,2,1,0:T(8,128)(2,1)}, u32[]{:S(2)}, u32[]{:S(2)}) collective-permute-start(bf16[8,5,128,256]{3,2,1,0:T(8,128)(2,1)} %constant_dynamic-update-slice_fusion.19), channel_id=1, source_target_pairs={{0,16},{8,24},{16,0},{24,8},{1,17},{9,25},{17,1},{25,9},{2,18},{10... | collective-permute-start | bytes 7864328 | tf_op jit(solution)/shard_map/ppermute | solution.py:16
  665.5 36.3 %collective-permute-start.57 = (bf16[9,128,256]{2,1,0:T(8,128)(2,1)}, bf16[9,128,256]{2,1,0:T(8,128)(2,1)}, u32[]{:S(2)}, u32[]{:S(2)}) collective-permute-start(bf16[9,128,256]{2,1,0:T(8,128)(2,1)} %get-tuple-element.209), channel_id=1, source_target_pairs={{6,4},{7,5},{14,12},{15,13},{22,20},{23,21},{30,28},{31,29}} | collective-permute-start | bytes 1769480 | tf_op jit(solution)/shard_map/ppermute | solution.py:16
  667.0 30.4 %collective-permute-start.54 = (bf16[9,128,256]{2,1,0:T(8,128)(2,1)}, bf16[9,128,256]{2,1,0:T(8,128)(2,1)}, u32[]{:S(2)}, u32[]{:S(2)}) collective-permute-start(bf16[9,128,256]{2,1,0:T(8,128)(2,1)} %get-tuple-element.208), channel_id=1, source_target_pairs={{0,2},{1,3},{8,10},{9,11},{16,18},{17,19},{24,26},{25,27}} | collective-permute-start | bytes 1769480 | tf_op jit(solution)/shard_map/ppermute | solution.py:16
  676.0 23.6 %collective-permute-start.44 = (bf16[4,3,128,256]{3,2,0,1:T(8,128)(2,1)}, bf16[4,3,128,256]{3,2,0,1:T(8,128)(2,1)}, u32[]{:S(2)}, u32[]{:S(2)}) collective-permute-start(bf16[4,3,128,256]{3,2,0,1:T(8,128)(2,1)} %get-tuple-element.221), channel_id=1, source_target_pairs={{0,1},{1,0},{2,3},{3,2},{4,5},{5,4},{6,7},{7,6},{8,9},{9,8},{10,11... | collective-permute-start | bytes 2359304 | tf_op jit(solution)/shard_map/ppermute | solution.py:16
  695.9 29.0 %collective-permute-start.43 = (bf16[4,5,128,256]{3,2,0,1:T(8,128)(2,1)}, bf16[4,5,128,256]{3,2,0,1:T(8,128)(2,1)}, u32[]{:S(2)}, u32[]{:S(2)}) collective-permute-start(bf16[4,5,128,256]{3,2,0,1:T(8,128)(2,1)} %fusion.23), channel_id=1, source_target_pairs={{0,1},{1,0},{2,3},{3,2},{4,5},{5,4},{6,7},{7,6},{8,9},{9,8},{10,11... | collective-permute-start | bytes 3932168 | tf_op jit(solution)/shard_map/ppermute | solution.py:16
  699.6 12.4 %collective-permute-start.55 = (bf16[9,128,256]{2,1,0:T(8,128)(2,1)}, bf16[9,128,256]{2,1,0:T(8,128)(2,1)}, u32[]{:S(2)}, u32[]{:S(2)}) collective-permute-start(bf16[9,128,256]{2,1,0:T(8,128)(2,1)} %fusion.26), channel_id=1, source_target_pairs={{0,2},{1,3},{2,4},{3,5},{8,10},{9,11},{10,12},{11,13},{16,18},{17,... | collective-permute-start | bytes 1769480 | tf_op jit(solution)/shard_map/ppermute | solution.py:16
  714.7 17.3 %collective-permute-start.58 = (bf16[9,128,256]{2,1,0:T(8,128)(2,1)S(1)}, bf16[9,128,256]{2,1,0:T(8,128)(2,1)S(1)}, u32[]{:S(2)}, u32[]{:S(2)}) collective-permute-start(bf16[9,128,256]{2,1,0:T(8,128)(2,1)S(1)} %get-tuple-element.147), channel_id=1, source_target_pairs={{4,2},{5,3},{6,4},{7,5},{12,10},{13,11},{14,12},{15,13},{20,18},{2... | collective-permute-start | bytes 1769480 | tf_op jit(solution)/shard_map/ppermute | solution.py:16
  729.7 11.1 %collective-permute-start.45 = (bf16[8,128,256]{2,1,0:T(8,128)(2,1)}, bf16[8,128,256]{2,1,0:T(8,128)(2,1)}, u32[]{:S(2)}, u32[]{:S(2)}) collective-permute-start(bf16[8,128,256]{2,1,0:T(8,128)(2,1)} %get-tuple-element.217), channel_id=1, source_target_pairs={{0,2},{1,3},{8,10},{9,11},{16,18},{17,19},{24,26},{25,27}} | collective-permute-start | bytes 1572872 | tf_op jit(solution)/shard_map/ppermute | solution.py:16
  734.1 19.4 %collective-permute-start.56 = (bf16[9,128,256]{2,1,0:T(8,128)(2,1)}, bf16[9,128,256]{2,1,0:T(8,128)(2,1)}, u32[]{:S(2)}, u32[]{:S(2)}) collective-permute-start(bf16[9,128,256]{2,1,0:T(8,128)(2,1)} %get-tuple-element.146), channel_id=1, source_target_pairs={{0,2},{1,3},{2,4},{3,5},{4,6},{5,7},{8,10},{9,11},{10,12},{11,13},... | collective-permute-start | bytes 1769480 | tf_op jit(solution)/shard_map/ppermute | solution.py:16
  736.2 17.2 %collective-permute-start.59 = (bf16[9,128,256]{2,1,0:T(8,128)(2,1)}, bf16[9,128,256]{2,1,0:T(8,128)(2,1)}, u32[]{:S(2)}, u32[]{:S(2)}) collective-permute-start(bf16[9,128,256]{2,1,0:T(8,128)(2,1)} %fusion.25), channel_id=1, source_target_pairs={{2,0},{3,1},{4,2},{5,3},{6,4},{7,5},{10,8},{11,9},{12,10},{13,11},... | collective-permute-start | bytes 1769480 | tf_op jit(solution)/shard_map/ppermute | solution.py:16
  737.5 18.5 %collective-permute-start.48 = (bf16[8,128,256]{2,1,0:T(8,128)(2,1)}, bf16[8,128,256]{2,1,0:T(8,128)(2,1)}, u32[]{:S(2)}, u32[]{:S(2)}) collective-permute-start(bf16[8,128,256]{2,1,0:T(8,128)(2,1)} %get-tuple-element.218), channel_id=1, source_target_pairs={{6,4},{7,5},{14,12},{15,13},{22,20},{23,21},{30,28},{31,29}} | collective-permute-start | bytes 1572872 | tf_op jit(solution)/shard_map/ppermute | solution.py:16
  742.9 21.8 %collective-permute-start.46 = (bf16[8,128,256]{2,1,0:T(8,128)(2,1)}, bf16[8,128,256]{2,1,0:T(8,128)(2,1)}, u32[]{:S(2)}, u32[]{:S(2)}) collective-permute-start(bf16[8,128,256]{2,1,0:T(8,128)(2,1)} %fusion.32), channel_id=1, source_target_pairs={{0,2},{1,3},{2,4},{3,5},{8,10},{9,11},{10,12},{11,13},{16,18},{17,... | collective-permute-start | bytes 1572872 | tf_op jit(solution)/shard_map/ppermute | solution.py:16
  755.9 12.1 %collective-permute-start.60 = (bf16[9,128,256]{2,1,0:T(8,128)(2,1)}, bf16[9,128,256]{2,1,0:T(8,128)(2,1)}, u32[]{:S(2)}, u32[]{:S(2)}) collective-permute-start(bf16[9,128,256]{2,1,0:T(8,128)(2,1)} %fusion.29), channel_id=1, source_target_pairs={{0,16},{8,24},{16,0},{24,8},{1,17},{9,25},{17,1},{25,9},{2,18},{10... | collective-permute-start | bytes 1769480 | tf_op jit(solution)/shard_map/ppermute | solution.py:16
  767.3 18.4 %collective-permute-start.49 = (bf16[8,128,256]{2,1,0:T(8,128)(2,1)S(1)}, bf16[8,128,256]{2,1,0:T(8,128)(2,1)S(1)}, u32[]{:S(2)}, u32[]{:S(2)}) collective-permute-start(bf16[8,128,256]{2,1,0:T(8,128)(2,1)S(1)} %get-tuple-element.216), channel_id=1, source_target_pairs={{4,2},{5,3},{6,4},{7,5},{12,10},{13,11},{14,12},{15,13},{20,18},{2... | collective-permute-start | bytes 1572872 | tf_op jit(solution)/shard_map/ppermute | solution.py:16
  770.4 33.7 %collective-permute-start.61 = (bf16[2,9,128,256]{3,2,1,0:T(8,128)(2,1)}, bf16[2,9,128,256]{3,2,1,0:T(8,128)(2,1)}, u32[]{:S(2)}, u32[]{:S(2)}) collective-permute-start(bf16[2,9,128,256]{3,2,1,0:T(8,128)(2,1)} %pad_maximum_fusion.11), channel_id=1, source_target_pairs={{0,8},{8,0},{16,24},{24,16},{1,9},{9,1},{17,25},{25,17},{2,10},{10... | collective-permute-start | bytes 3538952 | tf_op jit(solution)/shard_map/ppermute | solution.py:16
  781.6 15.8 %collective-permute-start.47 = (bf16[8,128,256]{2,1,0:T(8,128)(2,1)}, bf16[8,128,256]{2,1,0:T(8,128)(2,1)S(1)}, u32[]{:S(2)}, u32[]{:S(2)}) collective-permute-start(bf16[8,128,256]{2,1,0:T(8,128)(2,1)} %get-tuple-element.215), channel_id=1, source_target_pairs={{0,2},{1,3},{2,4},{3,5},{4,6},{5,7},{8,10},{9,11},{10,12},{11,13},... | collective-permute-start | bytes 1572872 | tf_op jit(solution)/shard_map/ppermute | solution.py:16
  786.9 15.8 %collective-permute-start.50 = (bf16[8,128,256]{2,1,0:T(8,128)(2,1)S(1)}, bf16[8,128,256]{2,1,0:T(8,128)(2,1)S(1)}, u32[]{:S(2)}, u32[]{:S(2)}) collective-permute-start(bf16[8,128,256]{2,1,0:T(8,128)(2,1)S(1)} %fusion.31), channel_id=1, source_target_pairs={{2,0},{3,1},{4,2},{5,3},{6,4},{7,5},{10,8},{11,9},{12,10},{13,11},... | collective-permute-start | bytes 1572872 | tf_op jit(solution)/shard_map/ppermute | solution.py:16
  804.0 12.7 %collective-permute-start.51 = (bf16[8,128,256]{2,1,0:T(8,128)(2,1)S(1)}, bf16[8,128,256]{2,1,0:T(8,128)(2,1)S(1)}, u32[]{:S(2)}, u32[]{:S(2)}) collective-permute-start(bf16[8,128,256]{2,1,0:T(8,128)(2,1)S(1)} %fusion.35), channel_id=1, source_target_pairs={{0,16},{8,24},{16,0},{24,8},{1,17},{9,25},{17,1},{25,9},{2,18},{10... | collective-permute-start | bytes 1572872 | tf_op jit(solution)/shard_map/ppermute | solution.py:16
  (114 other events, 1400.4 us)

commit v4 on v3

--- a/solution.py
+++ b/solution.py
@@ -503,6 +503,52 @@
     )(*given)
 
 
+FEED_BLOCK = 1024
+
+
+def feed_backward_kernel(grad_ref, down_ref, slope_ref, up_ref, dup_ref, sum_ref, out_ref):
+    low = (dot_nt(grad_ref[...], down_ref[...]) * slope_ref[...].astype(F32)).astype(BF)
+    dup_ref[...] = low
+    sum_ref[...] = low.astype(F32).sum(axis=0, keepdims=True)
+    part = dot_nt(low, up_ref[...])
+
+    @pl.when(pl.program_id(0) == 0)
+    def _():
+        out_ref[...] = part
+
+    @pl.when(pl.program_id(0) > 0)
+    def _():
+        out_ref[...] += part
+
+
+def feed_backward(down_low, feed_down, slope, feed_up):
+    rows, width = down_low.shape
+    hidden = feed_up.shape[1]
+    whole = pl.BlockSpec((rows, width), lambda i: (0, 0))
+    wide = pl.BlockSpec((rows, FEED_BLOCK), lambda i: (0, i))
+    up = pl.BlockSpec((width, FEED_BLOCK), lambda i: (0, i))
+    down = pl.BlockSpec((FEED_BLOCK, width), lambda i: (i, 0))
+    line = pl.BlockSpec((1, FEED_BLOCK), lambda i: (0, i))
+    return pl.pallas_call(
+        feed_backward_kernel,
+        grid=(hidden // FEED_BLOCK,),
+        out_shape=[
+            jax.ShapeDtypeStruct((rows, hidden), BF),
+            jax.ShapeDtypeStruct((1, hidden), F32),
+            jax.ShapeDtypeStruct((rows, width), F32),
+        ],
+        in_specs=[whole, down, wide, up],
+        out_specs=[wide, line, whole],
+        compiler_params=pltpu.CompilerParams(vmem_limit_bytes=VMEM_BYTES),
+        cost_estimate=pl.CostEstimate(
+            flops=4 * rows * width * hidden,
+            bytes_accessed=4 * (width + rows) * hidden,
+            transcendentals=0,
+        ),
+        name="feed_backward",
+    )(down_low, feed_down, slope, feed_up)
+
+
 def self_mask(seg_row, seg_column, length):
     key = lax.broadcasted_iota(jnp.int32, (length, length), 0)
     query = lax.broadcasted_iota(jnp.int32, (length, length), 1)
@@ -724,7 +770,7 @@
             far_two_y = swap_y(far_two)
         for i in range(item_count):
             if tuned and i == half:
-                arrived.append(back_and_forth(tie(sent[i], cross_queries, far_two, line_two_y)))
+                arrived.append(back_and_forth(tie(sent[i], cross_queries, line_two_y)))
             elif tuned and i > half:
                 arrived.append(
                     back_and_forth(tie(sent[i], *arrived[half:], outs[half - 1], far_two_y))
@@ -764,9 +810,9 @@
         )
         down_low = third_grad.astype(BF)
         grad_down = dot_tn(activation_low, down_low)
-        upward_low = (dot_nt(down_low, feed_down) * slope.astype(F32)).astype(BF)
+        upward_low, grad_feed_shift, second_grad = feed_backward(down_low, feed_down, slope, feed_up)
         grad_up = dot_tn(second_low, upward_low)
-        second_grad = third_grad + dot_nt(upward_low, feed_up)
+        second_grad = third_grad + second_grad
         cross_grad, second_gain, second_shift = second_norm_back(second_grad)
         cross_low = cross_grad.astype(BF)
         grad_cross_out = dot_tn(cross_attended, cross_low)
@@ -804,7 +850,7 @@
         self_incoming = dot_nt(self_low, self_out).astype(BF).reshape(three)
         if tuned:
             grad_pair = dot_tn(all_sources, all_grads).astype(BF)
-            sums_two = Reduce([(tie(hidden_low, memory_back[0]), cross_query_low), grad_pair])
+            sums_two = Reduce([(hidden_low, cross_query_low), tie(grad_pair, memory_back[0])])
             self_incoming = tie(self_incoming, sums_one.over_x(), *sums_two.sent)
         joined_grad = self_backward(segment_ids, qkv, self_incoming, self_logs)
         joined_grad = joined_grad.reshape(row_count, 3 * width)
@@ -830,7 +876,7 @@
             ]
         )
         grad_gain_rows = jnp.stack([first_gain, second_gain, third_gain])
-        grad_feed_shift = column_sum(upward_low)
+        grad_feed_shift = grad_feed_shift[0]
         block_low = block_out.astype(BF).reshape(decoder_in.shape)
         if tuned:
             count = shifts.shape[1]

time: 839 us -> 838 us (level)
  waiting for transfers between devices: 193 us -> 169 us
  matrix products: 142 us -> 123 us
  Pallas kernels: 179 us -> 195 us
  local copies, waits for them, and re-layouts: 102 us -> 113 us
  other arithmetic: 80.2 us -> 90.9 us
    ppermute x62, waiting for transfers between devices: 177 us -> 152 us  [move(): return lambda value: lax.ppermute(value, axis, pairs)]
    dot_general x6 -> x4, matrix products: 36.4 us -> 14.7 us  [dot_nt(): lax.dot_general(left, right, (((1,), (1,)), ((), ())), preferred_element_...]
    pallas_call x0 -> x1, Pallas kernels: none -> 15.8 us  [feed_backward(): pl.pallas_call(feed_backward_kernel, grid=(hidden // FEED_BLOCK,), out_sh...]
    unnamed x278 -> x246, local copies, waits for them, and re-layouts: 43.5 us -> 52.3 us
  transfers between devices with their start and end apart: 67 -> 67, of which waited for: 25 -> 23; matrix products, arithmetic and copies ran while one was open for 28% -> 30% of each run, Pallas kernels for 17% -> 17%
where the time goes in v4:
time: 838 us; the launch traced here: 830 us
  Pallas kernels  195 us (23%)
  waiting for transfers between devices  169 us (20%)
  starting transfers between devices  137 us (16%)
  matrix products  123 us (15%)
  local copies, waits for them, and re-layouts  113 us (13%)
  other arithmetic  90.9 us (11%)
    ppermute x62, waiting for transfers between devices, move(): return lambda value: lax.ppermute(value, axis, pairs)  152 us
    ppermute x62, starting transfers between devices, move(): return lambda value: lax.ppermute(value, axis, pairs)  104 us
    dot_general x19, matrix products, dot_tn(): lax.dot_general(left, right, (((0,), (0,)), ((), ())), preferred_element_...  73.3 us
    pallas_call x4, Pallas kernels, cross_backward(): pl.pallas_call(cross_backward_kernel, out_shape=[jax.ShapeDtypeStruct(que...  71.5 us
    pallas_call x4, Pallas kernels, cross_forward(): pl.pallas_call(cross_forward_kernel, out_shape=[jax.ShapeDtypeStruct(quer...  61.5 us
    unnamed x246, local copies, waits for them, and re-layouts  52.3 us
    convert_element_type x16, other arithmetic, add_low(): return total.astype(BF)  34.2 us
    all_to_all x5, starting transfers between devices, back_and_forth(): lax.all_to_all(blocks, 'blk', split_axis=0, concat_axis=0, tiled=True)  33.4 us
  transfers between devices with their start and end apart: 67, of which 23 were waited for; matrix products, arithmetic and copies ran while one was open for 30% of the time, Pallas kernels for 17%

profile of v4, /device:TPU:1, one launch (start us, length us, event | category | flops | bytes accessed | tf_op | source)
XLA Modules:
  0.0 830.1 jit_solution(6796384956439079698)
XLA Ops:
  6.1 4.1 collective-permute-start.2
  12.7 7.3 collective-permute-done.2
  41.1 9.8 %collective-permute-done.6 = bf16[128,1920]{1,0:T(8,128)(2,1)S(1)} collective-permute-done((bf16[128,1920]{1,0:T(8,128)(2,1)}, bf16[128,1920]{1,0:T(8,128)(2,1)S(1)}, u32[]{:S(2)}, u32[]{:S(2)}) %collective-permute-start.6) | collective-permute-done | bytes 491552 | tf_op jit(solution)/shard_map/ppermute | solution.py:16
  56.5 6.6 collective-permute-done.17
  67.3 4.8 stack.165
  73.3 8.5 %collective-permute-done.7.refs_7_ = bf16[3,128,1920]{2,1,0:T(8,128)(2,1)} collective-permute-done((bf16[3,128,1920]{2,1,0:T(8,128)(2,1)S(1)}, bf16[3,128,1920]{2,1,0:T(8,128)(2,1)}, u32[]{:S(2)}, u32[]{:S(2)}) %collective-permute-start.7) | collective-permute-done | bytes 1474592 | tf_op jit(solution)/shard_map/ppermute | solution.py:16
  84.0 10.4 %collective-permute-done.22 = bf16[128,2304]{1,0:T(8,128)(2,1)S(1)} collective-permute-done((bf16[128,2304]{1,0:T(8,128)(2,1)S(1)}, bf16[128,2304]{1,0:T(8,128)(2,1)S(1)}, u32[]{:S(2)}, u32[]{:S(2)}) %collective-permute-start.22) | collective-permute-done | bytes 589856 | tf_op jit(solution)/shard_map/ppermute | solution.py:16
  96.7 6.5 all-to-all-start
  106.3 11.2 %collective-permute-start.11 = (bf16[4,128,1920]{2,1,0:T(8,128)(2,1)S(1)}, bf16[4,128,1920]{2,1,0:T(8,128)(2,1)}, u32[]{:S(2)}, u32[]{:S(2)}) collective-permute-start(bf16[4,128,1920]{2,1,0:T(8,128)(2,1)S(1)} %pad_maximum_fusion.5.refs_6_), channel_id=1, source_target_pairs={{0,8},{8,0},{16,24},{24,16},{1,9},{9,1},{17,25},{25,17},{2,10},{10... | collective-permute-start | bytes 5898248 | tf_op jit(solution)/shard_map/ppermute | solution.py:16
  121.0 5.9 collective-permute-done.10.refs_9_
  126.9 11.6 %collective-permute-start.14 = (bf16[3,128,1920]{2,1,0:T(8,128)(2,1)}, bf16[3,128,1920]{2,1,0:T(8,128)(2,1)}, u32[]{:S(2)}, u32[]{:S(2)}) collective-permute-start(bf16[3,128,1920]{2,1,0:T(8,128)(2,1)} %collective-permute-done.10.refs_9_), channel_id=1, source_target_pairs={{0,8},{8,0},{16,24},{24,16},{1,9},{9,1},{17,25},{25,17},{2,10},{10... | collective-permute-start | bytes 4423688 | tf_op jit(solution)/shard_map/ppermute | solution.py:16
  140.0 4.8 slice_bitcast_fusion
  147.4 12.9 %place_rows.2 = (bf16[1024,128]{1,0:T(8,128)(2,1)}, bf16[1024,3072]{1,0:T(8,128)(2,1)}, bf16[1024,1024]{1,0:T(8,128)(2,1)}, bf16[1024,1024]{1,0:T(8,128)(2,1)}, bf16[1024,2048]{1,0:T(8,128)(2,1)}) custom-call(s32[10]{0:T(128)} %stack.136.refs_0_, bf16[128,128]{1,0:T(8,128)(2,1)} %get-tuple-element.278.refs_1_, bf16[128,3072]{1,0:T(8,128)(2,1)} %refs_2_.2, ...), custom_call_target="tpu_custom_call" | custom-call | bytes 29884416 | tf_op jit(solution)/shard_map/place_rows/pallas_call | solution.py:148
  161.1 7.6 multiply_convert_fusion.1
  168.7 6.1 self_forward.1
  181.8 4.5 collective-permute-done.23
  186.3 3.9 all-to-all-done
  190.3 10.3 %all-to-all-start.1 = ((bf16[8,128,1024]{2,1,0:T(8,128)(2,1)}), bf16[8,128,1024]{2,1,0:T(8,128)(2,1)}, u32[]{:S(2)}, u32[]{:S(2)}) async-start(bf16[8,128,1024]{2,1,0:T(8,128)(2,1)} %get-tuple-element.99), calls=%async_computation.1 | async-start | bytes 4194304 | tf_op jit(solution)/shard_map/all_to_all | solution.py:649
  205.3 4.9 fusion.163
  210.2 15.3 %cross_forward.4 = (bf16[128,1024]{1,0:T(8,128)(2,1)}, f32[8,1,256]{2,1,0:T(1,128)}, bf16[1024,2048]{1,0:T(8,128)(2,1)}, bf16[4,1024,1024]{2,1,0:T(8,128)(2,1)}) custom-call(s32[1]{0:T(128)} %get-tuple-element.281.lengths, bf16[128,1024]{1,0:T(8,128)(2,1)} %get-tuple-element.261.q_ref, bf16[1024,1024]{1,0:T(8,128)(2,1)} %bitcast.529, ...), custom_call_target="tpu_custom_call" | custom-call | flops 6442450944 | bytes 12582912 | tf_op jit(solution)/shard_map/cross_forward/pallas_call | solution.py:436
  225.5 15.4 %cross_forward.5 = (bf16[128,1024]{1,0:T(8,128)(2,1)}, f32[8,1,256]{2,1,0:T(1,128)}, bf16[1024,2048]{1,0:T(8,128)(2,1)}, bf16[4,1024,1024]{2,1,0:T(8,128)(2,1)}) custom-call(s32[1]{0:T(128)} %get-tuple-element.280.lengths, bf16[128,1024]{1,0:T(8,128)(2,1)} %get-tuple-element.260.q_ref, ...), custom_call_target="tpu_custom_call", output_to_operand_aliasing={{3}: (5, {})} | custom-call | flops 6442450944 | bytes 12582912 | tf_op jit(solution)/shard_map/cross_forward/pallas_call | solution.py:436
  240.9 6.5 all-to-all-done.1
  247.4 5.8 all-to-all-start.2
  253.2 3.0 pad_maximum_fusion.1.refs_4_
  257.6 3.2 pad_maximum_fusion.2.refs_6_
  262.1 15.4 %cross_forward.6 = (bf16[128,1024]{1,0:T(8,128)(2,1)}, f32[8,1,256]{2,1,0:T(1,128)}, bf16[1024,2048]{1,0:T(8,128)(2,1)}, bf16[4,1024,1024]{2,1,0:T(8,128)(2,1)}) custom-call(s32[1]{0:T(128)} %get-tuple-element.282.lengths, bf16[128,1024]{1,0:T(8,128)(2,1)} %get-tuple-element.259.q_ref, ...), custom_call_target="tpu_custom_call", output_to_operand_aliasing={{3}: (5, {})} | custom-call | flops 6442450944 | bytes 12582912 | tf_op jit(solution)/shard_map/cross_forward/pallas_call | solution.py:436
  277.5 16.1 %place_rows.3 = (bf16[1024,1024]{1,0:T(8,128)(2,1)}, bf16[1024,4096]{1,0:T(8,128)(2,1)}, bf16[4096,1024]{1,0:T(8,128)(2,1)}) custom-call(s32[10]{0:T(128)} %stack.136.refs_0_, bf16[128,1024]{1,0:T(8,128)(2,1)} %refs_1_.1, bf16[128,4096]{1,0:T(8,128)(2,1)} %refs_2_.3, bf16[512,1024]{1,0:T(8,128)(2,1)} %refs_3_.3, ...), custom_call_target="tpu_custom_call" | custom-call | bytes 37748736 | tf_op jit(solution)/shard_map/place_rows/pallas_call | solution.py:148
  293.7 6.4 all-to-all-done.2
  300.1 15.5 %cross_forward.7 = (bf16[128,1024]{1,0:T(8,128)(2,1)}, f32[8,1,256]{2,1,0:T(1,128)}, bf16[1024,2048]{1,0:T(8,128)(2,1)}, bf16[4,1024,1024]{2,1,0:T(8,128)(2,1)}) custom-call(s32[1]{0:T(128)} %get-tuple-element.279.lengths, bf16[128,1024]{1,0:T(8,128)(2,1)} %get-tuple-element.258.q_ref, ...), custom_call_target="tpu_custom_call", output_to_operand_aliasing={{3}: (5, {})} | custom-call | flops 6442450944 | bytes 12582912 | tf_op jit(solution)/shard_map/cross_forward/pallas_call | solution.py:436
  319.7 13.0 %fusion.6 = (bf16[512,4096]{1,0:T(8,128)(2,1)}, bf16[512,4096]{1,0:T(8,128)(2,1)S(1)}) fusion(f32[4096]{0:T(1024)S(1)} %convert.92, bf16[512,1024]{1,0:T(8,128)(2,1)S(1)} %fusion.18, bf16[1024,4096]{1,0:T(8,128)(2,1)S(1)} %bitcast.595), kind=kOutput, calls=%fused_computation.8 | convolution fusion | flops 4351590400 | bytes 17842176 | tf_op jit(solution)/shard_map/dot_general | solution.py:800
  332.8 4.8 fusion.175
  342.8 15.8 %feed_backward.1 = (bf16[512,4096]{1,0:T(8,128)(2,1)}, f32[1,4096]{1,0:T(1,128)}, f32[512,1024]{1,0:T(8,128)}) custom-call(bf16[512,1024]{1,0:T(8,128)(2,1)} %add_convert_fusion.16.grad_ref, bf16[4096,1024]{1,0:T(8,128)(2,1)} %get-tuple-element.110.down_ref, bf16[512,4096]{1,0:T(8,128)(2,1)} %get-tuple-element.170.slope_ref, ...), custom_call_target="tpu_custom_call" | custom-call | flops 8589934592 | bytes 25165824 | tf_op jit(solution)/shard_map/feed_backward/pallas_call | solution.py:532
  366.5 18.2 %cross_backward.4 = (bf16[128,1024]{1,0:T(8,128)(2,1)}, f32[1,1024]{1,0:T(1,128)}, bf16[4,1024,2048]{2,1,0:T(8,128)(2,1)}, bf16[8,2,128,1024]{3,2,1,0:T(8,128)(2,1)}) custom-call(s32[1]{0:T(128)} %get-tuple-element.281.lengths, bf16[128,1024]{1,0:T(8,128)(2,1)} %get-tuple-element.261.q_ref, bf16[128,1024]{1,0:T(8,128)(2,1)} %get-tuple-element.254.grad_ref, ...), custom_call_target="tpu_custom_call" | custom-call | flops 9663676416 | bytes 18874368 | tf_op jit(solution)/shard_map/cross_backward/pallas_call | solution.py:475
  384.8 6.7 convolution_convert_fusion
  395.0 4.4 convolution_convert_fusion.2
  400.8 3.0 convolution_convert_fusion.8
  404.3 17.6 %cross_backward.5 = (bf16[128,1024]{1,0:T(8,128)(2,1)}, f32[1,1024]{1,0:T(1,128)}, bf16[4,1024,2048]{2,1,0:T(8,128)(2,1)}, bf16[8,2,128,1024]{3,2,1,0:T(8,128)(2,1)}) custom-call(s32[1]{0:T(128)} %get-tuple-element.280.lengths, bf16[128,1024]{1,0:T(8,128)(2,1)} %get-tuple-element.260.q_ref, ...), custom_call_target="tpu_custom_call", output_to_operand_aliasing={{2}: (6, {}), {3}: (7, {})} | custom-call | flops 9663676416 | bytes 18874368 | tf_op jit(solution)/shard_map/cross_backward/pallas_call | solution.py:475
  421.9 4.9 all-to-all-start.3
  435.0 4.4 add_convert_fusion.5
  439.6 4.6 add_convert_fusion.4
  445.4 17.7 %cross_backward.6 = (bf16[128,1024]{1,0:T(8,128)(2,1)}, f32[1,1024]{1,0:T(1,128)}, bf16[4,1024,2048]{2,1,0:T(8,128)(2,1)}, bf16[8,2,128,1024]{3,2,1,0:T(8,128)(2,1)}) custom-call(s32[1]{0:T(128)} %get-tuple-element.282.lengths, bf16[128,1024]{1,0:T(8,128)(2,1)} %get-tuple-element.259.q_ref, ...), custom_call_target="tpu_custom_call", output_to_operand_aliasing={{2}: (6, {})} | custom-call | flops 9663676416 | bytes 18874368 | tf_op jit(solution)/shard_map/cross_backward/pallas_call | solution.py:475
  463.1 17.9 %cross_backward.7 = (bf16[128,1024]{1,0:T(8,128)(2,1)}, f32[1,1024]{1,0:T(1,128)}, bf16[4,1024,2048]{2,1,0:T(8,128)(2,1)}, bf16[8,2,128,1024]{3,2,1,0:T(8,128)(2,1)}) custom-call(s32[1]{0:T(128)} %get-tuple-element.279.lengths, bf16[128,1024]{1,0:T(8,128)(2,1)} %get-tuple-element.258.q_ref, ...), custom_call_target="tpu_custom_call", output_to_operand_aliasing={{2}: (6, {}), {3}: (7, {})} | custom-call | flops 9663676416 | bytes 18874368 | tf_op jit(solution)/shard_map/cross_backward/pallas_call | solution.py:475
  482.8 4.0 multiply_reduce_fusion.1
  492.3 21.3 %bitcast_convert_fusion = bf16[1024,2048]{1,0:T(8,128)(2,1)} fusion(bf16[4,1024,1024]{2,1,0:T(8,128)(2,1)} %get-tuple-element.137, bf16[4,1024,2048]{2,1,0:T(8,128)(2,1)S(1)} %copy-done.87), kind=kOutput, calls=%fused_computation.10 | convolution fusion | flops 17181966336 | bytes 29360128 | tf_op jit(solution)/shard_map/dot_general | solution.py:293
  515.3 3.2 add_convert_fusion.2
  528.3 5.9 all-to-all-start.4
  548.8 10.7 %self_backward.1 = bf16[4,128,3072]{2,1,0:T(8,128)(2,1)} custom-call(s32[4,1,128]{2,1,0:T(1,128)} %bitcast.566, s32[4,128,1]{2,1,0:T(8,128)} %copy.117.seg_column, bf16[4,128,3072]{2,1,0:T(8,128)(2,1)} %bitcast.502, bf16[4,128,1024]{2,1,0:T(8,128)(2,1)} %bitcast.541, f32[4,8,1,256]{3,2,1,0:T(1,128)} %get-tuple-element.142.log_ref), custom_call_target="tpu_custom_call" | custom-call | tf_op jit(solution)/shard_map/self_backward/pallas_call | solution.py:622
  565.9 3.5 fusion.7
  604.1 40.7 %collective-permute-done.53 = bf16[4,9,128,256]{3,2,1,0:T(8,128)(2,1)} collective-permute-done((bf16[4,9,128,256]{3,2,1,0:T(8,128)(2,1)}, bf16[4,9,128,256]{3,2,1,0:T(8,128)(2,1)}, u32[]{:S(2)}, u32[]{:S(2)}) %collective-permute-start.53) | collective-permute-done | bytes 2359328 | tf_op jit(solution)/shard_map/ppermute | solution.py:16
  644.8 3.3 add_convert_fusion
  649.3 8.4 %collective-permute-start.54 = (bf16[9,128,256]{2,1,0:T(8,128)(2,1)}, bf16[9,128,256]{2,1,0:T(8,128)(2,1)}, u32[]{:S(2)}, u32[]{:S(2)}) collective-permute-start(bf16[9,128,256]{2,1,0:T(8,128)(2,1)} %get-tuple-element.217), channel_id=1, source_target_pairs={{0,2},{1,3},{8,10},{9,11},{16,18},{17,19},{24,26},{25,27}} | collective-permute-start | bytes 1769480 | tf_op jit(solution)/shard_map/ppermute | solution.py:16
  677.9 3.1 constant_dynamic-slice_fusion.13
  688.3 10.2 %collective-permute-done.55 = bf16[9,128,256]{2,1,0:T(8,128)(2,1)} collective-permute-done((bf16[9,128,256]{2,1,0:T(8,128)(2,1)}, bf16[9,128,256]{2,1,0:T(8,128)(2,1)}, u32[]{:S(2)}, u32[]{:S(2)}) %collective-permute-start.55) | collective-permute-done | bytes 589856 | tf_op jit(solution)/shard_map/ppermute | solution.py:16
  703.9 7.6 collective-permute-done.43
  711.5 3.7 add_convert_fusion.1
  730.2 5.1 collective-permute-start.46
  735.3 5.4 collective-permute-done.56
  743.3 8.7 %collective-permute-done.46 = bf16[8,128,256]{2,1,0:T(8,128)(2,1)} collective-permute-done((bf16[8,128,256]{2,1,0:T(8,128)(2,1)}, bf16[8,128,256]{2,1,0:T(8,128)(2,1)}, u32[]{:S(2)}, u32[]{:S(2)}) %collective-permute-start.46) | collective-permute-done | bytes 524320 | tf_op jit(solution)/shard_map/ppermute | solution.py:16
  757.6 4.0 collective-permute-start.61
  761.6 7.2 add_convert_fusion.10
  768.8 4.1 collective-permute-start.47
  775.5 7.6 pad_maximum_fusion
  784.6 5.6 collective-permute-done.50
  793.9 10.3 %collective-permute-done.51 = bf16[8,128,256]{2,1,0:T(8,128)(2,1)S(1)} collective-permute-done((bf16[8,128,256]{2,1,0:T(8,128)(2,1)S(1)}, bf16[8,128,256]{2,1,0:T(8,128)(2,1)S(1)}, u32[]{:S(2)}, u32[]{:S(2)}) %collective-permute-start.51) | collective-permute-done | bytes 524320 | tf_op jit(solution)/shard_map/ppermute | solution.py:16
  (522 shorter events, 266.2 us)
Async XLA Ops:
  6.1 13.9 %collective-permute-start.2 = (bf16[128,1920]{1,0:T(8,128)(2,1)S(1)}, bf16[128,1920]{1,0:T(8,128)(2,1)S(1)}, u32[]{:S(2)}, u32[]{:S(2)}) collective-permute-start(bf16[128,1920]{1,0:T(8,128)(2,1)S(1)} %constant_dynamic-update-slice_fusion), channel_id=1, source_target_pairs={{0,2},{1,3},{2,4},{3,5},{4,6},{5,7},{8,10},{9,11},{10,12},{11,13},... | collective-permute-start | bytes 1474568 | tf_op jit(solution)/shard_map/ppermute | solution.py:16
  10.2 13.7 %collective-permute-start.1 = (bf16[128,1920]{1,0:T(8,128)(2,1)S(1)}, bf16[128,1920]{1,0:T(8,128)(2,1)S(1)}, u32[]{:S(2)}, u32[]{:S(2)}) collective-permute-start(bf16[128,1920]{1,0:T(8,128)(2,1)S(1)} %constant_dynamic-update-slice_fusion), channel_id=1, source_target_pairs={{2,0},{3,1},{4,2},{5,3},{6,4},{7,5},{10,8},{11,9},{12,10},{13,11},... | collective-permute-start | bytes 1474568 | tf_op jit(solution)/shard_map/ppermute | solution.py:16
  11.5 19.8 %collective-permute-start = (bf16[128,1920]{1,0:T(8,128)(2,1)S(1)}, bf16[128,1920]{1,0:T(8,128)(2,1)S(1)}, u32[]{:S(2)}, u32[]{:S(2)}) collective-permute-start(bf16[128,1920]{1,0:T(8,128)(2,1)S(1)} %constant_dynamic-update-slice_fusion), channel_id=1, source_target_pairs={{0,1},{1,0},{2,3},{3,2},{4,5},{5,4},{6,7},{7,6},{8,9},{9,8},{10,11... | collective-permute-start | bytes 1474568 | tf_op jit(solution)/shard_map/ppermute | solution.py:16
  20.0 11.2 %collective-permute-start.3 = (bf16[128,1920]{1,0:T(8,128)(2,1)S(1)}, bf16[128,1920]{1,0:T(8,128)(2,1)S(1)}, u32[]{:S(2)}, u32[]{:S(2)}) collective-permute-start(bf16[128,1920]{1,0:T(8,128)(2,1)S(1)} %collective-permute-done.2), channel_id=1, source_target_pairs={{2,4},{3,5},{4,6},{5,7},{10,12},{11,13},{12,14},{13,15},{18,20},{1... | collective-permute-start | bytes 1474568 | tf_op jit(solution)/shard_map/ppermute | solution.py:16
  23.8 14.8 %collective-permute-start.5 = (bf16[128,1920]{1,0:T(8,128)(2,1)S(1)}, bf16[128,1920]{1,0:T(8,128)(2,1)}, u32[]{:S(2)}, u32[]{:S(2)}) collective-permute-start(bf16[128,1920]{1,0:T(8,128)(2,1)S(1)} %collective-permute-done.1), channel_id=1, source_target_pairs={{2,0},{3,1},{4,2},{5,3},{10,8},{11,9},{12,10},{13,11},{18,16},{19,... | collective-permute-start | bytes 1474568 | tf_op jit(solution)/shard_map/ppermute | solution.py:16
  31.2 9.8 %collective-permute-start.4 = (bf16[128,1920]{1,0:T(8,128)(2,1)S(1)}, bf16[128,1920]{1,0:T(8,128)(2,1)}, u32[]{:S(2)}, u32[]{:S(2)}) collective-permute-start(bf16[128,1920]{1,0:T(8,128)(2,1)S(1)} %collective-permute-done.3), channel_id=1, source_target_pairs={{4,6},{5,7},{12,14},{13,15},{20,22},{21,23},{28,30},{29,31}} | collective-permute-start | bytes 1474568 | tf_op jit(solution)/shard_map/ppermute | solution.py:16
  34.1 18.4 %collective-permute-start.15 = (bf16[128,2304]{1,0:T(8,128)(2,1)}, bf16[128,2304]{1,0:T(8,128)(2,1)S(1)}, u32[]{:S(2)}, u32[]{:S(2)}) collective-permute-start(bf16[128,2304]{1,0:T(8,128)(2,1)} %constant_dynamic-update-slice_fusion.4), channel_id=1, source_target_pairs={{0,1},{1,0},{2,3},{3,2},{4,5},{5,4},{6,7},{7,6},{8,9},{9,8},{10,11... | collective-permute-start | bytes 1769480 | tf_op jit(solution)/shard_map/ppermute | solution.py:16
  35.4 17.2 %collective-permute-start.8 = (bf16[128,1920]{1,0:T(8,128)(2,1)S(1)}, bf16[128,1920]{1,0:T(8,128)(2,1)S(1)}, u32[]{:S(2)}, u32[]{:S(2)}) collective-permute-start(bf16[128,1920]{1,0:T(8,128)(2,1)S(1)} %collective-permute-done), channel_id=1, source_target_pairs={{0,16},{8,24},{16,0},{24,8},{1,17},{9,25},{17,1},{25,9},{2,18},{10... | collective-permute-start | bytes 1474568 | tf_op jit(solution)/shard_map/ppermute | solution.py:16
  38.6 12.3 %collective-permute-start.6 = (bf16[128,1920]{1,0:T(8,128)(2,1)}, bf16[128,1920]{1,0:T(8,128)(2,1)S(1)}, u32[]{:S(2)}, u32[]{:S(2)}) collective-permute-start(bf16[128,1920]{1,0:T(8,128)(2,1)} %collective-permute-done.5), channel_id=1, source_target_pairs={{2,0},{3,1},{10,8},{11,9},{18,16},{19,17},{26,24},{27,25}} | collective-permute-start | bytes 1474568 | tf_op jit(solution)/shard_map/ppermute | solution.py:16
  51.3 30.6 %collective-permute-start.7 = (bf16[3,128,1920]{2,1,0:T(8,128)(2,1)S(1)}, bf16[3,128,1920]{2,1,0:T(8,128)(2,1)}, u32[]{:S(2)}, u32[]{:S(2)}) collective-permute-start(bf16[3,128,1920]{2,1,0:T(8,128)(2,1)S(1)} %pad_maximum_fusion.10), channel_id=1, source_target_pairs={{0,1},{1,0},{2,3},{3,2},{4,5},{5,4},{6,7},{7,6},{8,9},{9,8},{10,11... | collective-permute-start | bytes 4423688 | tf_op jit(solution)/shard_map/ppermute | solution.py:16
  52.6 10.6 %collective-permute-start.17 = (bf16[128,2304]{1,0:T(8,128)(2,1)}, bf16[128,2304]{1,0:T(8,128)(2,1)S(1)}, u32[]{:S(2)}, u32[]{:S(2)}) collective-permute-start(bf16[128,2304]{1,0:T(8,128)(2,1)} %constant_dynamic-update-slice_fusion.4), channel_id=1, source_target_pairs={{0,2},{1,3},{2,4},{3,5},{4,6},{5,7},{8,10},{9,11},{10,12},{11,13},... | collective-permute-start | bytes 1769480 | tf_op jit(solution)/shard_map/ppermute | solution.py:16
  53.9 12.1 %collective-permute-start.16 = (bf16[128,2304]{1,0:T(8,128)(2,1)}, bf16[128,2304]{1,0:T(8,128)(2,1)S(1)}, u32[]{:S(2)}, u32[]{:S(2)}) collective-permute-start(bf16[128,2304]{1,0:T(8,128)(2,1)} %constant_dynamic-update-slice_fusion.4), channel_id=1, source_target_pairs={{2,0},{3,1},{4,2},{5,3},{6,4},{7,5},{10,8},{11,9},{12,10},{13,11},... | collective-permute-start | bytes 1769480 | tf_op jit(solution)/shard_map/ppermute | solution.py:16
  55.2 18.1 %collective-permute-start.19 = (bf16[128,2304]{1,0:T(8,128)(2,1)S(1)}, bf16[128,2304]{1,0:T(8,128)(2,1)S(1)}, u32[]{:S(2)}, u32[]{:S(2)}) collective-permute-start(bf16[128,2304]{1,0:T(8,128)(2,1)S(1)} %collective-permute-done.15), channel_id=1, source_target_pairs={{0,16},{8,24},{16,0},{24,8},{1,17},{9,25},{17,1},{25,9},{2,18},{10... | collective-permute-start | bytes 1769480 | tf_op jit(solution)/shard_map/ppermute | solution.py:16
  63.1 10.2 %collective-permute-start.18 = (bf16[128,2304]{1,0:T(8,128)(2,1)S(1)}, bf16[128,2304]{1,0:T(8,128)(2,1)S(1)}, u32[]{:S(2)}, u32[]{:S(2)}) collective-permute-start(bf16[128,2304]{1,0:T(8,128)(2,1)S(1)} %collective-permute-done.17), channel_id=1, source_target_pairs={{2,4},{3,5},{4,6},{5,7},{10,12},{11,13},{12,14},{13,15},{18,20},{1... | collective-permute-start | bytes 1769480 | tf_op jit(solution)/shard_map/ppermute | solution.py:16
  66.0 16.5 %collective-permute-start.21 = (bf16[128,2304]{1,0:T(8,128)(2,1)S(1)}, bf16[128,2304]{1,0:T(8,128)(2,1)S(1)}, u32[]{:S(2)}, u32[]{:S(2)}) collective-permute-start(bf16[128,2304]{1,0:T(8,128)(2,1)S(1)} %collective-permute-done.16), channel_id=1, source_target_pairs={{2,0},{3,1},{4,2},{5,3},{10,8},{11,9},{12,10},{13,11},{18,16},{19,... | collective-permute-start | bytes 1769480 | tf_op jit(solution)/shard_map/ppermute | solution.py:16
  72.1 24.6 %collective-permute-start.9 = (bf16[3,128,1920]{2,1,0:T(8,128)(2,1)S(1)}, bf16[3,128,1920]{2,1,0:T(8,128)(2,1)}, u32[]{:S(2)}, u32[]{:S(2)}) collective-permute-start(bf16[3,128,1920]{2,1,0:T(8,128)(2,1)S(1)} %pad_maximum_fusion.10), channel_id=1, source_target_pairs={{0,16},{8,24},{16,0},{24,8},{1,17},{9,25},{17,1},{25,9},{2,18},{10... | collective-permute-start | bytes 4423688 | tf_op jit(solution)/shard_map/ppermute | solution.py:16
  82.6 11.8 %collective-permute-start.22 = (bf16[128,2304]{1,0:T(8,128)(2,1)S(1)}, bf16[128,2304]{1,0:T(8,128)(2,1)S(1)}, u32[]{:S(2)}, u32[]{:S(2)}) collective-permute-start(bf16[128,2304]{1,0:T(8,128)(2,1)S(1)} %collective-permute-done.21), channel_id=1, source_target_pairs={{2,0},{3,1},{10,8},{11,9},{18,16},{19,17},{26,24},{27,25}} | collective-permute-start | bytes 1769480 | tf_op jit(solution)/shard_map/ppermute | solution.py:16
  96.7 93.6 %all-to-all-start = ((bf16[8,2,128,1024]{3,2,1,0:T(8,128)(2,1)}), bf16[8,2,128,1024]{3,2,1,0:T(8,128)(2,1)}, u32[]{:S(2)}, u32[]{:S(2)}) async-start(bf16[8,2,128,1024]{3,2,1,0:T(8,128)(2,1)} %stack.165), calls=%async_computation | async-start | bytes 8388608 | tf_op jit(solution)/shard_map/all_to_all | solution.py:649
  103.2 23.7 %collective-permute-start.10 = (bf16[3,128,1920]{2,1,0:T(8,128)(2,1)}, bf16[3,128,1920]{2,1,0:T(8,128)(2,1)}, u32[]{:S(2)}, u32[]{:S(2)}) collective-permute-start(bf16[3,128,1920]{2,1,0:T(8,128)(2,1)} %collective-permute-done.7.refs_7_), channel_id=1, source_target_pairs={{0,16},{8,24},{16,0},{24,8},{1,17},{9,25},{17,1},{25,9},{2,18},{10... | collective-permute-start | bytes 4423688 | tf_op jit(solution)/shard_map/ppermute | solution.py:16
  106.3 39.8 %collective-permute-start.11 = (bf16[4,128,1920]{2,1,0:T(8,128)(2,1)S(1)}, bf16[4,128,1920]{2,1,0:T(8,128)(2,1)}, u32[]{:S(2)}, u32[]{:S(2)}) collective-permute-start(bf16[4,128,1920]{2,1,0:T(8,128)(2,1)S(1)} %pad_maximum_fusion.5.refs_6_), channel_id=1, source_target_pairs={{0,8},{8,0},{16,24},{24,16},{1,9},{9,1},{17,25},{25,17},{2,10},{10... | collective-permute-start | bytes 5898248 | tf_op jit(solution)/shard_map/ppermute | solution.py:16
  120.4 26.9 %collective-permute-start.13 = (bf16[4,128,1920]{2,1,0:T(8,128)(2,1)}, bf16[4,128,1920]{2,1,0:T(8,128)(2,1)}, u32[]{:S(2)}, u32[]{:S(2)}) collective-permute-start(bf16[4,128,1920]{2,1,0:T(8,128)(2,1)} %pad_maximum_fusion.6.refs_8_), channel_id=1, source_target_pairs={{0,8},{8,0},{16,24},{24,16},{1,9},{9,1},{17,25},{25,17},{2,10},{10... | collective-permute-start | bytes 5898248 | tf_op jit(solution)/shard_map/ppermute | solution.py:16
  121.0 26.3 %collective-permute-start.12 = (bf16[3,128,1920]{2,1,0:T(8,128)(2,1)}, bf16[3,128,1920]{2,1,0:T(8,128)(2,1)}, u32[]{:S(2)}, u32[]{:S(2)}) collective-permute-start(bf16[3,128,1920]{2,1,0:T(8,128)(2,1)} %collective-permute-done.7.refs_7_), channel_id=1, source_target_pairs={{0,8},{8,0},{16,24},{24,16},{1,9},{9,1},{17,25},{25,17},{2,10},{10... | collective-permute-start | bytes 4423688 | tf_op jit(solution)/shard_map/ppermute | solution.py:16
  126.9 20.4 %collective-permute-start.14 = (bf16[3,128,1920]{2,1,0:T(8,128)(2,1)}, bf16[3,128,1920]{2,1,0:T(8,128)(2,1)}, u32[]{:S(2)}, u32[]{:S(2)}) collective-permute-start(bf16[3,128,1920]{2,1,0:T(8,128)(2,1)} %collective-permute-done.10.refs_9_), channel_id=1, source_target_pairs={{0,8},{8,0},{16,24},{24,16},{1,9},{9,1},{17,25},{25,17},{2,10},{10... | collective-permute-start | bytes 4423688 | tf_op jit(solution)/shard_map/ppermute | solution.py:16
  144.8 56.5 %collective-permute-start.24 = (bf16[3,128,2304]{2,1,0:T(8,128)(2,1)}, bf16[3,128,2304]{2,1,0:T(8,128)(2,1)}, u32[]{:S(2)}, u32[]{:S(2)}) collective-permute-start(bf16[3,128,2304]{2,1,0:T(8,128)(2,1)} %pad_maximum_fusion.7), channel_id=1, source_target_pairs={{0,1},{1,0},{2,3},{3,2},{4,5},{5,4},{6,7},{7,6},{8,9},{9,8},{10,11... | collective-permute-start | bytes 5308424 | tf_op jit(solution)/shard_map/ppermute | solution.py:16
  146.1 40.2 %collective-permute-start.23 = (bf16[3,128,2304]{2,1,0:T(8,128)(2,1)}, bf16[3,128,2304]{2,1,0:T(8,128)(2,1)}, u32[]{:S(2)}, u32[]{:S(2)}) collective-permute-start(bf16[3,128,2304]{2,1,0:T(8,128)(2,1)} %pad_maximum_fusion.7), channel_id=1, source_target_pairs={{0,16},{8,24},{16,0},{24,8},{1,17},{9,25},{17,1},{25,9},{2,18},{10... | collective-permute-start | bytes 5308424 | tf_op jit(solution)/shard_map/ppermute | solution.py:16
  190.3 57.1 %all-to-all-start.1 = ((bf16[8,128,1024]{2,1,0:T(8,128)(2,1)}), bf16[8,128,1024]{2,1,0:T(8,128)(2,1)}, u32[]{:S(2)}, u32[]{:S(2)}) async-start(bf16[8,128,1024]{2,1,0:T(8,128)(2,1)} %get-tuple-element.99), calls=%async_computation.1 | async-start | bytes 4194304 | tf_op jit(solution)/shard_map/all_to_all | solution.py:649
  201.3 39.6 %collective-permute-start.25 = (bf16[3,128,2304]{2,1,0:T(8,128)(2,1)}, bf16[3,128,2304]{2,1,0:T(8,128)(2,1)}, u32[]{:S(2)}, u32[]{:S(2)}) collective-permute-start(bf16[3,128,2304]{2,1,0:T(8,128)(2,1)} %collective-permute-done.24.refs_5_), channel_id=1, source_target_pairs={{0,16},{8,24},{16,0},{24,8},{1,17},{9,25},{17,1},{25,9},{2,18},{10... | collective-permute-start | bytes 5308424 | tf_op jit(solution)/shard_map/ppermute | solution.py:16
  247.4 52.8 %all-to-all-start.2 = ((bf16[8,128,1024]{2,1,0:T(8,128)(2,1)}), bf16[8,128,1024]{2,1,0:T(8,128)(2,1)}, u32[]{:S(2)}, u32[]{:S(2)}) async-start(bf16[8,128,1024]{2,1,0:T(8,128)(2,1)} %get-tuple-element.103), calls=%async_computation.2 | async-start | bytes 4194304 | tf_op jit(solution)/shard_map/all_to_all | solution.py:649
  256.2 21.3 %collective-permute-start.26 = (bf16[4,128,2304]{2,1,0:T(8,128)(2,1)}, bf16[4,128,2304]{2,1,0:T(8,128)(2,1)}, u32[]{:S(2)}, u32[]{:S(2)}) collective-permute-start(bf16[4,128,2304]{2,1,0:T(8,128)(2,1)} %pad_maximum_fusion.1.refs_4_), channel_id=1, source_target_pairs={{0,8},{8,0},{16,24},{24,16},{1,9},{9,1},{17,25},{25,17},{2,10},{10... | collective-permute-start | bytes 7077896 | tf_op jit(solution)/shard_map/ppermute | solution.py:16
  260.8 16.7 %collective-permute-start.28 = (bf16[4,128,2304]{2,1,0:T(8,128)(2,1)}, bf16[4,128,2304]{2,1,0:T(8,128)(2,1)}, u32[]{:S(2)}, u32[]{:S(2)}) collective-permute-start(bf16[4,128,2304]{2,1,0:T(8,128)(2,1)} %pad_maximum_fusion.2.refs_6_), channel_id=1, source_target_pairs={{0,8},{8,0},{16,24},{24,16},{1,9},{9,1},{17,25},{25,17},{2,10},{10... | collective-permute-start | bytes 7077896 | tf_op jit(solution)/shard_map/ppermute | solution.py:16
  260.8 16.7 %collective-permute-start.27 = (bf16[3,128,2304]{2,1,0:T(8,128)(2,1)}, bf16[3,128,2304]{2,1,0:T(8,128)(2,1)}, u32[]{:S(2)}, u32[]{:S(2)}) collective-permute-start(bf16[3,128,2304]{2,1,0:T(8,128)(2,1)} %collective-permute-done.24.refs_5_), channel_id=1, source_target_pairs={{0,8},{8,0},{16,24},{24,16},{1,9},{9,1},{17,25},{25,17},{2,10},{10... | collective-permute-start | bytes 5308424 | tf_op jit(solution)/shard_map/ppermute | solution.py:16
  261.3 16.2 %collective-permute-start.29 = (bf16[3,128,2304]{2,1,0:T(8,128)(2,1)}, bf16[3,128,2304]{2,1,0:T(8,128)(2,1)}, u32[]{:S(2)}, u32[]{:S(2)}) collective-permute-start(bf16[3,128,2304]{2,1,0:T(8,128)(2,1)} %collective-permute-done.25.refs_7_), channel_id=1, source_target_pairs={{0,8},{8,0},{16,24},{24,16},{1,9},{9,1},{17,25},{25,17},{2,10},{10... | collective-permute-start | bytes 5308424 | tf_op jit(solution)/shard_map/ppermute | solution.py:16
  391.5 43.4 %collective-permute-start.30 = (bf16[4096,512]{1,0:T(8,128)(2,1)}, bf16[4096,512]{1,0:T(8,128)(2,1)}, u32[]{:S(2)}, u32[]{:S(2)}) collective-permute-start(bf16[4096,512]{1,0:T(8,128)(2,1)} %convolution_convert_fusion), channel_id=1, source_target_pairs={{0,8},{8,0},{16,24},{24,16},{1,9},{9,1},{17,25},{25,17},{2,10},{10... | collective-permute-start | bytes 12582920 | tf_op jit(solution)/shard_map/ppermute | solution.py:16
  399.4 40.1 %collective-permute-start.31 = (bf16[1024,2048]{1,0:T(8,128)(2,1)}, bf16[1024,2048]{1,0:T(8,128)(2,1)}, u32[]{:S(2)}, u32[]{:S(2)}) collective-permute-start(bf16[1024,2048]{1,0:T(8,128)(2,1)} %convolution_convert_fusion.2), channel_id=1, source_target_pairs={{0,8},{8,0},{16,24},{24,16},{1,9},{9,1},{17,25},{25,17},{2,10},{10... | collective-permute-start | bytes 12582920 | tf_op jit(solution)/shard_map/ppermute | solution.py:16
  403.8 25.1 %collective-permute-start.32 = (bf16[1024,512]{1,0:T(8,128)(2,1)}, bf16[1024,512]{1,0:T(8,128)(2,1)}, u32[]{:S(2)}, u32[]{:S(2)}) collective-permute-start(bf16[1024,512]{1,0:T(8,128)(2,1)} %convolution_convert_fusion.8), channel_id=1, source_target_pairs={{0,8},{8,0},{16,24},{24,16},{1,9},{9,1},{17,25},{25,17},{2,10},{10... | collective-permute-start | bytes 3145736 | tf_op jit(solution)/shard_map/ppermute | solution.py:16
  421.9 106.4 %all-to-all-start.3 = ((bf16[8,2,128,1024]{3,2,1,0:T(8,128)(2,1)}), bf16[8,2,128,1024]{3,2,1,0:T(8,128)(2,1)}, u32[]{:S(2)}, u32[]{:S(2)}) async-start(bf16[8,2,128,1024]{3,2,1,0:T(8,128)(2,1)} %get-tuple-element.139), calls=%async_computation.3 | async-start | bytes 8388608 | tf_op jit(solution)/shard_map/all_to_all | solution.py:649
  431.4 115.4 %collective-permute-start.35 = (bf16[1024,256]{1,0:T(8,128)(2,1)}, bf16[1024,256]{1,0:T(8,128)(2,1)}, u32[]{:S(2)}, u32[]{:S(2)}) collective-permute-start(bf16[1024,256]{1,0:T(8,128)(2,1)} %add_convert_fusion.26), channel_id=1, source_target_pairs={{0,16},{8,24},{16,0},{24,8},{1,17},{9,25},{17,1},{25,9},{2,18},{10... | collective-permute-start | bytes 1572872 | tf_op jit(solution)/shard_map/ppermute | solution.py:16
  439.3 87.4 %collective-permute-start.33 = (bf16[4096,256]{1,0:T(8,128)(2,1)}, bf16[4096,256]{1,0:T(8,128)(2,1)S(1)}, u32[]{:S(2)}, u32[]{:S(2)}) collective-permute-start(bf16[4096,256]{1,0:T(8,128)(2,1)} %add_convert_fusion.5), channel_id=1, source_target_pairs={{0,16},{8,24},{16,0},{24,8},{1,17},{9,25},{17,1},{25,9},{2,18},{10... | collective-permute-start | bytes 6291464 | tf_op jit(solution)/shard_map/ppermute | solution.py:16
  444.1 94.8 %collective-permute-start.34 = (bf16[1024,1024]{1,0:T(8,128)(2,1)}, bf16[1024,1024]{1,0:T(8,128)(2,1)}, u32[]{:S(2)}, u32[]{:S(2)}) collective-permute-start(bf16[1024,1024]{1,0:T(8,128)(2,1)} %add_convert_fusion.4), channel_id=1, source_target_pairs={{0,16},{8,24},{16,0},{24,8},{1,17},{9,25},{17,1},{25,9},{2,18},{10... | collective-permute-start | bytes 6291464 | tf_op jit(solution)/shard_map/ppermute | solution.py:16
  491.3 34.1 %collective-permute-start.36 = (bf16[1024,512]{1,0:T(8,128)(2,1)S(1)}, bf16[1024,512]{1,0:T(8,128)(2,1)S(1)}, u32[]{:S(2)}, u32[]{:S(2)}) collective-permute-start(bf16[1024,512]{1,0:T(8,128)(2,1)S(1)} %convolution_convert_fusion.7), channel_id=1, source_target_pairs={{0,8},{8,0},{16,24},{24,16},{1,9},{9,1},{17,25},{25,17},{2,10},{10... | collective-permute-start | bytes 3145736 | tf_op jit(solution)/shard_map/ppermute | solution.py:16
  528.3 154.2 %all-to-all-start.4 = ((bf16[8,2,128,1024]{3,2,1,0:T(8,128)(2,1)}), bf16[8,2,128,1024]{3,2,1,0:T(8,128)(2,1)}, u32[]{:S(2)}, u32[]{:S(2)}) async-start(bf16[8,2,128,1024]{3,2,1,0:T(8,128)(2,1)} %get-tuple-element.144), calls=%async_computation.4 | async-start | bytes 8388608 | tf_op jit(solution)/shard_map/all_to_all | solution.py:649
  537.5 21.9 %collective-permute-start.37 = (bf16[1024,1024]{1,0:T(8,128)(2,1)}, bf16[1024,1024]{1,0:T(8,128)(2,1)}, u32[]{:S(2)}, u32[]{:S(2)}) collective-permute-start(bf16[1024,1024]{1,0:T(8,128)(2,1)} %pad_maximum_fusion.3), channel_id=1, source_target_pairs={{0,8},{8,0},{16,24},{24,16},{1,9},{9,1},{17,25},{25,17},{2,10},{10... | collective-permute-start | bytes 6291464 | tf_op jit(solution)/shard_map/ppermute | solution.py:16
  569.4 15.6 %collective-permute-start.39 = (bf16[1024,1536]{0,1:T(8,128)(2,1)}, bf16[1024,1536]{0,1:T(8,128)(2,1)}, u32[]{:S(2)}, u32[]{:S(2)}) collective-permute-start(bf16[1024,1536]{0,1:T(8,128)(2,1)} %fusion.7), channel_id=1, source_target_pairs={{0,8},{8,0},{16,24},{24,16},{1,9},{9,1},{17,25},{25,17},{2,10},{10... | collective-permute-start | bytes 9437192 | tf_op jit(solution)/shard_map/ppermute | solution.py:16
  573.5 8.8 %collective-permute-start.40 = (bf16[1024,512]{1,0:T(8,128)(2,1)}, bf16[1024,512]{1,0:T(8,128)(2,1)}, u32[]{:S(2)}, u32[]{:S(2)}) collective-permute-start(bf16[1024,512]{1,0:T(8,128)(2,1)} %pad_maximum_fusion.12), channel_id=1, source_target_pairs={{0,8},{8,0},{16,24},{24,16},{1,9},{9,1},{17,25},{25,17},{2,10},{10... | collective-permute-start | bytes 3145736 | tf_op jit(solution)/shard_map/ppermute | solution.py:16
  573.7 71.1 %collective-permute-start.53 = (bf16[4,9,128,256]{3,2,1,0:T(8,128)(2,1)}, bf16[4,9,128,256]{3,2,1,0:T(8,128)(2,1)}, u32[]{:S(2)}, u32[]{:S(2)}) collective-permute-start(bf16[4,9,128,256]{3,2,1,0:T(8,128)(2,1)} %get-tuple-element.241), channel_id=1, source_target_pairs={{0,1},{1,0},{2,3},{3,2},{4,5},{5,4},{6,7},{7,6},{8,9},{9,8},{10,11... | collective-permute-start | bytes 7077896 | tf_op jit(solution)/shard_map/ppermute | solution.py:16
  582.2 77.1 %collective-permute-start.42 = (bf16[8,3,128,256]{3,2,1,0:T(8,128)(2,1)}, bf16[8,3,128,256]{3,2,1,0:T(8,128)(2,1)}, u32[]{:S(2)}, u32[]{:S(2)}) collective-permute-start(bf16[8,3,128,256]{3,2,1,0:T(8,128)(2,1)} %pad_maximum_fusion.8), channel_id=1, source_target_pairs={{0,16},{8,24},{16,0},{24,8},{1,17},{9,25},{17,1},{25,9},{2,18},{10... | collective-permute-start | bytes 4718600 | tf_op jit(solution)/shard_map/ppermute | solution.py:16
  600.6 77.3 %collective-permute-start.41 = (bf16[8,5,128,256]{3,2,1,0:T(8,128)(2,1)}, bf16[8,5,128,256]{3,2,1,0:T(8,128)(2,1)}, u32[]{:S(2)}, u32[]{:S(2)}) collective-permute-start(bf16[8,5,128,256]{3,2,1,0:T(8,128)(2,1)} %constant_dynamic-update-slice_fusion.19), channel_id=1, source_target_pairs={{0,16},{8,24},{16,0},{24,8},{1,17},{9,25},{17,1},{25,9},{2,18},{10... | collective-permute-start | bytes 7864328 | tf_op jit(solution)/shard_map/ppermute | solution.py:16
  649.3 34.7 %collective-permute-start.54 = (bf16[9,128,256]{2,1,0:T(8,128)(2,1)}, bf16[9,128,256]{2,1,0:T(8,128)(2,1)}, u32[]{:S(2)}, u32[]{:S(2)}) collective-permute-start(bf16[9,128,256]{2,1,0:T(8,128)(2,1)} %get-tuple-element.217), channel_id=1, source_target_pairs={{0,2},{1,3},{8,10},{9,11},{16,18},{17,19},{24,26},{25,27}} | collective-permute-start | bytes 1769480 | tf_op jit(solution)/shard_map/ppermute | solution.py:16
  657.7 30.6 %collective-permute-start.57 = (bf16[9,128,256]{2,1,0:T(8,128)(2,1)}, bf16[9,128,256]{2,1,0:T(8,128)(2,1)}, u32[]{:S(2)}, u32[]{:S(2)}) collective-permute-start(bf16[9,128,256]{2,1,0:T(8,128)(2,1)} %get-tuple-element.218), channel_id=1, source_target_pairs={{6,4},{7,5},{14,12},{15,13},{22,20},{23,21},{30,28},{31,29}} | collective-permute-start | bytes 1769480 | tf_op jit(solution)/shard_map/ppermute | solution.py:16
  662.6 23.6 %collective-permute-start.44 = (bf16[4,3,128,256]{3,2,0,1:T(8,128)(2,1)}, bf16[4,3,128,256]{3,2,0,1:T(8,128)(2,1)}, u32[]{:S(2)}, u32[]{:S(2)}) collective-permute-start(bf16[4,3,128,256]{3,2,0,1:T(8,128)(2,1)} %get-tuple-element.230), channel_id=1, source_target_pairs={{0,1},{1,0},{2,3},{3,2},{4,5},{5,4},{6,7},{7,6},{8,9},{9,8},{10,11... | collective-permute-start | bytes 2359304 | tf_op jit(solution)/shard_map/ppermute | solution.py:16
  682.5 29.0 %collective-permute-start.43 = (bf16[4,5,128,256]{3,2,0,1:T(8,128)(2,1)}, bf16[4,5,128,256]{3,2,0,1:T(8,128)(2,1)}, u32[]{:S(2)}, u32[]{:S(2)}) collective-permute-start(bf16[4,5,128,256]{3,2,0,1:T(8,128)(2,1)} %fusion.23), channel_id=1, source_target_pairs={{0,1},{1,0},{2,3},{3,2},{4,5},{5,4},{6,7},{7,6},{8,9},{9,8},{10,11... | collective-permute-start | bytes 3932168 | tf_op jit(solution)/shard_map/ppermute | solution.py:16
  686.2 12.3 %collective-permute-start.55 = (bf16[9,128,256]{2,1,0:T(8,128)(2,1)}, bf16[9,128,256]{2,1,0:T(8,128)(2,1)}, u32[]{:S(2)}, u32[]{:S(2)}) collective-permute-start(bf16[9,128,256]{2,1,0:T(8,128)(2,1)} %fusion.26), channel_id=1, source_target_pairs={{0,2},{1,3},{2,4},{3,5},{8,10},{9,11},{10,12},{11,13},{16,18},{17,... | collective-permute-start | bytes 1769480 | tf_op jit(solution)/shard_map/ppermute | solution.py:16
  701.3 18.3 %collective-permute-start.58 = (bf16[9,128,256]{2,1,0:T(8,128)(2,1)S(1)}, bf16[9,128,256]{2,1,0:T(8,128)(2,1)S(1)}, u32[]{:S(2)}, u32[]{:S(2)}) collective-permute-start(bf16[9,128,256]{2,1,0:T(8,128)(2,1)S(1)} %get-tuple-element.153), channel_id=1, source_target_pairs={{4,2},{5,3},{6,4},{7,5},{12,10},{13,11},{14,12},{15,13},{20,18},{2... | collective-permute-start | bytes 1769480 | tf_op jit(solution)/shard_map/ppermute | solution.py:16
  717.5 10.6 %collective-permute-start.45 = (bf16[8,128,256]{2,1,0:T(8,128)(2,1)}, bf16[8,128,256]{2,1,0:T(8,128)(2,1)}, u32[]{:S(2)}, u32[]{:S(2)}) collective-permute-start(bf16[8,128,256]{2,1,0:T(8,128)(2,1)} %get-tuple-element.226), channel_id=1, source_target_pairs={{0,2},{1,3},{8,10},{9,11},{16,18},{17,19},{24,26},{25,27}} | collective-permute-start | bytes 1572872 | tf_op jit(solution)/shard_map/ppermute | solution.py:16
  721.6 19.1 %collective-permute-start.56 = (bf16[9,128,256]{2,1,0:T(8,128)(2,1)}, bf16[9,128,256]{2,1,0:T(8,128)(2,1)}, u32[]{:S(2)}, u32[]{:S(2)}) collective-permute-start(bf16[9,128,256]{2,1,0:T(8,128)(2,1)} %get-tuple-element.152), channel_id=1, source_target_pairs={{0,2},{1,3},{2,4},{3,5},{4,6},{5,7},{8,10},{9,11},{10,12},{11,13},... | collective-permute-start | bytes 1769480 | tf_op jit(solution)/shard_map/ppermute | solution.py:16
  723.7 17.0 %collective-permute-start.59 = (bf16[9,128,256]{2,1,0:T(8,128)(2,1)}, bf16[9,128,256]{2,1,0:T(8,128)(2,1)}, u32[]{:S(2)}, u32[]{:S(2)}) collective-permute-start(bf16[9,128,256]{2,1,0:T(8,128)(2,1)} %fusion.25), channel_id=1, source_target_pairs={{2,0},{3,1},{4,2},{5,3},{6,4},{7,5},{10,8},{11,9},{12,10},{13,11},... | collective-permute-start | bytes 1769480 | tf_op jit(solution)/shard_map/ppermute | solution.py:16
  725.0 18.2 %collective-permute-start.48 = (bf16[8,128,256]{2,1,0:T(8,128)(2,1)}, bf16[8,128,256]{2,1,0:T(8,128)(2,1)}, u32[]{:S(2)}, u32[]{:S(2)}) collective-permute-start(bf16[8,128,256]{2,1,0:T(8,128)(2,1)} %get-tuple-element.227), channel_id=1, source_target_pairs={{6,4},{7,5},{14,12},{15,13},{22,20},{23,21},{30,28},{31,29}} | collective-permute-start | bytes 1572872 | tf_op jit(solution)/shard_map/ppermute | solution.py:16
  730.2 21.8 %collective-permute-start.46 = (bf16[8,128,256]{2,1,0:T(8,128)(2,1)}, bf16[8,128,256]{2,1,0:T(8,128)(2,1)}, u32[]{:S(2)}, u32[]{:S(2)}) collective-permute-start(bf16[8,128,256]{2,1,0:T(8,128)(2,1)} %fusion.32), channel_id=1, source_target_pairs={{0,2},{1,3},{2,4},{3,5},{8,10},{9,11},{10,12},{11,13},{16,18},{17,... | collective-permute-start | bytes 1572872 | tf_op jit(solution)/shard_map/ppermute | solution.py:16
  743.1 12.1 %collective-permute-start.60 = (bf16[9,128,256]{2,1,0:T(8,128)(2,1)}, bf16[9,128,256]{2,1,0:T(8,128)(2,1)}, u32[]{:S(2)}, u32[]{:S(2)}) collective-permute-start(bf16[9,128,256]{2,1,0:T(8,128)(2,1)} %fusion.29), channel_id=1, source_target_pairs={{0,16},{8,24},{16,0},{24,8},{1,17},{9,25},{17,1},{25,9},{2,18},{10... | collective-permute-start | bytes 1769480 | tf_op jit(solution)/shard_map/ppermute | solution.py:16
  754.5 18.4 %collective-permute-start.49 = (bf16[8,128,256]{2,1,0:T(8,128)(2,1)S(1)}, bf16[8,128,256]{2,1,0:T(8,128)(2,1)S(1)}, u32[]{:S(2)}, u32[]{:S(2)}) collective-permute-start(bf16[8,128,256]{2,1,0:T(8,128)(2,1)S(1)} %get-tuple-element.225), channel_id=1, source_target_pairs={{4,2},{5,3},{6,4},{7,5},{12,10},{13,11},{14,12},{15,13},{20,18},{2... | collective-permute-start | bytes 1572872 | tf_op jit(solution)/shard_map/ppermute | solution.py:16
  757.6 34.1 %collective-permute-start.61 = (bf16[2,9,128,256]{3,2,1,0:T(8,128)(2,1)}, bf16[2,9,128,256]{3,2,1,0:T(8,128)(2,1)}, u32[]{:S(2)}, u32[]{:S(2)}) collective-permute-start(bf16[2,9,128,256]{3,2,1,0:T(8,128)(2,1)} %pad_maximum_fusion.11), channel_id=1, source_target_pairs={{0,8},{8,0},{16,24},{24,16},{1,9},{9,1},{17,25},{25,17},{2,10},{10... | collective-permute-start | bytes 3538952 | tf_op jit(solution)/shard_map/ppermute | solution.py:16
  768.8 15.8 %collective-permute-start.47 = (bf16[8,128,256]{2,1,0:T(8,128)(2,1)}, bf16[8,128,256]{2,1,0:T(8,128)(2,1)S(1)}, u32[]{:S(2)}, u32[]{:S(2)}) collective-permute-start(bf16[8,128,256]{2,1,0:T(8,128)(2,1)} %get-tuple-element.224), channel_id=1, source_target_pairs={{0,2},{1,3},{2,4},{3,5},{4,6},{5,7},{8,10},{9,11},{10,12},{11,13},... | collective-permute-start | bytes 1572872 | tf_op jit(solution)/shard_map/ppermute | solution.py:16
  774.2 16.1 %collective-permute-start.50 = (bf16[8,128,256]{2,1,0:T(8,128)(2,1)S(1)}, bf16[8,128,256]{2,1,0:T(8,128)(2,1)S(1)}, u32[]{:S(2)}, u32[]{:S(2)}) collective-permute-start(bf16[8,128,256]{2,1,0:T(8,128)(2,1)S(1)} %fusion.31), channel_id=1, source_target_pairs={{2,0},{3,1},{4,2},{5,3},{6,4},{7,5},{10,8},{11,9},{12,10},{13,11},... | collective-permute-start | bytes 1572872 | tf_op jit(solution)/shard_map/ppermute | solution.py:16
  791.5 12.7 %collective-permute-start.51 = (bf16[8,128,256]{2,1,0:T(8,128)(2,1)S(1)}, bf16[8,128,256]{2,1,0:T(8,128)(2,1)S(1)}, u32[]{:S(2)}, u32[]{:S(2)}) collective-permute-start(bf16[8,128,256]{2,1,0:T(8,128)(2,1)S(1)} %fusion.35), channel_id=1, source_target_pairs={{0,16},{8,24},{16,0},{24,8},{1,17},{9,25},{17,1},{25,9},{2,18},{10... | collective-permute-start | bytes 1572872 | tf_op jit(solution)/shard_map/ppermute | solution.py:16
  (98 other events, 822.2 us)

commit v5 on v4

--- a/solution.py
+++ b/solution.py
@@ -773,7 +773,7 @@
                 arrived.append(back_and_forth(tie(sent[i], cross_queries, line_two_y)))
             elif tuned and i > half:
                 arrived.append(
-                    back_and_forth(tie(sent[i], *arrived[half:], outs[half - 1], far_two_y))
+                    back_and_forth(tie(sent[i], *arrived[half:], outs[half - 1]))
                 )
             source = arrived[i]
             if tuned and i == item_count - 1:

time: 838 us -> 838 us (level)
  no operation moved by 1% of the time
where the time goes in v5:
time: 838 us; the launch traced here: 830 us
  Pallas kernels  195 us (23%)
  waiting for transfers between devices  169 us (20%)
  starting transfers between devices  137 us (16%)
  matrix products  123 us (15%)
  local copies, waits for them, and re-layouts  113 us (13%)
  other arithmetic  90.9 us (11%)
    ppermute x62, waiting for transfers between devices, move(): return lambda value: lax.ppermute(value, axis, pairs)  152 us
    ppermute x62, starting transfers between devices, move(): return lambda value: lax.ppermute(value, axis, pairs)  104 us
    dot_general x19, matrix products, dot_tn(): lax.dot_general(left, right, (((0,), (0,)), ((), ())), preferred_element_...  73.3 us
    pallas_call x4, Pallas kernels, cross_backward(): pl.pallas_call(cross_backward_kernel, out_shape=[jax.ShapeDtypeStruct(que...  71.5 us
    pallas_call x4, Pallas kernels, cross_forward(): pl.pallas_call(cross_forward_kernel, out_shape=[jax.ShapeDtypeStruct(quer...  61.5 us
    unnamed x246, local copies, waits for them, and re-layouts  52.3 us
    convert_element_type x16, other arithmetic, add_low(): return total.astype(BF)  34.2 us
    all_to_all x5, starting transfers between devices, back_and_forth(): lax.all_to_all(blocks, 'blk', split_axis=0, concat_axis=0, tiled=True)  33.4 us
  transfers between devices with their start and end apart: 67, of which 23 were waited for; matrix products, arithmetic and copies ran while one was open for 30% of the time, Pallas kernels for 17%

profile of v5, /device:TPU:1, one launch (start us, length us, event | category | flops | bytes accessed | tf_op | source)
XLA Modules:
  0.0 830.1 jit_solution(823335151912069747)
XLA Ops:
  6.1 4.1 collective-permute-start.2
  12.7 7.3 collective-permute-done.2
  41.1 9.8 %collective-permute-done.6 = bf16[128,1920]{1,0:T(8,128)(2,1)S(1)} collective-permute-done((bf16[128,1920]{1,0:T(8,128)(2,1)}, bf16[128,1920]{1,0:T(8,128)(2,1)S(1)}, u32[]{:S(2)}, u32[]{:S(2)}) %collective-permute-start.6) | collective-permute-done | bytes 491552 | tf_op jit(solution)/shard_map/ppermute | solution.py:16
  56.5 6.6 collective-permute-done.17
  67.3 4.8 stack.165
  73.3 8.5 %collective-permute-done.7.refs_7_ = bf16[3,128,1920]{2,1,0:T(8,128)(2,1)} collective-permute-done((bf16[3,128,1920]{2,1,0:T(8,128)(2,1)S(1)}, bf16[3,128,1920]{2,1,0:T(8,128)(2,1)}, u32[]{:S(2)}, u32[]{:S(2)}) %collective-permute-start.7) | collective-permute-done | bytes 1474592 | tf_op jit(solution)/shard_map/ppermute | solution.py:16
  84.0 10.4 %collective-permute-done.22 = bf16[128,2304]{1,0:T(8,128)(2,1)S(1)} collective-permute-done((bf16[128,2304]{1,0:T(8,128)(2,1)S(1)}, bf16[128,2304]{1,0:T(8,128)(2,1)S(1)}, u32[]{:S(2)}, u32[]{:S(2)}) %collective-permute-start.22) | collective-permute-done | bytes 589856 | tf_op jit(solution)/shard_map/ppermute | solution.py:16
  96.7 6.5 all-to-all-start
  106.3 11.2 %collective-permute-start.11 = (bf16[4,128,1920]{2,1,0:T(8,128)(2,1)S(1)}, bf16[4,128,1920]{2,1,0:T(8,128)(2,1)}, u32[]{:S(2)}, u32[]{:S(2)}) collective-permute-start(bf16[4,128,1920]{2,1,0:T(8,128)(2,1)S(1)} %pad_maximum_fusion.5.refs_6_), channel_id=1, source_target_pairs={{0,8},{8,0},{16,24},{24,16},{1,9},{9,1},{17,25},{25,17},{2,10},{10... | collective-permute-start | bytes 5898248 | tf_op jit(solution)/shard_map/ppermute | solution.py:16
  121.0 5.9 collective-permute-done.10.refs_9_
  126.9 11.6 %collective-permute-start.14 = (bf16[3,128,1920]{2,1,0:T(8,128)(2,1)}, bf16[3,128,1920]{2,1,0:T(8,128)(2,1)}, u32[]{:S(2)}, u32[]{:S(2)}) collective-permute-start(bf16[3,128,1920]{2,1,0:T(8,128)(2,1)} %collective-permute-done.10.refs_9_), channel_id=1, source_target_pairs={{0,8},{8,0},{16,24},{24,16},{1,9},{9,1},{17,25},{25,17},{2,10},{10... | collective-permute-start | bytes 4423688 | tf_op jit(solution)/shard_map/ppermute | solution.py:16
  140.0 4.8 slice_bitcast_fusion
  147.4 12.9 %place_rows.2 = (bf16[1024,128]{1,0:T(8,128)(2,1)}, bf16[1024,3072]{1,0:T(8,128)(2,1)}, bf16[1024,1024]{1,0:T(8,128)(2,1)}, bf16[1024,1024]{1,0:T(8,128)(2,1)}, bf16[1024,2048]{1,0:T(8,128)(2,1)}) custom-call(s32[10]{0:T(128)} %stack.136.refs_0_, bf16[128,128]{1,0:T(8,128)(2,1)} %get-tuple-element.278.refs_1_, bf16[128,3072]{1,0:T(8,128)(2,1)} %refs_2_.2, ...), custom_call_target="tpu_custom_call" | custom-call | bytes 29884416 | tf_op jit(solution)/shard_map/place_rows/pallas_call | solution.py:148
  161.1 7.6 multiply_convert_fusion.1
  168.7 6.1 self_forward.1
  181.8 4.5 collective-permute-done.23
  186.3 3.9 all-to-all-done
  190.3 10.3 %all-to-all-start.1 = ((bf16[8,128,1024]{2,1,0:T(8,128)(2,1)}), bf16[8,128,1024]{2,1,0:T(8,128)(2,1)}, u32[]{:S(2)}, u32[]{:S(2)}) async-start(bf16[8,128,1024]{2,1,0:T(8,128)(2,1)} %get-tuple-element.99), calls=%async_computation.1 | async-start | bytes 4194304 | tf_op jit(solution)/shard_map/all_to_all | solution.py:649
  205.3 4.9 fusion.163
  210.2 15.3 %cross_forward.4 = (bf16[128,1024]{1,0:T(8,128)(2,1)}, f32[8,1,256]{2,1,0:T(1,128)}, bf16[1024,2048]{1,0:T(8,128)(2,1)}, bf16[4,1024,1024]{2,1,0:T(8,128)(2,1)}) custom-call(s32[1]{0:T(128)} %get-tuple-element.281.lengths, bf16[128,1024]{1,0:T(8,128)(2,1)} %get-tuple-element.261.q_ref, bf16[1024,1024]{1,0:T(8,128)(2,1)} %bitcast.529, ...), custom_call_target="tpu_custom_call" | custom-call | flops 6442450944 | bytes 12582912 | tf_op jit(solution)/shard_map/cross_forward/pallas_call | solution.py:436
  225.5 15.4 %cross_forward.5 = (bf16[128,1024]{1,0:T(8,128)(2,1)}, f32[8,1,256]{2,1,0:T(1,128)}, bf16[1024,2048]{1,0:T(8,128)(2,1)}, bf16[4,1024,1024]{2,1,0:T(8,128)(2,1)}) custom-call(s32[1]{0:T(128)} %get-tuple-element.280.lengths, bf16[128,1024]{1,0:T(8,128)(2,1)} %get-tuple-element.260.q_ref, ...), custom_call_target="tpu_custom_call", output_to_operand_aliasing={{3}: (5, {})} | custom-call | flops 6442450944 | bytes 12582912 | tf_op jit(solution)/shard_map/cross_forward/pallas_call | solution.py:436
  240.9 6.5 all-to-all-done.1
  247.4 5.8 all-to-all-start.2
  253.2 3.0 pad_maximum_fusion.1.refs_4_
  257.6 3.2 pad_maximum_fusion.2.refs_6_
  262.1 15.4 %cross_forward.6 = (bf16[128,1024]{1,0:T(8,128)(2,1)}, f32[8,1,256]{2,1,0:T(1,128)}, bf16[1024,2048]{1,0:T(8,128)(2,1)}, bf16[4,1024,1024]{2,1,0:T(8,128)(2,1)}) custom-call(s32[1]{0:T(128)} %get-tuple-element.282.lengths, bf16[128,1024]{1,0:T(8,128)(2,1)} %get-tuple-element.259.q_ref, ...), custom_call_target="tpu_custom_call", output_to_operand_aliasing={{3}: (5, {})} | custom-call | flops 6442450944 | bytes 12582912 | tf_op jit(solution)/shard_map/cross_forward/pallas_call | solution.py:436
  277.5 16.1 %place_rows.3 = (bf16[1024,1024]{1,0:T(8,128)(2,1)}, bf16[1024,4096]{1,0:T(8,128)(2,1)}, bf16[4096,1024]{1,0:T(8,128)(2,1)}) custom-call(s32[10]{0:T(128)} %stack.136.refs_0_, bf16[128,1024]{1,0:T(8,128)(2,1)} %refs_1_.1, bf16[128,4096]{1,0:T(8,128)(2,1)} %refs_2_.3, bf16[512,1024]{1,0:T(8,128)(2,1)} %refs_3_.3, ...), custom_call_target="tpu_custom_call" | custom-call | bytes 37748736 | tf_op jit(solution)/shard_map/place_rows/pallas_call | solution.py:148
  293.7 6.4 all-to-all-done.2
  300.1 15.5 %cross_forward.7 = (bf16[128,1024]{1,0:T(8,128)(2,1)}, f32[8,1,256]{2,1,0:T(1,128)}, bf16[1024,2048]{1,0:T(8,128)(2,1)}, bf16[4,1024,1024]{2,1,0:T(8,128)(2,1)}) custom-call(s32[1]{0:T(128)} %get-tuple-element.279.lengths, bf16[128,1024]{1,0:T(8,128)(2,1)} %get-tuple-element.258.q_ref, ...), custom_call_target="tpu_custom_call", output_to_operand_aliasing={{3}: (5, {})} | custom-call | flops 6442450944 | bytes 12582912 | tf_op jit(solution)/shard_map/cross_forward/pallas_call | solution.py:436
  319.7 13.0 %fusion.6 = (bf16[512,4096]{1,0:T(8,128)(2,1)}, bf16[512,4096]{1,0:T(8,128)(2,1)S(1)}) fusion(f32[4096]{0:T(1024)S(1)} %convert.92, bf16[512,1024]{1,0:T(8,128)(2,1)S(1)} %fusion.18, bf16[1024,4096]{1,0:T(8,128)(2,1)S(1)} %bitcast.595), kind=kOutput, calls=%fused_computation.8 | convolution fusion | flops 4351590400 | bytes 17842176 | tf_op jit(solution)/shard_map/dot_general | solution.py:800
  332.8 4.8 fusion.175
  342.8 15.8 %feed_backward.1 = (bf16[512,4096]{1,0:T(8,128)(2,1)}, f32[1,4096]{1,0:T(1,128)}, f32[512,1024]{1,0:T(8,128)}) custom-call(bf16[512,1024]{1,0:T(8,128)(2,1)} %add_convert_fusion.16.grad_ref, bf16[4096,1024]{1,0:T(8,128)(2,1)} %get-tuple-element.110.down_ref, bf16[512,4096]{1,0:T(8,128)(2,1)} %get-tuple-element.170.slope_ref, ...), custom_call_target="tpu_custom_call" | custom-call | flops 8589934592 | bytes 25165824 | tf_op jit(solution)/shard_map/feed_backward/pallas_call | solution.py:532
  366.5 18.2 %cross_backward.4 = (bf16[128,1024]{1,0:T(8,128)(2,1)}, f32[1,1024]{1,0:T(1,128)}, bf16[4,1024,2048]{2,1,0:T(8,128)(2,1)}, bf16[8,2,128,1024]{3,2,1,0:T(8,128)(2,1)}) custom-call(s32[1]{0:T(128)} %get-tuple-element.281.lengths, bf16[128,1024]{1,0:T(8,128)(2,1)} %get-tuple-element.261.q_ref, bf16[128,1024]{1,0:T(8,128)(2,1)} %get-tuple-element.254.grad_ref, ...), custom_call_target="tpu_custom_call" | custom-call | flops 9663676416 | bytes 18874368 | tf_op jit(solution)/shard_map/cross_backward/pallas_call | solution.py:475
  384.8 6.7 convolution_convert_fusion
  395.0 4.4 convolution_convert_fusion.2
  400.8 3.0 convolution_convert_fusion.8
  404.3 17.6 %cross_backward.5 = (bf16[128,1024]{1,0:T(8,128)(2,1)}, f32[1,1024]{1,0:T(1,128)}, bf16[4,1024,2048]{2,1,0:T(8,128)(2,1)}, bf16[8,2,128,1024]{3,2,1,0:T(8,128)(2,1)}) custom-call(s32[1]{0:T(128)} %get-tuple-element.280.lengths, bf16[128,1024]{1,0:T(8,128)(2,1)} %get-tuple-element.260.q_ref, ...), custom_call_target="tpu_custom_call", output_to_operand_aliasing={{2}: (6, {}), {3}: (7, {})} | custom-call | flops 9663676416 | bytes 18874368 | tf_op jit(solution)/shard_map/cross_backward/pallas_call | solution.py:475
  421.9 4.9 all-to-all-start.3
  435.0 4.4 add_convert_fusion.5
  439.6 4.6 add_convert_fusion.4
  445.4 17.7 %cross_backward.6 = (bf16[128,1024]{1,0:T(8,128)(2,1)}, f32[1,1024]{1,0:T(1,128)}, bf16[4,1024,2048]{2,1,0:T(8,128)(2,1)}, bf16[8,2,128,1024]{3,2,1,0:T(8,128)(2,1)}) custom-call(s32[1]{0:T(128)} %get-tuple-element.282.lengths, bf16[128,1024]{1,0:T(8,128)(2,1)} %get-tuple-element.259.q_ref, ...), custom_call_target="tpu_custom_call", output_to_operand_aliasing={{2}: (6, {})} | custom-call | flops 9663676416 | bytes 18874368 | tf_op jit(solution)/shard_map/cross_backward/pallas_call | solution.py:475
  463.1 17.9 %cross_backward.7 = (bf16[128,1024]{1,0:T(8,128)(2,1)}, f32[1,1024]{1,0:T(1,128)}, bf16[4,1024,2048]{2,1,0:T(8,128)(2,1)}, bf16[8,2,128,1024]{3,2,1,0:T(8,128)(2,1)}) custom-call(s32[1]{0:T(128)} %get-tuple-element.279.lengths, bf16[128,1024]{1,0:T(8,128)(2,1)} %get-tuple-element.258.q_ref, ...), custom_call_target="tpu_custom_call", output_to_operand_aliasing={{2}: (6, {}), {3}: (7, {})} | custom-call | flops 9663676416 | bytes 18874368 | tf_op jit(solution)/shard_map/cross_backward/pallas_call | solution.py:475
  482.8 4.0 multiply_reduce_fusion.1
  492.3 21.3 %bitcast_convert_fusion = bf16[1024,2048]{1,0:T(8,128)(2,1)} fusion(bf16[4,1024,1024]{2,1,0:T(8,128)(2,1)} %get-tuple-element.137, bf16[4,1024,2048]{2,1,0:T(8,128)(2,1)S(1)} %copy-done.87), kind=kOutput, calls=%fused_computation.10 | convolution fusion | flops 17181966336 | bytes 29360128 | tf_op jit(solution)/shard_map/dot_general | solution.py:293
  515.3 3.2 add_convert_fusion.2
  528.3 5.9 all-to-all-start.4
  548.8 10.7 %self_backward.1 = bf16[4,128,3072]{2,1,0:T(8,128)(2,1)} custom-call(s32[4,1,128]{2,1,0:T(1,128)} %bitcast.566, s32[4,128,1]{2,1,0:T(8,128)} %copy.117.seg_column, bf16[4,128,3072]{2,1,0:T(8,128)(2,1)} %bitcast.502, bf16[4,128,1024]{2,1,0:T(8,128)(2,1)} %bitcast.541, f32[4,8,1,256]{3,2,1,0:T(1,128)} %get-tuple-element.142.log_ref), custom_call_target="tpu_custom_call" | custom-call | tf_op jit(solution)/shard_map/self_backward/pallas_call | solution.py:622
  565.9 3.5 fusion.7
  604.1 40.7 %collective-permute-done.53 = bf16[4,9,128,256]{3,2,1,0:T(8,128)(2,1)} collective-permute-done((bf16[4,9,128,256]{3,2,1,0:T(8,128)(2,1)}, bf16[4,9,128,256]{3,2,1,0:T(8,128)(2,1)}, u32[]{:S(2)}, u32[]{:S(2)}) %collective-permute-start.53) | collective-permute-done | bytes 2359328 | tf_op jit(solution)/shard_map/ppermute | solution.py:16
  644.8 3.3 add_convert_fusion
  649.3 8.4 %collective-permute-start.54 = (bf16[9,128,256]{2,1,0:T(8,128)(2,1)}, bf16[9,128,256]{2,1,0:T(8,128)(2,1)}, u32[]{:S(2)}, u32[]{:S(2)}) collective-permute-start(bf16[9,128,256]{2,1,0:T(8,128)(2,1)} %get-tuple-element.217), channel_id=1, source_target_pairs={{0,2},{1,3},{8,10},{9,11},{16,18},{17,19},{24,26},{25,27}} | collective-permute-start | bytes 1769480 | tf_op jit(solution)/shard_map/ppermute | solution.py:16
  677.9 3.1 constant_dynamic-slice_fusion.13
  688.3 10.2 %collective-permute-done.55 = bf16[9,128,256]{2,1,0:T(8,128)(2,1)} collective-permute-done((bf16[9,128,256]{2,1,0:T(8,128)(2,1)}, bf16[9,128,256]{2,1,0:T(8,128)(2,1)}, u32[]{:S(2)}, u32[]{:S(2)}) %collective-permute-start.55) | collective-permute-done | bytes 589856 | tf_op jit(solution)/shard_map/ppermute | solution.py:16
  703.9 7.6 collective-permute-done.43
  711.5 3.7 add_convert_fusion.1
  730.2 5.1 collective-permute-start.46
  735.3 5.4 collective-permute-done.56
  743.3 8.7 %collective-permute-done.46 = bf16[8,128,256]{2,1,0:T(8,128)(2,1)} collective-permute-done((bf16[8,128,256]{2,1,0:T(8,128)(2,1)}, bf16[8,128,256]{2,1,0:T(8,128)(2,1)}, u32[]{:S(2)}, u32[]{:S(2)}) %collective-permute-start.46) | collective-permute-done | bytes 524320 | tf_op jit(solution)/shard_map/ppermute | solution.py:16
  757.6 4.0 collective-permute-start.61
  761.6 7.2 add_convert_fusion.10
  768.8 4.1 collective-permute-start.47
  775.5 7.6 pad_maximum_fusion
  784.6 5.6 collective-permute-done.50
  793.9 10.3 %collective-permute-done.51 = bf16[8,128,256]{2,1,0:T(8,128)(2,1)S(1)} collective-permute-done((bf16[8,128,256]{2,1,0:T(8,128)(2,1)S(1)}, bf16[8,128,256]{2,1,0:T(8,128)(2,1)S(1)}, u32[]{:S(2)}, u32[]{:S(2)}) %collective-permute-start.51) | collective-permute-done | bytes 524320 | tf_op jit(solution)/shard_map/ppermute | solution.py:16
  (522 shorter events, 266.2 us)
Async XLA Ops:
  6.1 13.9 %collective-permute-start.2 = (bf16[128,1920]{1,0:T(8,128)(2,1)S(1)}, bf16[128,1920]{1,0:T(8,128)(2,1)S(1)}, u32[]{:S(2)}, u32[]{:S(2)}) collective-permute-start(bf16[128,1920]{1,0:T(8,128)(2,1)S(1)} %constant_dynamic-update-slice_fusion), channel_id=1, source_target_pairs={{0,2},{1,3},{2,4},{3,5},{4,6},{5,7},{8,10},{9,11},{10,12},{11,13},... | collective-permute-start | bytes 1474568 | tf_op jit(solution)/shard_map/ppermute | solution.py:16
  10.2 13.7 %collective-permute-start.1 = (bf16[128,1920]{1,0:T(8,128)(2,1)S(1)}, bf16[128,1920]{1,0:T(8,128)(2,1)S(1)}, u32[]{:S(2)}, u32[]{:S(2)}) collective-permute-start(bf16[128,1920]{1,0:T(8,128)(2,1)S(1)} %constant_dynamic-update-slice_fusion), channel_id=1, source_target_pairs={{2,0},{3,1},{4,2},{5,3},{6,4},{7,5},{10,8},{11,9},{12,10},{13,11},... | collective-permute-start | bytes 1474568 | tf_op jit(solution)/shard_map/ppermute | solution.py:16
  11.5 19.8 %collective-permute-start = (bf16[128,1920]{1,0:T(8,128)(2,1)S(1)}, bf16[128,1920]{1,0:T(8,128)(2,1)S(1)}, u32[]{:S(2)}, u32[]{:S(2)}) collective-permute-start(bf16[128,1920]{1,0:T(8,128)(2,1)S(1)} %constant_dynamic-update-slice_fusion), channel_id=1, source_target_pairs={{0,1},{1,0},{2,3},{3,2},{4,5},{5,4},{6,7},{7,6},{8,9},{9,8},{10,11... | collective-permute-start | bytes 1474568 | tf_op jit(solution)/shard_map/ppermute | solution.py:16
  20.0 11.2 %collective-permute-start.3 = (bf16[128,1920]{1,0:T(8,128)(2,1)S(1)}, bf16[128,1920]{1,0:T(8,128)(2,1)S(1)}, u32[]{:S(2)}, u32[]{:S(2)}) collective-permute-start(bf16[128,1920]{1,0:T(8,128)(2,1)S(1)} %collective-permute-done.2), channel_id=1, source_target_pairs={{2,4},{3,5},{4,6},{5,7},{10,12},{11,13},{12,14},{13,15},{18,20},{1... | collective-permute-start | bytes 1474568 | tf_op jit(solution)/shard_map/ppermute | solution.py:16
  23.8 14.8 %collective-permute-start.5 = (bf16[128,1920]{1,0:T(8,128)(2,1)S(1)}, bf16[128,1920]{1,0:T(8,128)(2,1)}, u32[]{:S(2)}, u32[]{:S(2)}) collective-permute-start(bf16[128,1920]{1,0:T(8,128)(2,1)S(1)} %collective-permute-done.1), channel_id=1, source_target_pairs={{2,0},{3,1},{4,2},{5,3},{10,8},{11,9},{12,10},{13,11},{18,16},{19,... | collective-permute-start | bytes 1474568 | tf_op jit(solution)/shard_map/ppermute | solution.py:16
  31.2 9.8 %collective-permute-start.4 = (bf16[128,1920]{1,0:T(8,128)(2,1)S(1)}, bf16[128,1920]{1,0:T(8,128)(2,1)}, u32[]{:S(2)}, u32[]{:S(2)}) collective-permute-start(bf16[128,1920]{1,0:T(8,128)(2,1)S(1)} %collective-permute-done.3), channel_id=1, source_target_pairs={{4,6},{5,7},{12,14},{13,15},{20,22},{21,23},{28,30},{29,31}} | collective-permute-start | bytes 1474568 | tf_op jit(solution)/shard_map/ppermute | solution.py:16
  34.1 18.4 %collective-permute-start.15 = (bf16[128,2304]{1,0:T(8,128)(2,1)}, bf16[128,2304]{1,0:T(8,128)(2,1)S(1)}, u32[]{:S(2)}, u32[]{:S(2)}) collective-permute-start(bf16[128,2304]{1,0:T(8,128)(2,1)} %constant_dynamic-update-slice_fusion.4), channel_id=1, source_target_pairs={{0,1},{1,0},{2,3},{3,2},{4,5},{5,4},{6,7},{7,6},{8,9},{9,8},{10,11... | collective-permute-start | bytes 1769480 | tf_op jit(solution)/shard_map/ppermute | solution.py:16
  35.4 17.2 %collective-permute-start.8 = (bf16[128,1920]{1,0:T(8,128)(2,1)S(1)}, bf16[128,1920]{1,0:T(8,128)(2,1)S(1)}, u32[]{:S(2)}, u32[]{:S(2)}) collective-permute-start(bf16[128,1920]{1,0:T(8,128)(2,1)S(1)} %collective-permute-done), channel_id=1, source_target_pairs={{0,16},{8,24},{16,0},{24,8},{1,17},{9,25},{17,1},{25,9},{2,18},{10... | collective-permute-start | bytes 1474568 | tf_op jit(solution)/shard_map/ppermute | solution.py:16
  38.6 12.3 %collective-permute-start.6 = (bf16[128,1920]{1,0:T(8,128)(2,1)}, bf16[128,1920]{1,0:T(8,128)(2,1)S(1)}, u32[]{:S(2)}, u32[]{:S(2)}) collective-permute-start(bf16[128,1920]{1,0:T(8,128)(2,1)} %collective-permute-done.5), channel_id=1, source_target_pairs={{2,0},{3,1},{10,8},{11,9},{18,16},{19,17},{26,24},{27,25}} | collective-permute-start | bytes 1474568 | tf_op jit(solution)/shard_map/ppermute | solution.py:16
  51.3 30.6 %collective-permute-start.7 = (bf16[3,128,1920]{2,1,0:T(8,128)(2,1)S(1)}, bf16[3,128,1920]{2,1,0:T(8,128)(2,1)}, u32[]{:S(2)}, u32[]{:S(2)}) collective-permute-start(bf16[3,128,1920]{2,1,0:T(8,128)(2,1)S(1)} %pad_maximum_fusion.10), channel_id=1, source_target_pairs={{0,1},{1,0},{2,3},{3,2},{4,5},{5,4},{6,7},{7,6},{8,9},{9,8},{10,11... | collective-permute-start | bytes 4423688 | tf_op jit(solution)/shard_map/ppermute | solution.py:16
  52.6 10.6 %collective-permute-start.17 = (bf16[128,2304]{1,0:T(8,128)(2,1)}, bf16[128,2304]{1,0:T(8,128)(2,1)S(1)}, u32[]{:S(2)}, u32[]{:S(2)}) collective-permute-start(bf16[128,2304]{1,0:T(8,128)(2,1)} %constant_dynamic-update-slice_fusion.4), channel_id=1, source_target_pairs={{0,2},{1,3},{2,4},{3,5},{4,6},{5,7},{8,10},{9,11},{10,12},{11,13},... | collective-permute-start | bytes 1769480 | tf_op jit(solution)/shard_map/ppermute | solution.py:16
  53.9 12.1 %collective-permute-start.16 = (bf16[128,2304]{1,0:T(8,128)(2,1)}, bf16[128,2304]{1,0:T(8,128)(2,1)S(1)}, u32[]{:S(2)}, u32[]{:S(2)}) collective-permute-start(bf16[128,2304]{1,0:T(8,128)(2,1)} %constant_dynamic-update-slice_fusion.4), channel_id=1, source_target_pairs={{2,0},{3,1},{4,2},{5,3},{6,4},{7,5},{10,8},{11,9},{12,10},{13,11},... | collective-permute-start | bytes 1769480 | tf_op jit(solution)/shard_map/ppermute | solution.py:16
  55.2 18.1 %collective-permute-start.19 = (bf16[128,2304]{1,0:T(8,128)(2,1)S(1)}, bf16[128,2304]{1,0:T(8,128)(2,1)S(1)}, u32[]{:S(2)}, u32[]{:S(2)}) collective-permute-start(bf16[128,2304]{1,0:T(8,128)(2,1)S(1)} %collective-permute-done.15), channel_id=1, source_target_pairs={{0,16},{8,24},{16,0},{24,8},{1,17},{9,25},{17,1},{25,9},{2,18},{10... | collective-permute-start | bytes 1769480 | tf_op jit(solution)/shard_map/ppermute | solution.py:16
  63.1 10.2 %collective-permute-start.18 = (bf16[128,2304]{1,0:T(8,128)(2,1)S(1)}, bf16[128,2304]{1,0:T(8,128)(2,1)S(1)}, u32[]{:S(2)}, u32[]{:S(2)}) collective-permute-start(bf16[128,2304]{1,0:T(8,128)(2,1)S(1)} %collective-permute-done.17), channel_id=1, source_target_pairs={{2,4},{3,5},{4,6},{5,7},{10,12},{11,13},{12,14},{13,15},{18,20},{1... | collective-permute-start | bytes 1769480 | tf_op jit(solution)/shard_map/ppermute | solution.py:16
  66.0 16.5 %collective-permute-start.21 = (bf16[128,2304]{1,0:T(8,128)(2,1)S(1)}, bf16[128,2304]{1,0:T(8,128)(2,1)S(1)}, u32[]{:S(2)}, u32[]{:S(2)}) collective-permute-start(bf16[128,2304]{1,0:T(8,128)(2,1)S(1)} %collective-permute-done.16), channel_id=1, source_target_pairs={{2,0},{3,1},{4,2},{5,3},{10,8},{11,9},{12,10},{13,11},{18,16},{19,... | collective-permute-start | bytes 1769480 | tf_op jit(solution)/shard_map/ppermute | solution.py:16
  72.1 24.6 %collective-permute-start.9 = (bf16[3,128,1920]{2,1,0:T(8,128)(2,1)S(1)}, bf16[3,128,1920]{2,1,0:T(8,128)(2,1)}, u32[]{:S(2)}, u32[]{:S(2)}) collective-permute-start(bf16[3,128,1920]{2,1,0:T(8,128)(2,1)S(1)} %pad_maximum_fusion.10), channel_id=1, source_target_pairs={{0,16},{8,24},{16,0},{24,8},{1,17},{9,25},{17,1},{25,9},{2,18},{10... | collective-permute-start | bytes 4423688 | tf_op jit(solution)/shard_map/ppermute | solution.py:16
  82.6 11.8 %collective-permute-start.22 = (bf16[128,2304]{1,0:T(8,128)(2,1)S(1)}, bf16[128,2304]{1,0:T(8,128)(2,1)S(1)}, u32[]{:S(2)}, u32[]{:S(2)}) collective-permute-start(bf16[128,2304]{1,0:T(8,128)(2,1)S(1)} %collective-permute-done.21), channel_id=1, source_target_pairs={{2,0},{3,1},{10,8},{11,9},{18,16},{19,17},{26,24},{27,25}} | collective-permute-start | bytes 1769480 | tf_op jit(solution)/shard_map/ppermute | solution.py:16
  96.7 93.6 %all-to-all-start = ((bf16[8,2,128,1024]{3,2,1,0:T(8,128)(2,1)}), bf16[8,2,128,1024]{3,2,1,0:T(8,128)(2,1)}, u32[]{:S(2)}, u32[]{:S(2)}) async-start(bf16[8,2,128,1024]{3,2,1,0:T(8,128)(2,1)} %stack.165), calls=%async_computation | async-start | bytes 8388608 | tf_op jit(solution)/shard_map/all_to_all | solution.py:649
  103.2 23.7 %collective-permute-start.10 = (bf16[3,128,1920]{2,1,0:T(8,128)(2,1)}, bf16[3,128,1920]{2,1,0:T(8,128)(2,1)}, u32[]{:S(2)}, u32[]{:S(2)}) collective-permute-start(bf16[3,128,1920]{2,1,0:T(8,128)(2,1)} %collective-permute-done.7.refs_7_), channel_id=1, source_target_pairs={{0,16},{8,24},{16,0},{24,8},{1,17},{9,25},{17,1},{25,9},{2,18},{10... | collective-permute-start | bytes 4423688 | tf_op jit(solution)/shard_map/ppermute | solution.py:16
  106.3 39.8 %collective-permute-start.11 = (bf16[4,128,1920]{2,1,0:T(8,128)(2,1)S(1)}, bf16[4,128,1920]{2,1,0:T(8,128)(2,1)}, u32[]{:S(2)}, u32[]{:S(2)}) collective-permute-start(bf16[4,128,1920]{2,1,0:T(8,128)(2,1)S(1)} %pad_maximum_fusion.5.refs_6_), channel_id=1, source_target_pairs={{0,8},{8,0},{16,24},{24,16},{1,9},{9,1},{17,25},{25,17},{2,10},{10... | collective-permute-start | bytes 5898248 | tf_op jit(solution)/shard_map/ppermute | solution.py:16
  120.4 26.9 %collective-permute-start.13 = (bf16[4,128,1920]{2,1,0:T(8,128)(2,1)}, bf16[4,128,1920]{2,1,0:T(8,128)(2,1)}, u32[]{:S(2)}, u32[]{:S(2)}) collective-permute-start(bf16[4,128,1920]{2,1,0:T(8,128)(2,1)} %pad_maximum_fusion.6.refs_8_), channel_id=1, source_target_pairs={{0,8},{8,0},{16,24},{24,16},{1,9},{9,1},{17,25},{25,17},{2,10},{10... | collective-permute-start | bytes 5898248 | tf_op jit(solution)/shard_map/ppermute | solution.py:16
  121.0 26.3 %collective-permute-start.12 = (bf16[3,128,1920]{2,1,0:T(8,128)(2,1)}, bf16[3,128,1920]{2,1,0:T(8,128)(2,1)}, u32[]{:S(2)}, u32[]{:S(2)}) collective-permute-start(bf16[3,128,1920]{2,1,0:T(8,128)(2,1)} %collective-permute-done.7.refs_7_), channel_id=1, source_target_pairs={{0,8},{8,0},{16,24},{24,16},{1,9},{9,1},{17,25},{25,17},{2,10},{10... | collective-permute-start | bytes 4423688 | tf_op jit(solution)/shard_map/ppermute | solution.py:16
  126.9 20.4 %collective-permute-start.14 = (bf16[3,128,1920]{2,1,0:T(8,128)(2,1)}, bf16[3,128,1920]{2,1,0:T(8,128)(2,1)}, u32[]{:S(2)}, u32[]{:S(2)}) collective-permute-start(bf16[3,128,1920]{2,1,0:T(8,128)(2,1)} %collective-permute-done.10.refs_9_), channel_id=1, source_target_pairs={{0,8},{8,0},{16,24},{24,16},{1,9},{9,1},{17,25},{25,17},{2,10},{10... | collective-permute-start | bytes 4423688 | tf_op jit(solution)/shard_map/ppermute | solution.py:16
  144.8 56.5 %collective-permute-start.24 = (bf16[3,128,2304]{2,1,0:T(8,128)(2,1)}, bf16[3,128,2304]{2,1,0:T(8,128)(2,1)}, u32[]{:S(2)}, u32[]{:S(2)}) collective-permute-start(bf16[3,128,2304]{2,1,0:T(8,128)(2,1)} %pad_maximum_fusion.7), channel_id=1, source_target_pairs={{0,1},{1,0},{2,3},{3,2},{4,5},{5,4},{6,7},{7,6},{8,9},{9,8},{10,11... | collective-permute-start | bytes 5308424 | tf_op jit(solution)/shard_map/ppermute | solution.py:16
  146.1 40.2 %collective-permute-start.23 = (bf16[3,128,2304]{2,1,0:T(8,128)(2,1)}, bf16[3,128,2304]{2,1,0:T(8,128)(2,1)}, u32[]{:S(2)}, u32[]{:S(2)}) collective-permute-start(bf16[3,128,2304]{2,1,0:T(8,128)(2,1)} %pad_maximum_fusion.7), channel_id=1, source_target_pairs={{0,16},{8,24},{16,0},{24,8},{1,17},{9,25},{17,1},{25,9},{2,18},{10... | collective-permute-start | bytes 5308424 | tf_op jit(solution)/shard_map/ppermute | solution.py:16
  190.3 57.1 %all-to-all-start.1 = ((bf16[8,128,1024]{2,1,0:T(8,128)(2,1)}), bf16[8,128,1024]{2,1,0:T(8,128)(2,1)}, u32[]{:S(2)}, u32[]{:S(2)}) async-start(bf16[8,128,1024]{2,1,0:T(8,128)(2,1)} %get-tuple-element.99), calls=%async_computation.1 | async-start | bytes 4194304 | tf_op jit(solution)/shard_map/all_to_all | solution.py:649
  201.3 60.0 %collective-permute-start.25 = (bf16[3,128,2304]{2,1,0:T(8,128)(2,1)}, bf16[3,128,2304]{2,1,0:T(8,128)(2,1)}, u32[]{:S(2)}, u32[]{:S(2)}) collective-permute-start(bf16[3,128,2304]{2,1,0:T(8,128)(2,1)} %collective-permute-done.24.refs_5_), channel_id=1, source_target_pairs={{0,16},{8,24},{16,0},{24,8},{1,17},{9,25},{17,1},{25,9},{2,18},{10... | collective-permute-start | bytes 5308424 | tf_op jit(solution)/shard_map/ppermute | solution.py:16
  247.4 52.8 %all-to-all-start.2 = ((bf16[8,128,1024]{2,1,0:T(8,128)(2,1)}), bf16[8,128,1024]{2,1,0:T(8,128)(2,1)}, u32[]{:S(2)}, u32[]{:S(2)}) async-start(bf16[8,128,1024]{2,1,0:T(8,128)(2,1)} %get-tuple-element.102), calls=%async_computation.2 | async-start | bytes 4194304 | tf_op jit(solution)/shard_map/all_to_all | solution.py:649
  256.2 21.3 %collective-permute-start.26 = (bf16[4,128,2304]{2,1,0:T(8,128)(2,1)}, bf16[4,128,2304]{2,1,0:T(8,128)(2,1)}, u32[]{:S(2)}, u32[]{:S(2)}) collective-permute-start(bf16[4,128,2304]{2,1,0:T(8,128)(2,1)} %pad_maximum_fusion.1.refs_4_), channel_id=1, source_target_pairs={{0,8},{8,0},{16,24},{24,16},{1,9},{9,1},{17,25},{25,17},{2,10},{10... | collective-permute-start | bytes 7077896 | tf_op jit(solution)/shard_map/ppermute | solution.py:16
  260.8 16.7 %collective-permute-start.28 = (bf16[4,128,2304]{2,1,0:T(8,128)(2,1)}, bf16[4,128,2304]{2,1,0:T(8,128)(2,1)}, u32[]{:S(2)}, u32[]{:S(2)}) collective-permute-start(bf16[4,128,2304]{2,1,0:T(8,128)(2,1)} %pad_maximum_fusion.2.refs_6_), channel_id=1, source_target_pairs={{0,8},{8,0},{16,24},{24,16},{1,9},{9,1},{17,25},{25,17},{2,10},{10... | collective-permute-start | bytes 7077896 | tf_op jit(solution)/shard_map/ppermute | solution.py:16
  260.8 16.7 %collective-permute-start.27 = (bf16[3,128,2304]{2,1,0:T(8,128)(2,1)}, bf16[3,128,2304]{2,1,0:T(8,128)(2,1)}, u32[]{:S(2)}, u32[]{:S(2)}) collective-permute-start(bf16[3,128,2304]{2,1,0:T(8,128)(2,1)} %collective-permute-done.24.refs_5_), channel_id=1, source_target_pairs={{0,8},{8,0},{16,24},{24,16},{1,9},{9,1},{17,25},{25,17},{2,10},{10... | collective-permute-start | bytes 5308424 | tf_op jit(solution)/shard_map/ppermute | solution.py:16
  261.3 16.2 %collective-permute-start.29 = (bf16[3,128,2304]{2,1,0:T(8,128)(2,1)}, bf16[3,128,2304]{2,1,0:T(8,128)(2,1)}, u32[]{:S(2)}, u32[]{:S(2)}) collective-permute-start(bf16[3,128,2304]{2,1,0:T(8,128)(2,1)} %collective-permute-done.25.refs_7_), channel_id=1, source_target_pairs={{0,8},{8,0},{16,24},{24,16},{1,9},{9,1},{17,25},{25,17},{2,10},{10... | collective-permute-start | bytes 5308424 | tf_op jit(solution)/shard_map/ppermute | solution.py:16
  391.5 43.4 %collective-permute-start.30 = (bf16[4096,512]{1,0:T(8,128)(2,1)}, bf16[4096,512]{1,0:T(8,128)(2,1)}, u32[]{:S(2)}, u32[]{:S(2)}) collective-permute-start(bf16[4096,512]{1,0:T(8,128)(2,1)} %convolution_convert_fusion), channel_id=1, source_target_pairs={{0,8},{8,0},{16,24},{24,16},{1,9},{9,1},{17,25},{25,17},{2,10},{10... | collective-permute-start | bytes 12582920 | tf_op jit(solution)/shard_map/ppermute | solution.py:16
  399.4 40.1 %collective-permute-start.31 = (bf16[1024,2048]{1,0:T(8,128)(2,1)}, bf16[1024,2048]{1,0:T(8,128)(2,1)}, u32[]{:S(2)}, u32[]{:S(2)}) collective-permute-start(bf16[1024,2048]{1,0:T(8,128)(2,1)} %convolution_convert_fusion.2), channel_id=1, source_target_pairs={{0,8},{8,0},{16,24},{24,16},{1,9},{9,1},{17,25},{25,17},{2,10},{10... | collective-permute-start | bytes 12582920 | tf_op jit(solution)/shard_map/ppermute | solution.py:16
  403.8 25.1 %collective-permute-start.32 = (bf16[1024,512]{1,0:T(8,128)(2,1)}, bf16[1024,512]{1,0:T(8,128)(2,1)}, u32[]{:S(2)}, u32[]{:S(2)}) collective-permute-start(bf16[1024,512]{1,0:T(8,128)(2,1)} %convolution_convert_fusion.8), channel_id=1, source_target_pairs={{0,8},{8,0},{16,24},{24,16},{1,9},{9,1},{17,25},{25,17},{2,10},{10... | collective-permute-start | bytes 3145736 | tf_op jit(solution)/shard_map/ppermute | solution.py:16
  421.9 106.4 %all-to-all-start.3 = ((bf16[8,2,128,1024]{3,2,1,0:T(8,128)(2,1)}), bf16[8,2,128,1024]{3,2,1,0:T(8,128)(2,1)}, u32[]{:S(2)}, u32[]{:S(2)}) async-start(bf16[8,2,128,1024]{3,2,1,0:T(8,128)(2,1)} %get-tuple-element.139), calls=%async_computation.3 | async-start | bytes 8388608 | tf_op jit(solution)/shard_map/all_to_all | solution.py:649
  431.4 115.4 %collective-permute-start.35 = (bf16[1024,256]{1,0:T(8,128)(2,1)}, bf16[1024,256]{1,0:T(8,128)(2,1)}, u32[]{:S(2)}, u32[]{:S(2)}) collective-permute-start(bf16[1024,256]{1,0:T(8,128)(2,1)} %add_convert_fusion.26), channel_id=1, source_target_pairs={{0,16},{8,24},{16,0},{24,8},{1,17},{9,25},{17,1},{25,9},{2,18},{10... | collective-permute-start | bytes 1572872 | tf_op jit(solution)/shard_map/ppermute | solution.py:16
  439.3 87.4 %collective-permute-start.33 = (bf16[4096,256]{1,0:T(8,128)(2,1)}, bf16[4096,256]{1,0:T(8,128)(2,1)S(1)}, u32[]{:S(2)}, u32[]{:S(2)}) collective-permute-start(bf16[4096,256]{1,0:T(8,128)(2,1)} %add_convert_fusion.5), channel_id=1, source_target_pairs={{0,16},{8,24},{16,0},{24,8},{1,17},{9,25},{17,1},{25,9},{2,18},{10... | collective-permute-start | bytes 6291464 | tf_op jit(solution)/shard_map/ppermute | solution.py:16
  444.1 94.8 %collective-permute-start.34 = (bf16[1024,1024]{1,0:T(8,128)(2,1)}, bf16[1024,1024]{1,0:T(8,128)(2,1)}, u32[]{:S(2)}, u32[]{:S(2)}) collective-permute-start(bf16[1024,1024]{1,0:T(8,128)(2,1)} %add_convert_fusion.4), channel_id=1, source_target_pairs={{0,16},{8,24},{16,0},{24,8},{1,17},{9,25},{17,1},{25,9},{2,18},{10... | collective-permute-start | bytes 6291464 | tf_op jit(solution)/shard_map/ppermute | solution.py:16
  491.3 34.1 %collective-permute-start.36 = (bf16[1024,512]{1,0:T(8,128)(2,1)S(1)}, bf16[1024,512]{1,0:T(8,128)(2,1)S(1)}, u32[]{:S(2)}, u32[]{:S(2)}) collective-permute-start(bf16[1024,512]{1,0:T(8,128)(2,1)S(1)} %convolution_convert_fusion.7), channel_id=1, source_target_pairs={{0,8},{8,0},{16,24},{24,16},{1,9},{9,1},{17,25},{25,17},{2,10},{10... | collective-permute-start | bytes 3145736 | tf_op jit(solution)/shard_map/ppermute | solution.py:16
  528.3 154.2 %all-to-all-start.4 = ((bf16[8,2,128,1024]{3,2,1,0:T(8,128)(2,1)}), bf16[8,2,128,1024]{3,2,1,0:T(8,128)(2,1)}, u32[]{:S(2)}, u32[]{:S(2)}) async-start(bf16[8,2,128,1024]{3,2,1,0:T(8,128)(2,1)} %get-tuple-element.144), calls=%async_computation.4 | async-start | bytes 8388608 | tf_op jit(solution)/shard_map/all_to_all | solution.py:649
  537.5 21.9 %collective-permute-start.37 = (bf16[1024,1024]{1,0:T(8,128)(2,1)}, bf16[1024,1024]{1,0:T(8,128)(2,1)}, u32[]{:S(2)}, u32[]{:S(2)}) collective-permute-start(bf16[1024,1024]{1,0:T(8,128)(2,1)} %pad_maximum_fusion.3), channel_id=1, source_target_pairs={{0,8},{8,0},{16,24},{24,16},{1,9},{9,1},{17,25},{25,17},{2,10},{10... | collective-permute-start | bytes 6291464 | tf_op jit(solution)/shard_map/ppermute | solution.py:16
  569.4 15.6 %collective-permute-start.39 = (bf16[1024,1536]{0,1:T(8,128)(2,1)}, bf16[1024,1536]{0,1:T(8,128)(2,1)}, u32[]{:S(2)}, u32[]{:S(2)}) collective-permute-start(bf16[1024,1536]{0,1:T(8,128)(2,1)} %fusion.7), channel_id=1, source_target_pairs={{0,8},{8,0},{16,24},{24,16},{1,9},{9,1},{17,25},{25,17},{2,10},{10... | collective-permute-start | bytes 9437192 | tf_op jit(solution)/shard_map/ppermute | solution.py:16
  573.5 8.8 %collective-permute-start.40 = (bf16[1024,512]{1,0:T(8,128)(2,1)}, bf16[1024,512]{1,0:T(8,128)(2,1)}, u32[]{:S(2)}, u32[]{:S(2)}) collective-permute-start(bf16[1024,512]{1,0:T(8,128)(2,1)} %pad_maximum_fusion.12), channel_id=1, source_target_pairs={{0,8},{8,0},{16,24},{24,16},{1,9},{9,1},{17,25},{25,17},{2,10},{10... | collective-permute-start | bytes 3145736 | tf_op jit(solution)/shard_map/ppermute | solution.py:16
  573.7 71.1 %collective-permute-start.53 = (bf16[4,9,128,256]{3,2,1,0:T(8,128)(2,1)}, bf16[4,9,128,256]{3,2,1,0:T(8,128)(2,1)}, u32[]{:S(2)}, u32[]{:S(2)}) collective-permute-start(bf16[4,9,128,256]{3,2,1,0:T(8,128)(2,1)} %get-tuple-element.241), channel_id=1, source_target_pairs={{0,1},{1,0},{2,3},{3,2},{4,5},{5,4},{6,7},{7,6},{8,9},{9,8},{10,11... | collective-permute-start | bytes 7077896 | tf_op jit(solution)/shard_map/ppermute | solution.py:16
  582.2 77.1 %collective-permute-start.42 = (bf16[8,3,128,256]{3,2,1,0:T(8,128)(2,1)}, bf16[8,3,128,256]{3,2,1,0:T(8,128)(2,1)}, u32[]{:S(2)}, u32[]{:S(2)}) collective-permute-start(bf16[8,3,128,256]{3,2,1,0:T(8,128)(2,1)} %pad_maximum_fusion.8), channel_id=1, source_target_pairs={{0,16},{8,24},{16,0},{24,8},{1,17},{9,25},{17,1},{25,9},{2,18},{10... | collective-permute-start | bytes 4718600 | tf_op jit(solution)/shard_map/ppermute | solution.py:16
  600.6 77.3 %collective-permute-start.41 = (bf16[8,5,128,256]{3,2,1,0:T(8,128)(2,1)}, bf16[8,5,128,256]{3,2,1,0:T(8,128)(2,1)}, u32[]{:S(2)}, u32[]{:S(2)}) collective-permute-start(bf16[8,5,128,256]{3,2,1,0:T(8,128)(2,1)} %constant_dynamic-update-slice_fusion.19), channel_id=1, source_target_pairs={{0,16},{8,24},{16,0},{24,8},{1,17},{9,25},{17,1},{25,9},{2,18},{10... | collective-permute-start | bytes 7864328 | tf_op jit(solution)/shard_map/ppermute | solution.py:16
  649.3 34.7 %collective-permute-start.54 = (bf16[9,128,256]{2,1,0:T(8,128)(2,1)}, bf16[9,128,256]{2,1,0:T(8,128)(2,1)}, u32[]{:S(2)}, u32[]{:S(2)}) collective-permute-start(bf16[9,128,256]{2,1,0:T(8,128)(2,1)} %get-tuple-element.217), channel_id=1, source_target_pairs={{0,2},{1,3},{8,10},{9,11},{16,18},{17,19},{24,26},{25,27}} | collective-permute-start | bytes 1769480 | tf_op jit(solution)/shard_map/ppermute | solution.py:16
  657.7 30.6 %collective-permute-start.57 = (bf16[9,128,256]{2,1,0:T(8,128)(2,1)}, bf16[9,128,256]{2,1,0:T(8,128)(2,1)}, u32[]{:S(2)}, u32[]{:S(2)}) collective-permute-start(bf16[9,128,256]{2,1,0:T(8,128)(2,1)} %get-tuple-element.218), channel_id=1, source_target_pairs={{6,4},{7,5},{14,12},{15,13},{22,20},{23,21},{30,28},{31,29}} | collective-permute-start | bytes 1769480 | tf_op jit(solution)/shard_map/ppermute | solution.py:16
  662.6 23.6 %collective-permute-start.44 = (bf16[4,3,128,256]{3,2,0,1:T(8,128)(2,1)}, bf16[4,3,128,256]{3,2,0,1:T(8,128)(2,1)}, u32[]{:S(2)}, u32[]{:S(2)}) collective-permute-start(bf16[4,3,128,256]{3,2,0,1:T(8,128)(2,1)} %get-tuple-element.230), channel_id=1, source_target_pairs={{0,1},{1,0},{2,3},{3,2},{4,5},{5,4},{6,7},{7,6},{8,9},{9,8},{10,11... | collective-permute-start | bytes 2359304 | tf_op jit(solution)/shard_map/ppermute | solution.py:16
  682.5 29.0 %collective-permute-start.43 = (bf16[4,5,128,256]{3,2,0,1:T(8,128)(2,1)}, bf16[4,5,128,256]{3,2,0,1:T(8,128)(2,1)}, u32[]{:S(2)}, u32[]{:S(2)}) collective-permute-start(bf16[4,5,128,256]{3,2,0,1:T(8,128)(2,1)} %fusion.23), channel_id=1, source_target_pairs={{0,1},{1,0},{2,3},{3,2},{4,5},{5,4},{6,7},{7,6},{8,9},{9,8},{10,11... | collective-permute-start | bytes 3932168 | tf_op jit(solution)/shard_map/ppermute | solution.py:16
  686.2 12.3 %collective-permute-start.55 = (bf16[9,128,256]{2,1,0:T(8,128)(2,1)}, bf16[9,128,256]{2,1,0:T(8,128)(2,1)}, u32[]{:S(2)}, u32[]{:S(2)}) collective-permute-start(bf16[9,128,256]{2,1,0:T(8,128)(2,1)} %fusion.26), channel_id=1, source_target_pairs={{0,2},{1,3},{2,4},{3,5},{8,10},{9,11},{10,12},{11,13},{16,18},{17,... | collective-permute-start | bytes 1769480 | tf_op jit(solution)/shard_map/ppermute | solution.py:16
  701.3 18.3 %collective-permute-start.58 = (bf16[9,128,256]{2,1,0:T(8,128)(2,1)S(1)}, bf16[9,128,256]{2,1,0:T(8,128)(2,1)S(1)}, u32[]{:S(2)}, u32[]{:S(2)}) collective-permute-start(bf16[9,128,256]{2,1,0:T(8,128)(2,1)S(1)} %get-tuple-element.153), channel_id=1, source_target_pairs={{4,2},{5,3},{6,4},{7,5},{12,10},{13,11},{14,12},{15,13},{20,18},{2... | collective-permute-start | bytes 1769480 | tf_op jit(solution)/shard_map/ppermute | solution.py:16
  717.5 10.6 %collective-permute-start.45 = (bf16[8,128,256]{2,1,0:T(8,128)(2,1)}, bf16[8,128,256]{2,1,0:T(8,128)(2,1)}, u32[]{:S(2)}, u32[]{:S(2)}) collective-permute-start(bf16[8,128,256]{2,1,0:T(8,128)(2,1)} %get-tuple-element.226), channel_id=1, source_target_pairs={{0,2},{1,3},{8,10},{9,11},{16,18},{17,19},{24,26},{25,27}} | collective-permute-start | bytes 1572872 | tf_op jit(solution)/shard_map/ppermute | solution.py:16
  721.6 19.1 %collective-permute-start.56 = (bf16[9,128,256]{2,1,0:T(8,128)(2,1)}, bf16[9,128,256]{2,1,0:T(8,128)(2,1)}, u32[]{:S(2)}, u32[]{:S(2)}) collective-permute-start(bf16[9,128,256]{2,1,0:T(8,128)(2,1)} %get-tuple-element.152), channel_id=1, source_target_pairs={{0,2},{1,3},{2,4},{3,5},{4,6},{5,7},{8,10},{9,11},{10,12},{11,13},... | collective-permute-start | bytes 1769480 | tf_op jit(solution)/shard_map/ppermute | solution.py:16
  723.7 17.0 %collective-permute-start.59 = (bf16[9,128,256]{2,1,0:T(8,128)(2,1)}, bf16[9,128,256]{2,1,0:T(8,128)(2,1)}, u32[]{:S(2)}, u32[]{:S(2)}) collective-permute-start(bf16[9,128,256]{2,1,0:T(8,128)(2,1)} %fusion.25), channel_id=1, source_target_pairs={{2,0},{3,1},{4,2},{5,3},{6,4},{7,5},{10,8},{11,9},{12,10},{13,11},... | collective-permute-start | bytes 1769480 | tf_op jit(solution)/shard_map/ppermute | solution.py:16
  725.0 18.2 %collective-permute-start.48 = (bf16[8,128,256]{2,1,0:T(8,128)(2,1)}, bf16[8,128,256]{2,1,0:T(8,128)(2,1)}, u32[]{:S(2)}, u32[]{:S(2)}) collective-permute-start(bf16[8,128,256]{2,1,0:T(8,128)(2,1)} %get-tuple-element.227), channel_id=1, source_target_pairs={{6,4},{7,5},{14,12},{15,13},{22,20},{23,21},{30,28},{31,29}} | collective-permute-start | bytes 1572872 | tf_op jit(solution)/shard_map/ppermute | solution.py:16
  730.2 21.8 %collective-permute-start.46 = (bf16[8,128,256]{2,1,0:T(8,128)(2,1)}, bf16[8,128,256]{2,1,0:T(8,128)(2,1)}, u32[]{:S(2)}, u32[]{:S(2)}) collective-permute-start(bf16[8,128,256]{2,1,0:T(8,128)(2,1)} %fusion.32), channel_id=1, source_target_pairs={{0,2},{1,3},{2,4},{3,5},{8,10},{9,11},{10,12},{11,13},{16,18},{17,... | collective-permute-start | bytes 1572872 | tf_op jit(solution)/shard_map/ppermute | solution.py:16
  743.1 12.1 %collective-permute-start.60 = (bf16[9,128,256]{2,1,0:T(8,128)(2,1)}, bf16[9,128,256]{2,1,0:T(8,128)(2,1)}, u32[]{:S(2)}, u32[]{:S(2)}) collective-permute-start(bf16[9,128,256]{2,1,0:T(8,128)(2,1)} %fusion.29), channel_id=1, source_target_pairs={{0,16},{8,24},{16,0},{24,8},{1,17},{9,25},{17,1},{25,9},{2,18},{10... | collective-permute-start | bytes 1769480 | tf_op jit(solution)/shard_map/ppermute | solution.py:16
  754.5 18.4 %collective-permute-start.49 = (bf16[8,128,256]{2,1,0:T(8,128)(2,1)S(1)}, bf16[8,128,256]{2,1,0:T(8,128)(2,1)S(1)}, u32[]{:S(2)}, u32[]{:S(2)}) collective-permute-start(bf16[8,128,256]{2,1,0:T(8,128)(2,1)S(1)} %get-tuple-element.225), channel_id=1, source_target_pairs={{4,2},{5,3},{6,4},{7,5},{12,10},{13,11},{14,12},{15,13},{20,18},{2... | collective-permute-start | bytes 1572872 | tf_op jit(solution)/shard_map/ppermute | solution.py:16
  757.6 34.1 %collective-permute-start.61 = (bf16[2,9,128,256]{3,2,1,0:T(8,128)(2,1)}, bf16[2,9,128,256]{3,2,1,0:T(8,128)(2,1)}, u32[]{:S(2)}, u32[]{:S(2)}) collective-permute-start(bf16[2,9,128,256]{3,2,1,0:T(8,128)(2,1)} %pad_maximum_fusion.11), channel_id=1, source_target_pairs={{0,8},{8,0},{16,24},{24,16},{1,9},{9,1},{17,25},{25,17},{2,10},{10... | collective-permute-start | bytes 3538952 | tf_op jit(solution)/shard_map/ppermute | solution.py:16
  768.8 15.8 %collective-permute-start.47 = (bf16[8,128,256]{2,1,0:T(8,128)(2,1)}, bf16[8,128,256]{2,1,0:T(8,128)(2,1)S(1)}, u32[]{:S(2)}, u32[]{:S(2)}) collective-permute-start(bf16[8,128,256]{2,1,0:T(8,128)(2,1)} %get-tuple-element.224), channel_id=1, source_target_pairs={{0,2},{1,3},{2,4},{3,5},{4,6},{5,7},{8,10},{9,11},{10,12},{11,13},... | collective-permute-start | bytes 1572872 | tf_op jit(solution)/shard_map/ppermute | solution.py:16
  774.2 16.1 %collective-permute-start.50 = (bf16[8,128,256]{2,1,0:T(8,128)(2,1)S(1)}, bf16[8,128,256]{2,1,0:T(8,128)(2,1)S(1)}, u32[]{:S(2)}, u32[]{:S(2)}) collective-permute-start(bf16[8,128,256]{2,1,0:T(8,128)(2,1)S(1)} %fusion.31), channel_id=1, source_target_pairs={{2,0},{3,1},{4,2},{5,3},{6,4},{7,5},{10,8},{11,9},{12,10},{13,11},... | collective-permute-start | bytes 1572872 | tf_op jit(solution)/shard_map/ppermute | solution.py:16
  791.5 12.7 %collective-permute-start.51 = (bf16[8,128,256]{2,1,0:T(8,128)(2,1)S(1)}, bf16[8,128,256]{2,1,0:T(8,128)(2,1)S(1)}, u32[]{:S(2)}, u32[]{:S(2)}) collective-permute-start(bf16[8,128,256]{2,1,0:T(8,128)(2,1)S(1)} %fusion.35), channel_id=1, source_target_pairs={{0,16},{8,24},{16,0},{24,8},{1,17},{9,25},{17,1},{25,9},{2,18},{10... | collective-permute-start | bytes 1572872 | tf_op jit(solution)/shard_map/ppermute | solution.py:16
  (98 other events, 822.2 us)
